TPU v7x, 128 devices: a whole 4x4x4 slice. The times are simulated.
128 devices in a mesh: ep: 32 (over z, x, core), tp: 4 (over y).
Axes of the slice: x: 4, y: 4, z: 4, core: 2. Of those that a mesh axis runs over, the one named last changes fastest.
Arguments:
- hidden_in: bfloat16 [32768, 1024], P(('ep', 'tp')), may hold values from -6 to 6
- segment_ids: int32 [32, 1024], P('ep'), may hold values from 0 to 3, never falling along the last dimension, each value on 1 to 512 neighbouring positions
- expert_ids: int32 [32768, 8], P(('ep', 'tp')), may hold values from 0 to 31, as said below
- slot_index: int32 [32768, 8], P(('ep', 'tp')), may hold values from 0 to 95, as said below
- attn_gain: bfloat16 [1024], replicated, may hold values from 0.5 to 1.5
- w_query: bfloat16 [1024, 1024], P(None, 'tp'), may hold values from -0.75 to 0.75
- w_key: bfloat16 [1024, 512], P(None, 'tp'), may hold values from -0.75 to 0.75
- w_value: bfloat16 [1024, 512], P(None, 'tp'), may hold values from -0.1875 to 0.1875
- w_output: bfloat16 [1024, 1024], P('tp'), may hold values from -3 to 3
- ffn_gain: bfloat16 [1024], replicated, may hold values from 0.5 to 1.5
- w_router: bfloat16 [1024, 32], replicated, may hold values from -0.09375 to 0.09375
- w_gate_up: bfloat16 [32, 1024, 2, 512], P('ep'), may hold values from -0.1875 to 0.1875
- w_down: bfloat16 [32, 512, 1024], P('ep'), may hold values from -6 to 6
- cotangent: bfloat16 [32768, 1024], P(('ep', 'tp')), may hold values from -6 to 6
Outputs:
- output: bfloat16 [32768, 1024], P(('ep', 'tp'))
- grad_hidden: float32 [32768, 1024], P(('ep', 'tp'))
- grad_attn_gain: float32 [1024], replicated
- grad_query: float32 [1024, 1024], P(None, 'tp')
- grad_key: float32 [1024, 512], P(None, 'tp')
- grad_value: float32 [1024, 512], P(None, 'tp')
- grad_output: float32 [1024, 1024], P('tp')
- grad_ffn_gain: float32 [1024], replicated
- grad_router: float32 [1024, 32], replicated
- grad_gate_up: float32 [32, 1024, 2, 512], P('ep')
- grad_down: float32 [32, 512, 1024], P('ep')
Inputs may be any that keep to these rules, and one draw needn't show every extreme that they name: `segment_ids`: segment numbers never fall along a sequence. `expert_ids`: each row names 8 different experts. Among the rows of one device (aligned blocks of 256 rows) no expert is named more than 96 times, and some expert is named exactly 96 times by the rows of every device. `slot_index`: within the rows of one device, the rows naming one expert hold distinct slots, numbered from 0 up to that count minus one.
All inputs are finite; a program needn't handle non-finite values.
Results may differ from a plain program's by a relative error of at most 0.024.
Values may be sent and summed in bfloat16 or wider, within the bound.
No kernel may reach another device: no remote copies, remote signals or barrier semaphores. Data moves between devices by JAX's collectives and lax.ppermute only.
A program may use at most 192 MiB of HBM per device.

v0:
```python
import jax
import jax.numpy as jnp
from jax import lax
from jax.sharding import PartitionSpec as P

H = 16
KVH = 8
HD = 64


ATT_SCALE = 0.015625
RES_SCALE = 0.22
NORM_EPS = 1e-06
ROPE_BASE = 10000.0
NEG_FILL = -1e30
HIGHEST = lax.Precision.HIGHEST


def rope_tables(length, width):
    halfway = width // 2
    freqs = ROPE_BASE ** (-jnp.arange(halfway, dtype=jnp.float32) * 2.0 / width)
    angles = jnp.arange(length, dtype=jnp.float32)[:, None] * freqs[None, :]
    cosine = jnp.concatenate([jnp.cos(angles), jnp.cos(angles)], axis=1)
    sine = jnp.concatenate([jnp.sin(angles), jnp.sin(angles)], axis=1)
    return (cosine, sine)


def rotate(vector, cosine, sine):
    halfway = vector.shape[-1] // 2
    turned = jnp.concatenate([-vector[..., halfway:], vector[..., :halfway]], axis=-1)
    return vector * cosine[:, None, :] + turned * sine[:, None, :]


def unrotate(vector, cosine, sine):
    halfway = vector.shape[-1] // 2
    moved = vector * sine[:, None, :]
    unturned = jnp.concatenate([moved[..., halfway:], -moved[..., :halfway]], axis=-1)
    return vector * cosine[:, None, :] + unturned


def norm_parts(vector, gain):
    inverse = lax.rsqrt(jnp.mean(vector * vector, axis=-1, keepdims=True) + NORM_EPS)
    plain = vector * inverse
    return (plain * gain, plain, inverse)


def norm_back(incoming, plain, inverse, gain):
    scaled = incoming * gain
    inner_mean = jnp.mean(scaled * plain, axis=-1, keepdims=True)
    return (inverse * (scaled - plain * inner_mean), jnp.sum(incoming * plain, axis=0))


def block_scores(query_block, keys_rot, segments_here, begin_row, positions, block_rows):
    query_pos = begin_row + jnp.arange(block_rows, dtype=jnp.int32)
    query_seg = lax.dynamic_slice_in_dim(segments_here, begin_row, block_rows, 0)
    allowed = (query_seg[:, None] == segments_here[None, :]) & (
        positions[None, :] <= query_pos[:, None]
    )
    scores = (
        jnp.einsum("qkgd,tkd->kgqt", query_block, keys_rot, preferred_element_type=jnp.float32)
        * ATT_SCALE
    )
    return jnp.where(allowed[None, None], scores, NEG_FILL)


def attention_forward(queries, keys_rot, values, segments_here):
    length = queries.shape[0]
    block_rows = min(512, length)
    positions = jnp.arange(length, dtype=jnp.int32)

    def one_block(begin_row):
        query_block = lax.dynamic_slice_in_dim(queries, begin_row, block_rows, 0)
        scores = block_scores(
            query_block, keys_rot, segments_here, begin_row, positions, block_rows
        )
        row_max = jnp.max(scores, axis=-1, keepdims=True)
        weights = jnp.exp(scores - row_max)
        row_sum = jnp.sum(weights, axis=-1, keepdims=True)
        probs = (weights / row_sum).astype(jnp.bfloat16)
        attended = jnp.einsum("kgqt,tkd->qkgd", probs, values, preferred_element_type=jnp.float32)
        return (attended.astype(jnp.bfloat16), (row_max + jnp.log(row_sum))[..., 0])

    begins = jnp.arange(length // block_rows) * block_rows
    attended, log_totals = lax.map(one_block, begins)
    return (attended.reshape(length, -1), log_totals)


def attention_backward(queries, keys_rot, values, segments_here, log_totals, grad_mixed):
    length = queries.shape[0]
    block_rows = min(512, length)
    positions = jnp.arange(length, dtype=jnp.int32)

    def one_block(carried, inputs):
        dkeys, dvalues = carried
        begin_row, block_totals = inputs
        query_block = lax.dynamic_slice_in_dim(queries, begin_row, block_rows, 0)
        grad_block = lax.dynamic_slice_in_dim(grad_mixed, begin_row, block_rows, 0)
        scores = block_scores(
            query_block, keys_rot, segments_here, begin_row, positions, block_rows
        )
        probs = jnp.exp(scores - block_totals[..., None])
        probs_low = probs.astype(jnp.bfloat16)
        dprobs = jnp.einsum(
            "qkgd,tkd->kgqt", grad_block, values, preferred_element_type=jnp.float32
        )
        dscores = (probs * (dprobs - jnp.sum(probs * dprobs, axis=-1, keepdims=True))).astype(
            jnp.bfloat16
        )
        dquery_block = (
            jnp.einsum("kgqt,tkd->qkgd", dscores, keys_rot, preferred_element_type=jnp.float32)
            * ATT_SCALE
        )
        dkeys = (
            dkeys
            + jnp.einsum("kgqt,qkgd->tkd", dscores, query_block, preferred_element_type=jnp.float32)
            * ATT_SCALE
        )
        dvalues = dvalues + jnp.einsum(
            "kgqt,qkgd->tkd", probs_low, grad_block, preferred_element_type=jnp.float32
        )
        return ((dkeys, dvalues), dquery_block)

    begins = jnp.arange(length // block_rows) * block_rows
    zero_init = jnp.zeros(keys_rot.shape, jnp.float32)
    (dkeys, dvalues), dqueries = lax.scan(one_block, (zero_init, zero_init), (begins, log_totals))
    return (dqueries.reshape(queries.shape), dkeys, dvalues)


def expert_apply(shaped, w_gate_up, w_down):
    gate_up = jnp.einsum("secd,edgf->secgf", shaped, w_gate_up, preferred_element_type=jnp.float32)
    inner_act = (jax.nn.silu(gate_up[..., 0, :]) * gate_up[..., 1, :]).astype(jnp.bfloat16)
    return jnp.einsum(
        "secf,efd->secd", inner_act, w_down, preferred_element_type=jnp.float32
    ).astype(jnp.bfloat16)


def shards(
    hidden_in,
    segment_ids,
    expert_ids,
    slot_index,
    attn_gain,
    w_query,
    w_key,
    w_value,
    w_output,
    ffn_gain,
    w_router,
    w_gate_up,
    w_down,
    cotangent,
):
    local_rows = hidden_in.shape[0]
    model_width = hidden_in.shape[1]
    group_rows = lax.all_gather(hidden_in, "tp", axis=0, tiled=True)
    length = group_rows.shape[0]
    segments_here = segment_ids[0]
    kv_local = w_key.shape[1] // HD
    group_size = H // KVH
    gain_one = attn_gain.astype(jnp.float32)
    gain_two = ffn_gain.astype(jnp.float32)
    normed, _, _ = norm_parts(group_rows.astype(jnp.float32), gain_one)
    normed_low = normed.astype(jnp.bfloat16)
    cosine, sine = rope_tables(length, HD)
    query_pre = jnp.dot(normed_low, w_query, preferred_element_type=jnp.float32).reshape(
        length, kv_local * group_size, HD
    )
    key_pre = jnp.dot(normed_low, w_key, preferred_element_type=jnp.float32).reshape(
        length, kv_local, HD
    )
    values = (
        jnp.dot(normed_low, w_value, preferred_element_type=jnp.float32)
        .astype(jnp.bfloat16)
        .reshape(length, kv_local, HD)
    )
    queries = (
        rotate(query_pre, cosine, sine)
        .astype(jnp.bfloat16)
        .reshape(length, kv_local, group_size, HD)
    )
    keys_rot = rotate(key_pre, cosine, sine).astype(jnp.bfloat16)
    mixed, log_totals = attention_forward(queries, keys_rot, values, segments_here)
    branch = lax.psum_scatter(
        jnp.dot(mixed, w_output, preferred_element_type=jnp.float32),
        "tp",
        scatter_dimension=0,
        tiled=True,
    )
    local_in = hidden_in.astype(jnp.float32)
    middle = local_in + RES_SCALE * branch
    routed, plain_two, inverse_two = norm_parts(middle, gain_two)
    routed_low = routed.astype(jnp.bfloat16)
    logits = jnp.dot(routed_low, w_router, preferred_element_type=jnp.float32)
    gates = jax.nn.softmax(jnp.take_along_axis(logits, expert_ids, axis=1), axis=-1)
    experts_all = w_router.shape[1]
    route_count = expert_ids.shape[1]
    capacity = 3 * local_rows * route_count // (2 * experts_all)
    flat_pos = (expert_ids * capacity + slot_index).reshape(-1)
    owners = (
        jnp.full((experts_all * capacity,), local_rows, jnp.int32)
        .at[flat_pos]
        .set(jnp.repeat(jnp.arange(local_rows, dtype=jnp.int32), route_count))
    )
    padded = jnp.concatenate([routed_low, jnp.zeros((1, model_width), jnp.bfloat16)], axis=0)
    outgoing = padded[owners].reshape(experts_all, capacity, model_width)
    local_experts = w_gate_up.shape[0]
    arrived_rows = lax.all_to_all(outgoing, "ep", split_axis=0, concat_axis=0, tiled=True)
    sources = lax.axis_size("ep")
    slots_here = arrived_rows.shape[1]
    shaped = arrived_rows.reshape(sources, local_experts, slots_here, model_width)
    produced = expert_apply(shaped, w_gate_up, w_down).reshape(
        sources * local_experts, slots_here, model_width
    )
    returned_rows = lax.all_to_all(produced, "ep", split_axis=0, concat_axis=0, tiled=True)
    picked = returned_rows.reshape(experts_all * capacity, model_width)[flat_pos].reshape(
        local_rows, route_count, model_width
    )
    expert_sum = jnp.sum(gates[:, :, None] * picked, axis=1)
    output = (middle + RES_SCALE * expert_sum).astype(jnp.bfloat16)
    upstream = cotangent.astype(jnp.float32)
    dexpert = RES_SCALE * upstream
    dgates = jnp.sum(dexpert[:, None, :] * picked, axis=-1)
    dchosen = gates * (dgates - jnp.sum(gates * dgates, axis=-1, keepdims=True))
    onehot = (
        expert_ids[:, :, None] == jnp.arange(experts_all, dtype=jnp.int32)[None, None, :]
    ).astype(jnp.float32)
    dlogits = jnp.sum(onehot * dchosen[:, :, None], axis=1)
    dslots = (gates[:, :, None] * dexpert[:, None, :]).astype(jnp.bfloat16).reshape(-1, model_width)
    outgoing_grad = (
        jnp.zeros((experts_all * capacity, model_width), jnp.bfloat16).at[flat_pos].set(dslots)
    )
    outgoing_grad = outgoing_grad.reshape(experts_all, capacity, model_width)
    arrived_grad = lax.all_to_all(outgoing_grad, "ep", split_axis=0, concat_axis=0, tiled=True)
    sources = lax.axis_size("ep")
    shaped_rows = arrived_rows.reshape(sources, local_experts, capacity, model_width)
    shaped_grad = arrived_grad.reshape(sources, local_experts, capacity, model_width)
    gate_up = jnp.einsum(
        "secd,edgf->secgf", shaped_rows, w_gate_up, preferred_element_type=jnp.float32
    )
    gate_part = gate_up[..., 0, :]
    up_part = gate_up[..., 1, :]
    sigmoid_gate = jax.nn.sigmoid(gate_part)
    silu_gate = gate_part * sigmoid_gate
    inner_act = (silu_gate * up_part).astype(jnp.bfloat16)
    grad_down = jnp.einsum(
        "secf,secd->efd", inner_act, shaped_grad, preferred_element_type=jnp.float32
    )
    dinner = jnp.einsum("secd,efd->secf", shaped_grad, w_down, preferred_element_type=jnp.float32)
    dgate_part = dinner * up_part * sigmoid_gate * (1.0 + gate_part * (1.0 - sigmoid_gate))
    dup_part = dinner * silu_gate
    dgate_up = jnp.stack([dgate_part, dup_part], axis=-2).astype(jnp.bfloat16)
    grad_gate_up = jnp.einsum(
        "secd,secgf->edgf", shaped_rows, dgate_up, preferred_element_type=jnp.float32
    )
    drows = jnp.einsum("secgf,edgf->secd", dgate_up, w_gate_up, preferred_element_type=jnp.float32)
    drows = drows.astype(jnp.bfloat16).reshape(sources * local_experts, capacity, model_width)
    drows_back = lax.all_to_all(drows, "ep", split_axis=0, concat_axis=0, tiled=True)
    gathered_grad = drows_back.reshape(experts_all * capacity, model_width)[flat_pos]
    drouted = jnp.sum(
        gathered_grad.reshape(local_rows, route_count, model_width), axis=1, dtype=jnp.float32
    )
    router_float = w_router.astype(jnp.float32)
    drouted = drouted + jnp.einsum("te,de->td", dlogits, router_float, precision=HIGHEST)
    grad_router = jnp.einsum(
        "td,te->de", routed_low.astype(jnp.float32), dlogits, precision=HIGHEST
    )
    dmiddle_norm, grad_ffn_gain = norm_back(drouted, plain_two, inverse_two, gain_two)
    dmiddle = upstream + dmiddle_norm
    dbranch = (RES_SCALE * dmiddle).astype(jnp.bfloat16)
    group_grad = lax.all_gather(dbranch, "tp", axis=0, tiled=True)
    grad_output = jnp.einsum("lc,ld->cd", mixed, group_grad, preferred_element_type=jnp.float32)
    dmixed = jnp.einsum("ld,cd->lc", group_grad, w_output, preferred_element_type=jnp.float32)
    dmixed = dmixed.astype(jnp.bfloat16).reshape(length, kv_local, group_size, HD)
    dqueries, dkeys, dvalues = attention_backward(
        queries, keys_rot, values, segments_here, log_totals, dmixed
    )
    dquery_pre = unrotate(dqueries.reshape(length, kv_local * group_size, HD), cosine, sine)
    dquery_pre = dquery_pre.astype(jnp.bfloat16).reshape(length, -1)
    dkey_pre = unrotate(dkeys, cosine, sine).astype(jnp.bfloat16).reshape(length, -1)
    dvalue_low = dvalues.astype(jnp.bfloat16).reshape(length, -1)
    grad_query = jnp.einsum("ld,lc->dc", normed_low, dquery_pre, preferred_element_type=jnp.float32)
    grad_key = jnp.einsum("ld,lc->dc", normed_low, dkey_pre, preferred_element_type=jnp.float32)
    grad_value = jnp.einsum("ld,lc->dc", normed_low, dvalue_low, preferred_element_type=jnp.float32)
    total_rows = jnp.einsum("lc,dc->ld", dquery_pre, w_query, preferred_element_type=jnp.float32)
    total_rows = total_rows + jnp.einsum(
        "lc,dc->ld", dkey_pre, w_key, preferred_element_type=jnp.float32
    )
    dnormed = lax.psum_scatter(
        (
            total_rows
            + jnp.einsum("lc,dc->ld", dvalue_low, w_value, preferred_element_type=jnp.float32)
        ).astype(jnp.bfloat16),
        "tp",
        scatter_dimension=0,
        tiled=True,
    ).astype(jnp.float32)
    _, plain_one, inverse_one = norm_parts(local_in, gain_one)
    dlocal, grad_attn_gain = norm_back(dnormed, plain_one, inverse_one, gain_one)
    grad_hidden = dmiddle + dlocal
    grad_gate_up, grad_down = (
        lax.psum(grad_gate_up.astype(jnp.bfloat16), "tp").astype(jnp.float32),
        lax.psum(grad_down.astype(jnp.bfloat16), "tp").astype(jnp.float32),
    )
    grad_query, grad_key, grad_value, grad_output = (
        lax.psum(grad_query.astype(jnp.bfloat16), "ep").astype(jnp.float32),
        lax.psum(grad_key.astype(jnp.bfloat16), "ep").astype(jnp.float32),
        lax.psum(grad_value.astype(jnp.bfloat16), "ep").astype(jnp.float32),
        lax.psum(grad_output.astype(jnp.bfloat16), "ep").astype(jnp.float32),
    )
    grad_router, grad_attn_gain, grad_ffn_gain = lax.psum(
        (grad_router, grad_attn_gain, grad_ffn_gain), ("ep", "tp")
    )
    return (
        output,
        grad_hidden,
        grad_attn_gain,
        grad_query,
        grad_key,
        grad_value,
        grad_output,
        grad_ffn_gain,
        grad_router,
        grad_gate_up,
        grad_down,
    )


def solution(mesh):
    placed = (
        P(("ep", "tp"), None),
        P("ep", None),
        P(("ep", "tp"), None),
        P(("ep", "tp"), None),
        P(),
        P(None, "tp"),
        P(None, "tp"),
        P(None, "tp"),
        P("tp", None),
        P(),
        P(),
        P("ep", None, None, None),
        P("ep", None, None),
        P(("ep", "tp"), None),
    )
    return jax.shard_map(
        shards,
        mesh=mesh,
        in_specs=placed,
        out_specs=(
            P(("ep", "tp"), None),
            P(("ep", "tp"), None),
            P(),
            P(None, "tp"),
            P(None, "tp"),
            P(None, "tp"),
            P("tp", None),
            P(),
            P(),
            P("ep", None, None, None),
            P("ep", None, None),
        ),
        check_vma=False,
    )
```

profile of v0, /device:TPU:1, one launch (start us, length us, event | category | flops | bytes accessed | tf_op | source)
XLA Modules:
  0.0 908.3 jit_solution(7569588072652408106)
XLA Ops:
  9.3 34.5 %all-gather.3.cloned.1.call-done = bf16[1024,1024]{1,0:T(8,128)(2,1)} async-done(((bf16[256,1024]{1,0:T(8,128)(2,1)}), bf16[1024,1024]{1,0:T(8,128)(2,1)}) %all-gather.3.cloned.1.call-update) | async-done | bytes 2097168 | tf_op jit(solution)/shard_map/all_gather | solution.py:155
  43.8 2.1 fusion.81
  45.9 2.2 fusion.83
  51.2 23.4 %while.28 = (s32[]{:T(128)}, bf16[2,512,2,2,64]{1,4,3,2,0:T(8,128)(2,1)}, f32[2,2,2,512]{3,2,1,0:T(2,128)S(1)}, s32[2]{0:T(128)S(1)}, s32[1024]{0:T(1024)S(1)}, ...) while((s32[]{:T(128)}, ...), condition=%wide.region_4.5_spmd.clone, body=%wide.region_1.4_spmd.clone.sunk | while | flops 563739136 | bytes 28392116 | solution.py:84
  55.1 1.9 bitcast_reduce_fusion.2
  57.0 2.4 fusion.202
  59.4 3.5 fusion.203
  66.8 1.9 bitcast_reduce_fusion.2
  68.7 2.4 fusion.202
  71.1 3.5 fusion.203
  74.7 2.0 copy.80
  77.6 2.8 fusion.142
  80.9 8.2 scatter_custom_fusion
  89.1 38.3 %reduce-scatter.3.cloned.1.call-done = f32[256,1024]{1,0:T(8,128)} async-done(((f32[1024,1024]{1,0:T(8,128)}), f32[256,1024]{1,0:T(8,128)}) %reduce-scatter.3.cloned.1.call-update) | async-done | bytes 1048592 | tf_op jit(solution)/shard_map/reduce_scatter | solution.py:183
  127.4 2.1 multiply_reduce_fusion.2
  130.7 14.0 %gather_fusion = bf16[3072,1024]{1,0:T(8,128)(2,1)} fusion(bf16[257,1024]{1,0:T(8,128)(2,1)S(1)} %concatenate.39, s32[3072]{0:T(1024)S(1)} %fusion.126), kind=kCustom, calls=%fused_computation | custom fusion | bytes 12595200 | tf_op jit(solution)/shard_map/gather | solution.py:205
  144.8 7.8 all-to-all-start
  153.2 16.8 %gather_fusion.3 = f32[2048]{0:T(1024)S(1)} fusion(f32[256,32]{0,1:T(8,128)S(1)} %fusion.143, s32[2048]{0:T(1024)S(1)} %reshape.540), kind=kCustom, calls=%fused_computation.3 | custom fusion | bytes 32768 | tf_op jit(solution)/shard_map/jit(take_along_axis)/gather | solution.py:194
  170.5 14.4 %scatter_custom_fusion.1 = bf16[3072,1024]{1,0:T(8,128)(2,1)} fusion(s32[2048]{0:T(1024)S(1)} %bitcast.425, f32[256,1024]{1,0:T(8,128)S(1)} %convert_multiply_fusion.7, f32[2048]{0:T(1024)S(1)} %mul.389, bf16[]{:T(256)} %constant.49.clone.1), kind=kCustom, calls=%fused_computation.112 | custom fusion | flops 4194304 | bytes 7348226 | tf_op jit(solution)/shard_map/scatter | solution.py:230
  184.9 40.6 %all-to-all-done = bf16[32,96,1024]{2,1,0:T(8,128)(2,1)} async-done(((bf16[32,96,1024]{2,1,0:T(8,128)(2,1)}), bf16[32,96,1024]{2,1,0:T(8,128)(2,1)}, u32[]{:S(2)}, u32[]{:S(2)}) %all-to-all-start) | async-done | bytes 6291488 | tf_op jit(solution)/shard_map/all_to_all | solution.py:207
  225.5 10.1 %all-to-all-start.2 = ((bf16[32,96,1024]{2,1,0:T(8,128)(2,1)}), bf16[32,96,1024]{2,1,0:T(8,128)(2,1)}, u32[]{:S(2)}, u32[]{:S(2)}) async-start(bf16[32,96,1024]{2,1,0:T(8,128)(2,1)} %bitcast.397), calls=%async_computation.3 | async-start | bytes 12582912 | tf_op jit(solution)/shard_map/all_to_all | solution.py:233
  235.7 9.6 %fusion.78 = f32[32,1,96,2,512]{4,2,3,0,1:T(8,128)S(1)} fusion(bf16[32,96,1024]{2,1,0:T(8,128)(2,1)} %all-to-all-done, bf16[1024,2,512]{2,1,0:T(2,128)(2,1)} %bitcast.427), kind=kOutput, calls=%fused_computation.108 | convolution fusion | flops 6442450944 | bytes 20971520 | tf_op jit(solution)/shard_map/secd,edgf->secgf/dot_general | solution.py:130
  245.2 4.5 copy-done.68
  249.8 5.6 convolution_convert_fusion
  255.4 53.1 %all-to-all-done.2 = bf16[32,96,1024]{2,1,0:T(8,128)(2,1)} async-done(((bf16[32,96,1024]{2,1,0:T(8,128)(2,1)}), bf16[32,96,1024]{2,1,0:T(8,128)(2,1)}, u32[]{:S(2)}, u32[]{:S(2)}) %all-to-all-start.2) | async-done | bytes 6291488 | tf_op jit(solution)/shard_map/all_to_all | solution.py:233
  308.5 9.6 %all-to-all-start.1 = ((bf16[32,96,1024]{2,1,0:T(8,128)(2,1)}), bf16[32,96,1024]{2,1,0:T(8,128)(2,1)}, u32[]{:S(2)}, u32[]{:S(2)}) async-start(bf16[32,96,1024]{2,1,0:T(8,128)(2,1)} %convolution_convert_fusion), calls=%async_computation.2 | async-start | bytes 12582912 | tf_op jit(solution)/shard_map/all_to_all | solution.py:214
  318.2 10.4 %fusion.94 = (bf16[32,96,1,512]{3,1,0,2:T(8,128)(2,1)S(1)}, bf16[32,96,1,512]{3,1,0,2:T(8,128)(2,1)S(1)}) fusion(f32[32,1,96,2,512]{4,2,3,0,1:T(8,128)} %copy-done.68, bf16[32,96,1024]{2,1,0:T(8,128)(2,1)} %all-to-all-done.2, bf16[1,512,1024]{2,1,0:T(8,128)(2,1)S(1)} %copy-done), kind=kOutput, calls=%fused_computation.122 | convolution fusion | flops 3241672704 | bytes 26214400 | tf_op jit(solution)/shard_map/secd,efd->secf/dot_general | solution.py:248
  331.3 8.7 bitcast_convert_fusion
  340.0 51.2 %all-to-all-done.1 = bf16[32,96,1024]{2,1,0:T(8,128)(2,1)} async-done(((bf16[32,96,1024]{2,1,0:T(8,128)(2,1)}), bf16[32,96,1024]{2,1,0:T(8,128)(2,1)}, u32[]{:S(2)}, u32[]{:S(2)}) %all-to-all-start.1) | async-done | bytes 6291488 | tf_op jit(solution)/shard_map/all_to_all | solution.py:214
  391.2 9.8 %all-to-all-start.3 = ((bf16[32,96,1024]{2,1,0:T(8,128)(2,1)}), bf16[32,96,1024]{2,1,0:T(8,128)(2,1)}, u32[]{:S(2)}, u32[]{:S(2)}) async-start(bf16[32,96,1024]{2,1,0:T(8,128)(2,1)} %bitcast_convert_fusion), calls=%async_computation.4 | async-start | bytes 12582912 | tf_op jit(solution)/shard_map/all_to_all | solution.py:257
  401.6 14.5 %gather_fusion.1 = bf16[2048,1024]{1,0:T(8,128)(2,1)} fusion(bf16[3072,1024]{1,0:T(8,128)(2,1)} %bitcast.23, s32[2048]{0:T(1024)S(1)} %broadcast_clamp_fusion), kind=kCustom, calls=%fused_computation.1 | custom fusion | bytes 8396800 | tf_op jit(solution)/shard_map/gather | solution.py:215
  416.1 6.2 fusion.53
  422.4 51.7 %all-to-all-done.3 = bf16[32,96,1024]{2,1,0:T(8,128)(2,1)} async-done(((bf16[32,96,1024]{2,1,0:T(8,128)(2,1)}), bf16[32,96,1024]{2,1,0:T(8,128)(2,1)}, u32[]{:S(2)}, u32[]{:S(2)}) %all-to-all-start.3) | async-done | bytes 6291488 | tf_op jit(solution)/shard_map/all_to_all | solution.py:257
  474.0 14.6 %gather_fusion.2 = bf16[2048,1024]{1,0:T(8,128)(2,1)} fusion(bf16[3072,1024]{1,0:T(8,128)(2,1)} %bitcast.38, s32[2048]{0:T(1024)S(1)} %broadcast_clamp_fusion), kind=kCustom, calls=%fused_computation.2 | custom fusion | bytes 8396800 | tf_op jit(solution)/shard_map/gather | solution.py:258
  488.7 5.5 convert_reduce_fusion
  498.0 11.1 %fusion.106 = bf16[1,512,1024]{2,1,0:T(8,128)(2,1)} fusion(bf16[32,96,1024]{2,1,0:T(8,128)(2,1)} %all-to-all-done.2, f32[32,1,96,2,512]{4,2,3,0,1:T(8,128)} %copy-done.68), kind=kOutput, calls=%fused_computation.134 | convolution fusion | flops 3231186944 | bytes 19922944 | tf_op jit(solution)/shard_map/secf,secd->efd/dot_general | solution.py:245
  509.1 9.9 %fusion.95 = bf16[1,1024,2,512]{3,1,2,0:T(8,128)(2,1)} fusion(bf16[32,96,1,512]{3,1,0,2:T(8,128)(2,1)S(1)} %copy-done.67, bf16[32,96,1,512]{3,1,0,2:T(8,128)(2,1)S(1)} %copy-done.65, bf16[32,96,1024]{2,1,0:T(8,128)(2,1)} %all-to-all-done), kind=kOutput, calls=%fused_computation.123 | convolution fusion | flops 6456082432 | bytes 14680064 | tf_op jit(solution)/shard_map/secd,secgf->edgf/dot_general | solution.py:252
  519.2 9.5 %all-gather.5.cloned.1.call-done = bf16[1024,1024]{1,0:T(8,128)(2,1)} async-done(((bf16[256,1024]{1,0:T(8,128)(2,1)}), bf16[1024,1024]{1,0:T(8,128)(2,1)}) %all-gather.5.cloned.1.call-update) | async-done | bytes 2097168 | tf_op jit(solution)/shard_map/all_gather | solution.py:270
  528.7 2.3 convolution_convert_fusion.3
  531.1 69.1 %while.29 = (s32[]{:T(128)}, f32[1024,2,64]{0,2,1:T(8,128)S(1)}, f32[1024,2,64]{0,2,1:T(8,128)}, f32[2,512,2,2,64]{1,0,4,3,2:T(2,128)}, s32[2]{0:T(128)S(1)}, /*...) while((s32[]{:T(128)}, f32[1024,2,64]{0,2,1:T(8,128)S(1)}, ...), condition=%wide.region_20.21_spmd.clone, body=%wide.region_18.20_spmd.clone.sunk | while | flops 1375992320 | bytes 126163296 | solution.py:125
  536.4 3.5 fusion.214
  539.9 2.4 fusion.215
  542.3 2.0 copy-done.3
  546.3 10.4 %dynamic_update_slice.22 = f32[2,512,2,2,64]{1,0,4,3,2:T(2,128)} dynamic-update-slice(f32[2,512,2,2,64]{1,0,4,3,2:T(2,128)} %get-tuple-element.524, f32[1,512,2,2,64]{1,0,4,3,2:T(1,128)S(1)} %copy.131, s32[]{:T(128)} %get-tuple-element.521, s32[]{:T(128)} %constant.48.clone.1..sunk.1, s32[]{:T(128)} %constant.48.clone.1..sunk.1, s32[]{:T(128)} %constant.48.clone.1..sunk.1, s32[]{:T(128)} %constant.48.clone.1..sunk.1) | dynamic-update-slice | bytes 1048580 | tf_op jit(solution)/shard_map/while/body/jit(dynamic_update_index_in_dim)/dynamic_update_slice | solution.py:125
  556.7 3.2 fusion.216
  559.9 4.8 fusion.217
  570.8 3.5 fusion.214
  574.3 2.4 fusion.215
  576.7 2.0 copy-done.3
  580.7 10.4 %dynamic_update_slice.22 = f32[2,512,2,2,64]{1,0,4,3,2:T(2,128)} dynamic-update-slice(f32[2,512,2,2,64]{1,0,4,3,2:T(2,128)} %get-tuple-element.524, f32[1,512,2,2,64]{1,0,4,3,2:T(1,128)S(1)} %copy.131, s32[]{:T(128)} %get-tuple-element.521, s32[]{:T(128)} %constant.48.clone.1..sunk.1, s32[]{:T(128)} %constant.48.clone.1..sunk.1, s32[]{:T(128)} %constant.48.clone.1..sunk.1, s32[]{:T(128)} %constant.48.clone.1..sunk.1) | dynamic-update-slice | bytes 1048580 | tf_op jit(solution)/shard_map/while/body/jit(dynamic_update_index_in_dim)/dynamic_update_slice | solution.py:125
  591.1 3.3 fusion.216
  594.4 4.9 fusion.217
  600.2 2.2 reshape_reshape.6
  612.6 2.8 fusion.144
  617.6 2.1 add_convert_fusion
  619.9 5.8 copy.94
  627.3 2.1 fusion.146
  629.5 92.4 %all-reduce.10.cloned.1.call-done = (bf16[1024,256]{1,0:T(8,128)(2,1)}, bf16[1024,128]{1,0:T(8,128)(2,1)}, bf16[1024,128]{1,0:T(8,128)(2,1)}, bf16[256,1024]{1,0:T(8,128)(2,1)}) async-done(((bf16[1024,256]{1,0:T(8,128)(2,1)}, bf16[1024,128]{1,0:T(8,128)(2,1)}, bf16[1024,128]{1,0:T(8,128)(2,1)}, bf16[256,1024]{1,0:T(8,128)(2,1)}), (bf16[1024,256]{1,0:T(8,128)(2,1)}, bf16[1024,128]{1,0:T(8,128)(2,1)}, ...) | async-done | bytes 1572880 | tf_op jit(solution)/shard_map/psum | solution.py:305
  721.9 2.1 convert_element_type.195
  723.9 2.1 convert_element_type.201
  729.6 24.1 %reduce-scatter.5.cloned.1.call-done = bf16[256,1024]{1,0:T(8,128)(2,1)} async-done(((bf16[1024,1024]{1,0:T(8,128)(2,1)}), bf16[256,1024]{1,0:T(8,128)(2,1)}) %reduce-scatter.5.cloned.1.call-update) | async-done | bytes 524304 | tf_op jit(solution)/shard_map/reduce_scatter | solution.py:288
  755.5 3.4 fusion.111
  758.9 65.1 %all-reduce.1 = (f32[1024]{0:T(1024)}, f32[1024]{0:T(1024)}) all-reduce(f32[1024]{0:T(1024)S(1)} %get-tuple-element.258, f32[1024]{0:T(1024)S(1)} %copy-done.54), channel_id=1, replica_groups=mesh['ep'=32,'tp'=4] {'ep','tp'}, use_global_device_ids=true, to_apply=%region_24.25 | all-reduce | flops 2048 | bytes 16384 | tf_op jit(solution)/shard_map/psum | solution.py:310
  823.9 75.7 %all-reduce.8.cloned.1.call-done = f32[1024,32]{0,1:T(8,128)} async-done(((f32[1024,32]{0,1:T(8,128)}), f32[1024,32]{0,1:T(8,128)}) %all-reduce.8.cloned.1.call-update) | async-done | bytes 131088 | tf_op jit(solution)/shard_map/psum | solution.py:310
  (255 shorter events, 52.7 us)
Async XLA Ops:
  7.2 242.6 %copy-start = (bf16[1,512,1024]{2,1,0:T(8,128)(2,1)S(1)}, bf16[1,512,1024]{2,1,0:T(8,128)(2,1)}, u32[]{:S(2)}) copy-start(bf16[1,512,1024]{2,1,0:T(8,128)(2,1)} %param.30) | copy-start | bytes 3145732
  7.2 40.9 %copy-start.32 = (bf16[1024,128]{1,0:T(8,128)(2,1)S(1)}, bf16[1024,128]{1,0:T(8,128)(2,1)}, u32[]{:S(2)}) copy-start(bf16[1024,128]{1,0:T(8,128)(2,1)} %param.24) | copy-start | bytes 786436
  7.2 41.8 %copy-start.27 = (bf16[1024,256]{1,0:T(8,128)(2,1)S(1)}, bf16[1024,256]{1,0:T(8,128)(2,1)}, u32[]{:S(2)}) copy-start(bf16[1024,256]{1,0:T(8,128)(2,1)} %param.23) | copy-start | bytes 1572868
  7.2 36.6 %all-gather.3.cloned.1.call-start = ((), (), s32[]{:S(2)}) async-start(), calls=%async_computation.6 | async-start | bytes 2621440 | tf_op jit(solution)/shard_map/all_gather | solution.py:155
  8.0 119.5 %reduce-scatter.3.cloned.1.call-start = ((), (), s32[]{:S(2)}) async-start(), calls=%async_computation.7 | async-start | bytes 5242880 | tf_op jit(solution)/shard_map/reduce_scatter | solution.py:183
  8.7 40.2 %copy-start.49 = (f32[1024]{0:T(1024)}, f32[1024]{0:T(1024)S(1)}, u32[]{:S(2)}) copy-start(f32[1024]{0:T(1024)S(1)} %convert_element_type.169) | copy-start | bytes 12292
  9.3 41.6 %copy-start.20 = (f32[1024,64]{0,1:T(8,128)}, f32[1024,64]{0,1:T(8,128)S(1)}, u32[]{:S(2)}) copy-start(f32[1024,64]{0,1:T(8,128)S(1)} %get-tuple-element.333) | copy-start | bytes 786436
  9.3 41.6 %copy-start.22 = (f32[1024,64]{0,1:T(8,128)}, f32[1024,64]{0,1:T(8,128)S(1)}, u32[]{:S(2)}) copy-start(f32[1024,64]{0,1:T(8,128)S(1)} %get-tuple-element.332) | copy-start | bytes 786436
  45.9 4.0 copy-start.30
  51.2 26.4 %copy-start.36 = (bf16[256,1024]{1,0:T(8,128)(2,1)S(1)}, bf16[256,1024]{1,0:T(8,128)(2,1)}, u32[]{:S(2)}) copy-start(bf16[256,1024]{1,0:T(8,128)(2,1)} %param.26) | copy-start | bytes 1572868
  74.7 5.7 copy-start.62
  74.7 5.7 copy-start.6
  74.7 5.7 copy-start.11
  74.7 5.7 copy-start.14
  74.7 5.7 copy-start.44
  77.6 49.9 %copy-start.19 = (bf16[256,1024]{1,0:T(8,128)(2,1)S(1)}, bf16[256,1024]{1,0:T(8,128)(2,1)}, u32[]{:S(2)}) copy-start(bf16[256,1024]{1,0:T(8,128)(2,1)} %param.18) | copy-start | bytes 1572868
  80.5 64.3 %copy-start.46 = (f32[1024]{0:T(1024)}, f32[1024]{0:T(1024)S(1)}, u32[]{:S(2)}) copy-start(f32[1024]{0:T(1024)S(1)} %convert_element_type.174) | copy-start | bytes 12292
  129.6 15.2 %copy-start.51 = (f32[256]{0:T(256)}, f32[256]{0:T(256)S(1)}, u32[]{:S(2)}) copy-start(f32[256]{0:T(256)S(1)} %add_rsqrt_fusion.2) | copy-start | bytes 3076
  130.7 22.3 %copy-start.18 = (bf16[256,1024]{1,0:T(8,128)(2,1)}, bf16[256,1024]{1,0:T(8,128)(2,1)S(1)}, u32[]{:S(2)}) copy-start(bf16[256,1024]{1,0:T(8,128)(2,1)S(1)} %multiply_convert_fusion.1) | copy-start | bytes 1572868
  144.7 8.1 copy-start.24
  144.8 8.2 copy-start.43
  144.8 80.8 %all-to-all-start = ((bf16[32,96,1024]{2,1,0:T(8,128)(2,1)}), bf16[32,96,1024]{2,1,0:T(8,128)(2,1)}, u32[]{:S(2)}, u32[]{:S(2)}) async-start(bf16[32,96,1024]{2,1,0:T(8,128)(2,1)} %bitcast.398), calls=%async_computation.1 | async-start | bytes 12582912 | tf_op jit(solution)/shard_map/all_to_all | solution.py:207
  225.5 83.0 %all-to-all-start.2 = ((bf16[32,96,1024]{2,1,0:T(8,128)(2,1)}), bf16[32,96,1024]{2,1,0:T(8,128)(2,1)}, u32[]{:S(2)}, u32[]{:S(2)}) async-start(bf16[32,96,1024]{2,1,0:T(8,128)(2,1)} %bitcast.397), calls=%async_computation.3 | async-start | bytes 12582912 | tf_op jit(solution)/shard_map/all_to_all | solution.py:233
  245.2 4.5 copy-start.68
  308.5 82.7 %all-to-all-start.1 = ((bf16[32,96,1024]{2,1,0:T(8,128)(2,1)}), bf16[32,96,1024]{2,1,0:T(8,128)(2,1)}, u32[]{:S(2)}, u32[]{:S(2)}) async-start(bf16[32,96,1024]{2,1,0:T(8,128)(2,1)} %convolution_convert_fusion), calls=%async_computation.2 | async-start | bytes 12582912 | tf_op jit(solution)/shard_map/all_to_all | solution.py:214
  318.2 13.1 %copy-start.60 = (bf16[1,1024,2,512]{3,2,1,0:T(2,128)(2,1)S(1)}, bf16[1,1024,2,512]{3,2,1,0:T(2,128)(2,1)}, u32[]{:S(2)}) copy-start(bf16[1,1024,2,512]{3,2,1,0:T(2,128)(2,1)} %param.29) | copy-start | bytes 6291460
  391.2 82.8 %all-to-all-start.3 = ((bf16[32,96,1024]{2,1,0:T(8,128)(2,1)}), bf16[32,96,1024]{2,1,0:T(8,128)(2,1)}, u32[]{:S(2)}, u32[]{:S(2)}) async-start(bf16[32,96,1024]{2,1,0:T(8,128)(2,1)} %bitcast_convert_fusion), calls=%async_computation.4 | async-start | bytes 12582912 | tf_op jit(solution)/shard_map/all_to_all | solution.py:257
  401.0 127.7 %all-gather.5.cloned.1.call-start = ((), (), s32[]{:S(2)}) async-start(), calls=%async_computation.8 | async-start | bytes 2621440 | tf_op jit(solution)/shard_map/all_gather | solution.py:270
  422.4 71.8 %copy-start.40 = (f32[256,32]{0,1:T(8,128)}, f32[256,32]{0,1:T(8,128)S(1)}, u32[]{:S(2)}) copy-start(f32[256,32]{0,1:T(8,128)S(1)} %select_reduce_fusion) | copy-start | bytes 98308
  474.0 20.1 %copy-start.9 = (f32[256,1024]{1,0:T(8,128)S(1)}, f32[256,1024]{1,0:T(8,128)}, u32[]{:S(2)}) copy-start(f32[256,1024]{1,0:T(8,128)} %copy-done.8) | copy-start | bytes 3145732
  474.0 20.1 %copy-start.47 = (f32[1024]{0:T(1024)S(1)}, f32[1024]{0:T(1024)}, u32[]{:S(2)}) copy-start(f32[1024]{0:T(1024)} %copy-done.46) | copy-start | bytes 12292
  474.0 20.1 %copy-start.52 = (f32[256]{0:T(256)S(1)}, f32[256]{0:T(256)}, u32[]{:S(2)}) copy-start(f32[256]{0:T(256)} %copy-done.51) | copy-start | bytes 3076
  495.7 13.4 %copy-start.55 = (f32[256]{0:T(256)}, f32[256]{0:T(256)S(1)}, u32[]{:S(2)}) copy-start(f32[256]{0:T(256)S(1)} %broadcast_multiply_fusion.3) | copy-start | bytes 3076
  497.9 122.0 %all-reduce.12.cloned.1.call-start = ((), (), s32[]{:S(2)}) async-start(), calls=%async_computation.12 | async-start | bytes 6291456 | tf_op jit(solution)/shard_map/psum | solution.py:301
  497.9 11.1 %copy-start.65 = (bf16[32,96,1,512]{3,1,0,2:T(8,128)(2,1)S(1)}, bf16[32,96,1,512]{3,1,0,2:T(8,128)(2,1)}, u32[]{:S(2)}) copy-start(bf16[32,96,1,512]{3,1,0,2:T(8,128)(2,1)} %copy-done.64) | copy-start | bytes 9437188
  498.0 11.1 %copy-start.67 = (bf16[32,96,1,512]{3,1,0,2:T(8,128)(2,1)S(1)}, bf16[32,96,1,512]{3,1,0,2:T(8,128)(2,1)}, u32[]{:S(2)}) copy-start(bf16[32,96,1,512]{3,1,0,2:T(8,128)(2,1)} %copy-done.66) | copy-start | bytes 9437188
  509.0 19.7 %copy-start.37 = (bf16[256,1024]{1,0:T(8,128)(2,1)S(1)}, bf16[256,1024]{1,0:T(8,128)(2,1)}, u32[]{:S(2)}) copy-start(bf16[256,1024]{1,0:T(8,128)(2,1)} %param.26) | copy-start | bytes 1572868
  518.9 12.1 %copy-start.7 = (bf16[1024,2,64]{0,2,1:T(8,128)(2,1)S(1)}, bf16[1024,2,64]{0,2,1:T(8,128)(2,1)}, u32[]{:S(2)}) copy-start(bf16[1024,2,64]{0,2,1:T(8,128)(2,1)} %copy-done.6) | copy-start | bytes 786436
  518.9 12.1 %copy-start.12 = (bf16[1024,2,2,64]{0,3,2,1:T(8,128)(2,1)S(1)}, bf16[1024,2,2,64]{0,3,2,1:T(8,128)(2,1)}, u32[]{:S(2)}) copy-start(bf16[1024,2,2,64]{0,3,2,1:T(8,128)(2,1)} %copy-done.11) | copy-start | bytes 1572868
  518.9 12.1 %copy-start.15 = (bf16[1024,2,64]{0,2,1:T(8,128)(2,1)S(1)}, bf16[1024,2,64]{0,2,1:T(8,128)(2,1)}, u32[]{:S(2)}) copy-start(bf16[1024,2,64]{0,2,1:T(8,128)(2,1)} %copy-done.14) | copy-start | bytes 786436
  518.9 12.2 %copy-start.35 = (s32[1,1024]{1,0:T(1,128)S(1)}, s32[1,1024]{1,0:T(1,128)}, u32[]{:S(2)}) copy-start(s32[1,1024]{1,0:T(1,128)} %param.19) | copy-start | bytes 12292
  518.9 12.2 %copy-start.45 = (f32[2,2,2,512]{3,2,1,0:T(2,128)S(1)}, f32[2,2,2,512]{3,2,1,0:T(2,128)}, u32[]{:S(2)}) copy-start(f32[2,2,2,512]{3,2,1,0:T(2,128)} %copy-done.44) | copy-start | bytes 49156
  518.9 12.2 %copy-start.63 = (s32[2]{0:T(128)S(1)}, s32[2]{0:T(128)}, u32[]{:S(2)}) copy-start(s32[2]{0:T(128)} %copy-done.62) | copy-start | bytes 28
  519.0 202.9 %all-reduce.10.cloned.1.call-start = ((), (), s32[]{:S(2)}) async-start(), calls=%async_computation.11 | async-start | bytes 3145728 | tf_op jit(solution)/shard_map/psum | solution.py:305
  531.1 73.8 %copy-start.21 = (f32[1024,64]{0,1:T(8,128)S(1)}, f32[1024,64]{0,1:T(8,128)}, u32[]{:S(2)}) copy-start(f32[1024,64]{0,1:T(8,128)} %copy-done.20) | copy-start | bytes 786436
  570.8 3.5 copy-start.2
  600.2 5.1 copy-start.23
  606.5 4.5 copy-start.26
  606.5 4.5 copy-start.61
  608.0 4.6 copy-start.28
  611.0 4.4 copy-start.33
  612.6 3.6 copy-start.31
  615.4 138.4 %reduce-scatter.5.cloned.1.call-start = ((), (), s32[]{:S(2)}) async-start(), calls=%async_computation.9 | async-start | bytes 2621440 | tf_op jit(solution)/shard_map/reduce_scatter | solution.py:288
  619.7 7.6 copy-start.41
  619.8 279.9 %all-reduce.8.cloned.1.call-start = ((), (), s32[]{:S(2)}) async-start(), calls=%async_computation.10 | async-start | bytes 262144 | tf_op jit(solution)/shard_map/psum | solution.py:310
  619.9 5.9 copy-start.29
  619.9 133.9 %copy-start.50 = (f32[1024]{0:T(1024)S(1)}, f32[1024]{0:T(1024)}, u32[]{:S(2)}) copy-start(f32[1024]{0:T(1024)} %copy-done.49) | copy-start | bytes 12292
  625.7 129.7 %copy-start.10 = (f32[256,1024]{1,0:T(8,128)S(1)}, f32[256,1024]{1,0:T(8,128)}, u32[]{:S(2)}) copy-start(f32[256,1024]{1,0:T(8,128)} %copy-done.8) | copy-start | bytes 3145732
  625.7 129.7 %copy-start.17 = (f32[256,1024]{1,0:T(8,128)S(1)}, f32[256,1024]{1,0:T(8,128)}, u32[]{:S(2)}) copy-start(f32[256,1024]{1,0:T(8,128)} %copy-done.16) | copy-start | bytes 3145732
  625.7 129.7 %copy-start.48 = (f32[1024]{0:T(1024)S(1)}, f32[1024]{0:T(1024)}, u32[]{:S(2)}) copy-start(f32[1024]{0:T(1024)} %copy-done.46) | copy-start | bytes 12292
  625.7 129.7 %copy-start.53 = (f32[256]{0:T(256)S(1)}, f32[256]{0:T(256)}, u32[]{:S(2)}) copy-start(f32[256]{0:T(256)} %copy-done.51) | copy-start | bytes 3076
  625.7 129.7 %copy-start.56 = (f32[256]{0:T(256)S(1)}, f32[256]{0:T(256)}, u32[]{:S(2)}) copy-start(f32[256]{0:T(256)} %copy-done.55) | copy-start | bytes 3076
  627.3 131.5 %copy-start.54 = (f32[1024]{0:T(1024)S(1)}, f32[1024]{0:T(1024)}, u32[]{:S(2)}) copy-start(f32[1024]{0:T(1024)} %get-tuple-element.256) | copy-start | bytes 12292
  627.3 273.9 %copy-start.1 = (bf16[1,512,1024]{2,1,0:T(8,128)(2,1)S(1)}, bf16[1,512,1024]{2,1,0:T(8,128)(2,1)}, u32[]{:S(2)}) copy-start(bf16[1,512,1024]{2,1,0:T(8,128)(2,1)} %param.30) | copy-start | bytes 3145732
  (20 other events, 42.4 us)
Sparse Core Ops, SparseCore 0:
  9.7 34.0 all-gather.2
  80.5 46.8 reduce-scatter.2
  498.0 30.6 all-gather.4
  531.8 75.9 all-reduce.11
  615.5 106.3 all-reduce.9
  724.1 29.5 reduce-scatter.4
  759.8 139.8 all-reduce.7
where the time goes:
time: 919 us; the launch traced here: 908 us
  waiting for transfers between devices  472 us (51%)
  local copies, waits for them, and re-layouts  125 us (14%)
  matrix products  118 us (13%)
  other arithmetic  66.5 us (7%)
  blocking collectives  65.1 us (7%)
  starting transfers between devices  38.3 us (4%)
  between operations  15.4 us (2%)
    psum x1, waiting for transfers between devices, shards(): lax.psum(grad_query.astype(jnp.bfloat16), 'ep').astype(jnp.float32)  92.4 us
    psum x1, waiting for transfers between devices, shards(): lax.psum((grad_router, grad_attn_gain, grad_ffn_gain), ('ep', 'tp'))  75.7 us
    psum x1, blocking collectives, shards(): lax.psum((grad_router, grad_attn_gain, grad_ffn_gain), ('ep', 'tp'))  65.1 us
    all_to_all x1, waiting for transfers between devices, shards(): lax.all_to_all(outgoing_grad, 'ep', split_axis=0, concat_axis=0, tiled=True)  53.1 us
    all_to_all x1, waiting for transfers between devices, shards(): lax.all_to_all(drows, 'ep', split_axis=0, concat_axis=0, tiled=True)  51.7 us
    all_to_all x1, waiting for transfers between devices, shards(): lax.all_to_all(produced, 'ep', split_axis=0, concat_axis=0, tiled=True)  51.2 us
    all_to_all x1, waiting for transfers between devices, shards(): lax.all_to_all(outgoing, 'ep', split_axis=0, concat_axis=0, tiled=True)  40.6 us
    reduce_scatter x1, waiting for transfers between devices, shards(): lax.psum_scatter(jnp.dot(mixed, w_output, preferred_element_type=jnp.floa...  38.3 us
  transfers between devices with their start and end apart: 11, of which 10 were waited for; matrix products, arithmetic and copies ran while one was open for 24% of the time, Pallas kernels for 0%

commit v1 on v0

v1 whole, which is shorter than its diff:
```python
import jax
import jax.numpy as jnp
from jax import lax
from jax.experimental import pallas as pl
from jax.experimental.pallas import tpu as pltpu
from jax.sharding import PartitionSpec as P

HD = 64
ATT_SCALE = 0.015625
RES_SCALE = 0.22
NORM_EPS = 1e-06
ROPE_BASE = 10000.0
NEG_FILL = -1e30
HIGHEST = lax.Precision.HIGHEST
F32 = jnp.float32
BF16 = jnp.bfloat16

ROWS = 256
WIDTH = 1024
HALF = 512
CAP = 96
EXPERTS = 32
RING = 4
HEADS = 4
LANES = 128
VMEM_BYTES = 58 * 1024 * 1024
WHOLE = pl.BlockSpec(memory_space=pltpu.VMEM)
SCALARS = pl.BlockSpec(memory_space=pltpu.SMEM)
ANYWHERE = pl.BlockSpec(memory_space=pl.ANY)


def params():
    return pltpu.CompilerParams(vmem_limit_bytes=VMEM_BYTES)


def dot(a, b, precision=None):
    return jnp.dot(a, b, preferred_element_type=F32, precision=precision)


def dot_nt(a, b):
    return lax.dot_general(a, b, (((1,), (1,)), ((), ())), preferred_element_type=F32)


def dot_tn(a, b):
    return lax.dot_general(a, b, (((0,), (0,)), ((), ())), preferred_element_type=F32)


def place(z, x, core):
    return ((z % RING) * RING + (x % RING)) * 2 + core


def push(value, dz, dx, dc):
    if (dz % RING, dx % RING, dc) == (0, 0, 0):
        return value
    pairs = [
        (place(z, x, c), place(z + dz, x + dx, c ^ dc))
        for z in range(RING)
        for x in range(RING)
        for c in range(2)
    ]
    return lax.ppermute(value, "ep", pairs)


def push_tp(value, dy):
    if dy % RING == 0:
        return value
    return lax.ppermute(value, "tp", [(y, (y + dy) % RING) for y in range(RING)])


def swap_halves(v):
    lane = lax.broadcasted_iota(jnp.int32, v.shape, 1)
    return jnp.where(lane % HD < HD // 2, pltpu.roll(v, LANES - HD // 2, 1), pltpu.roll(v, HD // 2, 1))


def block_at(index):
    return pl.ds(pl.multiple_of(index * ROWS, ROWS), ROWS)


def key_range(block):
    return max(0, block - 2) * ROWS, (block + 1) * ROWS


def mask_bias(block, seg_col, seg_row):
    lo, hi = key_range(block)
    key_pos = lo + lax.broadcasted_iota(jnp.int32, (hi - lo, ROWS), 0)
    query_pos = block * ROWS + lax.broadcasted_iota(jnp.int32, (hi - lo, ROWS), 1)
    same = seg_col[lo:hi, :] == seg_row[:, block * ROWS : (block + 1) * ROWS]
    return jnp.where(same & (key_pos <= query_pos), 0.0, NEG_FILL)


def attend_kernel(
    rank, x0, x1, x2, x3, gain, wq, wk, wv, wo, cos, sin, seg_col, seg_row,
    normed, q_out, k_out, v_out, mixed, lse, br0, br1, br2, br3, vt, bias,
):
    me = rank[0]
    lane = lax.broadcasted_iota(jnp.int32, (ROWS, LANES), 1)
    for d, x_ref in enumerate((x0, x1, x2, x3)):
        at = block_at((me + d) % RING)
        x = x_ref[...].astype(F32)
        inverse = lax.rsqrt(jnp.mean(x * x, axis=-1, keepdims=True) + NORM_EPS)
        low = (x * inverse * gain[...]).astype(BF16)
        normed[at, :] = low
        cos_here, sin_here = cos[at, :], sin[at, :]

        def rope(v):
            return v * cos_here + swap_halves(v) * sin_here

        query = dot(low, wq[...])
        for pair in range(2):
            q = rope(query[:, pair * LANES : (pair + 1) * LANES]) * ATT_SCALE
            other = pltpu.roll(q, HD, 1)
            keep = (lane < HD) if pair == 0 else (lane >= HD)
            first, second = (q, other) if pair == 0 else (other, q)
            at_head = 2 * pair * LANES
            q_out[at, at_head : at_head + LANES] = jnp.where(keep, first, 0.0).astype(BF16)
            q_out[at, at_head + LANES : at_head + 2 * LANES] = jnp.where(keep, second, 0.0).astype(BF16)
        k_out[at, :] = rope(dot(low, wk[...])).astype(BF16)
        v_out[at, :] = dot(low, wv[...]).astype(BF16)
    vt[...] = v_out[...].astype(F32).T.astype(BF16)
    for b in range(RING):
        lo, hi = key_range(b)
        rows = slice(b * ROWS, (b + 1) * ROWS)
        bias[0 : hi - lo, :] = mask_bias(b, seg_col, seg_row)
        outs = []
        for h in range(HEADS):
            q = q_out[rows, h * LANES : (h + 1) * LANES]
            scores = dot_nt(k_out[lo:hi, :], q) + bias[0 : hi - lo, :]
            top = jnp.max(scores, axis=0, keepdims=True)
            weights = jnp.exp(scores - top)
            total = jnp.sum(weights, axis=0, keepdims=True)
            out = dot(vt[:, lo:hi], weights.astype(BF16)) * (1.0 / total)
            outs.append(out.T)
            lse[h : h + 1, rows] = top + jnp.log(total)
        mixed[rows, 0:LANES] = jnp.where(lane < HD, outs[0], pltpu.roll(outs[1], HD, 1)).astype(BF16)
        mixed[rows, LANES:] = jnp.where(lane < HD, pltpu.roll(outs[2], HD, 1), outs[3]).astype(BF16)
        branch = dot(mixed[rows, :], wo[...]).astype(BF16)
        relative = (b - me + RING) % RING
        for d, br in enumerate((br0, br1, br2, br3)):

            @pl.when(relative == d)
            def _():
                br[...] = branch


def attend(rank, pieces, gain, wq, wk, wv, wo, cos, sin, seg_col, seg_row):
    length = RING * ROWS
    return pl.pallas_call(
        attend_kernel,
        out_shape=[
            jax.ShapeDtypeStruct((length, WIDTH), BF16),
            jax.ShapeDtypeStruct((length, HEADS * LANES), BF16),
            jax.ShapeDtypeStruct((length, LANES), BF16),
            jax.ShapeDtypeStruct((length, LANES), BF16),
            jax.ShapeDtypeStruct((length, HEADS * HD), BF16),
            jax.ShapeDtypeStruct((8, length), F32),
        ]
        + [jax.ShapeDtypeStruct((ROWS, WIDTH), BF16)] * RING,
        in_specs=[SCALARS] + [WHOLE] * 13,
        out_specs=[WHOLE] * 10,
        scratch_shapes=[pltpu.VMEM((LANES, length), BF16), pltpu.VMEM((3 * ROWS, ROWS), F32)],
        compiler_params=params(),
        cost_estimate=pl.CostEstimate(flops=6_000_000_000, bytes_accessed=14_000_000, transcendentals=4_000_000),
        name="attend",
    )(rank, *pieces, gain, wq, wk, wv, wo, cos, sin, seg_col, seg_row)


def route_kernel(x, b0, b1, b2, b3, gain, wr, chosen, middle, half_a, half_b, gates_t):
    branch = b0[...].astype(F32) + b1[...].astype(F32) + b2[...].astype(F32) + b3[...].astype(F32)
    mid = x[...].astype(F32) + RES_SCALE * branch
    middle[...] = mid
    inverse = lax.rsqrt(jnp.mean(mid * mid, axis=-1, keepdims=True) + NORM_EPS)
    routed = (mid * inverse * gain[...]).astype(BF16)
    half_a[...] = routed[:, :HALF]
    half_b[...] = routed[:, HALF:]
    logits = jnp.where(chosen[...] > 0.0, dot(routed, wr[...]), NEG_FILL)
    weights = jnp.exp(logits - jnp.max(logits, axis=-1, keepdims=True))
    gates_t[...] = (weights / jnp.sum(weights, axis=-1, keepdims=True)).T


def route(x, branches, gain, wr, chosen):
    return pl.pallas_call(
        route_kernel,
        out_shape=[
            jax.ShapeDtypeStruct((ROWS, WIDTH), F32),
            jax.ShapeDtypeStruct((ROWS, HALF), BF16),
            jax.ShapeDtypeStruct((ROWS, HALF), BF16),
            jax.ShapeDtypeStruct((EXPERTS, ROWS), F32),
        ],
        in_specs=[WHOLE] * 8,
        out_specs=[WHOLE] * 4,
        compiler_params=params(),
        cost_estimate=pl.CostEstimate(flops=20_000_000, bytes_accessed=5_000_000, transcendentals=8192),
        name="route",
    )(x, *branches, gain, wr, chosen)


def slot_matrix(slots, row):
    slot = lax.broadcasted_iota(jnp.int32, (CAP, ROWS), 0).astype(F32)
    return jnp.where(slot == slots[row : row + 1, :], 1.0, 0.0)


def line_matrix(slots, d):
    return jnp.concatenate([slot_matrix(slots, d * 8 + j).astype(BF16) for j in range(8)], axis=0)


def dispatch_kernel(slots_a, slots_b, *refs):
    for half, slots in enumerate((slots_a, slots_b)):
        rows, pieces = refs[4 * half : 4 * half + 4], refs[8 + 8 * half : 16 + 8 * half]
        for d in range(RING):
            filled = dot(line_matrix(slots, d), rows[d][...]).astype(BF16)
            for j in range(8):
                pieces[j][d * CAP : (d + 1) * CAP, :] = filled[j * CAP : (j + 1) * CAP, :]


def combine_kernel(slots_a, slots_b, *refs):
    for half, slots in enumerate((slots_a, slots_b)):
        pieces, rows = refs[8 * half : 8 * half + 8], refs[16 + 4 * half : 20 + 4 * half]
        for d in range(RING):
            filled = jnp.concatenate([pieces[j][d * CAP : (d + 1) * CAP, :] for j in range(8)], axis=0)
            rows[d][...] = dot_tn(line_matrix(slots, d), filled).astype(BF16)


SLOT_COST = pl.CostEstimate(flops=1_700_000_000, bytes_accessed=8_500_000, transcendentals=0)


def dispatch(slots_a, slots_b, half_a, half_b):
    along_z = [push(half_a, -d, 0, 0) for d in range(RING)]
    along_x = [push(half_b, 0, -d, 0) for d in range(RING)]
    pieces = pl.pallas_call(
        dispatch_kernel,
        out_shape=[jax.ShapeDtypeStruct((RING * CAP, HALF), BF16)] * 16,
        in_specs=[WHOLE] * 10,
        out_specs=[WHOLE] * 16,
        compiler_params=params(),
        cost_estimate=SLOT_COST,
        name="dispatch",
    )(slots_a, slots_b, *along_z, *along_x)
    return exchange(pieces)


def exchange(pieces):
    pieces_a, pieces_b = pieces[:8], pieces[8:]
    got_a, got_b = [None] * 8, [None] * 8
    for d in (1, 3, 2, 0):
        for dc in (0, 1):
            source = ((-d) % RING) * 2 + dc
            got_a[source] = push(pieces_a[d * 2 + dc], 0, d, dc)
            got_b[source] = push(pieces_b[d * 2 + dc], d, 0, dc)
    return got_a + got_b


def combine(slots_a, slots_b, pieces):
    pieces = exchange(pieces)
    partial = pl.pallas_call(
        combine_kernel,
        out_shape=[jax.ShapeDtypeStruct((ROWS, HALF), BF16)] * 8,
        in_specs=[WHOLE] * 18,
        out_specs=[WHOLE] * 8,
        compiler_params=params(),
        cost_estimate=SLOT_COST,
        name="combine",
    )(slots_a, slots_b, *pieces)
    return [push(partial[d], d, 0, 0) for d in range(RING)] + [
        push(partial[4 + d], 0, d, 0) for d in range(RING)
    ]


STEPS = 8
STEP_ROWS = RING * CAP


def expert_kernel(slots, gates, wgu, wgu_t, wd, wd_t, *refs):
    ra, rb, ca, cb = (refs[8 * i : 8 * i + 8] for i in range(4))
    qa, qb, ma, mb = (refs[32 + 8 * i : 40 + 8 * i] for i in range(4))
    dgate_out, disp_out, dgu_out, inner_out, dex_out = refs[64:69]
    rows_in, cot_in, back_out, moe_out, in_sem, out_sem = refs[69:]
    step = pl.program_id(0)

    def copies(j, pairs, sems, outward):
        slot, dx, dc, made = j % 2, j // 2, j % 2, []
        for which, (half_a, half_b, buf) in enumerate(pairs):
            ends = [(half_a[j], buf.at[slot, :, pl.ds(0, HALF)])]
            for dz in range(RING):
                ends.append(
                    (half_b[dz * 2 + dc].at[pl.ds(dx * CAP, CAP)], buf.at[slot, pl.ds(dz * CAP, CAP), pl.ds(HALF, HALF)])
                )
            for n, (far, near) in enumerate(ends):
                source, target = (near, far) if outward else (far, near)
                made.append(pltpu.make_async_copy(source, target, sems.at[slot, which * 5 + n]))
        return made

    def fetches(j):
        return copies(j, ((ra, rb, rows_in), (ca, cb, cot_in)), in_sem, False)

    def stores(j):
        return copies(j, ((qa, qb, back_out), (ma, mb, moe_out)), out_sem, True)

    for j in range(STEPS):

        @pl.when(step == j)
        def _():
            if j == 0:
                for copy in fetches(0):
                    copy.start()
            if j + 1 < STEPS:
                for copy in fetches(j + 1):
                    copy.start()
            for copy in fetches(j):
                copy.wait()
            if j >= 2:
                for copy in stores(j - 2):
                    copy.wait()

    slot = step % 2
    fills = [slot_matrix(slots.at[0], dz) for dz in range(RING)]
    gate_slot = jnp.concatenate(
        [jnp.sum(fills[dz] * gates[0, dz : dz + 1, :], axis=1, keepdims=True) for dz in range(RING)], axis=0
    )
    rows = rows_in[slot]
    disp_out[...] = rows
    gate_up = dot(rows, wgu[...])
    gate, up = gate_up[:, :HALF], gate_up[:, HALF:]
    sigmoid = jax.nn.sigmoid(gate)
    silu = gate * sigmoid
    inner = (silu * up).astype(BF16)
    inner_out[...] = inner
    made = dot(inner, wd[...]).astype(BF16).astype(F32)
    dmoe = RES_SCALE * cot_in[slot].astype(F32)
    dgate_slot = jnp.sum(dmoe * made, axis=1, keepdims=True)
    for dz in range(RING):
        dgate_out[0, dz : dz + 1, :] = jnp.sum(
            fills[dz] * dgate_slot[dz * CAP : (dz + 1) * CAP, :], axis=0, keepdims=True
        )
    moe_out[slot] = (gate_slot * made).astype(BF16)
    dex = (gate_slot * dmoe).astype(BF16)
    dex_out[...] = dex
    dinner = dot(dex, wd_t[...])
    dgate = dinner * up * sigmoid * (1.0 + gate * (1.0 - sigmoid))
    dgu = jnp.concatenate([dgate.astype(BF16), (dinner * silu).astype(BF16)], axis=1)
    dgu_out[...] = dgu
    back_out[slot] = dot(dgu, wgu_t[...]).astype(BF16)

    for j in range(STEPS):

        @pl.when(step == j)
        def _():
            for copy in stores(j):
                copy.start()
            if j == STEPS - 1:
                for copy in stores(j - 1) + stores(j):
                    copy.wait()


def experts(slots, gates, wgu, wgu_t, wd, wd_t, rows, cots):
    piece = jax.ShapeDtypeStruct((STEP_ROWS, HALF), BF16)
    total = STEPS * STEP_ROWS
    by_step = pl.BlockSpec((1, RING, ROWS), lambda s: (s, 0, 0))
    wide = pl.BlockSpec((STEP_ROWS, WIDTH), lambda s: (s, 0))
    narrow = pl.BlockSpec((STEP_ROWS, HALF), lambda s: (s, 0))
    buf = pltpu.VMEM((2, STEP_ROWS, WIDTH), BF16)
    made = pl.pallas_call(
        expert_kernel,
        grid=(STEPS,),
        out_shape=[piece] * 32
        + [
            jax.ShapeDtypeStruct((STEPS, RING, ROWS), F32),
            jax.ShapeDtypeStruct((total, WIDTH), BF16),
            jax.ShapeDtypeStruct((total, WIDTH), BF16),
            jax.ShapeDtypeStruct((total, HALF), BF16),
            jax.ShapeDtypeStruct((total, WIDTH), BF16),
        ],
        in_specs=[by_step, by_step] + [WHOLE] * 4 + [ANYWHERE] * 32,
        out_specs=[ANYWHERE] * 32 + [by_step, wide, wide, narrow, wide],
        scratch_shapes=[buf, buf, buf, buf, pltpu.SemaphoreType.DMA((2, 10)), pltpu.SemaphoreType.DMA((2, 10))],
        compiler_params=params(),
        cost_estimate=pl.CostEstimate(flops=19_000_000_000, bytes_accessed=60_000_000, transcendentals=1_600_000),
        name="experts",
    )(slots, gates, wgu, wgu_t, wd, wd_t, *rows, *cots)
    return made[:16], made[16:32], made[32], made[33], made[34], made[35], made[36]


def unroute_kernel(*refs):
    parts, (gates_t, dgates_t, middle, cot, gain, wr_t, dmiddle, dbranch, sums) = refs[:8], refs[8:]

    def four(pieces):
        a, b, c, d = (piece[...].astype(F32) for piece in pieces)
        return (a + b) + (c + d)

    gates, dgates = gates_t[...], dgates_t[...]
    dlogits = gates * (dgates - jnp.sum(gates * dgates, axis=0, keepdims=True))
    drouted = jnp.concatenate([four(parts[:4]), four(parts[4:])], axis=1)
    drouted = drouted + dot(dlogits.T, wr_t[...], HIGHEST)
    mid = middle[...]
    inverse = lax.rsqrt(jnp.mean(mid * mid, axis=-1, keepdims=True) + NORM_EPS)
    plain = mid * inverse
    routed = (plain * gain[...]).astype(BF16).astype(F32)
    sums[0:EXPERTS, :] = dot(dlogits, routed, HIGHEST)
    sums[EXPERTS : EXPERTS + 8, :] = jnp.broadcast_to(jnp.sum(drouted * plain, axis=0, keepdims=True), (8, WIDTH))
    scaled = drouted * gain[...]
    along = jnp.mean(scaled * plain, axis=-1, keepdims=True)
    total = cot[...].astype(F32) + inverse * (scaled - plain * along)
    dmiddle[...] = total
    dbranch[...] = (RES_SCALE * total).astype(BF16)


def unroute(parts, gates_t, dgates_t, middle, cot, gain, wr_t):
    return pl.pallas_call(
        unroute_kernel,
        out_shape=[
            jax.ShapeDtypeStruct((ROWS, WIDTH), F32),
            jax.ShapeDtypeStruct((ROWS, WIDTH), BF16),
            jax.ShapeDtypeStruct((EXPERTS + 8, WIDTH), F32),
        ],
        in_specs=[WHOLE] * 14,
        out_specs=[WHOLE] * 3,
        compiler_params=params(),
        cost_estimate=pl.CostEstimate(flops=200_000_000, bytes_accessed=6_000_000, transcendentals=0),
        name="unroute",
    )(*parts, gates_t, dgates_t, middle, cot, gain, wr_t)


def unmix_kernel(rank, d0, d1, d2, d3, mixed, wo, dmixed, grad_out):
    me = rank[0]
    lane = lax.broadcasted_iota(jnp.int32, (ROWS, LANES), 1)
    for d, ref in enumerate((d0, d1, d2, d3)):
        at = block_at((me + d) % RING)
        low = dot_nt(ref[...], wo[...])
        for pair in range(2):
            both = low[:, pair * LANES : (pair + 1) * LANES]
            other = pltpu.roll(both, HD, 1)
            keep = (lane < HD) if pair == 0 else (lane >= HD)
            first, second = (both, other) if pair == 0 else (other, both)
            at_head = 2 * pair * LANES
            dmixed[at, at_head : at_head + LANES] = jnp.where(keep, first, 0.0).astype(BF16)
            dmixed[at, at_head + LANES : at_head + 2 * LANES] = jnp.where(keep, second, 0.0).astype(BF16)
        term = dot_tn(mixed[at, :], ref[...])
        total = term if d == 0 else total + term
    grad_out[...] = total.astype(BF16)


def unmix(rank, pieces, mixed, wo):
    length = RING * ROWS
    return pl.pallas_call(
        unmix_kernel,
        out_shape=[
            jax.ShapeDtypeStruct((length, HEADS * LANES), BF16),
            jax.ShapeDtypeStruct((HEADS * HD, WIDTH), BF16),
        ],
        in_specs=[SCALARS] + [WHOLE] * 6,
        out_specs=[WHOLE] * 2,
        compiler_params=params(),
        cost_estimate=pl.CostEstimate(flops=1_100_000_000, bytes_accessed=5_000_000, transcendentals=0),
        name="unmix",
    )(rank, *pieces, mixed, wo)


def unattend_kernel(
    rank, q_in, k_in, v_in, lse, dmixed, normed, gain_col, wq, wk, wv, cos, sin, seg_col, seg_row,
    dn0, dn1, dn2, dn3, grads, dgain, kt, bias, dk, dv, dqkv,
):
    me = rank[0]
    lane = lax.broadcasted_iota(jnp.int32, (ROWS, LANES), 1)
    kt[...] = k_in[...].astype(F32).T.astype(BF16)
    dk[...] = jnp.zeros_like(dk)
    dv[...] = jnp.zeros_like(dv)

    def unrope(v, rows):
        return v * cos[rows, :] - swap_halves(v) * sin[rows, :]

    for b in range(RING):
        lo, hi = key_range(b)
        rows = slice(b * ROWS, (b + 1) * ROWS)
        bias[0 : hi - lo, :] = mask_bias(b, seg_col, seg_row)
        dqs = []
        for h in range(HEADS):
            cols = slice(h * LANES, (h + 1) * LANES)
            q, do = q_in[rows, cols], dmixed[rows, cols]
            scores = dot_nt(k_in[lo:hi, :], q) + bias[0 : hi - lo, :]
            probs = jnp.exp(scores - lse[h : h + 1, rows])
            dprobs = dot_nt(v_in[lo:hi, :], do)
            delta = jnp.sum(probs * dprobs, axis=0, keepdims=True)
            dscores = (probs * (dprobs - delta)).astype(BF16)
            dv[lo:hi, :] += dot(probs.astype(BF16), do)
            dk[lo:hi, :] += dot(dscores, q)
            dqs.append(dot(kt[:, lo:hi], dscores).T * ATT_SCALE)
        first = jnp.where(lane < HD, dqs[0], pltpu.roll(dqs[1], HD, 1))
        second = jnp.where(lane < HD, pltpu.roll(dqs[2], HD, 1), dqs[3])
        dqkv[rows, 0:LANES] = unrope(first, rows).astype(BF16)
        dqkv[rows, LANES : 2 * LANES] = unrope(second, rows).astype(BF16)
    for b in range(RING):
        rows = slice(b * ROWS, (b + 1) * ROWS)
        dqkv[rows, 2 * LANES : 3 * LANES] = unrope(dk[rows, :], rows).astype(BF16)
        dqkv[rows, 3 * LANES :] = dv[rows, :].astype(BF16)
        dn = dot_nt(dqkv[rows, : 2 * LANES], wq[...])
        dn = dn + dot_nt(dqkv[rows, 2 * LANES : 3 * LANES], wk[...])
        dn = (dn + dot_nt(dqkv[rows, 3 * LANES :], wv[...])).astype(BF16)
        relative = (b - me + RING) % RING
        for d, ref in enumerate((dn0, dn1, dn2, dn3)):

            @pl.when(relative == d)
            def _():
                ref[...] = dn

    for b in range(RING):
        rows = slice(b * ROWS, (b + 1) * ROWS)
        grad = dot_tn(normed[:, rows], dqkv[...])
        grads[rows, :] = grad.astype(BF16)
        terms = jnp.sum(wq[rows, :].astype(F32) * grad[:, : 2 * LANES], axis=1, keepdims=True)
        terms += jnp.sum(wk[rows, :].astype(F32) * grad[:, 2 * LANES : 3 * LANES], axis=1, keepdims=True)
        terms += jnp.sum(wv[rows, :].astype(F32) * grad[:, 3 * LANES :], axis=1, keepdims=True)
        dgain[rows, :] = terms / gain_col[rows, :]


def unattend(rank, q, k, v, lse, dmixed, normed, gain_col, wq, wk, wv, cos, sin, seg_col, seg_row):
    length = RING * ROWS
    return pl.pallas_call(
        unattend_kernel,
        out_shape=[jax.ShapeDtypeStruct((ROWS, WIDTH), BF16)] * RING
        + [jax.ShapeDtypeStruct((WIDTH, HALF), BF16), jax.ShapeDtypeStruct((WIDTH, 1), F32)],
        in_specs=[SCALARS] + [WHOLE] * 14,
        out_specs=[WHOLE] * 6,
        scratch_shapes=[
            pltpu.VMEM((LANES, length), BF16),
            pltpu.VMEM((3 * ROWS, ROWS), F32),
            pltpu.VMEM((length, LANES), F32),
            pltpu.VMEM((length, LANES), F32),
            pltpu.VMEM((length, HALF), BF16),
        ],
        compiler_params=params(),
        cost_estimate=pl.CostEstimate(flops=10_000_000_000, bytes_accessed=14_000_000, transcendentals=4_000_000),
        name="unattend",
    )(rank, q, k, v, lse, dmixed, normed, gain_col, wq, wk, wv, cos, sin, seg_col, seg_row)


def rope_tables(length):
    freqs = ROPE_BASE ** (-jnp.arange(HD // 2, dtype=F32) * 2.0 / HD)
    angles = jnp.arange(length, dtype=F32)[:, None] * freqs[None, :]
    cosine, sine = jnp.cos(angles), jnp.sin(angles)
    return jnp.concatenate([cosine] * 4, axis=1), jnp.concatenate([-sine, sine] * 2, axis=1)


def shards(
    hidden_in, segment_ids, expert_ids, slot_index, attn_gain, w_query, w_key, w_value, w_output,
    ffn_gain, w_router, w_gate_up, w_down, cotangent,
):
    length = RING * ROWS
    here, rank = lax.axis_index("ep"), lax.axis_index("tp")
    z, x, core = here // 8, (here // 2) % 4, here % 2
    rank_in = rank.astype(jnp.int32).reshape(1)

    named = expert_ids[:, :, None] == jnp.arange(EXPERTS, dtype=jnp.int32)[None, None, :]
    slot_of = jnp.sum(jnp.where(named, slot_index[:, :, None] + 1, 0), axis=1) - 1
    chosen = (slot_of >= 0).astype(F32)
    all_slots = lax.all_gather(slot_of.astype(F32).T, "ep", axis=0, tiled=True)

    near = jnp.arange(RING, dtype=jnp.int32)
    cores = jnp.arange(2, dtype=jnp.int32)
    four, mid, two = near[:, None, None], near[None, :, None], cores[None, None, :]
    rows_a = place(z + four, x, core) * EXPERTS + place(z, x + mid, core ^ two)
    rows_b = place(z, x + four, core) * EXPERTS + place(z + mid, x, core ^ two)
    blocks = place(z + near[None, None, :], x + near[:, None, None], core ^ cores[None, :, None]).reshape(-1)
    rows_e = blocks * EXPERTS + here
    slots_a = jnp.take(all_slots, rows_a.reshape(-1), axis=0)
    slots_b = jnp.take(all_slots, rows_b.reshape(-1), axis=0)
    slots_e = jnp.take(all_slots, rows_e, axis=0).reshape(STEPS, RING, ROWS)

    gain_one = attn_gain.astype(F32).reshape(1, WIDTH)
    gain_two = ffn_gain.astype(F32).reshape(1, WIDTH)
    cos, sin = rope_tables(length)
    seg_row = segment_ids
    seg_col = segment_ids.reshape(length, 1)

    group = [push_tp(hidden_in, -d) for d in range(RING)]
    cots = dispatch(slots_a, slots_b, cotangent[:, :HALF], cotangent[:, HALF:])
    made = attend(rank_in, group, gain_one, w_query, w_key, w_value, w_output, cos, sin, seg_col, seg_row)
    normed, q, k, v, mixed, lse = made[:6]
    branches = [push_tp(made[6 + d], d) for d in range(RING)]
    middle, half_a, half_b, gates_t = route(hidden_in, branches, gain_two, w_router, chosen)
    all_gates = lax.all_gather(gates_t, "ep", axis=0, tiled=True)
    gates_e = jnp.take(all_gates, rows_e, axis=0).reshape(STEPS, RING, ROWS)
    rows = dispatch(slots_a, slots_b, half_a, half_b)

    wgu = w_gate_up.reshape(WIDTH, 2 * HALF)
    wd = w_down.reshape(HALF, WIDTH)
    back, moe_slots, dgate_rows, disp, dgu, inner, dex = experts(
        slots_e, gates_e, wgu, wgu.T, wd, wd.T, rows, cots
    )
    devices = jnp.arange(EXPERTS, dtype=jnp.int32)
    dz, dx, dc = (devices // 8 - z) % 4, ((devices // 2) % 4 - x) % 4, (devices % 2) ^ core
    order = (dx * 2 + dc) * RING + dz
    dgates = jnp.take(dgate_rows.reshape(EXPERTS, ROWS), order, axis=0).reshape(EXPERTS, 1, ROWS)
    dgates_t = lax.all_to_all(dgates, "ep", split_axis=0, concat_axis=0, tiled=True).reshape(EXPERTS, ROWS)
    parts = combine(slots_a, slots_b, back)

    grad_gate_up = dot_tn(disp, dgu).astype(BF16)
    grad_down = dot_tn(inner, dex).astype(BF16)
    grad_gate_up, grad_down = lax.psum((grad_gate_up, grad_down), "tp")

    dmiddle, dbranch, sums = unroute(parts, gates_t, dgates_t, middle, cotangent, gain_two, w_router.T.astype(F32))
    sums = lax.psum(sums, ("ep", "tp"))
    group_grad = [push_tp(dbranch, -d) for d in range(RING)]

    moe_parts = combine(slots_a, slots_b, moe_slots)

    dmixed, grad_output = unmix(rank_in, group_grad, mixed, w_output)
    grad_output = lax.psum(grad_output, "ep")
    last = unattend(
        rank_in, q, k, v, lse, dmixed, normed, gain_one.reshape(WIDTH, 1), w_query, w_key, w_value, cos, sin,
        seg_col, seg_row,
    )
    grads = lax.psum(last[4], "ep")
    dgain = lax.all_gather(last[5].reshape(8, LANES), ("ep", "tp"), axis=0)
    grad_attn_gain = jnp.sum(dgain, axis=0).reshape(WIDTH)
    dn = [push_tp(last[d], d).astype(F32) for d in range(RING)]
    dnormed = (dn[0] + dn[1]) + (dn[2] + dn[3])

    local = hidden_in.astype(F32)
    inverse = lax.rsqrt(jnp.mean(local * local, axis=-1, keepdims=True) + NORM_EPS)
    plain = local * inverse
    scaled = dnormed * gain_one
    along = jnp.mean(scaled * plain, axis=-1, keepdims=True)
    grad_hidden = dmiddle + inverse * (scaled - plain * along)

    def four_sum(p):
        a, b, c, d = (piece.astype(F32) for piece in p)
        return (a + b) + (c + d)

    moe = jnp.concatenate([four_sum(moe_parts[:4]), four_sum(moe_parts[4:])], axis=1)
    output = (middle + RES_SCALE * moe).astype(BF16)
    return (
        output,
        grad_hidden,
        grad_attn_gain,
        grads[:, : 2 * LANES].astype(F32),
        grads[:, 2 * LANES : 3 * LANES].astype(F32),
        grads[:, 3 * LANES :].astype(F32),
        grad_output.astype(F32),
        sums[EXPERTS],
        sums[:EXPERTS].T,
        grad_gate_up.astype(F32).reshape(1, WIDTH, 2, HALF),
        grad_down.astype(F32).reshape(1, HALF, WIDTH),
    )


def solution(mesh):
    placed = (
        P(("ep", "tp"), None),
        P("ep", None),
        P(("ep", "tp"), None),
        P(("ep", "tp"), None),
        P(),
        P(None, "tp"),
        P(None, "tp"),
        P(None, "tp"),
        P("tp", None),
        P(),
        P(),
        P("ep", None, None, None),
        P("ep", None, None),
        P(("ep", "tp"), None),
    )
    return jax.shard_map(
        shards,
        mesh=mesh,
        in_specs=placed,
        out_specs=(
            P(("ep", "tp"), None),
            P(("ep", "tp"), None),
            P(),
            P(None, "tp"),
            P(None, "tp"),
            P(None, "tp"),
            P("tp", None),
            P(),
            P(),
            P("ep", None, None, None),
            P("ep", None, None),
        ),
        check_vma=False,
    )
```

time: 919 us -> 838 us (0.912)
  starting transfers between devices: 38.3 us -> 162 us
  Pallas kernels: 0 us -> 103 us
  matrix products: 118 us -> 18.8 us
  local copies, waits for them, and re-layouts: 125 us -> 35 us
  waiting for transfers between devices: 472 us -> 415 us
  other arithmetic: 66.5 us -> 31 us
  blocking collectives: 65.1 us -> 49.8 us
    ppermute x0 -> x92, waiting for transfers between devices: none -> 223 us  [the longest x80 164 us: push(): return lax.ppermute(value, 'ep', pairs)]
    all_to_all x4 -> x1, waiting for transfers between devices: 197 us -> 6.65 us  [shards(): lax.all_to_all(dgates, 'ep', split_axis=0, concat_axis=0, tiled=True)]
    ppermute x0 -> x92, starting transfers between devices: none -> 156 us  [the longest x80 143 us: push(): return lax.ppermute(value, 'ep', pairs)]
    pallas_call x0 -> x10, Pallas kernels: none -> 103 us  [the longest x1 35.5 us: experts(): pl.pallas_call(expert_kernel, grid=(STEPS,), out_shape=[piece] * 32 + [ja...]
    dot_general x35 -> x2, matrix products: 118 us -> 18.8 us  [dot_tn(): lax.dot_general(a, b, (((0,), (0,)), ((), ())), preferred_element_type=F32)]
    psum x1 -> x0, blocking collectives: 65.1 us -> none  [shards(): lax.psum((grad_router, grad_attn_gain, grad_ffn_gain), ('ep', 'tp'))]
    reduce_scatter x2 -> x0, waiting for transfers between devices: 62.4 us -> none  [the longest x1 38.3 us: shards(): lax.psum_scatter(jnp.dot(mixed, w_output, preferred_element_type=jnp.floa...]
    gather x8 -> x5, local copies, waits for them, and re-layouts: 60.3 us -> 7.9 us  [the longest x1 1.83 us: shards(): gates_e = jnp.take(all_gates, rows_e, axis=0).reshape(STEPS, RING, ROWS)]
  transfers between devices with their start and end apart: 11 -> 98, of which waited for: 10 -> 37; matrix products, arithmetic and copies ran while one was open for 24% -> 9% of each run, Pallas kernels for 0% -> 7%
where the time goes in v1:
time: 838 us; the launch traced here: 830 us
  waiting for transfers between devices  415 us (50%)
  starting transfers between devices  162 us (19%)
  Pallas kernels  103 us (12%)
  blocking collectives  49.8 us (6%)
  local copies, waits for them, and re-layouts  35 us (4%)
  other arithmetic  31 us (4%)
  matrix products  18.8 us (2%)
  between operations  15.1 us (2%)
    ppermute x80, waiting for transfers between devices, push(): return lax.ppermute(value, 'ep', pairs)  164 us
    ppermute x80, starting transfers between devices, push(): return lax.ppermute(value, 'ep', pairs)  143 us
    psum x1, waiting for transfers between devices, shards(): grad_gate_up, grad_down = lax.psum((grad_gate_up, grad_down), 'tp')  72.2 us
    psum x1, waiting for transfers between devices, shards(): sums = lax.psum(sums, ('ep', 'tp'))  62.1 us
    ppermute x12, waiting for transfers between devices, push_tp(): lax.ppermute(value, 'tp', [(y, (y + dy) % RING) for y in range(RING)])  59.2 us
    psum x1, waiting for transfers between devices, shards(): grads = lax.psum(last[4], 'ep')  51.1 us
    all_gather x1, blocking collectives, shards(): dgain = lax.all_gather(last[5].reshape(8, LANES), ('ep', 'tp'), axis=0)  49.8 us
    pallas_call x1, Pallas kernels, experts(): pl.pallas_call(expert_kernel, grid=(STEPS,), out_shape=[piece] * 32 + [ja...  35.5 us
  transfers between devices with their start and end apart: 98, of which 37 were waited for; matrix products, arithmetic and copies ran while one was open for 9% of the time, Pallas kernels for 7%

profile of v1, /device:TPU:1, one launch (start us, length us, event | category | flops | bytes accessed | tf_op | source)
XLA Modules:
  0.0 829.6 jit_solution(13918950041421176061)
XLA Ops:
  7.2 3.6 collective-permute-start
  21.6 11.3 %collective-permute-done.x1 = bf16[256,1024]{1,0:T(8,128)(2,1)S(1)} collective-permute-done((bf16[256,1024]{1,0:T(8,128)(2,1)}, bf16[256,1024]{1,0:T(8,128)(2,1)S(1)}, u32[]{:S(2)}, u32[]{:S(2)}) %collective-permute-start) | collective-permute-done | bytes 524320 | tf_op jit(solution)/shard_map/ppermute | solution.py:67
  32.9 4.9 collective-permute-done.2.x3
  37.8 17.4 %attend.1 = (bf16[1024,1024]{1,0:T(8,128)(2,1)}, bf16[1024,512]{1,0:T(8,128)(2,1)}, bf16[1024,128]{1,0:T(8,128)(2,1)}, bf16[1024,128]{1,0:T(8,128)(2,1)}, bf16[1...) custom-call(s32[1]{0:T(128)} %bitcast.rank, ...), custom_call_target="tpu_custom_call" | custom-call | flops 6000000000 | bytes 14000000 | tf_op jit(solution)/shard_map/attend/pallas_call | solution.py:147
  60.1 20.8 %collective-permute-done.3.b1 = bf16[256,1024]{1,0:T(8,128)(2,1)S(1)} collective-permute-done((bf16[256,1024]{1,0:T(8,128)(2,1)}, bf16[256,1024]{1,0:T(8,128)(2,1)S(1)}, u32[]{:S(2)}, u32[]{:S(2)}) %collective-permute-start.3) | collective-permute-done | bytes 524320 | tf_op jit(solution)/shard_map/ppermute | solution.py:67
  82.0 3.3 route.1
  85.3 3.7 collective-permute-start.6
  94.7 4.6 collective-permute-done.6.refs_1_
  102.9 3.5 collective-permute-start.26
  110.2 5.1 dispatch.2
  115.3 3.3 collective-permute-start.12
  123.8 7.9 collective-permute-done.30.refs_6_
  132.2 5.8 collective-permute-done.31.refs_7_
  138.0 3.2 collective-permute-start.16
  141.2 7.7 collective-permute-start.17
  151.8 3.5 collective-permute-done.16.refs_5_
  155.3 3.5 collective-permute-start.21
  158.8 4.9 collective-permute-done.17.refs_6_
  165.2 9.0 %collective-permute-done.18.refs_7_ = bf16[384,512]{1,0:T(8,128)(2,1)} collective-permute-done((bf16[384,512]{1,0:T(8,128)(2,1)}, bf16[384,512]{1,0:T(8,128)(2,1)}, u32[]{:S(2)}, u32[]{:S(2)}) %collective-permute-start.18) | collective-permute-done | bytes 393248 | tf_op jit(solution)/shard_map/ppermute | solution.py:61
  177.9 5.1 dispatch.3
  183.8 3.6 collective-permute-done.23.refs_13_
  187.4 3.7 collective-permute-start.34
  191.1 4.6 collective-permute-done.24.refs_14_
  197.3 6.9 collective-permute-done.25.refs_15_
  208.3 18.7 %collective-permute-start.40 = (bf16[384,512]{1,0:T(8,128)(2,1)}, bf16[384,512]{1,0:T(8,128)(2,1)}, u32[]{:S(2)}, u32[]{:S(2)}) collective-permute-start(bf16[384,512]{1,0:T(8,128)(2,1)} %get-tuple-element.156), channel_id=1, source_target_pairs={{0,96},{4,100},{8,104},{12,108},{16,112},{20,116},{24,120},{28,124... | collective-permute-start | bytes 1179656 | tf_op jit(solution)/shard_map/ppermute | solution.py:61
  227.2 7.7 collective-permute-start.41
  239.3 4.4 collective-permute-done.40.refs_26_
  246.3 4.8 copy.80
  260.2 4.5 collective-permute-done.44.refs_30_
  264.6 8.4 %collective-permute-done.45.refs_31_ = bf16[384,512]{1,0:T(8,128)(2,1)} collective-permute-done((bf16[384,512]{1,0:T(8,128)(2,1)}, bf16[384,512]{1,0:T(8,128)(2,1)}, u32[]{:S(2)}, u32[]{:S(2)}) %collective-permute-start.45) | collective-permute-done | bytes 393248 | tf_op jit(solution)/shard_map/ppermute | solution.py:61
  273.1 35.5 %experts.1 = (bf16[384,512]{1,0:T(8,128)(2,1)}, bf16[384,512]{1,0:T(8,128)(2,1)}, bf16[384,512]{1,0:T(8,128)(2,1)}, bf16[384,512]{1,0:T(8,128)(2,1)}, bf16[384,5...) custom-call(f32[8,4,256]{2,1,0:T(4,128)} %reshape.593.slots, ...), custom_call_target="tpu_custom_call" | custom-call | flops 19000000512 | bytes 60000000 | tf_op jit(solution)/shard_map/experts/pallas_call | solution.py:361
  309.1 3.0 collective-permute-start.67
  312.7 3.0 collective-permute-start.70
  317.2 3.8 collective-permute-done.67.refs_2_
  320.9 25.1 %collective-permute-done.68.refs_3_ = bf16[384,512]{1,0:T(8,128)(2,1)S(1)} collective-permute-done((bf16[384,512]{1,0:T(8,128)(2,1)}, bf16[384,512]{1,0:T(8,128)(2,1)S(1)}, u32[]{:S(2)}, u32[]{:S(2)}) %collective-permute-start.68) | collective-permute-done | bytes 393248 | tf_op jit(solution)/shard_map/ppermute | solution.py:61
  352.6 5.4 collective-permute-done.74.refs_10_
  359.2 8.1 collective-permute-done.75.refs_11_
  367.3 3.6 collective-permute-done.77.refs_13_
  370.9 8.1 collective-permute-done.78.refs_14_
  378.9 8.4 %collective-permute-done.79.refs_15_ = bf16[384,512]{1,0:T(8,128)(2,1)S(1)} collective-permute-done((bf16[384,512]{1,0:T(8,128)(2,1)}, bf16[384,512]{1,0:T(8,128)(2,1)S(1)}, u32[]{:S(2)}, u32[]{:S(2)}) %collective-permute-start.79) | collective-permute-done | bytes 393248 | tf_op jit(solution)/shard_map/ppermute | solution.py:61
  388.1 5.3 combine.3
  397.6 4.2 collective-permute-start.84
  401.9 6.2 collective-permute-done.80.refs_1_
  408.0 3.0 collective-permute-start.85
  411.8 5.0 all-to-all-start
  417.5 6.6 all-to-all-done
  425.9 4.8 unroute.1
  437.0 19.0 %collective-permute-done.86.d1 = bf16[256,1024]{1,0:T(8,128)(2,1)S(1)} collective-permute-done((bf16[256,1024]{1,0:T(8,128)(2,1)}, bf16[256,1024]{1,0:T(8,128)(2,1)S(1)}, u32[]{:S(2)}, u32[]{:S(2)}) %collective-permute-start.86) | collective-permute-done | bytes 524320 | tf_op jit(solution)/shard_map/ppermute | solution.py:67
  457.8 10.7 %convolution_convert_fusion = bf16[1024,1024]{0,1:T(8,128)(2,1)S(1)} fusion(bf16[3072,1024]{1,0:T(8,128)(2,1)} %get-tuple-element.228, bf16[3072,1024]{1,0:T(8,128)(2,1)} %get-tuple-element.229), kind=kOutput, calls=%fused_computation.5 | convolution fusion | flops 6443499520 | bytes 14680064 | tf_op jit(solution)/shard_map/dot_general | solution.py:45
  471.4 4.3 collective-permute-start.50
  475.7 4.3 unmix.1
  481.9 16.9 %unattend.1 = (bf16[256,1024]{1,0:T(8,128)(2,1)}, bf16[256,1024]{1,0:T(8,128)(2,1)}, bf16[256,1024]{1,0:T(8,128)(2,1)}, bf16[256,1024]{1,0:T(8,128)(2,1)}, bf16[1024,512]{1,0:T(8,128)(2,1)}, /*index=5*/f32[1024,1]{1,0:T(8,128)}) custom-call(s32[1]{0:T(128)} %bitcast.rank, bf16[1024,512]{1,0:T(8,128)(2,1)} %get-tuple-element.212.q_in, ...), custom_call_target="tpu_custom_call" | custom-call | flops 10000000000 | bytes 14000000 | tf_op jit(solution)/shard_map/unattend/pallas_call | solution.py:516
  506.3 8.1 fusion
  514.5 4.0 copy.87
  521.3 8.3 collective-permute-done.58.refs_14_
  529.6 8.4 %collective-permute-done.59.refs_15_ = bf16[384,512]{1,0:T(8,128)(2,1)} collective-permute-done((bf16[384,512]{1,0:T(8,128)(2,1)}, bf16[384,512]{1,0:T(8,128)(2,1)}, u32[]{:S(2)}, u32[]{:S(2)}) %collective-permute-start.59) | collective-permute-done | bytes 393248 | tf_op jit(solution)/shard_map/ppermute | solution.py:61
  538.1 5.4 combine.2
  552.4 5.4 collective-permute-start.60
  557.8 3.8 collective-permute-done.63
  567.3 62.1 %all-reduce.6.cloned.1.call-done = f32[40,1024]{1,0:T(8,128)} async-done(((f32[40,1024]{1,0:T(8,128)}), f32[40,1024]{1,0:T(8,128)}) %all-reduce.6.cloned.1.call-update) | async-done | bytes 163856 | tf_op jit(solution)/shard_map/psum | solution.py:600
  632.5 49.8 %all_gather.11 = f32[128,8,128]{2,1,0:T(8,128)S(1)} all-gather(f32[1,8,128]{2,1,0:T(8,128)S(1)} %bitcast.45), channel_id=1, replica_groups=mesh['ep'=32,'tp'=4] {'ep','tp'}, dimensions={0}, use_global_device_ids=true | all-gather | bytes 528384 | tf_op jit(solution)/shard_map/all_gather | solution.py:612
  686.3 51.1 %all-reduce.8.cloned.1.call-done = (bf16[1024,512]{1,0:T(8,128)(2,1)}, bf16[256,1024]{1,0:T(8,128)(2,1)}) async-done(((bf16[1024,512]{1,0:T(8,128)(2,1)}, bf16[256,1024]{1,0:T(8,128)(2,1)}), (bf16[1024,512]{1,0:T(8,128)(2,1)}, bf16[256,1024]{1,0:T(8,128)(2,1)})) %all-reduce.8.cloned.1.call-update) | async-done | bytes 1572880 | tf_op jit(solution)/shard_map/psum | solution.py:611
  743.7 72.2 %all-reduce.10.cloned.1.call-done = (bf16[1,1024,2,512]{3,2,1,0:T(2,128)(2,1)}, bf16[1,512,1024]{2,1,0:T(8,128)(2,1)}) async-done(((bf16[1,1024,2,512]{3,2,1,0:T(2,128)(2,1)}, bf16[1,512,1024]{2,1,0:T(8,128)(2,1)}), (bf16[1,1024,2,512]{3,2,1,0:T(2,128)(2,1)}, bf16[1,512,1024]{2,1,0:T(8,128)(2,1)})) %all-reduce.10.cloned.1.call-update) | async-done | bytes 3145744 | tf_op jit(solution)/shard_map/psum | solution.py:597
  815.9 5.1 reshape.601
  (372 shorter events, 136.6 us)
Async XLA Ops:
  7.2 85.7 %all-gather.3.cloned.1.call-start = ((), (), s32[]{:S(2)}) async-start(), calls=%async_computation.1 | async-start | bytes 1081344 | tf_op jit(solution)/shard_map/all_gather | solution.py:554
  7.2 25.6 %collective-permute-start = (bf16[256,1024]{1,0:T(8,128)(2,1)}, bf16[256,1024]{1,0:T(8,128)(2,1)S(1)}, u32[]{:S(2)}, u32[]{:S(2)}) collective-permute-start(bf16[256,1024]{1,0:T(8,128)(2,1)} %x.1), channel_id=1, source_target_pairs={{0,3},{1,0},{2,1},{3,2},{4,7},{5,4},{6,5},{7,6},{8,11},{9,8},{10,9... | collective-permute-start | bytes 1572872 | tf_op jit(solution)/shard_map/ppermute | solution.py:67
  10.9 22.0 %collective-permute-start.1 = (bf16[256,1024]{1,0:T(8,128)(2,1)}, bf16[256,1024]{1,0:T(8,128)(2,1)S(1)}, u32[]{:S(2)}, u32[]{:S(2)}) collective-permute-start(bf16[256,1024]{1,0:T(8,128)(2,1)} %x.1), channel_id=1, source_target_pairs={{0,2},{1,3},{2,0},{3,1},{4,6},{5,7},{6,4},{7,5},{8,10},{9,11},{10,... | collective-permute-start | bytes 1572872 | tf_op jit(solution)/shard_map/ppermute | solution.py:67
  11.2 26.6 %collective-permute-start.2 = (bf16[256,1024]{1,0:T(8,128)(2,1)}, bf16[256,1024]{1,0:T(8,128)(2,1)}, u32[]{:S(2)}, u32[]{:S(2)}) collective-permute-start(bf16[256,1024]{1,0:T(8,128)(2,1)} %x.1), channel_id=1, source_target_pairs={{0,1},{1,2},{2,3},{3,0},{4,5},{5,6},{6,7},{7,4},{8,9},{9,10},{10,1... | collective-permute-start | bytes 1572872 | tf_op jit(solution)/shard_map/ppermute | solution.py:67
  14.2 242.8 %all-gather.5.cloned.1.call-start = ((), (), s32[]{:S(2)}) async-start(), calls=%async_computation.2 | async-start | bytes 1081344 | tf_op jit(solution)/shard_map/all_gather | solution.py:579
  55.2 25.7 %collective-permute-start.3 = (bf16[256,1024]{1,0:T(8,128)(2,1)}, bf16[256,1024]{1,0:T(8,128)(2,1)S(1)}, u32[]{:S(2)}, u32[]{:S(2)}) collective-permute-start(bf16[256,1024]{1,0:T(8,128)(2,1)} %get-tuple-element.123), channel_id=1, source_target_pairs={{0,1},{1,2},{2,3},{3,0},{4,5},{5,6},{6,7},{7,4},{8,9},{9,10},{10,1... | collective-permute-start | bytes 1572872 | tf_op jit(solution)/shard_map/ppermute | solution.py:67
  55.2 25.6 %collective-permute-start.4 = (bf16[256,1024]{1,0:T(8,128)(2,1)}, bf16[256,1024]{1,0:T(8,128)(2,1)S(1)}, u32[]{:S(2)}, u32[]{:S(2)}) collective-permute-start(bf16[256,1024]{1,0:T(8,128)(2,1)} %get-tuple-element.124), channel_id=1, source_target_pairs={{0,2},{1,3},{2,0},{3,1},{4,6},{5,7},{6,4},{7,5},{8,10},{9,11},{10,... | collective-permute-start | bytes 1572872 | tf_op jit(solution)/shard_map/ppermute | solution.py:67
  55.9 25.3 %collective-permute-start.5 = (bf16[256,1024]{1,0:T(8,128)(2,1)}, bf16[256,1024]{1,0:T(8,128)(2,1)S(1)}, u32[]{:S(2)}, u32[]{:S(2)}) collective-permute-start(bf16[256,1024]{1,0:T(8,128)(2,1)} %get-tuple-element.125), channel_id=1, source_target_pairs={{0,3},{1,0},{2,1},{3,2},{4,7},{5,4},{6,5},{7,6},{8,11},{9,8},{10,9... | collective-permute-start | bytes 1572872 | tf_op jit(solution)/shard_map/ppermute | solution.py:67
  115.3 25.9 %collective-permute-start.12 = (bf16[384,512]{1,0:T(8,128)(2,1)}, bf16[384,512]{1,0:T(8,128)(2,1)S(1)}, u32[]{:S(2)}, u32[]{:S(2)}) collective-permute-start(bf16[384,512]{1,0:T(8,128)(2,1)} %get-tuple-element.131), channel_id=1, source_target_pairs={{0,4},{4,0},{8,12},{12,8},{16,20},{20,16},{24,28},{28,24},{32,36},... | collective-permute-start | bytes 1179656 | tf_op jit(solution)/shard_map/ppermute | solution.py:61
  118.6 30.3 %collective-permute-start.13 = (bf16[384,512]{1,0:T(8,128)(2,1)}, bf16[384,512]{1,0:T(8,128)(2,1)S(1)}, u32[]{:S(2)}, u32[]{:S(2)}) collective-permute-start(bf16[384,512]{1,0:T(8,128)(2,1)} %get-tuple-element.132), channel_id=1, source_target_pairs={{0,24},{4,28},{8,0},{12,4},{16,8},{20,12},{24,16},{28,20},{32,56},... | collective-permute-start | bytes 1179656 | tf_op jit(solution)/shard_map/ppermute | solution.py:61
  120.6 28.4 %collective-permute-start.14 = (bf16[384,512]{1,0:T(8,128)(2,1)}, bf16[384,512]{1,0:T(8,128)(2,1)S(1)}, u32[]{:S(2)}, u32[]{:S(2)}) collective-permute-start(bf16[384,512]{1,0:T(8,128)(2,1)} %get-tuple-element.133), channel_id=1, source_target_pairs={{0,28},{4,24},{8,4},{12,0},{16,12},{20,8},{24,20},{28,16},{32,60},... | collective-permute-start | bytes 1179656 | tf_op jit(solution)/shard_map/ppermute | solution.py:61
  141.2 22.5 %collective-permute-start.17 = (bf16[384,512]{1,0:T(8,128)(2,1)}, bf16[384,512]{1,0:T(8,128)(2,1)}, u32[]{:S(2)}, u32[]{:S(2)}) collective-permute-start(bf16[384,512]{1,0:T(8,128)(2,1)} %get-tuple-element.136), channel_id=1, source_target_pairs={{0,8},{4,12},{8,16},{12,20},{16,24},{20,28},{24,0},{28,4},{32,40},... | collective-permute-start | bytes 1179656 | tf_op jit(solution)/shard_map/ppermute | solution.py:61
  149.0 25.2 %collective-permute-start.18 = (bf16[384,512]{1,0:T(8,128)(2,1)}, bf16[384,512]{1,0:T(8,128)(2,1)}, u32[]{:S(2)}, u32[]{:S(2)}) collective-permute-start(bf16[384,512]{1,0:T(8,128)(2,1)} %get-tuple-element.137), channel_id=1, source_target_pairs={{0,12},{4,8},{8,20},{12,16},{16,28},{20,24},{24,4},{28,0},{32,44},... | collective-permute-start | bytes 1179656 | tf_op jit(solution)/shard_map/ppermute | solution.py:61
  149.0 27.0 %collective-permute-start.19 = (bf16[384,512]{1,0:T(8,128)(2,1)}, bf16[384,512]{1,0:T(8,128)(2,1)}, u32[]{:S(2)}, u32[]{:S(2)}) collective-permute-start(bf16[384,512]{1,0:T(8,128)(2,1)} %get-tuple-element.139), channel_id=1, source_target_pairs={{0,4},{4,0},{8,12},{12,8},{16,20},{20,16},{24,28},{28,24},{32,36},... | collective-permute-start | bytes 1179656 | tf_op jit(solution)/shard_map/ppermute | solution.py:61
  149.5 33.5 %collective-permute-start.20 = (bf16[384,512]{1,0:T(8,128)(2,1)}, bf16[384,512]{1,0:T(8,128)(2,1)S(1)}, u32[]{:S(2)}, u32[]{:S(2)}) collective-permute-start(bf16[384,512]{1,0:T(8,128)(2,1)} %get-tuple-element.140), channel_id=1, source_target_pairs={{0,96},{4,100},{8,104},{12,108},{16,112},{20,116},{24,120},{28,124... | collective-permute-start | bytes 1179656 | tf_op jit(solution)/shard_map/ppermute | solution.py:61
  155.3 27.8 %collective-permute-start.21 = (bf16[384,512]{1,0:T(8,128)(2,1)}, bf16[384,512]{1,0:T(8,128)(2,1)S(1)}, u32[]{:S(2)}, u32[]{:S(2)}) collective-permute-start(bf16[384,512]{1,0:T(8,128)(2,1)} %get-tuple-element.141), channel_id=1, source_target_pairs={{0,100},{4,96},{8,108},{12,104},{16,116},{20,112},{24,124},{28,120... | collective-permute-start | bytes 1179656 | tf_op jit(solution)/shard_map/ppermute | solution.py:61
  163.7 19.8 %collective-permute-start.22 = (bf16[384,512]{1,0:T(8,128)(2,1)}, bf16[384,512]{1,0:T(8,128)(2,1)S(1)}, u32[]{:S(2)}, u32[]{:S(2)}) collective-permute-start(bf16[384,512]{1,0:T(8,128)(2,1)} %get-tuple-element.142), channel_id=1, source_target_pairs={{0,64},{4,68},{8,72},{12,76},{16,80},{20,84},{24,88},{28,92},{32,9... | collective-permute-start | bytes 1179656 | tf_op jit(solution)/shard_map/ppermute | solution.py:61
  176.0 19.8 %collective-permute-start.24 = (bf16[384,512]{1,0:T(8,128)(2,1)}, bf16[384,512]{1,0:T(8,128)(2,1)S(1)}, u32[]{:S(2)}, u32[]{:S(2)}) collective-permute-start(bf16[384,512]{1,0:T(8,128)(2,1)} %get-tuple-element.144), channel_id=1, source_target_pairs={{0,32},{4,36},{8,40},{12,44},{16,48},{20,52},{24,56},{28,60},{32,6... | collective-permute-start | bytes 1179656 | tf_op jit(solution)/shard_map/ppermute | solution.py:61
  183.0 21.2 %collective-permute-start.25 = (bf16[384,512]{1,0:T(8,128)(2,1)S(1)}, bf16[384,512]{1,0:T(8,128)(2,1)S(1)}, u32[]{:S(2)}, u32[]{:S(2)}) collective-permute-start(bf16[384,512]{1,0:T(8,128)(2,1)S(1)} %copy-done.61), channel_id=1, source_target_pairs={{0,36},{4,32},{8,44},{12,40},{16,52},{20,48},{24,60},{28,56},{32,6... | collective-permute-start | bytes 1179656 | tf_op jit(solution)/shard_map/ppermute | solution.py:61
  183.1 22.8 %collective-permute-start.32 = (bf16[384,512]{1,0:T(8,128)(2,1)}, bf16[384,512]{1,0:T(8,128)(2,1)S(1)}, u32[]{:S(2)}, u32[]{:S(2)}) collective-permute-start(bf16[384,512]{1,0:T(8,128)(2,1)} %get-tuple-element.147), channel_id=1, source_target_pairs={{0,4},{4,0},{8,12},{12,8},{16,20},{20,16},{24,28},{28,24},{32,36},... | collective-permute-start | bytes 1179656 | tf_op jit(solution)/shard_map/ppermute | solution.py:61
  183.5 24.2 %collective-permute-start.33 = (bf16[384,512]{1,0:T(8,128)(2,1)}, bf16[384,512]{1,0:T(8,128)(2,1)S(1)}, u32[]{:S(2)}, u32[]{:S(2)}) collective-permute-start(bf16[384,512]{1,0:T(8,128)(2,1)} %get-tuple-element.148), channel_id=1, source_target_pairs={{0,24},{4,28},{8,0},{12,4},{16,8},{20,12},{24,16},{28,20},{32,56},... | collective-permute-start | bytes 1179656 | tf_op jit(solution)/shard_map/ppermute | solution.py:61
  187.4 20.5 %collective-permute-start.34 = (bf16[384,512]{1,0:T(8,128)(2,1)}, bf16[384,512]{1,0:T(8,128)(2,1)S(1)}, u32[]{:S(2)}, u32[]{:S(2)}) collective-permute-start(bf16[384,512]{1,0:T(8,128)(2,1)} %get-tuple-element.149), channel_id=1, source_target_pairs={{0,28},{4,24},{8,4},{12,0},{16,12},{20,8},{24,20},{28,16},{32,60},... | collective-permute-start | bytes 1179656 | tf_op jit(solution)/shard_map/ppermute | solution.py:61
  204.2 23.0 %collective-permute-start.36 = (bf16[384,512]{1,0:T(8,128)(2,1)}, bf16[384,512]{1,0:T(8,128)(2,1)S(1)}, u32[]{:S(2)}, u32[]{:S(2)}) collective-permute-start(bf16[384,512]{1,0:T(8,128)(2,1)} %get-tuple-element.151), channel_id=1, source_target_pairs={{0,20},{4,16},{8,28},{12,24},{16,4},{20,0},{24,12},{28,8},{32,52},... | collective-permute-start | bytes 1179656 | tf_op jit(solution)/shard_map/ppermute | solution.py:61
  205.9 28.9 %collective-permute-start.37 = (bf16[384,512]{1,0:T(8,128)(2,1)}, bf16[384,512]{1,0:T(8,128)(2,1)}, u32[]{:S(2)}, u32[]{:S(2)}) collective-permute-start(bf16[384,512]{1,0:T(8,128)(2,1)} %get-tuple-element.152), channel_id=1, source_target_pairs={{0,8},{4,12},{8,16},{12,20},{16,24},{20,28},{24,0},{28,4},{32,40},... | collective-permute-start | bytes 1179656 | tf_op jit(solution)/shard_map/ppermute | solution.py:61
  207.7 28.9 %collective-permute-start.38 = (bf16[384,512]{1,0:T(8,128)(2,1)}, bf16[384,512]{1,0:T(8,128)(2,1)}, u32[]{:S(2)}, u32[]{:S(2)}) collective-permute-start(bf16[384,512]{1,0:T(8,128)(2,1)} %get-tuple-element.153), channel_id=1, source_target_pairs={{0,12},{4,8},{8,20},{12,16},{16,28},{20,24},{24,4},{28,0},{32,44},... | collective-permute-start | bytes 1179656 | tf_op jit(solution)/shard_map/ppermute | solution.py:61
  207.9 30.3 %collective-permute-start.39 = (bf16[384,512]{1,0:T(8,128)(2,1)}, bf16[384,512]{1,0:T(8,128)(2,1)}, u32[]{:S(2)}, u32[]{:S(2)}) collective-permute-start(bf16[384,512]{1,0:T(8,128)(2,1)} %get-tuple-element.155), channel_id=1, source_target_pairs={{0,4},{4,0},{8,12},{12,8},{16,20},{20,16},{24,28},{28,24},{32,36},... | collective-permute-start | bytes 1179656 | tf_op jit(solution)/shard_map/ppermute | solution.py:61
  208.3 35.4 %collective-permute-start.40 = (bf16[384,512]{1,0:T(8,128)(2,1)}, bf16[384,512]{1,0:T(8,128)(2,1)}, u32[]{:S(2)}, u32[]{:S(2)}) collective-permute-start(bf16[384,512]{1,0:T(8,128)(2,1)} %get-tuple-element.156), channel_id=1, source_target_pairs={{0,96},{4,100},{8,104},{12,108},{16,112},{20,116},{24,120},{28,124... | collective-permute-start | bytes 1179656 | tf_op jit(solution)/shard_map/ppermute | solution.py:61
  227.2 32.9 %collective-permute-start.41 = (bf16[384,512]{1,0:T(8,128)(2,1)}, bf16[384,512]{1,0:T(8,128)(2,1)}, u32[]{:S(2)}, u32[]{:S(2)}) collective-permute-start(bf16[384,512]{1,0:T(8,128)(2,1)} %get-tuple-element.157), channel_id=1, source_target_pairs={{0,100},{4,96},{8,108},{12,104},{16,116},{20,112},{24,124},{28,120... | collective-permute-start | bytes 1179656 | tf_op jit(solution)/shard_map/ppermute | solution.py:61
  234.9 25.3 %collective-permute-start.42 = (bf16[384,512]{1,0:T(8,128)(2,1)}, bf16[384,512]{1,0:T(8,128)(2,1)}, u32[]{:S(2)}, u32[]{:S(2)}) collective-permute-start(bf16[384,512]{1,0:T(8,128)(2,1)} %get-tuple-element.158), channel_id=1, source_target_pairs={{0,64},{4,68},{8,72},{12,76},{16,80},{20,84},{24,88},{28,92},{32,9... | collective-permute-start | bytes 1179656 | tf_op jit(solution)/shard_map/ppermute | solution.py:61
  236.6 23.5 %collective-permute-start.43 = (bf16[384,512]{1,0:T(8,128)(2,1)}, bf16[384,512]{1,0:T(8,128)(2,1)}, u32[]{:S(2)}, u32[]{:S(2)}) collective-permute-start(bf16[384,512]{1,0:T(8,128)(2,1)} %get-tuple-element.159), channel_id=1, source_target_pairs={{0,68},{4,64},{8,76},{12,72},{16,84},{20,80},{24,92},{28,88},{32,1... | collective-permute-start | bytes 1179656 | tf_op jit(solution)/shard_map/ppermute | solution.py:61
  238.2 26.5 %collective-permute-start.44 = (bf16[384,512]{1,0:T(8,128)(2,1)}, bf16[384,512]{1,0:T(8,128)(2,1)}, u32[]{:S(2)}, u32[]{:S(2)}) collective-permute-start(bf16[384,512]{1,0:T(8,128)(2,1)} %get-tuple-element.160), channel_id=1, source_target_pairs={{0,32},{4,36},{8,40},{12,44},{16,48},{20,52},{24,56},{28,60},{32,6... | collective-permute-start | bytes 1179656 | tf_op jit(solution)/shard_map/ppermute | solution.py:61
  243.7 29.4 %collective-permute-start.45 = (bf16[384,512]{1,0:T(8,128)(2,1)}, bf16[384,512]{1,0:T(8,128)(2,1)}, u32[]{:S(2)}, u32[]{:S(2)}) collective-permute-start(bf16[384,512]{1,0:T(8,128)(2,1)} %get-tuple-element.161), channel_id=1, source_target_pairs={{0,36},{4,32},{8,44},{12,40},{16,52},{20,48},{24,60},{28,56},{32,6... | collective-permute-start | bytes 1179656 | tf_op jit(solution)/shard_map/ppermute | solution.py:61
  312.1 33.9 %collective-permute-start.68 = (bf16[384,512]{1,0:T(8,128)(2,1)}, bf16[384,512]{1,0:T(8,128)(2,1)S(1)}, u32[]{:S(2)}, u32[]{:S(2)}) collective-permute-start(bf16[384,512]{1,0:T(8,128)(2,1)} %get-tuple-element.189), channel_id=1, source_target_pairs={{0,28},{4,24},{8,4},{12,0},{16,12},{20,8},{24,20},{28,16},{32,60},... | collective-permute-start | bytes 1179656 | tf_op jit(solution)/shard_map/ppermute | solution.py:61
  312.2 34.9 %collective-permute-start.69 = (bf16[384,512]{1,0:T(8,128)(2,1)}, bf16[384,512]{1,0:T(8,128)(2,1)S(1)}, u32[]{:S(2)}, u32[]{:S(2)}) collective-permute-start(bf16[384,512]{1,0:T(8,128)(2,1)} %get-tuple-element.190), channel_id=1, source_target_pairs={{0,16},{4,20},{8,24},{12,28},{16,0},{20,4},{24,8},{28,12},{32,48},... | collective-permute-start | bytes 1179656 | tf_op jit(solution)/shard_map/ppermute | solution.py:61
  312.7 34.4 %collective-permute-start.70 = (bf16[384,512]{1,0:T(8,128)(2,1)}, bf16[384,512]{1,0:T(8,128)(2,1)S(1)}, u32[]{:S(2)}, u32[]{:S(2)}) collective-permute-start(bf16[384,512]{1,0:T(8,128)(2,1)} %get-tuple-element.191), channel_id=1, source_target_pairs={{0,20},{4,16},{8,28},{12,24},{16,4},{20,0},{24,12},{28,8},{32,52},... | collective-permute-start | bytes 1179656 | tf_op jit(solution)/shard_map/ppermute | solution.py:61
  315.7 33.6 %collective-permute-start.71 = (bf16[384,512]{1,0:T(8,128)(2,1)}, bf16[384,512]{1,0:T(8,128)(2,1)S(1)}, u32[]{:S(2)}, u32[]{:S(2)}) collective-permute-start(bf16[384,512]{1,0:T(8,128)(2,1)} %get-tuple-element.192), channel_id=1, source_target_pairs={{0,8},{4,12},{8,16},{12,20},{16,24},{20,28},{24,0},{28,4},{32,40},... | collective-permute-start | bytes 1179656 | tf_op jit(solution)/shard_map/ppermute | solution.py:61
  320.9 29.7 %collective-permute-start.72 = (bf16[384,512]{1,0:T(8,128)(2,1)}, bf16[384,512]{1,0:T(8,128)(2,1)S(1)}, u32[]{:S(2)}, u32[]{:S(2)}) collective-permute-start(bf16[384,512]{1,0:T(8,128)(2,1)} %get-tuple-element.193), channel_id=1, source_target_pairs={{0,12},{4,8},{8,20},{12,16},{16,28},{20,24},{24,4},{28,0},{32,44},... | collective-permute-start | bytes 1179656 | tf_op jit(solution)/shard_map/ppermute | solution.py:61
  347.1 20.2 %collective-permute-start.75 = (bf16[384,512]{1,0:T(8,128)(2,1)}, bf16[384,512]{1,0:T(8,128)(2,1)S(1)}, u32[]{:S(2)}, u32[]{:S(2)}) collective-permute-start(bf16[384,512]{1,0:T(8,128)(2,1)} %get-tuple-element.197), channel_id=1, source_target_pairs={{0,100},{4,96},{8,108},{12,104},{16,116},{20,112},{24,124},{28,120... | collective-permute-start | bytes 1179656 | tf_op jit(solution)/shard_map/ppermute | solution.py:61
  350.6 20.3 %collective-permute-start.77 = (bf16[384,512]{1,0:T(8,128)(2,1)}, bf16[384,512]{1,0:T(8,128)(2,1)S(1)}, u32[]{:S(2)}, u32[]{:S(2)}) collective-permute-start(bf16[384,512]{1,0:T(8,128)(2,1)} %get-tuple-element.199), channel_id=1, source_target_pairs={{0,68},{4,64},{8,76},{12,72},{16,84},{20,80},{24,92},{28,88},{32,1... | collective-permute-start | bytes 1179656 | tf_op jit(solution)/shard_map/ppermute | solution.py:61
  352.6 26.4 %collective-permute-start.78 = (bf16[384,512]{1,0:T(8,128)(2,1)}, bf16[384,512]{1,0:T(8,128)(2,1)S(1)}, u32[]{:S(2)}, u32[]{:S(2)}) collective-permute-start(bf16[384,512]{1,0:T(8,128)(2,1)} %get-tuple-element.200), channel_id=1, source_target_pairs={{0,32},{4,36},{8,40},{12,44},{16,48},{20,52},{24,56},{28,60},{32,6... | collective-permute-start | bytes 1179656 | tf_op jit(solution)/shard_map/ppermute | solution.py:61
  358.0 29.4 %collective-permute-start.79 = (bf16[384,512]{1,0:T(8,128)(2,1)}, bf16[384,512]{1,0:T(8,128)(2,1)S(1)}, u32[]{:S(2)}, u32[]{:S(2)}) collective-permute-start(bf16[384,512]{1,0:T(8,128)(2,1)} %get-tuple-element.201), channel_id=1, source_target_pairs={{0,36},{4,32},{8,44},{12,40},{16,52},{20,48},{24,60},{28,56},{32,6... | collective-permute-start | bytes 1179656 | tf_op jit(solution)/shard_map/ppermute | solution.py:61
  394.2 30.6 %collective-permute-start.81 = (bf16[256,512]{1,0:T(8,128)(2,1)}, bf16[256,512]{1,0:T(8,128)(2,1)S(1)}, u32[]{:S(2)}, u32[]{:S(2)}) collective-permute-start(bf16[256,512]{1,0:T(8,128)(2,1)} %get-tuple-element.204), channel_id=1, source_target_pairs={{0,64},{4,68},{8,72},{12,76},{16,80},{20,84},{24,88},{28,92},{32,9... | collective-permute-start | bytes 786440 | tf_op jit(solution)/shard_map/ppermute | solution.py:61
  395.6 29.2 %collective-permute-start.82 = (bf16[256,512]{1,0:T(8,128)(2,1)}, bf16[256,512]{1,0:T(8,128)(2,1)S(1)}, u32[]{:S(2)}, u32[]{:S(2)}) collective-permute-start(bf16[256,512]{1,0:T(8,128)(2,1)} %get-tuple-element.205), channel_id=1, source_target_pairs={{0,96},{4,100},{8,104},{12,108},{16,112},{20,116},{24,120},{28,124... | collective-permute-start | bytes 786440 | tf_op jit(solution)/shard_map/ppermute | solution.py:61
  397.6 27.2 %collective-permute-start.83 = (bf16[256,512]{1,0:T(8,128)(2,1)}, bf16[256,512]{1,0:T(8,128)(2,1)S(1)}, u32[]{:S(2)}, u32[]{:S(2)}) collective-permute-start(bf16[256,512]{1,0:T(8,128)(2,1)} %get-tuple-element.207), channel_id=1, source_target_pairs={{0,8},{4,12},{8,16},{12,20},{16,24},{20,28},{24,0},{28,4},{32,40},... | collective-permute-start | bytes 786440 | tf_op jit(solution)/shard_map/ppermute | solution.py:61
  397.6 27.2 %collective-permute-start.84 = (bf16[256,512]{1,0:T(8,128)(2,1)}, bf16[256,512]{1,0:T(8,128)(2,1)S(1)}, u32[]{:S(2)}, u32[]{:S(2)}) collective-permute-start(bf16[256,512]{1,0:T(8,128)(2,1)} %get-tuple-element.208), channel_id=1, source_target_pairs={{0,16},{4,20},{8,24},{12,28},{16,0},{20,4},{24,8},{28,12},{32,48},... | collective-permute-start | bytes 786440 | tf_op jit(solution)/shard_map/ppermute | solution.py:61
  416.8 212.6 %all-reduce.6.cloned.1.call-start = ((), (), s32[]{:S(2)}) async-start(), calls=%async_computation.3 | async-start | bytes 327680 | tf_op jit(solution)/shard_map/psum | solution.py:600
  430.8 25.3 %collective-permute-start.86 = (bf16[256,1024]{1,0:T(8,128)(2,1)}, bf16[256,1024]{1,0:T(8,128)(2,1)S(1)}, u32[]{:S(2)}, u32[]{:S(2)}) collective-permute-start(bf16[256,1024]{1,0:T(8,128)(2,1)} %get-tuple-element.216.d0), channel_id=1, source_target_pairs={{0,3},{1,0},{2,1},{3,2},{4,7},{5,4},{6,5},{7,6},{8,11},{9,8},{10,9... | collective-permute-start | bytes 1572872 | tf_op jit(solution)/shard_map/ppermute | solution.py:67
  433.7 23.2 %collective-permute-start.87 = (bf16[256,1024]{1,0:T(8,128)(2,1)}, bf16[256,1024]{1,0:T(8,128)(2,1)S(1)}, u32[]{:S(2)}, u32[]{:S(2)}) collective-permute-start(bf16[256,1024]{1,0:T(8,128)(2,1)} %get-tuple-element.216.d0), channel_id=1, source_target_pairs={{0,2},{1,3},{2,0},{3,1},{4,6},{5,7},{6,4},{7,5},{8,10},{9,11},{10,... | collective-permute-start | bytes 1572872 | tf_op jit(solution)/shard_map/ppermute | solution.py:67
  434.8 45.2 %collective-permute-start.46 = (bf16[384,512]{1,0:T(8,128)(2,1)}, bf16[384,512]{1,0:T(8,128)(2,1)S(1)}, u32[]{:S(2)}, u32[]{:S(2)}) collective-permute-start(bf16[384,512]{1,0:T(8,128)(2,1)} %get-tuple-element.163), channel_id=1, source_target_pairs={{0,4},{4,0},{8,12},{12,8},{16,20},{20,16},{24,28},{28,24},{32,36},... | collective-permute-start | bytes 1179656 | tf_op jit(solution)/shard_map/ppermute | solution.py:61
  435.7 44.7 %collective-permute-start.47 = (bf16[384,512]{1,0:T(8,128)(2,1)}, bf16[384,512]{1,0:T(8,128)(2,1)S(1)}, u32[]{:S(2)}, u32[]{:S(2)}) collective-permute-start(bf16[384,512]{1,0:T(8,128)(2,1)} %get-tuple-element.164), channel_id=1, source_target_pairs={{0,24},{4,28},{8,0},{12,4},{16,8},{20,12},{24,16},{28,20},{32,56},... | collective-permute-start | bytes 1179656 | tf_op jit(solution)/shard_map/ppermute | solution.py:61
  436.6 43.8 %collective-permute-start.48 = (bf16[384,512]{1,0:T(8,128)(2,1)}, bf16[384,512]{1,0:T(8,128)(2,1)S(1)}, u32[]{:S(2)}, u32[]{:S(2)}) collective-permute-start(bf16[384,512]{1,0:T(8,128)(2,1)} %get-tuple-element.165), channel_id=1, source_target_pairs={{0,28},{4,24},{8,4},{12,0},{16,12},{20,8},{24,20},{28,16},{32,60},... | collective-permute-start | bytes 1179656 | tf_op jit(solution)/shard_map/ppermute | solution.py:61
  456.1 25.0 %collective-permute-start.49 = (bf16[384,512]{1,0:T(8,128)(2,1)}, bf16[384,512]{1,0:T(8,128)(2,1)}, u32[]{:S(2)}, u32[]{:S(2)}) collective-permute-start(bf16[384,512]{1,0:T(8,128)(2,1)} %get-tuple-element.166), channel_id=1, source_target_pairs={{0,16},{4,20},{8,24},{12,28},{16,0},{20,4},{24,8},{28,12},{32,48},... | collective-permute-start | bytes 1179656 | tf_op jit(solution)/shard_map/ppermute | solution.py:61
  468.5 268.9 %all-reduce.8.cloned.1.call-start = ((), (), s32[]{:S(2)}) async-start(), calls=%async_computation.4 | async-start | bytes 3145728 | tf_op jit(solution)/shard_map/psum | solution.py:611
  471.4 27.5 %collective-permute-start.50 = (bf16[384,512]{1,0:T(8,128)(2,1)}, bf16[384,512]{1,0:T(8,128)(2,1)}, u32[]{:S(2)}, u32[]{:S(2)}) collective-permute-start(bf16[384,512]{1,0:T(8,128)(2,1)} %get-tuple-element.167), channel_id=1, source_target_pairs={{0,20},{4,16},{8,28},{12,24},{16,4},{20,0},{24,12},{28,8},{32,52},... | collective-permute-start | bytes 1179656 | tf_op jit(solution)/shard_map/ppermute | solution.py:61
  480.0 19.6 %collective-permute-start.51 = (bf16[384,512]{1,0:T(8,128)(2,1)}, bf16[384,512]{1,0:T(8,128)(2,1)}, u32[]{:S(2)}, u32[]{:S(2)}) collective-permute-start(bf16[384,512]{1,0:T(8,128)(2,1)} %get-tuple-element.168), channel_id=1, source_target_pairs={{0,8},{4,12},{8,16},{12,20},{16,24},{20,28},{24,0},{28,4},{32,40},... | collective-permute-start | bytes 1179656 | tf_op jit(solution)/shard_map/ppermute | solution.py:61
  480.4 22.7 %collective-permute-start.52 = (bf16[384,512]{1,0:T(8,128)(2,1)}, bf16[384,512]{1,0:T(8,128)(2,1)}, u32[]{:S(2)}, u32[]{:S(2)}) collective-permute-start(bf16[384,512]{1,0:T(8,128)(2,1)} %get-tuple-element.169), channel_id=1, source_target_pairs={{0,12},{4,8},{8,20},{12,16},{16,28},{20,24},{24,4},{28,0},{32,44},... | collective-permute-start | bytes 1179656 | tf_op jit(solution)/shard_map/ppermute | solution.py:61
  480.4 24.0 %collective-permute-start.53 = (bf16[384,512]{1,0:T(8,128)(2,1)}, bf16[384,512]{1,0:T(8,128)(2,1)}, u32[]{:S(2)}, u32[]{:S(2)}) collective-permute-start(bf16[384,512]{1,0:T(8,128)(2,1)} %get-tuple-element.171), channel_id=1, source_target_pairs={{0,4},{4,0},{8,12},{12,8},{16,20},{20,16},{24,28},{28,24},{32,36},... | collective-permute-start | bytes 1179656 | tf_op jit(solution)/shard_map/ppermute | solution.py:61
  481.0 23.9 %collective-permute-start.54 = (bf16[384,512]{1,0:T(8,128)(2,1)}, bf16[384,512]{1,0:T(8,128)(2,1)}, u32[]{:S(2)}, u32[]{:S(2)}) collective-permute-start(bf16[384,512]{1,0:T(8,128)(2,1)} %get-tuple-element.172), channel_id=1, source_target_pairs={{0,96},{4,100},{8,104},{12,108},{16,112},{20,116},{24,120},{28,124... | collective-permute-start | bytes 1179656 | tf_op jit(solution)/shard_map/ppermute | solution.py:61
  498.9 317.0 %all-reduce.10.cloned.1.call-start = ((), (), s32[]{:S(2)}) async-start(), calls=%async_computation.5 | async-start | bytes 6291456 | tf_op jit(solution)/shard_map/psum | solution.py:597
  504.4 25.2 %collective-permute-start.58 = (bf16[384,512]{1,0:T(8,128)(2,1)}, bf16[384,512]{1,0:T(8,128)(2,1)}, u32[]{:S(2)}, u32[]{:S(2)}) collective-permute-start(bf16[384,512]{1,0:T(8,128)(2,1)} %get-tuple-element.176), channel_id=1, source_target_pairs={{0,32},{4,36},{8,40},{12,44},{16,48},{20,52},{24,56},{28,60},{32,6... | collective-permute-start | bytes 1179656 | tf_op jit(solution)/shard_map/ppermute | solution.py:61
  504.9 33.1 %collective-permute-start.59 = (bf16[384,512]{1,0:T(8,128)(2,1)}, bf16[384,512]{1,0:T(8,128)(2,1)}, u32[]{:S(2)}, u32[]{:S(2)}) collective-permute-start(bf16[384,512]{1,0:T(8,128)(2,1)} %get-tuple-element.177), channel_id=1, source_target_pairs={{0,36},{4,32},{8,44},{12,40},{16,52},{20,48},{24,60},{28,56},{32,6... | collective-permute-start | bytes 1179656 | tf_op jit(solution)/shard_map/ppermute | solution.py:61
  563.9 119.2 %collective-permute-start.91 = (bf16[256,1024]{1,0:T(8,128)(2,1)}, bf16[256,1024]{1,0:T(8,128)(2,1)S(1)}, u32[]{:S(2)}, u32[]{:S(2)}) collective-permute-start(bf16[256,1024]{1,0:T(8,128)(2,1)} %get-tuple-element.223), channel_id=1, source_target_pairs={{0,3},{1,0},{2,1},{3,2},{4,7},{5,4},{6,5},{7,6},{8,11},{9,8},{10,9... | collective-permute-start | bytes 1572872 | tf_op jit(solution)/shard_map/ppermute | solution.py:67
  565.4 117.7 %collective-permute-start.90 = (bf16[256,1024]{1,0:T(8,128)(2,1)}, bf16[256,1024]{1,0:T(8,128)(2,1)S(1)}, u32[]{:S(2)}, u32[]{:S(2)}) collective-permute-start(bf16[256,1024]{1,0:T(8,128)(2,1)} %get-tuple-element.222), channel_id=1, source_target_pairs={{0,2},{1,3},{2,0},{3,1},{4,6},{5,7},{6,4},{7,5},{8,10},{9,11},{10,... | collective-permute-start | bytes 1572872 | tf_op jit(solution)/shard_map/ppermute | solution.py:67
  565.4 117.7 %collective-permute-start.89 = (bf16[256,1024]{1,0:T(8,128)(2,1)}, bf16[256,1024]{1,0:T(8,128)(2,1)S(1)}, u32[]{:S(2)}, u32[]{:S(2)}) collective-permute-start(bf16[256,1024]{1,0:T(8,128)(2,1)} %get-tuple-element.221), channel_id=1, source_target_pairs={{0,1},{1,2},{2,3},{3,0},{4,5},{5,6},{6,7},{7,4},{8,9},{9,10},{10,1... | collective-permute-start | bytes 1572872 | tf_op jit(solution)/shard_map/ppermute | solution.py:67
  (108 other events, 2845.7 us)
Sparse Core Ops, SparseCore 0:
  14.3 45.5 all-gather.2
  123.9 51.8 all-gather.4
  468.7 160.6 all-reduce.5
  633.0 104.4 all-reduce.7
  740.4 75.4 all-reduce.9

commit v2 on v1

v2 whole, which is shorter than its diff:
```python
import jax
import jax.numpy as jnp
from jax import lax
from jax.experimental import pallas as pl
from jax.experimental.pallas import tpu as pltpu
from jax.sharding import PartitionSpec as P

HD = 64
ATT_SCALE = 0.015625
RES_SCALE = 0.22
NORM_EPS = 1e-06
ROPE_BASE = 10000.0
NEG_FILL = -1e30
HIGHEST = lax.Precision.HIGHEST
F32 = jnp.float32
BF16 = jnp.bfloat16

ROWS = 256
WIDTH = 1024
HALF = 512
CAP = 96
EXPERTS = 32
RING = 4
HEADS = 4
LANES = 128
VMEM_BYTES = 58 * 1024 * 1024
WHOLE = pl.BlockSpec(memory_space=pltpu.VMEM)
SCALARS = pl.BlockSpec(memory_space=pltpu.SMEM)
ANYWHERE = pl.BlockSpec(memory_space=pl.ANY)


def params():
    return pltpu.CompilerParams(vmem_limit_bytes=VMEM_BYTES)


NO_COST = pl.CostEstimate(flops=0, bytes_accessed=0, transcendentals=0)


def dot(a, b, precision=None):
    return jnp.dot(a, b, preferred_element_type=F32, precision=precision)


def dot_nt(a, b):
    return lax.dot_general(a, b, (((1,), (1,)), ((), ())), preferred_element_type=F32)


def dot_tn(a, b):
    return lax.dot_general(a, b, (((0,), (0,)), ((), ())), preferred_element_type=F32)


def place(z, x, core):
    return ((z % RING) * RING + (x % RING)) * 2 + core


def push(value, dz, dx, dc):
    if (dz % RING, dx % RING, dc) == (0, 0, 0):
        return value
    pairs = [
        (place(z, x, c), place(z + dz, x + dx, c ^ dc))
        for z in range(RING)
        for x in range(RING)
        for c in range(2)
    ]
    return lax.ppermute(value, "ep", pairs)


def push_tp(value, dy):
    if dy % RING == 0:
        return value
    return lax.ppermute(value, "tp", [(y, (y + dy) % RING) for y in range(RING)])


def after(values, *others):
    count = len(values)
    return pl.pallas_call(
        lambda *refs: None,
        out_shape=[jax.ShapeDtypeStruct(v.shape, v.dtype) for v in values],
        in_specs=[ANYWHERE] * (count + len(others)),
        out_specs=[ANYWHERE] * count,
        input_output_aliases={i: i for i in range(count)},
        cost_estimate=NO_COST,
        name="after",
    )(*values, *others)


def gather_tp(rows):
    after_me, before_me = push_tp(rows, -1), push_tp(rows, 1)
    half = rows.shape[0] // 2
    across = push_tp(after_me[:half], -1), push_tp(before_me[half:], 1)
    return rows, after_me, across, before_me


def scatter_tp(pieces):
    half = pieces[2].shape[0] // 2
    first, rest = push_tp(pieces[2][:half], 1), push_tp(pieces[2][half:], -1)
    ahead = (pieces[1][:half].astype(F32) + first.astype(F32)).astype(BF16)
    behind = (pieces[3][half:].astype(F32) + rest.astype(F32)).astype(BF16)
    ahead = jnp.concatenate([ahead, pieces[1][half:]], axis=0)
    behind = jnp.concatenate([pieces[3][:half], behind], axis=0)
    return pieces[0], push_tp(ahead, 1), push_tp(behind, -1)


def ignoring(kernel, first, count):
    return lambda *refs: kernel(*refs[:first], *refs[first + count :])


def swap_halves(v):
    lane = lax.broadcasted_iota(jnp.int32, v.shape, 1)
    return jnp.where(lane % HD < HD // 2, pltpu.roll(v, LANES - HD // 2, 1), pltpu.roll(v, HD // 2, 1))


def block_at(index):
    return pl.ds(pl.multiple_of(index * ROWS, ROWS), ROWS)


def key_range(block):
    return max(0, block - 2) * ROWS, (block + 1) * ROWS


def mask_bias(block, seg_col, seg_row):
    lo, hi = key_range(block)
    key_pos = lo + lax.broadcasted_iota(jnp.int32, (hi - lo, ROWS), 0)
    query_pos = block * ROWS + lax.broadcasted_iota(jnp.int32, (hi - lo, ROWS), 1)
    same = seg_col[lo:hi, :] == seg_row[:, block * ROWS : (block + 1) * ROWS]
    return jnp.where(same & (key_pos <= query_pos), 0.0, NEG_FILL)


def attend_kernel(
    rank, x0, x1, x2, x2_rest, x3, gain, wq, wk, wv, wo, cos, sin, seg_col, seg_row,
    normed, q_out, k_out, v_out, mixed, lse, br0, br1, br2, br3, vt, bias,
):
    me = rank[0]
    lane = lax.broadcasted_iota(jnp.int32, (ROWS, LANES), 1)
    for d, x_ref in enumerate((x0, x1, x2, x3)):
        at = block_at((me + d) % RING)
        x = jnp.concatenate([x2[...], x2_rest[...]], axis=0) if d == 2 else x_ref[...]
        x = x.astype(F32)
        inverse = lax.rsqrt(jnp.mean(x * x, axis=-1, keepdims=True) + NORM_EPS)
        low = (x * inverse * gain[...]).astype(BF16)
        normed[at, :] = low
        cos_here, sin_here = cos[at, :], sin[at, :]

        def rope(v):
            return v * cos_here + swap_halves(v) * sin_here

        query = dot(low, wq[...])
        for pair in range(2):
            q = rope(query[:, pair * LANES : (pair + 1) * LANES]) * ATT_SCALE
            other = pltpu.roll(q, HD, 1)
            keep = (lane < HD) if pair == 0 else (lane >= HD)
            first, second = (q, other) if pair == 0 else (other, q)
            at_head = 2 * pair * LANES
            q_out[at, at_head : at_head + LANES] = jnp.where(keep, first, 0.0).astype(BF16)
            q_out[at, at_head + LANES : at_head + 2 * LANES] = jnp.where(keep, second, 0.0).astype(BF16)
        k_out[at, :] = rope(dot(low, wk[...])).astype(BF16)
        v_out[at, :] = dot(low, wv[...]).astype(BF16)
    vt[...] = v_out[...].astype(F32).T.astype(BF16)
    for b in range(RING):
        lo, hi = key_range(b)
        rows = slice(b * ROWS, (b + 1) * ROWS)
        bias[0 : hi - lo, :] = mask_bias(b, seg_col, seg_row)
        outs = []
        for h in range(HEADS):
            q = q_out[rows, h * LANES : (h + 1) * LANES]
            scores = dot_nt(k_out[lo:hi, :], q) + bias[0 : hi - lo, :]
            top = jnp.max(scores, axis=0, keepdims=True)
            weights = jnp.exp(scores - top)
            total = jnp.sum(weights, axis=0, keepdims=True)
            out = dot(vt[:, lo:hi], weights.astype(BF16)) * (1.0 / total)
            outs.append(out.T)
            lse[h : h + 1, rows] = top + jnp.log(total)
        mixed[rows, 0:LANES] = jnp.where(lane < HD, outs[0], pltpu.roll(outs[1], HD, 1)).astype(BF16)
        mixed[rows, LANES:] = jnp.where(lane < HD, pltpu.roll(outs[2], HD, 1), outs[3]).astype(BF16)
        branch = dot(mixed[rows, :], wo[...]).astype(BF16)
        relative = (b - me + RING) % RING
        for d, br in enumerate((br0, br1, br2, br3)):

            @pl.when(relative == d)
            def _():
                br[...] = branch


def attend(rank, pieces, gain, wq, wk, wv, wo, cos, sin, seg_col, seg_row, *others):
    length = RING * ROWS
    return pl.pallas_call(
        ignoring(attend_kernel, 15, len(others)),
        out_shape=[
            jax.ShapeDtypeStruct((length, WIDTH), BF16),
            jax.ShapeDtypeStruct((length, HEADS * LANES), BF16),
            jax.ShapeDtypeStruct((length, LANES), BF16),
            jax.ShapeDtypeStruct((length, LANES), BF16),
            jax.ShapeDtypeStruct((length, HEADS * HD), BF16),
            jax.ShapeDtypeStruct((8, length), F32),
        ]
        + [jax.ShapeDtypeStruct((ROWS, WIDTH), BF16)] * RING,
        in_specs=[SCALARS] + [WHOLE] * 14 + [ANYWHERE] * len(others),
        out_specs=[WHOLE] * 10,
        scratch_shapes=[pltpu.VMEM((LANES, length), BF16), pltpu.VMEM((3 * ROWS, ROWS), F32)],
        compiler_params=params(),
        cost_estimate=NO_COST,
        name="attend",
    )(rank, pieces[0], pieces[1], *pieces[2], pieces[3], gain, wq, wk, wv, wo, cos, sin, seg_col, seg_row, *others)


def high_low(v):
    high = v.astype(BF16)
    return jnp.concatenate([high, (v - high.astype(F32)).astype(BF16)], axis=1)


def high_plus_low(v):
    return v[:, :ROWS].astype(F32) + v[:, ROWS:].astype(F32)


def route_kernel(x, b0, b1, b2, b3, gain, wr, chosen, middle, half_a, half_b, gates_t):
    branch = b0[...].astype(F32) + b1[...].astype(F32) + b2[...].astype(F32) + b3[...].astype(F32)
    mid = x[...].astype(F32) + RES_SCALE * branch
    middle[...] = mid
    inverse = lax.rsqrt(jnp.mean(mid * mid, axis=-1, keepdims=True) + NORM_EPS)
    routed = (mid * inverse * gain[...]).astype(BF16)
    half_b[...] = routed[:, HALF:]
    logits = jnp.where(chosen[...] > 0.0, dot(routed, wr[...]), NEG_FILL)
    weights = jnp.exp(logits - jnp.max(logits, axis=-1, keepdims=True))
    gates = (weights / jnp.sum(weights, axis=-1, keepdims=True)).T
    gates_t[...] = gates
    half_a[0:ROWS, :] = routed[:, :HALF]
    half_a[ROWS:, :] = high_low(gates)


def route(x, branches, gain, wr, chosen, *others):
    return pl.pallas_call(
        ignoring(route_kernel, 8, len(others)),
        out_shape=[
            jax.ShapeDtypeStruct((ROWS, WIDTH), F32),
            jax.ShapeDtypeStruct((ROWS + EXPERTS, HALF), BF16),
            jax.ShapeDtypeStruct((ROWS, HALF), BF16),
            jax.ShapeDtypeStruct((EXPERTS, ROWS), F32),
        ],
        in_specs=[WHOLE] * 8 + [ANYWHERE] * len(others),
        out_specs=[WHOLE] * 4,
        compiler_params=params(),
        cost_estimate=pl.CostEstimate(flops=20_000_000, bytes_accessed=5_000_000, transcendentals=8192),
        name="route",
    )(x, *branches, gain, wr, chosen, *others)


PIECE = 8 * CAP
EXTRA = 16


def line_row(d, p, e):
    return p * 8 + e * 4 + d


def slot_matrix(row):
    slot = lax.broadcasted_iota(jnp.int32, (CAP, ROWS), 0).astype(F32)
    return jnp.where(slot == row, 1.0, 0.0)


def line_matrix(slots, d):
    rows = [line_row(d, p, e) for p in range(RING) for e in range(2)]
    return jnp.concatenate([slot_matrix(slots[r : r + 1, :]).astype(BF16) for r in rows], axis=0)


def expert_row(spot, half, d, p, e):
    z, x, core = spot[1], spot[2], spot[3]
    if half == 0:
        x = (x + p) % RING
    else:
        z = (z + p) % RING
    return (z * RING + x) * 2 + (core + e) % 2


def fill_pieces(slots, rows, pieces):
    for d in range(RING):
        filled = dot(line_matrix(slots, d), rows[d][0:ROWS, :]).astype(BF16)
        for p in range(RING):
            for e in range(2):
                at = (e * 4 + d) * CAP
                pieces[p][at : at + CAP, :] = filled[(p * 2 + e) * CAP : (p * 2 + e + 1) * CAP, :]


def pick_rows(spot, half, blocks, table, picked):
    for d in range(RING):
        table[...] = blocks[d][ROWS:, :].astype(F32)
        for p in range(RING):
            for e in range(2):
                r = line_row(d, p, e)
                picked[r : r + 1, :] = table[pl.ds(expert_row(spot, half, d, p, e), 1), :]


def add_extra(pieces, picked):
    for p in range(RING):
        extra = picked[p * 8 : (p + 1) * 8, :]
        pieces[p][PIECE:, :] = jnp.concatenate([extra, jnp.zeros_like(extra)], axis=0).astype(BF16)


def dispatch_cot_kernel(spot, *refs):
    blocks, pieces, slots, (table, picked) = refs[:8], refs[8:16], refs[16:18], refs[18:]
    for half in range(2):
        mine = slice(4 * half, 4 * half + 4)
        pick_rows(spot, half, blocks[mine], table, picked)
        slots[half][...] = picked[:, :ROWS]
        fill_pieces(slots[half], blocks[mine], pieces[mine])
        if half == 0:
            add_extra(pieces[mine], picked)


def dispatch_rows_kernel(spot, slots_a, slots_b, *refs):
    blocks, pieces, (table, picked) = refs[:8], refs[8:16], refs[16:]
    fill_pieces(slots_a, blocks[:4], pieces[:4])
    fill_pieces(slots_b, blocks[4:], pieces[4:])
    pick_rows(spot, 0, blocks[:4], table, picked)
    add_extra(pieces[:4], picked)


def combine_kernel(with_extra, slots_a, slots_b, *refs):
    everyone = range(RING)
    for half, slots in enumerate((slots_a, slots_b)):
        pieces, rows = refs[4 * half : 4 * half + 4], refs[8 + 4 * half : 12 + 4 * half]
        for d in everyone:
            filled = jnp.concatenate(
                [pieces[p][(e * 4 + d) * CAP : (e * 4 + d + 1) * CAP, :] for p in everyone for e in range(2)], axis=0
            )
            rows[d][0:ROWS, :] = dot_tn(line_matrix(slots, d), filled).astype(BF16)
        if half == 0 and with_extra:
            tables = [pieces[p][PIECE:, :].astype(F32) for p in everyone]
            for d in everyone:
                picked = [tables[p][e * 4 + d : e * 4 + d + 1, :] for p in everyone for e in range(2)]
                extra = jnp.concatenate(picked + [jnp.zeros((8, HALF), F32)], axis=0)
                rows[d][ROWS:, :] = extra.astype(BF16)


SLOT_COST = pl.CostEstimate(flops=1_000_000_000, bytes_accessed=5_000_000, transcendentals=0)
TABLE = pltpu.VMEM((EXPERTS, HALF), F32)


def shape_of(rows, dtype=BF16):
    return jax.ShapeDtypeStruct((rows, HALF), dtype)


def payload_kernel(cot, table, half_a, half_b):
    for half, out in enumerate((half_a, half_b)):
        out[0:ROWS, :] = cot[:, half * HALF : (half + 1) * HALF]
        out[ROWS:, :] = table[...]


def payload(cot, table, *others):
    return pl.pallas_call(
        ignoring(payload_kernel, 2, len(others)),
        out_shape=[shape_of(ROWS + EXPERTS)] * 2,
        in_specs=[WHOLE] * 2 + [ANYWHERE] * len(others),
        out_specs=[WHOLE] * 2,
        compiler_params=params(),
        name="payload",
    )(cot, table, *others)


def spread_cot(cot, table, *others):
    half_a, half_b = payload(cot, table)
    a1, a3, b1 = push(half_a, -1, 0, 0), push(half_a, -3, 0, 0), push(half_b, 0, -1, 0)
    later_a, later_b = payload(cot, table, a1, a3, b1, *others)
    b3, a2, b2 = push(later_b, 0, -3, 0), push(later_a, -2, 0, 0), push(later_b, 0, -2, 0)
    return [half_a, a1, a2, a3, half_b, b1, b2, b3]


def spread_rows(half_a, half_b):
    return [push(half_a, -d, 0, 0) for d in range(RING)] + [push(half_b, 0, -d, 0) for d in range(RING)]


def made_pieces(kernel, operands, slot_outputs=0, others=()):
    count = len(operands)
    return pl.pallas_call(
        ignoring(kernel, count, len(others)),
        out_shape=[shape_of(PIECE + EXTRA)] * RING
        + [shape_of(PIECE)] * RING
        + [jax.ShapeDtypeStruct((EXPERTS, ROWS), F32)] * slot_outputs,
        in_specs=[SCALARS if v.ndim == 1 else WHOLE for v in operands] + [ANYWHERE] * len(others),
        out_specs=[WHOLE] * (8 + slot_outputs),
        scratch_shapes=[TABLE] * 2,
        compiler_params=params(),
        cost_estimate=SLOT_COST,
        name="dispatch",
    )(*operands, *others)


def exchange(pieces):
    got = exchange_near(pieces)
    got[2] = push(pieces[2], 0, 2, 0)
    (last,) = after((pieces[6],), got[5], got[7])
    got[6] = push(last, 2, 0, 0)
    return got


def exchange_near(pieces):
    got = [pieces[0], None, None, None, pieces[4], None, None, None]
    got[3], got[1] = push(pieces[1], 0, 1, 0), push(pieces[3], 0, 3, 0)
    got[7], got[5] = push(pieces[5], 1, 0, 0), push(pieces[7], 3, 0, 0)
    return got


def exchange_far(pieces, got, with_them, *others):
    held = after((pieces[2], pieces[6], *with_them), got[1], got[3], got[5], got[7], *others)
    got[2], got[6] = push(held[0], 0, 2, 0), push(held[1], 2, 0, 0)
    return held[2:]


def combine(slots_a, slots_b, pieces, with_extra, *others):
    rows_a = shape_of(ROWS + EXTRA) if with_extra else shape_of(ROWS)
    return pl.pallas_call(
        ignoring(lambda *refs: combine_kernel(with_extra, *refs), 10, len(others)),
        out_shape=[rows_a] * RING + [shape_of(ROWS)] * RING,
        in_specs=[WHOLE] * 10 + [ANYWHERE] * len(others),
        out_specs=[WHOLE] * 8,
        compiler_params=params(),
        cost_estimate=SLOT_COST,
        name="combine",
    )(slots_a, slots_b, *pieces, *others)


def to_owners(partial):
    got = [None] * 8
    for d in range(RING):
        got[-d % RING] = push(partial[d], d, 0, 0)
        got[4 + -d % RING] = push(partial[4 + d], 0, d, 0)
    return got


STEPS = 8
STEP_ROWS = RING * CAP


def expert_kernel(*refs):
    ra, rb, ca, cb = (refs[4 * i : 4 * i + 4] for i in range(4))
    weights = refs[16:18]
    qa, qb, ma, mb = (refs[18 + 4 * i : 22 + 4 * i] for i in range(4))
    disp_out, dgu_out, inner_out, dex_out = refs[34:38]
    wgu, wd, rows_in, cot_in, gates_in, slots_in, back_out, moe_out, dgate_out, extra_out = refs[38:48]
    weight_sem, in_sem, out_sem, extra_sem = refs[48:]
    step = pl.program_id(0)

    def loads(e):
        up, down = weights[e].at[pl.ds(0, WIDTH)], weights[e].at[pl.ds(WIDTH, HALF)]
        return [
            pltpu.make_async_copy(up, wgu.at[e], weight_sem.at[e, 0]),
            pltpu.make_async_copy(down, wd.at[e], weight_sem.at[e, 1]),
        ]

    def copies(j, groups, sems, outward):
        slot, e, dx, made = j % 2, j // 4, j % 4, []
        for which, (half_a, half_b, buf) in enumerate(groups):
            ends = [(half_a[dx].at[pl.ds(e * STEP_ROWS, STEP_ROWS)], buf.at[slot, :, pl.ds(0, HALF)])]
            for dz in range(RING):
                far = half_b[dz].at[pl.ds((e * 4 + dx) * CAP, CAP)]
                ends.append((far, buf.at[slot, pl.ds(dz * CAP, CAP), pl.ds(HALF, HALF)]))
            for n, (far, near) in enumerate(ends):
                source, target = (near, far) if outward else (far, near)
                made.append(pltpu.make_async_copy(source, target, sems.at[slot, which * 6 + n]))
        return made

    def fetches(j):
        made = copies(j, ((ra, rb, rows_in), (ca, cb, cot_in)), in_sem, False)
        slot, dx = j % 2, j % 4
        for which, (far, near) in enumerate(((ra, gates_in), (ca, slots_in))):
            made.append(
                pltpu.make_async_copy(far[dx].at[pl.ds(PIECE, EXTRA)], near.at[slot], in_sem.at[slot, which * 6 + 5])
            )
        return made

    def stores(j):
        return copies(j, ((qa, qb, back_out), (ma, mb, moe_out)), out_sem, True)

    for j in range(STEPS):

        @pl.when(step == j)
        def _():
            if j == 0:
                for copy in fetches(0) + loads(0) + loads(1):
                    copy.start()
            if j + 1 < STEPS:
                for copy in fetches(j + 1):
                    copy.start()
            for copy in fetches(j):
                copy.wait()
            if j % 4 == 0:
                for copy in loads(j // 4):
                    copy.wait()
            if j >= 2:
                for copy in stores(j - 2):
                    copy.wait()

    slot = step % 2
    e = step // 4
    gates = high_plus_low(gates_in[slot])
    slots = slots_in[slot].astype(F32)
    gates = jnp.where(e == 0, gates[0:4, :], gates[4:8, :])
    slots = jnp.where(e == 0, slots[0:4, :ROWS], slots[4:8, :ROWS])
    fills = [slot_matrix(slots[dz : dz + 1, :]) for dz in range(RING)]
    gate_slot = jnp.concatenate(
        [jnp.sum(fills[dz] * gates[dz : dz + 1, :], axis=1, keepdims=True) for dz in range(RING)], axis=0
    )
    rows = rows_in[slot]
    disp_out[...] = rows
    gate_up = dot(rows, wgu[e])
    gate, up = gate_up[:, :HALF], gate_up[:, HALF:]
    sigmoid = jax.nn.sigmoid(gate)
    silu = gate * sigmoid
    inner = (silu * up).astype(BF16)
    inner_out[...] = inner
    made = dot(inner, wd[e]).astype(BF16).astype(F32)
    dmoe = RES_SCALE * cot_in[slot].astype(F32)
    dgate_slot = jnp.sum(dmoe * made, axis=1, keepdims=True)
    dgates = [
        jnp.sum(fills[dz] * dgate_slot[dz * CAP : (dz + 1) * CAP, :], axis=0, keepdims=True) for dz in range(RING)
    ]
    at_row = pl.multiple_of((step % 4) * 8, 8)
    dgates = jnp.concatenate(dgates + dgates, axis=0)
    first = lax.broadcasted_iota(jnp.int32, (8, ROWS), 0) < 4
    dgate_out[pl.ds(at_row, 8), :] = jnp.where(first == (e == 0), dgates, dgate_out[pl.ds(at_row, 8), :])
    moe_out[slot] = (gate_slot * made).astype(BF16)
    dex = (gate_slot * dmoe).astype(BF16)
    dex_out[...] = dex
    dinner = dot_nt(dex, wd[e])
    dgate = dinner * up * sigmoid * (1.0 + gate * (1.0 - sigmoid))
    dgu = jnp.concatenate([dgate.astype(BF16), (dinner * silu).astype(BF16)], axis=1)
    dgu_out[...] = dgu
    back_out[slot] = dot_nt(dgu, wgu[e]).astype(BF16)

    for j in range(STEPS):

        @pl.when(step == j)
        def _():
            for copy in stores(j):
                copy.start()
            if j == STEPS - 1:
                last = []
                for dx in range(RING):
                    extra = high_low(dgate_out[dx * 8 : (dx + 1) * 8, :]).astype(F32)
                    extra_out[dx] = jnp.concatenate([extra, jnp.zeros_like(extra)], axis=0).astype(BF16)
                    last.append(
                        pltpu.make_async_copy(
                            extra_out.at[dx], qa[dx].at[pl.ds(PIECE, EXTRA)], extra_sem.at[dx]
                        )
                    )
                for copy in last:
                    copy.start()
                for copy in stores(j - 1) + stores(j) + last:
                    copy.wait()


def experts(rows, cots, weights):
    total = STEPS * STEP_ROWS
    wide = pl.BlockSpec((STEP_ROWS, WIDTH), lambda s: (s, 0))
    narrow = pl.BlockSpec((STEP_ROWS, HALF), lambda s: (s, 0))
    buf = pltpu.VMEM((2, STEP_ROWS, WIDTH), BF16)
    small = pltpu.VMEM((2, EXTRA, HALF), BF16)
    made = pl.pallas_call(
        expert_kernel,
        grid=(STEPS,),
        out_shape=[shape_of(PIECE + EXTRA)] * RING
        + [shape_of(PIECE)] * 12
        + [
            jax.ShapeDtypeStruct((total, WIDTH), BF16),
            jax.ShapeDtypeStruct((total, WIDTH), BF16),
            jax.ShapeDtypeStruct((total, HALF), BF16),
            jax.ShapeDtypeStruct((total, WIDTH), BF16),
        ],
        in_specs=[ANYWHERE] * 18,
        out_specs=[ANYWHERE] * 16 + [wide, wide, narrow, wide],
        scratch_shapes=[
            pltpu.VMEM((2, WIDTH, WIDTH), BF16),
            pltpu.VMEM((2, HALF, WIDTH), BF16),
            buf, buf, small, small, buf, buf,
            pltpu.VMEM((EXPERTS, ROWS), F32),
            pltpu.VMEM((RING, EXTRA, HALF), BF16),
            pltpu.SemaphoreType.DMA((2, 2)),
            pltpu.SemaphoreType.DMA((2, 12)),
            pltpu.SemaphoreType.DMA((2, 12)),
            pltpu.SemaphoreType.DMA((RING,)),
        ],
        compiler_params=params(),
        cost_estimate=pl.CostEstimate(flops=19_000_000_000, bytes_accessed=60_000_000, transcendentals=1_600_000),
        name="experts",
    )(*rows, *cots, *weights)
    return made[:8], made[8:16], made[16:]


def weight_grads_kernel(which, disp, dgu, inner, dex, out, disp_in, dgu_in, inner_in, dex_in, made, sems, out_sems):
    rows = pl.ds(which * 4 * STEP_ROWS, 4 * STEP_ROWS)
    pairs = ((disp, disp_in), (dgu, dgu_in), (inner, inner_in), (dex, dex_in))
    fetches = [pltpu.make_async_copy(far.at[rows], near, sems.at[i]) for i, (far, near) in enumerate(pairs)]
    stores = [
        pltpu.make_async_copy(made.at[pl.ds(i * HALF, HALF)], out.at[pl.ds(i * HALF, HALF)], out_sems.at[i])
        for i in range(3)
    ]
    for copy in fetches:
        copy.start()
    fetches[0].wait()
    fetches[1].wait()
    for i in range(2):
        made[i * HALF : (i + 1) * HALF, :] = dot_tn(disp_in[:, i * HALF : (i + 1) * HALF], dgu_in[...]).astype(BF16)
        stores[i].start()
    fetches[2].wait()
    fetches[3].wait()
    made[WIDTH:, :] = dot_tn(inner_in[...], dex_in[...]).astype(BF16)
    stores[2].start()
    for copy in stores:
        copy.wait()


def weight_grads(which, saved):
    wide, narrow = pltpu.VMEM((4 * STEP_ROWS, WIDTH), BF16), pltpu.VMEM((4 * STEP_ROWS, HALF), BF16)
    return pl.pallas_call(
        lambda *refs: weight_grads_kernel(which, *refs),
        out_shape=jax.ShapeDtypeStruct((WIDTH + HALF, WIDTH), BF16),
        in_specs=[ANYWHERE] * 4,
        out_specs=ANYWHERE,
        scratch_shapes=[
            wide, wide, narrow, wide, pltpu.VMEM((WIDTH + HALF, WIDTH), BF16),
            pltpu.SemaphoreType.DMA((4,)), pltpu.SemaphoreType.DMA((3,)),
        ],
        compiler_params=params(),
        cost_estimate=NO_COST,
        name="weight_grads",
    )(*saved)


def unroute_kernel(spot, *refs):
    parts, (gates_t, middle, cot, gain, wr_t, dmiddle, dbranch, sums, gates, dlogits) = refs[:8], refs[8:]

    def four(pieces):
        a, b, c, d = (piece[0:ROWS, :].astype(F32) for piece in pieces)
        return (a + b) + (c + d)

    order = [
        (((spot[1] + dz) % RING) * RING + (spot[2] + dx) % RING) * 2 + (spot[3] + e) % 2
        for dz in range(RING)
        for dx in range(RING)
        for e in range(2)
    ]
    for i, at in enumerate(order):
        gates[i : i + 1, :] = gates_t[pl.ds(at, 1), :]
    tables = [part[ROWS:, :].astype(F32) for part in parts[:4]]
    dgates = jnp.concatenate([t[0:8, :ROWS] + t[0:8, ROWS:] for t in tables], axis=0)
    made = gates[...] * (dgates - jnp.sum(gates[...] * dgates, axis=0, keepdims=True))
    for i, at in enumerate(order):
        dlogits[pl.ds(at, 1), :] = made[i : i + 1, :]
    drouted = jnp.concatenate([four(parts[:4]), four(parts[4:])], axis=1)
    drouted = drouted + dot(dlogits[...].T, wr_t[...], HIGHEST)
    mid = middle[...]
    inverse = lax.rsqrt(jnp.mean(mid * mid, axis=-1, keepdims=True) + NORM_EPS)
    plain = mid * inverse
    routed = (plain * gain[...]).astype(BF16).astype(F32)
    sums[0:EXPERTS, :] = dot(dlogits[...], routed, HIGHEST)
    sums[EXPERTS : EXPERTS + 8, :] = jnp.broadcast_to(jnp.sum(drouted * plain, axis=0, keepdims=True), (8, WIDTH))
    scaled = drouted * gain[...]
    along = jnp.mean(scaled * plain, axis=-1, keepdims=True)
    total = cot[...].astype(F32) + inverse * (scaled - plain * along)
    dmiddle[...] = total
    dbranch[...] = (RES_SCALE * total).astype(BF16)


def unroute(spot, parts, gates_t, middle, cot, gain, wr_t, *others):
    return pl.pallas_call(
        ignoring(unroute_kernel, 14, len(others)),
        out_shape=[
            jax.ShapeDtypeStruct((ROWS, WIDTH), F32),
            jax.ShapeDtypeStruct((ROWS, WIDTH), BF16),
            jax.ShapeDtypeStruct((EXPERTS + 8, WIDTH), F32),
        ],
        in_specs=[SCALARS] + [WHOLE] * 13 + [ANYWHERE] * len(others),
        out_specs=[WHOLE] * 3,
        scratch_shapes=[pltpu.VMEM((EXPERTS, ROWS), F32), pltpu.VMEM((EXPERTS, ROWS), F32)],
        compiler_params=params(),
        cost_estimate=pl.CostEstimate(flops=100_000_000_000, bytes_accessed=6_000_000, transcendentals=0),
        name="unroute",
    )(spot, *parts, gates_t, middle, cot, gain, wr_t, *others)


def unmix_kernel(rank, d0, d1, d2, d2_rest, d3, mixed, wo, dmixed, grad_out):
    me = rank[0]
    lane = lax.broadcasted_iota(jnp.int32, (ROWS, LANES), 1)
    for d, ref in enumerate((d0, d1, d2, d3)):
        at = block_at((me + d) % RING)
        grad = jnp.concatenate([d2[...], d2_rest[...]], axis=0) if d == 2 else ref[...]
        low = dot_nt(grad, wo[...])
        for pair in range(2):
            both = low[:, pair * LANES : (pair + 1) * LANES]
            other = pltpu.roll(both, HD, 1)
            keep = (lane < HD) if pair == 0 else (lane >= HD)
            first, second = (both, other) if pair == 0 else (other, both)
            at_head = 2 * pair * LANES
            dmixed[at, at_head : at_head + LANES] = jnp.where(keep, first, 0.0).astype(BF16)
            dmixed[at, at_head + LANES : at_head + 2 * LANES] = jnp.where(keep, second, 0.0).astype(BF16)
        term = dot_tn(mixed[at, :], grad)
        total = term if d == 0 else total + term
    grad_out[...] = total.astype(BF16)


def unmix(rank, pieces, mixed, wo, *others):
    length = RING * ROWS
    return pl.pallas_call(
        ignoring(unmix_kernel, 8, len(others)),
        out_shape=[
            jax.ShapeDtypeStruct((length, HEADS * LANES), BF16),
            jax.ShapeDtypeStruct((HEADS * HD, WIDTH), BF16),
        ],
        in_specs=[SCALARS] + [WHOLE] * 7 + [ANYWHERE] * len(others),
        out_specs=[WHOLE] * 2,
        compiler_params=params(),
        cost_estimate=pl.CostEstimate(flops=1_100_000_000, bytes_accessed=5_000_000, transcendentals=0),
        name="unmix",
    )(rank, pieces[0], pieces[1], *pieces[2], pieces[3], mixed, wo, *others)


def unattend_kernel(
    spot, q_in, k_in, v_in, lse, dmixed, normed, gain, wq, wk, wv, cos, sin, seg_col, seg_row,
    dqkv, dgain, dn0, dn1, dn2, dn3, kt, bias, dk, dv,
):
    me = spot[0]
    lane = lax.broadcasted_iota(jnp.int32, (ROWS, LANES), 1)
    kt[...] = k_in[...].astype(F32).T.astype(BF16)
    dk[...] = jnp.zeros_like(dk)
    dv[...] = jnp.zeros_like(dv)

    def unrope(v, rows):
        return v * cos[rows, :] - swap_halves(v) * sin[rows, :]

    for b in range(RING):
        lo, hi = key_range(b)
        rows = slice(b * ROWS, (b + 1) * ROWS)
        bias[0 : hi - lo, :] = mask_bias(b, seg_col, seg_row)
        dqs = []
        for h in range(HEADS):
            cols = slice(h * LANES, (h + 1) * LANES)
            q, do = q_in[rows, cols], dmixed[rows, cols]
            scores = dot_nt(k_in[lo:hi, :], q) + bias[0 : hi - lo, :]
            probs = jnp.exp(scores - lse[h : h + 1, rows])
            dprobs = dot_nt(v_in[lo:hi, :], do)
            delta = jnp.sum(probs * dprobs, axis=0, keepdims=True)
            dscores = (probs * (dprobs - delta)).astype(BF16)
            dv[lo:hi, :] += dot(probs.astype(BF16), do)
            dk[lo:hi, :] += dot(dscores, q)
            dqs.append(dot(kt[:, lo:hi], dscores).T * ATT_SCALE)
        first = jnp.where(lane < HD, dqs[0], pltpu.roll(dqs[1], HD, 1))
        second = jnp.where(lane < HD, pltpu.roll(dqs[2], HD, 1), dqs[3])
        dqkv[rows, 0:LANES] = unrope(first, rows).astype(BF16)
        dqkv[rows, LANES : 2 * LANES] = unrope(second, rows).astype(BF16)
    for b in range(RING):
        rows = slice(b * ROWS, (b + 1) * ROWS)
        dqkv[rows, 2 * LANES : 3 * LANES] = unrope(dk[rows, :], rows).astype(BF16)
        dqkv[rows, 3 * LANES :] = dv[rows, :].astype(BF16)
        dn = dot_nt(dqkv[rows, : 2 * LANES], wq[...])
        dn = dn + dot_nt(dqkv[rows, 2 * LANES : 3 * LANES], wk[...])
        dn = dn + dot_nt(dqkv[rows, 3 * LANES :], wv[...])
        term = jnp.sum(dn * normed[rows, :].astype(F32), axis=0, keepdims=True)
        gain_sum = term if b == 0 else gain_sum + term
        dn = dn.astype(BF16)
        relative = (b - me + RING) % RING
        for d, ref in enumerate((dn0, dn1, dn2, dn3)):

            @pl.when(relative == d)
            def _():
                ref[...] = dn

    dgain[...] = jnp.broadcast_to(gain_sum / gain[...], (8, WIDTH))


def unattend(spot, q, k, v, lse, dmixed, normed, gain, wq, wk, wv, cos, sin, seg_col, seg_row):
    length = RING * ROWS
    return pl.pallas_call(
        unattend_kernel,
        out_shape=[
            jax.ShapeDtypeStruct((length, HALF), BF16),
            jax.ShapeDtypeStruct((8, WIDTH), F32),
        ]
        + [jax.ShapeDtypeStruct((ROWS, WIDTH), BF16)] * RING,
        in_specs=[SCALARS] + [WHOLE] * 14,
        out_specs=[WHOLE] * 6,
        scratch_shapes=[
            pltpu.VMEM((LANES, length), BF16),
            pltpu.VMEM((3 * ROWS, ROWS), F32),
            pltpu.VMEM((length, LANES), F32),
            pltpu.VMEM((length, LANES), F32),
        ],
        compiler_params=params(),
        cost_estimate=pl.CostEstimate(flops=300_000_000_000, bytes_accessed=14_000_000, transcendentals=4_000_000),
        name="unattend",
    )(spot, q, k, v, lse, dmixed, normed, gain, wq, wk, wv, cos, sin, seg_col, seg_row)


PAY = 832
QUARTER = PAY // RING
GAINS = 768 + EXPERTS


def pack_kernel(spot, normed, dqkv, grad_out, s0, s1, s2, s3, own, other):
    core = spot[3]
    sums = (s0[...] + s1[...]) + (s2[...] + s3[...])
    row = lax.broadcasted_iota(jnp.int32, (32, HALF), 0)
    for side, out in enumerate((own, other)):
        cols = pl.ds(pl.multiple_of(((core + side) % 2) * HALF, HALF), HALF)
        left = (core + side) % 2 == 0
        out[0:HALF, :] = dot_tn(normed[:, cols], dqkv[...]).astype(BF16)
        out[HALF:768, :] = grad_out[:, cols]
        here = jnp.where(left, sums[:, :HALF], sums[:, HALF:])
        out[768:GAINS, :] = here[0:EXPERTS, :].astype(BF16)
        out[GAINS:, :] = jnp.where(row == 0, here[EXPERTS : EXPERTS + 1, :], 0.0).astype(BF16)


def add_all(refs):
    total = refs[0][...].astype(F32)
    for ref in refs[1:]:
        total = total + ref[...].astype(F32)
    return total.astype(BF16)


def quarter_rows(index):
    return pl.ds(pl.multiple_of(index * QUARTER, 16), QUARTER)


def reduce_core_kernel(spot, own, got, g0, g1, g2, g3, p0, p1, p2, p3, total):
    total[...] = add_all((own, got))
    gain = (g0[...] + g1[...]) + (g2[...] + g3[...])
    mine = jnp.where(spot[3] == 0, gain[0:1, :HALF], gain[0:1, HALF:])
    row = lax.broadcasted_iota(jnp.int32, (32, HALF), 0)
    total[GAINS:, :] = jnp.where(row == 1, mine, total[GAINS:, :].astype(F32)).astype(BF16)
    for d, piece in enumerate((p0, p1, p2, p3)):
        piece[...] = total[quarter_rows((spot[2] + d) % RING), :]


def sum_kernel(spot, a, b, c, d, out):
    out[...] = add_all((a, b, c, d))


def gather_x_kernel(spot, a, b, c, d, out):
    for d, piece in enumerate((a, b, c, d)):
        out[quarter_rows((spot[2] + d) % RING), :] = piece[...]


def unpack_kernel(spot, own, got, query, key, value, grad_out, router, gains):
    for side, half in enumerate((own, got)):
        at = pl.ds(pl.multiple_of(((spot[3] + side) % 2) * HALF, HALF), HALF)
        query[at, :] = half[0:HALF, : 2 * LANES].astype(F32)
        key[at, :] = half[0:HALF, 2 * LANES : 3 * LANES].astype(F32)
        value[at, :] = half[0:HALF, 3 * LANES :].astype(F32)
        grad_out[:, at] = half[HALF:768, :].astype(F32)
        router[:, at] = half[768:GAINS, :].astype(F32)
        gains[:, at] = half[GAINS:, :].astype(F32)[0:8, :]


def small_call(kernel, spot, refs, shapes, scratch=None, flops=1_000_000, others=()):
    return pl.pallas_call(
        ignoring(kernel, 1 + len(refs), len(others)),
        out_shape=[jax.ShapeDtypeStruct(shape, dtype) for shape, dtype in shapes],
        in_specs=[SCALARS] + [WHOLE] * len(refs) + [ANYWHERE] * len(others),
        out_specs=[WHOLE] * len(shapes),
        scratch_shapes=[pltpu.VMEM(scratch, BF16)] if scratch else [],
        compiler_params=params(),
        cost_estimate=pl.CostEstimate(flops=flops, bytes_accessed=2_000_000, transcendentals=0),
    )(spot, *refs, *others)


def sum_over_ep(spot, normed, dqkv, grad_out, sums, gains, moe_got, beside, finished):
    own, other = small_call(
        pack_kernel, spot, (normed, dqkv, grad_out, *sums), [((PAY, HALF), BF16)] * 2, flops=0, others=moe_got
    )
    got = push(other, 0, 0, 1)
    pieces = small_call(
        reduce_core_kernel, spot, (own, got, *gains), [((QUARTER, HALF), BF16)] * 4, (PAY, HALF)
    )
    beside[0](pieces[0])
    pieces = [push(pieces[d], 0, d, 0) for d in range(RING)]
    quarter = [((QUARTER, HALF), BF16)]
    (line,) = small_call(sum_kernel, spot, pieces, quarter)
    beside[1](line)
    (line,) = small_call(sum_kernel, spot, [push(line, d, 0, 0) for d in range(RING)], quarter)
    beside[2](line)
    pieces = [push(line, 0, -d, 0) for d in range(RING)]
    (half,) = small_call(gather_x_kernel, spot, pieces, [((PAY, HALF), BF16)], others=finished)
    made = small_call(
        unpack_kernel,
        spot,
        (half, push(half, 0, 0, 1)),
        [
            ((WIDTH, 2 * LANES), F32),
            ((WIDTH, LANES), F32),
            ((WIDTH, LANES), F32),
            ((ROWS, WIDTH), F32),
            ((EXPERTS, WIDTH), F32),
            ((8, WIDTH), F32),
        ],
    )
    return made


def rope_tables(length):
    freqs = ROPE_BASE ** (-jnp.arange(HD // 2, dtype=F32) * 2.0 / HD)
    angles = jnp.arange(length, dtype=F32)[:, None] * freqs[None, :]
    cosine, sine = jnp.cos(angles), jnp.sin(angles)
    return jnp.concatenate([cosine] * 4, axis=1), jnp.concatenate([-sine, sine] * 2, axis=1)


def shards(
    hidden_in, segment_ids, expert_ids, slot_index, attn_gain, w_query, w_key, w_value, w_output,
    ffn_gain, w_router, w_gate_up, w_down, cotangent,
):
    length = RING * ROWS
    here, rank = lax.axis_index("ep"), lax.axis_index("tp")
    spot = jnp.stack([rank, here // 8, (here // 2) % 4, here % 2]).astype(jnp.int32)

    named = expert_ids[:, :, None] == jnp.arange(EXPERTS, dtype=jnp.int32)[None, None, :]
    slot_of = jnp.sum(jnp.where(named, slot_index[:, :, None] + 1, 0), axis=1) - 1
    chosen = (slot_of >= 0).astype(F32)
    table = jnp.pad(slot_of.T.astype(BF16), ((0, 0), (0, HALF - ROWS)))

    gain_one = attn_gain.astype(F32).reshape(1, WIDTH)
    gain_two = ffn_gain.astype(F32).reshape(1, WIDTH)
    cos, sin = rope_tables(length)
    seg_row = segment_ids
    seg_col = segment_ids.reshape(length, 1)

    group = gather_tp(hidden_in)
    blocks = spread_cot(cotangent, table, group[1], group[3])
    made = made_pieces(dispatch_cot_kernel, (spot, *blocks), 2, (*group[2], cos, sin, seg_col))
    slots_a, slots_b = made[8:]
    cot_pieces = made[:8]
    cots = exchange_near(cot_pieces)
    weights = jnp.concatenate([w_gate_up.reshape(WIDTH, 2 * HALF), w_down.reshape(HALF, WIDTH)], axis=0)
    (weights,) = after((weights,), slots_a)
    weights = weights, push(weights, 0, 0, 1)

    made = attend(spot, group, gain_one, w_query, w_key, w_value, w_output, cos, sin, seg_col, seg_row, slots_a)
    normed, q, k, v, mixed, lse = made[:6]
    sent = exchange_far(cot_pieces, cots, made[7:10], lse, weights[1])
    branches = [made[6]] + [push_tp(sent[d], d + 1) for d in range(RING - 1)]
    middle, half_a, half_b, gates_t = route(
        hidden_in, branches, gain_two, w_router, chosen, cots[2], cots[6]
    )
    blocks = spread_rows(half_a, half_b)
    rows = exchange(made_pieces(dispatch_rows_kernel, (spot, slots_a, slots_b, *blocks)))

    back, moe_slots, saved = experts(rows, cots, weights)
    got = exchange_near(back)
    (grads_other,) = exchange_far(back, got, (weight_grads(1, saved),))
    grads_other = push(grads_other, 0, 0, 1)
    grads_own = weight_grads(0, saved)
    grads_e = (grads_own.astype(F32) + grads_other.astype(F32)).astype(BF16)
    parts = to_owners(combine(slots_a, slots_b, got, True, grads_e))

    dmiddle, dbranch, sums = unroute(
        spot, parts, gates_t, middle, cotangent, gain_two, w_router.T.astype(F32), grads_e
    )
    grads_e = lax.psum_scatter(grads_e, "tp", scatter_dimension=0, tiled=True)
    group_grad = gather_tp(dbranch)
    sums = [push_tp(sums, d) for d in range(RING)]

    moe_got = [moe_slots[0], None, None, None, moe_slots[4], None, None, None]
    one, two, three = after((moe_slots[1], moe_slots[3], moe_slots[5]), dbranch)
    moe_got[3], moe_got[1], moe_got[7] = push(one, 0, 1, 0), push(two, 0, 3, 0), push(three, 1, 0, 0)
    one, two = after((moe_slots[7], moe_slots[2]), moe_got[3], moe_got[1], moe_got[7])
    moe_got[5], moe_got[2] = push(one, 3, 0, 0), push(two, 0, 2, 0)
    (one,) = after((moe_slots[6],), moe_got[5], moe_got[2])
    moe_got[6] = push(one, 2, 0, 0)

    (grads_e,) = after((grads_e,), *group_grad[2])
    grads_e = lax.all_gather(grads_e, "tp", axis=0, tiled=True).astype(F32)
    grad_up = grads_e[:WIDTH].reshape(1, WIDTH, 2, HALF)
    grad_down = grads_e[WIDTH:].reshape(1, HALF, WIDTH)
    dmixed, grad_output = unmix(spot, group_grad, mixed, w_output, moe_got[1], moe_got[3], moe_got[7], *sums[1:])
    last = unattend(
        spot, q, k, v, lse, dmixed, normed, gain_one, w_query, w_key, w_value, cos, sin, seg_col, seg_row
    )
    gain = last[1] + push(last[1], 0, 0, 1)
    gains = [push_tp(gain, d) for d in range(RING)]
    dn, moe_parts = [], []

    def beside_x(piece):
        dn.extend(scatter_tp(after(last[2:6], piece)))

    def beside_z(line):
        moe_parts.extend(combine(slots_a, slots_b, after(moe_got, line), False))

    def beside_last(line):
        moe_parts[:] = to_owners(after(moe_parts, line))

    grad_query, grad_key, grad_value, grad_output, grad_router, grad_gains = sum_over_ep(
        spot, normed, last[0], grad_output, sums, gains, (moe_got[2], moe_got[5]), (beside_x, beside_z, beside_last),
        (grad_up, grad_down),
    )
    dnormed = dn[0].astype(F32) + dn[1].astype(F32) + dn[2].astype(F32)

    local = hidden_in.astype(F32)
    inverse = lax.rsqrt(jnp.mean(local * local, axis=-1, keepdims=True) + NORM_EPS)
    plain = local * inverse
    scaled = dnormed * gain_one
    along = jnp.mean(scaled * plain, axis=-1, keepdims=True)
    grad_hidden = dmiddle + inverse * (scaled - plain * along)

    def four_sum(p):
        a, b, c, d = (piece.astype(F32) for piece in p)
        return (a + b) + (c + d)

    moe = jnp.concatenate([four_sum(moe_parts[:4]), four_sum(moe_parts[4:])], axis=1)
    output = (middle + RES_SCALE * moe).astype(BF16)
    return (
        output,
        grad_hidden,
        grad_gains[1],
        grad_query,
        grad_key,
        grad_value,
        grad_output,
        grad_gains[0],
        grad_router.T,
        grad_up,
        grad_down,
    )


def solution(mesh):
    placed = (
        P(("ep", "tp"), None),
        P("ep", None),
        P(("ep", "tp"), None),
        P(("ep", "tp"), None),
        P(),
        P(None, "tp"),
        P(None, "tp"),
        P(None, "tp"),
        P("tp", None),
        P(),
        P(),
        P("ep", None, None, None),
        P("ep", None, None),
        P(("ep", "tp"), None),
    )
    return jax.shard_map(
        shards,
        mesh=mesh,
        in_specs=placed,
        out_specs=(
            P(("ep", "tp"), None),
            P(("ep", "tp"), None),
            P(),
            P(None, "tp"),
            P(None, "tp"),
            P(None, "tp"),
            P("tp", None),
            P(),
            P(),
            P("ep", None, None, None),
            P("ep", None, None),
        ),
        check_vma=False,
    )
```

time: 838 us -> 507 us (0.61)
  waiting for transfers between devices: 415 us -> 156 us
  starting transfers between devices: 162 us -> 111 us
  blocking collectives: 49.8 us -> 0 us
  Pallas kernels: 103 us -> 143 us
  matrix products: 18.8 us -> 0 us
    psum x3 -> x0, waiting for transfers between devices: 185 us -> none  [the longest x1 72.2 us: shards(): grad_gate_up, grad_down = lax.psum((grad_gate_up, grad_down), 'tp')]
    ppermute x80 -> x62, waiting for transfers between devices: 164 us -> 97.2 us  [push(): return lax.ppermute(value, 'ep', pairs)]
    ppermute x80 -> x62, starting transfers between devices: 143 us -> 84.3 us  [push(): return lax.ppermute(value, 'ep', pairs)]
    all_gather x1 -> x0, blocking collectives: 49.8 us -> none  [shards(): dgain = lax.all_gather(last[5].reshape(8, LANES), ('ep', 'tp'), axis=0)]
    pallas_call x10 -> x31, Pallas kernels: 103 us -> 143 us  [the longest x1 34.6 us: experts(): pl.pallas_call(expert_kernel, grid=(STEPS,), out_shape=[shape_of(PIECE +...]
    dot_general x2 -> x0, matrix products: 18.8 us -> none  [dot_tn(): lax.dot_general(a, b, (((0,), (0,)), ((), ())), preferred_element_type=F32)]
    ppermute x12 -> x21, starting transfers between devices: 13.6 us -> 26.6 us  [push_tp(): lax.ppermute(value, 'tp', [(y, (y + dy) % RING) for y in range(RING)])]
    slice x2 -> x9, local copies, waits for them, and re-layouts: 1.39 us -> 12 us  [the longest x1 4.1 us: shards(): grad_up = grads_e[:WIDTH].reshape(1, WIDTH, 2, HALF)]
  transfers between devices with their start and end apart: 98 -> 85, of which waited for: 37 -> 33; matrix products, arithmetic and copies ran while one was open for 9% -> 10% of each run, Pallas kernels for 7% -> 16%
where the time goes in v2:
time: 507 us; the launch traced here: 497 us
  waiting for transfers between devices  156 us (31%)
  Pallas kernels  143 us (28%)
  starting transfers between devices  111 us (22%)
  local copies, waits for them, and re-layouts  41.7 us (8%)
  other arithmetic  29.7 us (6%)
  between operations  15 us (3%)
    ppermute x62, waiting for transfers between devices, push(): return lax.ppermute(value, 'ep', pairs)  97.2 us
    ppermute x62, starting transfers between devices, push(): return lax.ppermute(value, 'ep', pairs)  84.3 us
    ppermute x21, waiting for transfers between devices, push_tp(): lax.ppermute(value, 'tp', [(y, (y + dy) % RING) for y in range(RING)])  59.2 us
    pallas_call x1, Pallas kernels, experts(): pl.pallas_call(expert_kernel, grid=(STEPS,), out_shape=[shape_of(PIECE +...  34.6 us
    ppermute x21, starting transfers between devices, push_tp(): lax.ppermute(value, 'tp', [(y, (y + dy) % RING) for y in range(RING)])  26.6 us
    unnamed x157, local copies, waits for them, and re-layouts  18.9 us
    pallas_call x2, Pallas kernels, weight_grads(): pl.pallas_call(lambda *refs: weight_grads_kernel(which, *refs), out_shape...  18.3 us
    pallas_call x6, Pallas kernels, small_call(): pl.pallas_call(ignoring(kernel, 1 + len(refs), len(others)), out_shape=[j...  17.3 us
  transfers between devices with their start and end apart: 85, of which 33 were waited for; matrix products, arithmetic and copies ran while one was open for 10% of the time, Pallas kernels for 16%

profile of v2, /device:TPU:1, one launch (start us, length us, event | category | flops | bytes accessed | tf_op | source)
XLA Modules:
  0.0 497.0 jit_solution(4420545531250645647)
XLA Ops:
  11.4 4.6 collective-permute-start.4
  16.0 2.7 collective-permute-start
  18.7 2.5 collective-permute-start.6
  21.2 2.9 fusion.11
  25.9 2.1 copy.93
  28.7 4.4 pad_maximum_fusion.1
  40.0 2.7 collective-permute-start.1
  46.0 4.4 collective-permute-done.3.refs_10_.refs_4_
  50.5 3.0 collective-permute-done.9.refs_8_
  54.4 6.1 %dispatch.2 = (bf16[784,512]{1,0:T(8,128)(2,1)}, bf16[784,512]{1,0:T(8,128)(2,1)}, bf16[784,512]{1,0:T(8,128)(2,1)}, bf16[784,512]{1,0:T(8,128)(2,1)}, bf16[768,...) custom-call(s32[4]{0:T(128)} %pad_add_fusion.refs_0_.spot, ...), custom_call_target="tpu_custom_call" | custom-call | flops 1000000000 | bytes 5000000 | tf_op jit(solution)/shard_map/dispatch/pallas_call | solution.py:372
  61.8 2.1 collective-permute-start.10
  66.6 16.9 %attend.1 = (bf16[1024,1024]{1,0:T(8,128)(2,1)}, bf16[1024,512]{1,0:T(8,128)(2,1)}, bf16[1024,128]{1,0:T(8,128)(2,1)}, bf16[1024,128]{1,0:T(8,128)(2,1)}, bf16[1...) custom-call(s32[4]{0:T(128)} %pad_add_fusion.refs_0_.spot, ...), custom_call_target="tpu_custom_call" | custom-call | tf_op jit(solution)/shard_map/attend/pallas_call | solution.py:185
  95.2 8.5 %collective-permute-done.15.refs_2_ = bf16[256,1024]{1,0:T(8,128)(2,1)S(1)} collective-permute-done((bf16[256,1024]{1,0:T(8,128)(2,1)}, bf16[256,1024]{1,0:T(8,128)(2,1)S(1)}, u32[]{:S(2)}, u32[]{:S(2)}) %collective-permute-start.15) | collective-permute-done | bytes 524320 | tf_op jit(solution)/shard_map/ppermute | solution.py:70
  103.7 9.3 %collective-permute-done.16.refs_3_ = bf16[256,1024]{1,0:T(8,128)(2,1)S(1)} collective-permute-done((bf16[256,1024]{1,0:T(8,128)(2,1)}, bf16[256,1024]{1,0:T(8,128)(2,1)S(1)}, u32[]{:S(2)}, u32[]{:S(2)}) %collective-permute-start.16) | collective-permute-done | bytes 524320 | tf_op jit(solution)/shard_map/ppermute | solution.py:70
  113.0 3.1 collective-permute-done.17.refs_4_
  117.3 3.5 route.1
  128.9 3.3 collective-permute-done.24.refs_9_
  132.2 5.0 %collective-permute-done.25.refs_10_ = bf16[256,512]{1,0:T(8,128)(2,1)S(1)} collective-permute-done((bf16[256,512]{1,0:T(8,128)(2,1)}, bf16[256,512]{1,0:T(8,128)(2,1)S(1)}, u32[]{:S(2)}, u32[]{:S(2)}) %collective-permute-start.25) | collective-permute-done | bytes 262176 | tf_op jit(solution)/shard_map/ppermute | solution.py:64
  137.2 3.7 collective-permute-done.22.refs_6_
  141.6 6.1 %dispatch.3 = (bf16[784,512]{1,0:T(8,128)(2,1)}, bf16[784,512]{1,0:T(8,128)(2,1)}, bf16[784,512]{1,0:T(8,128)(2,1)}, bf16[784,512]{1,0:T(8,128)(2,1)}, bf16[768,...) custom-call(s32[4]{0:T(128)} %pad_add_fusion.refs_0_.spot, ...), custom_call_target="tpu_custom_call" | custom-call | flops 1000000000 | bytes 5000000 | tf_op jit(solution)/shard_map/dispatch/pallas_call | solution.py:372
  151.8 12.6 %collective-permute-done.29.refs_1_.refs_5_ = bf16[768,512]{1,0:T(8,128)(2,1)S(1)} collective-permute-done((bf16[768,512]{1,0:T(8,128)(2,1)}, bf16[768,512]{1,0:T(8,128)(2,1)S(1)}, u32[]{:S(2)}, u32[]{:S(2)}) %collective-permute-start.29) | collective-permute-done | bytes 786464 | tf_op jit(solution)/shard_map/ppermute | solution.py:64
  167.1 21.2 %collective-permute-done.28.refs_3_ = bf16[784,512]{1,0:T(8,128)(2,1)} collective-permute-done((bf16[784,512]{1,0:T(8,128)(2,1)}, bf16[784,512]{1,0:T(8,128)(2,1)}, u32[]{:S(2)}, u32[]{:S(2)}) %collective-permute-start.28) | collective-permute-done | bytes 802848 | tf_op jit(solution)/shard_map/ppermute | solution.py:64
  189.2 34.6 %experts.1 = (bf16[784,512]{1,0:T(8,128)(2,1)}, bf16[784,512]{1,0:T(8,128)(2,1)}, bf16[784,512]{1,0:T(8,128)(2,1)}, bf16[784,512]{1,0:T(8,128)(2,1)}, bf16[768,5...) custom-call(bf16[784,512]{1,0:T(8,128)(2,1)} %get-tuple-element.164., ...), custom_call_target="tpu_custom_call" | custom-call | flops 19000000512 | bytes 60000000 | tf_op jit(solution)/shard_map/experts/pallas_call | solution.py:556
  226.9 9.2 %weight_grads.2.refs_2_ = bf16[1536,1024]{1,0:T(8,128)(2,1)} custom-call(bf16[3072,1024]{1,0:T(8,128)(2,1)} %get-tuple-element.182.refs_0_, bf16[3072,1024]{1,0:T(8,128)(2,1)} %get-tuple-element.183.refs_1_, bf16[3072,512]{1,0:T(8,128)(2,1)} %get-tuple-element.184.refs_2_, bf16[3072,1024]{1,0:T(8,128)(2,1)} %get-tuple-element.185.refs_3_), custom_call_target="tpu_custom_call" | custom-call | tf_op jit(solution)/shard_map/weight_grads/pallas_call | solution.py:612
  236.1 6.2 %collective-permute-done.34.refs_5_.refs_7_ = bf16[768,512]{1,0:T(8,128)(2,1)S(1)} collective-permute-done((bf16[768,512]{1,0:T(8,128)(2,1)}, bf16[768,512]{1,0:T(8,128)(2,1)S(1)}, u32[]{:S(2)}, u32[]{:S(2)}) %collective-permute-start.34) | collective-permute-done | bytes 786464 | tf_op jit(solution)/shard_map/ppermute | solution.py:64
  242.3 3.2 collective-permute-done.35.refs_6_.refs_9_
  246.9 2.6 collective-permute-start.38
  251.2 9.2 %weight_grads.3 = bf16[1536,1024]{1,0:T(8,128)(2,1)} custom-call(bf16[3072,1024]{1,0:T(8,128)(2,1)} %get-tuple-element.182.refs_0_, bf16[3072,1024]{1,0:T(8,128)(2,1)} %get-tuple-element.183.refs_1_, bf16[3072,512]{1,0:T(8,128)(2,1)} %get-tuple-element.184.refs_2_, bf16[3072,1024]{1,0:T(8,128)(2,1)} %get-tuple-element.185.refs_3_), custom_call_target="tpu_custom_call" | custom-call | tf_op jit(solution)/shard_map/weight_grads/pallas_call | solution.py:612
  260.3 5.1 %add_convert_fusion.refs_10_.refs_14_ = bf16[1536,1024]{1,0:T(8,128)(2,1)} fusion(bf16[1536,1024]{1,0:T(8,128)(2,1)S(1)} %collective-permute-done.38, bf16[1536,1024]{1,0:T(8,128)(2,1)} %weight_grads.3), kind=kLoop, calls=%fused_computation | loop fusion | flops 6291456 | bytes 9437184 | tf_op jit(solution)/shard_map/convert_element_type | solution.py:947
  265.4 6.3 %collective-permute-done.37.refs_8_ = bf16[768,512]{1,0:T(8,128)(2,1)S(1)} collective-permute-done((bf16[768,512]{1,0:T(8,128)(2,1)}, bf16[768,512]{1,0:T(8,128)(2,1)S(1)}, u32[]{:S(2)}, u32[]{:S(2)}) %collective-permute-start.37) | collective-permute-done | bytes 786464 | tf_op jit(solution)/shard_map/ppermute | solution.py:64
  272.9 5.7 %combine.2 = (bf16[272,512]{1,0:T(8,128)(2,1)}, bf16[272,512]{1,0:T(8,128)(2,1)}, bf16[272,512]{1,0:T(8,128)(2,1)}, bf16[272,512]{1,0:T(8,128)(2,1)}, bf16[256,5...) custom-call(f32[32,256]{1,0:T(8,128)} %get-tuple-element.143.refs_15_.refs_1_.re, ...), custom_call_target="tpu_custom_call" | custom-call | flops 1000000000 | bytes 5000000 | tf_op jit(solution)/shard_map/combine/pallas_call | solution.py:409
  282.4 3.1 collective-permute-done.42.refs_6_
  286.5 2.2 collective-permute-done.43.refs_7_
  288.7 5.4 %collective-permute-done.44.refs_8_ = bf16[256,512]{1,0:T(8,128)(2,1)S(1)} collective-permute-done((bf16[256,512]{1,0:T(8,128)(2,1)}, bf16[256,512]{1,0:T(8,128)(2,1)S(1)}, u32[]{:S(2)}, u32[]{:S(2)}) %collective-permute-start.44) | collective-permute-done | bytes 262176 | tf_op jit(solution)/shard_map/ppermute | solution.py:64
  296.7 5.3 %unroute.1 = (f32[256,1024]{1,0:T(8,128)}, bf16[256,1024]{1,0:T(8,128)(2,1)}, f32[40,1024]{1,0:T(8,128)}) custom-call(s32[4]{0:T(128)} %pad_add_fusion.refs_0_.spot, bf16[272,512]{1,0:T(8,128)(2,1)} %get-tuple-element.193.refs_1_, bf16[272,512]{1,0:T(8,128)(2,1)} %copy-done.68, bf16[272,512]{1,0:T(8,128)(2,1)} %copy-done.69, bf16[272,512]{1,0:T(8,128)(2,1)} %copy-done.70, ...), custom_call_target="tpu_custom_call" | custom-call | flops 99999997952 | bytes 6000000 | tf_op jit(solution)/shard_map/unroute/pallas_call | solution.py:663
  304.6 3.9 collective-permute-start.51
  308.5 22.6 %collective-permute-done.51.refs_2_ = bf16[256,1024]{1,0:T(8,128)(2,1)S(1)} collective-permute-done((bf16[256,1024]{1,0:T(8,128)(2,1)}, bf16[256,1024]{1,0:T(8,128)(2,1)S(1)}, u32[]{:S(2)}, u32[]{:S(2)}) %collective-permute-start.51) | collective-permute-done | bytes 524320 | tf_op jit(solution)/shard_map/ppermute | solution.py:70
  331.9 3.4 collective-permute-start.52
  336.2 3.8 collective-permute-start.56
  340.9 6.2 %collective-permute-done.55.refs_11_.refs_5_ = f32[40,1024]{1,0:T(8,128)} collective-permute-done((f32[40,1024]{1,0:T(8,128)}, f32[40,1024]{1,0:T(8,128)}, u32[]{:S(2)}, u32[]{:S(2)}) %collective-permute-start.55) | collective-permute-done | bytes 163872 | tf_op jit(solution)/shard_map/ppermute | solution.py:70
  347.9 3.3 collective-permute-start.49
  351.2 4.3 unmix.1
  355.5 16.0 %unattend.1 = (bf16[1024,512]{1,0:T(8,128)(2,1)}, f32[8,1024]{1,0:T(8,128)}, bf16[256,1024]{1,0:T(8,128)(2,1)}, bf16[256,1024]{1,0:T(8,128)(2,1)}, bf16[256,1024]{1,0:T(8,128)(2,1)}, /*index=5*/bf16[256,1024]{1,0:T(8,128)(2,1)}) custom-call(s32[4]{0:T(128)} %pad_add_fusion.refs_0_.spot, bf16[1024,512]{1,0:T(8,128)(2,1)} %get-tuple-element.213.q_in, ...), custom_call_target="tpu_custom_call" | custom-call | flops 299999985664 | bytes 14000000 | tf_op jit(solution)/shard_map/unattend/pallas_call | solution.py:770
  371.6 4.7 shard_map.221
  376.3 4.5 collective-permute-start.58
  380.8 4.3 collective-permute-start.50
  386.9 2.3 collective-permute-start.62
  389.3 2.8 collective-permute-done.60.refs_4_
  394.4 2.8 shard_map.222
  410.7 2.0 shard_map.223.refs_8_.refs_1_
  415.5 5.4 %combine.3 = (bf16[256,512]{1,0:T(8,128)(2,1)}, bf16[256,512]{1,0:T(8,128)(2,1)}, bf16[256,512]{1,0:T(8,128)(2,1)}, bf16[256,512]{1,0:T(8,128)(2,1)}, bf16[256,5...) custom-call(f32[32,256]{1,0:T(8,128)} %get-tuple-element.143.refs_15_.refs_1_.re, ...), custom_call_target="tpu_custom_call" | custom-call | flops 1000000000 | bytes 5000000 | tf_op jit(solution)/shard_map/combine/pallas_call | solution.py:409
  425.5 4.4 collective-permute-start.69
  433.4 7.5 %collective-permute-done.69 = bf16[256,512]{1,0:T(8,128)(2,1)S(1)} collective-permute-done((bf16[256,512]{1,0:T(8,128)(2,1)}, bf16[256,512]{1,0:T(8,128)(2,1)S(1)}, u32[]{:S(2)}, u32[]{:S(2)}) %collective-permute-start.69) | collective-permute-done | bytes 262176 | tf_op jit(solution)/shard_map/ppermute | solution.py:64
  441.5 3.7 collective-permute-start.73
  445.2 2.3 collective-permute-start.74
  449.4 2.1 collective-permute-start.79
  451.5 3.4 collective-permute-start.80
  454.9 3.7 collective-permute-done.74
  459.5 4.1 slice.60
  463.6 6.7 %reshape.73.refs_5_ = f32[1,1024,2,512]{3,2,1,0:T(2,128)} reshape(f32[1024,1024]{1,0:T(8,128)} %slice.60) | data formatting | bytes 8388608 | tf_op jit(solution)/shard_map/reshape | solution.py:967
  472.7 2.4 shard_map.225.refs_1_
  475.1 3.9 collective-permute-start.82
  481.7 2.6 fusion.5
  485.2 3.3 shard_map.226
  (337 shorter events, 110.5 us)
Async XLA Ops:
  7.2 348.3 %reduce-scatter.2.cloned.1.call-start = ((), (), s32[]{:S(2)}) async-start(), calls=%async_computation.1 | async-start | bytes 3932160 | tf_op jit(solution)/shard_map/reduce_scatter | solution.py:953
  11.4 21.6 %collective-permute-start.4 = (bf16[288,512]{1,0:T(8,128)(2,1)}, bf16[288,512]{1,0:T(8,128)(2,1)S(1)}, u32[]{:S(2)}, u32[]{:S(2)}) collective-permute-start(bf16[288,512]{1,0:T(8,128)(2,1)} %get-tuple-element.139.refs_1_), channel_id=1, source_target_pairs={{0,96},{4,100},{8,104},{12,108},{16,112},{20,116},{24,120},{28,124... | collective-permute-start | bytes 884744 | tf_op jit(solution)/shard_map/ppermute | solution.py:64
  16.0 17.1 %collective-permute-start.5 = (bf16[288,512]{1,0:T(8,128)(2,1)}, bf16[288,512]{1,0:T(8,128)(2,1)}, u32[]{:S(2)}, u32[]{:S(2)}) collective-permute-start(bf16[288,512]{1,0:T(8,128)(2,1)} %get-tuple-element.139.refs_1_), channel_id=1, source_target_pairs={{0,32},{4,36},{8,40},{12,44},{16,48},{20,52},{24,56},{28,60},{32,6... | collective-permute-start | bytes 884744 | tf_op jit(solution)/shard_map/ppermute | solution.py:64
  16.0 17.1 %collective-permute-start = (bf16[256,1024]{1,0:T(8,128)(2,1)}, bf16[256,1024]{1,0:T(8,128)(2,1)S(1)}, u32[]{:S(2)}, u32[]{:S(2)}) collective-permute-start(bf16[256,1024]{1,0:T(8,128)(2,1)} %refs_0_.5), channel_id=1, source_target_pairs={{0,3},{1,0},{2,1},{3,2},{4,7},{5,4},{6,5},{7,6},{8,11},{9,8},{10,9... | collective-permute-start | bytes 1572872 | tf_op jit(solution)/shard_map/ppermute | solution.py:70
  18.7 14.4 %collective-permute-start.2 = (bf16[256,1024]{1,0:T(8,128)(2,1)}, bf16[256,1024]{1,0:T(8,128)(2,1)S(1)}, u32[]{:S(2)}, u32[]{:S(2)}) collective-permute-start(bf16[256,1024]{1,0:T(8,128)(2,1)} %refs_0_.5), channel_id=1, source_target_pairs={{0,1},{1,2},{2,3},{3,0},{4,5},{5,6},{6,7},{7,4},{8,9},{9,10},{10,1... | collective-permute-start | bytes 1572872 | tf_op jit(solution)/shard_map/ppermute | solution.py:70
  18.7 14.3 %collective-permute-start.6 = (bf16[288,512]{1,0:T(8,128)(2,1)}, bf16[288,512]{1,0:T(8,128)(2,1)}, u32[]{:S(2)}, u32[]{:S(2)}) collective-permute-start(bf16[288,512]{1,0:T(8,128)(2,1)} %get-tuple-element.140.refs_5_), channel_id=1, source_target_pairs={{0,24},{4,28},{8,0},{12,4},{16,8},{20,12},{24,16},{28,20},{32,56},... | collective-permute-start | bytes 884744 | tf_op jit(solution)/shard_map/ppermute | solution.py:64
  36.6 13.9 %collective-permute-start.8 = (bf16[288,512]{1,0:T(8,128)(2,1)}, bf16[288,512]{1,0:T(8,128)(2,1)S(1)}, u32[]{:S(2)}, u32[]{:S(2)}) collective-permute-start(bf16[288,512]{1,0:T(8,128)(2,1)} %get-tuple-element.142), channel_id=1, source_target_pairs={{0,16},{4,20},{8,24},{12,28},{16,0},{20,4},{24,8},{28,12},{32,48},... | collective-permute-start | bytes 884744 | tf_op jit(solution)/shard_map/ppermute | solution.py:64
  37.7 15.8 %collective-permute-start.9 = (bf16[288,512]{1,0:T(8,128)(2,1)}, bf16[288,512]{1,0:T(8,128)(2,1)S(1)}, u32[]{:S(2)}, u32[]{:S(2)}) collective-permute-start(bf16[288,512]{1,0:T(8,128)(2,1)} %get-tuple-element.142), channel_id=1, source_target_pairs={{0,8},{4,12},{8,16},{12,20},{16,24},{20,28},{24,0},{28,4},{32,40},... | collective-permute-start | bytes 884744 | tf_op jit(solution)/shard_map/ppermute | solution.py:64
  38.0 15.5 %collective-permute-start.7 = (bf16[288,512]{1,0:T(8,128)(2,1)}, bf16[288,512]{1,0:T(8,128)(2,1)S(1)}, u32[]{:S(2)}, u32[]{:S(2)}) collective-permute-start(bf16[288,512]{1,0:T(8,128)(2,1)} %get-tuple-element.141), channel_id=1, source_target_pairs={{0,64},{4,68},{8,72},{12,76},{16,80},{20,84},{24,88},{28,92},{32,9... | collective-permute-start | bytes 884744 | tf_op jit(solution)/shard_map/ppermute | solution.py:64
  60.5 24.7 %collective-permute-start.14 = (bf16[1536,1024]{1,0:T(8,128)(2,1)}, bf16[1536,1024]{1,0:T(8,128)(2,1)S(1)}, u32[]{:S(2)}, u32[]{:S(2)}) collective-permute-start(bf16[1536,1024]{1,0:T(8,128)(2,1)} %after.11.refs_16_), channel_id=1, source_target_pairs={{0,4},{4,0},{8,12},{12,8},{16,20},{20,16},{24,28},{28,24},{32,36},... | collective-permute-start | bytes 9437192 | tf_op jit(solution)/shard_map/ppermute | solution.py:64
  61.8 23.4 %collective-permute-start.10 = (bf16[784,512]{1,0:T(8,128)(2,1)}, bf16[784,512]{1,0:T(8,128)(2,1)S(1)}, u32[]{:S(2)}, u32[]{:S(2)}) collective-permute-start(bf16[784,512]{1,0:T(8,128)(2,1)} %get-tuple-element.150), channel_id=1, source_target_pairs={{0,24},{4,28},{8,0},{12,4},{16,8},{20,12},{24,16},{28,20},{32,56},... | collective-permute-start | bytes 2408456 | tf_op jit(solution)/shard_map/ppermute | solution.py:64
  63.8 21.3 %collective-permute-start.11 = (bf16[784,512]{1,0:T(8,128)(2,1)}, bf16[784,512]{1,0:T(8,128)(2,1)S(1)}, u32[]{:S(2)}, u32[]{:S(2)}) collective-permute-start(bf16[784,512]{1,0:T(8,128)(2,1)} %get-tuple-element.151), channel_id=1, source_target_pairs={{0,8},{4,12},{8,16},{12,20},{16,24},{20,28},{24,0},{28,4},{32,40},... | collective-permute-start | bytes 2408456 | tf_op jit(solution)/shard_map/ppermute | solution.py:64
  63.8 19.9 %collective-permute-start.12 = (bf16[768,512]{1,0:T(8,128)(2,1)}, bf16[768,512]{1,0:T(8,128)(2,1)S(1)}, u32[]{:S(2)}, u32[]{:S(2)}) collective-permute-start(bf16[768,512]{1,0:T(8,128)(2,1)} %get-tuple-element.152), channel_id=1, source_target_pairs={{0,96},{4,100},{8,104},{12,108},{16,112},{20,116},{24,120},{28,124... | collective-permute-start | bytes 2359304 | tf_op jit(solution)/shard_map/ppermute | solution.py:64
  65.2 19.9 %collective-permute-start.13 = (bf16[768,512]{1,0:T(8,128)(2,1)}, bf16[768,512]{1,0:T(8,128)(2,1)}, u32[]{:S(2)}, u32[]{:S(2)}) collective-permute-start(bf16[768,512]{1,0:T(8,128)(2,1)} %get-tuple-element.153), channel_id=1, source_target_pairs={{0,32},{4,36},{8,40},{12,44},{16,48},{20,52},{24,56},{28,60},{32,6... | collective-permute-start | bytes 2359304 | tf_op jit(solution)/shard_map/ppermute | solution.py:64
  87.3 28.9 %collective-permute-start.18 = (bf16[784,512]{1,0:T(8,128)(2,1)}, bf16[784,512]{1,0:T(8,128)(2,1)S(1)}, u32[]{:S(2)}, u32[]{:S(2)}) collective-permute-start(bf16[784,512]{1,0:T(8,128)(2,1)} %get-tuple-element.158), channel_id=1, source_target_pairs={{0,16},{4,20},{8,24},{12,28},{16,0},{20,4},{24,8},{28,12},{32,48},... | collective-permute-start | bytes 2408456 | tf_op jit(solution)/shard_map/ppermute | solution.py:64
  88.3 27.8 %collective-permute-start.19 = (bf16[768,512]{1,0:T(8,128)(2,1)}, bf16[768,512]{1,0:T(8,128)(2,1)S(1)}, u32[]{:S(2)}, u32[]{:S(2)}) collective-permute-start(bf16[768,512]{1,0:T(8,128)(2,1)} %get-tuple-element.159), channel_id=1, source_target_pairs={{0,64},{4,68},{8,72},{12,76},{16,80},{20,84},{24,88},{28,92},{32,9... | collective-permute-start | bytes 2359304 | tf_op jit(solution)/shard_map/ppermute | solution.py:64
  89.9 13.7 %collective-permute-start.15 = (bf16[256,1024]{1,0:T(8,128)(2,1)}, bf16[256,1024]{1,0:T(8,128)(2,1)S(1)}, u32[]{:S(2)}, u32[]{:S(2)}) collective-permute-start(bf16[256,1024]{1,0:T(8,128)(2,1)} %get-tuple-element.155), channel_id=1, source_target_pairs={{0,1},{1,2},{2,3},{3,0},{4,5},{5,6},{6,7},{7,4},{8,9},{9,10},{10,1... | collective-permute-start | bytes 1572872 | tf_op jit(solution)/shard_map/ppermute | solution.py:70
  89.9 23.0 %collective-permute-start.16 = (bf16[256,1024]{1,0:T(8,128)(2,1)}, bf16[256,1024]{1,0:T(8,128)(2,1)S(1)}, u32[]{:S(2)}, u32[]{:S(2)}) collective-permute-start(bf16[256,1024]{1,0:T(8,128)(2,1)} %get-tuple-element.156), channel_id=1, source_target_pairs={{0,2},{1,3},{2,0},{3,1},{4,6},{5,7},{6,4},{7,5},{8,10},{9,11},{10,... | collective-permute-start | bytes 1572872 | tf_op jit(solution)/shard_map/ppermute | solution.py:70
  91.6 24.5 %collective-permute-start.17 = (bf16[256,1024]{1,0:T(8,128)(2,1)}, bf16[256,1024]{1,0:T(8,128)(2,1)}, u32[]{:S(2)}, u32[]{:S(2)}) collective-permute-start(bf16[256,1024]{1,0:T(8,128)(2,1)} %get-tuple-element.157), channel_id=1, source_target_pairs={{0,3},{1,0},{2,1},{3,2},{4,7},{5,4},{6,5},{7,6},{8,11},{9,8},{10,9... | collective-permute-start | bytes 1572872 | tf_op jit(solution)/shard_map/ppermute | solution.py:70
  122.6 14.6 %collective-permute-start.20 = (bf16[288,512]{1,0:T(8,128)(2,1)}, bf16[288,512]{1,0:T(8,128)(2,1)S(1)}, u32[]{:S(2)}, u32[]{:S(2)}) collective-permute-start(bf16[288,512]{1,0:T(8,128)(2,1)} %get-tuple-element.162.refs_3_), channel_id=1, source_target_pairs={{0,96},{4,100},{8,104},{12,108},{16,112},{20,116},{24,120},{28,124... | collective-permute-start | bytes 884744 | tf_op jit(solution)/shard_map/ppermute | solution.py:64
  123.9 13.3 %collective-permute-start.21 = (bf16[288,512]{1,0:T(8,128)(2,1)}, bf16[288,512]{1,0:T(8,128)(2,1)S(1)}, u32[]{:S(2)}, u32[]{:S(2)}) collective-permute-start(bf16[288,512]{1,0:T(8,128)(2,1)} %get-tuple-element.162.refs_3_), channel_id=1, source_target_pairs={{0,64},{4,68},{8,72},{12,76},{16,80},{20,84},{24,88},{28,92},{32,9... | collective-permute-start | bytes 884744 | tf_op jit(solution)/shard_map/ppermute | solution.py:64
  124.3 16.6 %collective-permute-start.22 = (bf16[288,512]{1,0:T(8,128)(2,1)}, bf16[288,512]{1,0:T(8,128)(2,1)S(1)}, u32[]{:S(2)}, u32[]{:S(2)}) collective-permute-start(bf16[288,512]{1,0:T(8,128)(2,1)} %get-tuple-element.162.refs_3_), channel_id=1, source_target_pairs={{0,32},{4,36},{8,40},{12,44},{16,48},{20,52},{24,56},{28,60},{32,6... | collective-permute-start | bytes 884744 | tf_op jit(solution)/shard_map/ppermute | solution.py:64
  147.7 16.8 %collective-permute-start.29 = (bf16[768,512]{1,0:T(8,128)(2,1)}, bf16[768,512]{1,0:T(8,128)(2,1)S(1)}, u32[]{:S(2)}, u32[]{:S(2)}) collective-permute-start(bf16[768,512]{1,0:T(8,128)(2,1)} %get-tuple-element.169), channel_id=1, source_target_pairs={{0,96},{4,100},{8,104},{12,108},{16,112},{20,116},{24,120},{28,124... | collective-permute-start | bytes 2359304 | tf_op jit(solution)/shard_map/ppermute | solution.py:64
  147.8 16.7 %collective-permute-start.30 = (bf16[768,512]{1,0:T(8,128)(2,1)}, bf16[768,512]{1,0:T(8,128)(2,1)S(1)}, u32[]{:S(2)}, u32[]{:S(2)}) collective-permute-start(bf16[768,512]{1,0:T(8,128)(2,1)} %get-tuple-element.171), channel_id=1, source_target_pairs={{0,32},{4,36},{8,40},{12,44},{16,48},{20,52},{24,56},{28,60},{32,6... | collective-permute-start | bytes 2359304 | tf_op jit(solution)/shard_map/ppermute | solution.py:64
  149.3 17.8 %collective-permute-start.26 = (bf16[784,512]{1,0:T(8,128)(2,1)}, bf16[784,512]{1,0:T(8,128)(2,1)S(1)}, u32[]{:S(2)}, u32[]{:S(2)}) collective-permute-start(bf16[784,512]{1,0:T(8,128)(2,1)} %get-tuple-element.165), channel_id=1, source_target_pairs={{0,24},{4,28},{8,0},{12,4},{16,8},{20,12},{24,16},{28,20},{32,56},... | collective-permute-start | bytes 2408456 | tf_op jit(solution)/shard_map/ppermute | solution.py:64
  149.4 17.7 %collective-permute-start.27 = (bf16[784,512]{1,0:T(8,128)(2,1)}, bf16[784,512]{1,0:T(8,128)(2,1)S(1)}, u32[]{:S(2)}, u32[]{:S(2)}) collective-permute-start(bf16[784,512]{1,0:T(8,128)(2,1)} %get-tuple-element.166), channel_id=1, source_target_pairs={{0,16},{4,20},{8,24},{12,28},{16,0},{20,4},{24,8},{28,12},{32,48},... | collective-permute-start | bytes 2408456 | tf_op jit(solution)/shard_map/ppermute | solution.py:64
  151.1 37.2 %collective-permute-start.28 = (bf16[784,512]{1,0:T(8,128)(2,1)}, bf16[784,512]{1,0:T(8,128)(2,1)}, u32[]{:S(2)}, u32[]{:S(2)}) collective-permute-start(bf16[784,512]{1,0:T(8,128)(2,1)} %get-tuple-element.167), channel_id=1, source_target_pairs={{0,8},{4,12},{8,16},{12,20},{16,24},{20,28},{24,0},{28,4},{32,40},... | collective-permute-start | bytes 2408456 | tf_op jit(solution)/shard_map/ppermute | solution.py:64
  165.6 22.6 %collective-permute-start.31 = (bf16[768,512]{1,0:T(8,128)(2,1)}, bf16[768,512]{1,0:T(8,128)(2,1)S(1)}, u32[]{:S(2)}, u32[]{:S(2)}) collective-permute-start(bf16[768,512]{1,0:T(8,128)(2,1)} %after.13), channel_id=1, source_target_pairs={{0,64},{4,68},{8,72},{12,76},{16,80},{20,84},{24,88},{28,92},{32,9... | collective-permute-start | bytes 2359304 | tf_op jit(solution)/shard_map/ppermute | solution.py:64
  223.8 21.7 %collective-permute-start.32 = (bf16[784,512]{1,0:T(8,128)(2,1)}, bf16[784,512]{1,0:T(8,128)(2,1)S(1)}, u32[]{:S(2)}, u32[]{:S(2)}) collective-permute-start(bf16[784,512]{1,0:T(8,128)(2,1)} %get-tuple-element.179), channel_id=1, source_target_pairs={{0,24},{4,28},{8,0},{12,4},{16,8},{20,12},{24,16},{28,20},{32,56},... | collective-permute-start | bytes 2408456 | tf_op jit(solution)/shard_map/ppermute | solution.py:64
  223.8 21.7 %collective-permute-start.33 = (bf16[784,512]{1,0:T(8,128)(2,1)}, bf16[784,512]{1,0:T(8,128)(2,1)S(1)}, u32[]{:S(2)}, u32[]{:S(2)}) collective-permute-start(bf16[784,512]{1,0:T(8,128)(2,1)} %get-tuple-element.186), channel_id=1, source_target_pairs={{0,8},{4,12},{8,16},{12,20},{16,24},{20,28},{24,0},{28,4},{32,40},... | collective-permute-start | bytes 2408456 | tf_op jit(solution)/shard_map/ppermute | solution.py:64
  225.3 17.0 %collective-permute-start.34 = (bf16[768,512]{1,0:T(8,128)(2,1)}, bf16[768,512]{1,0:T(8,128)(2,1)S(1)}, u32[]{:S(2)}, u32[]{:S(2)}) collective-permute-start(bf16[768,512]{1,0:T(8,128)(2,1)} %get-tuple-element.187), channel_id=1, source_target_pairs={{0,96},{4,100},{8,104},{12,108},{16,112},{20,116},{24,120},{28,124... | collective-permute-start | bytes 2359304 | tf_op jit(solution)/shard_map/ppermute | solution.py:64
  226.6 18.9 %collective-permute-start.35 = (bf16[768,512]{1,0:T(8,128)(2,1)}, bf16[768,512]{1,0:T(8,128)(2,1)S(1)}, u32[]{:S(2)}, u32[]{:S(2)}) collective-permute-start(bf16[768,512]{1,0:T(8,128)(2,1)} %get-tuple-element.188), channel_id=1, source_target_pairs={{0,32},{4,36},{8,40},{12,44},{16,48},{20,52},{24,56},{28,60},{32,6... | collective-permute-start | bytes 2359304 | tf_op jit(solution)/shard_map/ppermute | solution.py:64
  246.9 13.4 %collective-permute-start.38 = (bf16[1536,1024]{1,0:T(8,128)(2,1)}, bf16[1536,1024]{1,0:T(8,128)(2,1)S(1)}, u32[]{:S(2)}, u32[]{:S(2)}) collective-permute-start(bf16[1536,1024]{1,0:T(8,128)(2,1)} %get-tuple-element.192), channel_id=1, source_target_pairs={{0,4},{4,0},{8,12},{12,8},{16,20},{20,16},{24,28},{28,24},{32,36},... | collective-permute-start | bytes 9437192 | tf_op jit(solution)/shard_map/ppermute | solution.py:64
  249.5 22.2 %collective-permute-start.36 = (bf16[784,512]{1,0:T(8,128)(2,1)}, bf16[784,512]{1,0:T(8,128)(2,1)S(1)}, u32[]{:S(2)}, u32[]{:S(2)}) collective-permute-start(bf16[784,512]{1,0:T(8,128)(2,1)} %get-tuple-element.189), channel_id=1, source_target_pairs={{0,16},{4,20},{8,24},{12,28},{16,0},{20,4},{24,8},{28,12},{32,48},... | collective-permute-start | bytes 2408456 | tf_op jit(solution)/shard_map/ppermute | solution.py:64
  251.2 20.6 %collective-permute-start.37 = (bf16[768,512]{1,0:T(8,128)(2,1)}, bf16[768,512]{1,0:T(8,128)(2,1)S(1)}, u32[]{:S(2)}, u32[]{:S(2)}) collective-permute-start(bf16[768,512]{1,0:T(8,128)(2,1)} %get-tuple-element.191), channel_id=1, source_target_pairs={{0,64},{4,68},{8,72},{12,76},{16,80},{20,84},{24,88},{28,92},{32,9... | collective-permute-start | bytes 2359304 | tf_op jit(solution)/shard_map/ppermute | solution.py:64
  279.4 14.8 %collective-permute-start.39 = (bf16[272,512]{1,0:T(8,128)(2,1)}, bf16[272,512]{1,0:T(8,128)(2,1)S(1)}, u32[]{:S(2)}, u32[]{:S(2)}) collective-permute-start(bf16[272,512]{1,0:T(8,128)(2,1)} %get-tuple-element.194), channel_id=1, source_target_pairs={{0,96},{4,100},{8,104},{12,108},{16,112},{20,116},{24,120},{28,124... | collective-permute-start | bytes 835592 | tf_op jit(solution)/shard_map/ppermute | solution.py:64
  279.5 14.7 %collective-permute-start.40 = (bf16[272,512]{1,0:T(8,128)(2,1)}, bf16[272,512]{1,0:T(8,128)(2,1)S(1)}, u32[]{:S(2)}, u32[]{:S(2)}) collective-permute-start(bf16[272,512]{1,0:T(8,128)(2,1)} %get-tuple-element.195), channel_id=1, source_target_pairs={{0,64},{4,68},{8,72},{12,76},{16,80},{20,84},{24,88},{28,92},{32,9... | collective-permute-start | bytes 835592 | tf_op jit(solution)/shard_map/ppermute | solution.py:64
  280.4 15.6 %collective-permute-start.41 = (bf16[272,512]{1,0:T(8,128)(2,1)}, bf16[272,512]{1,0:T(8,128)(2,1)S(1)}, u32[]{:S(2)}, u32[]{:S(2)}) collective-permute-start(bf16[272,512]{1,0:T(8,128)(2,1)} %get-tuple-element.196), channel_id=1, source_target_pairs={{0,32},{4,36},{8,40},{12,44},{16,48},{20,52},{24,56},{28,60},{32,6... | collective-permute-start | bytes 835592 | tf_op jit(solution)/shard_map/ppermute | solution.py:64
  286.5 173.0 %all-gather.2.cloned.1.call-start = ((), (), s32[]{:S(2)}) async-start(), calls=%async_computation.2 | async-start | bytes 3932160 | tf_op jit(solution)/shard_map/all_gather | solution.py:966
  302.0 34.1 %collective-permute-start.45 = (bf16[768,512]{1,0:T(8,128)(2,1)}, bf16[768,512]{1,0:T(8,128)(2,1)S(1)}, u32[]{:S(2)}, u32[]{:S(2)}) collective-permute-start(bf16[768,512]{1,0:T(8,128)(2,1)} %get-tuple-element.203), channel_id=1, source_target_pairs={{0,24},{4,28},{8,0},{12,4},{16,8},{20,12},{24,16},{28,20},{32,56},... | collective-permute-start | bytes 2359304 | tf_op jit(solution)/shard_map/ppermute | solution.py:64
  302.5 33.7 %collective-permute-start.46 = (bf16[768,512]{1,0:T(8,128)(2,1)}, bf16[768,512]{1,0:T(8,128)(2,1)S(1)}, u32[]{:S(2)}, u32[]{:S(2)}) collective-permute-start(bf16[768,512]{1,0:T(8,128)(2,1)} %get-tuple-element.206), channel_id=1, source_target_pairs={{0,8},{4,12},{8,16},{12,20},{16,24},{20,28},{24,0},{28,4},{32,40},... | collective-permute-start | bytes 2359304 | tf_op jit(solution)/shard_map/ppermute | solution.py:64
  303.5 36.5 %collective-permute-start.47 = (bf16[768,512]{1,0:T(8,128)(2,1)}, bf16[768,512]{1,0:T(8,128)(2,1)S(1)}, u32[]{:S(2)}, u32[]{:S(2)}) collective-permute-start(bf16[768,512]{1,0:T(8,128)(2,1)} %get-tuple-element.207), channel_id=1, source_target_pairs={{0,32},{4,36},{8,40},{12,44},{16,48},{20,52},{24,56},{28,60},{32,6... | collective-permute-start | bytes 2359304 | tf_op jit(solution)/shard_map/ppermute | solution.py:64
  304.6 26.6 %collective-permute-start.51 = (bf16[256,1024]{1,0:T(8,128)(2,1)}, bf16[256,1024]{1,0:T(8,128)(2,1)S(1)}, u32[]{:S(2)}, u32[]{:S(2)}) collective-permute-start(bf16[256,1024]{1,0:T(8,128)(2,1)} %get-tuple-element.202.refs_3_.refs_1_), channel_id=1, source_target_pairs={{0,3},{1,0},{2,1},{3,2},{4,7},{5,4},{6,5},{7,6},{8,11},{9,8},{10,9... | collective-permute-start | bytes 1572872 | tf_op jit(solution)/shard_map/ppermute | solution.py:70
  308.5 26.8 %collective-permute-start.53 = (bf16[256,1024]{1,0:T(8,128)(2,1)}, bf16[256,1024]{1,0:T(8,128)(2,1)S(1)}, u32[]{:S(2)}, u32[]{:S(2)}) collective-permute-start(bf16[256,1024]{1,0:T(8,128)(2,1)} %get-tuple-element.202.refs_3_.refs_1_), channel_id=1, source_target_pairs={{0,1},{1,2},{2,3},{3,0},{4,5},{5,6},{6,7},{7,4},{8,9},{9,10},{10,1... | collective-permute-start | bytes 1572872 | tf_op jit(solution)/shard_map/ppermute | solution.py:70
  331.9 19.3 %collective-permute-start.52 = (bf16[128,1024]{1,0:T(8,128)(2,1)}, bf16[128,1024]{1,0:T(8,128)(2,1)}, u32[]{:S(2)}, u32[]{:S(2)}) collective-permute-start(bf16[128,1024]{1,0:T(8,128)(2,1)} %slice.58), channel_id=1, source_target_pairs={{0,3},{1,0},{2,1},{3,2},{4,7},{5,4},{6,5},{7,6},{8,11},{9,8},{10,9... | collective-permute-start | bytes 786440 | tf_op jit(solution)/shard_map/ppermute | solution.py:70
  336.1 15.1 %collective-permute-start.54 = (bf16[128,1024]{1,0:T(8,128)(2,1)}, bf16[128,1024]{1,0:T(8,128)(2,1)}, u32[]{:S(2)}, u32[]{:S(2)}) collective-permute-start(bf16[128,1024]{1,0:T(8,128)(2,1)} %slice.59), channel_id=1, source_target_pairs={{0,1},{1,2},{2,3},{3,0},{4,5},{5,6},{6,7},{7,4},{8,9},{9,10},{10,1... | collective-permute-start | bytes 786440 | tf_op jit(solution)/shard_map/ppermute | solution.py:70
  336.1 10.9 %collective-permute-start.55 = (f32[40,1024]{1,0:T(8,128)}, f32[40,1024]{1,0:T(8,128)}, u32[]{:S(2)}, u32[]{:S(2)}) collective-permute-start(f32[40,1024]{1,0:T(8,128)} %get-tuple-element.217.refs_4_), channel_id=1, source_target_pairs={{0,1},{1,2},{2,3},{3,0},{4,5},{5,6},{6,7},{7,4},{8,9},{9,10},{10,1... | collective-permute-start | bytes 491528 | tf_op jit(solution)/shard_map/ppermute | solution.py:70
  336.2 11.6 %collective-permute-start.56 = (f32[40,1024]{1,0:T(8,128)}, f32[40,1024]{1,0:T(8,128)}, u32[]{:S(2)}, u32[]{:S(2)}) collective-permute-start(f32[40,1024]{1,0:T(8,128)} %get-tuple-element.217.refs_4_), channel_id=1, source_target_pairs={{0,2},{1,3},{2,0},{3,1},{4,6},{5,7},{6,4},{7,5},{8,10},{9,11},{10,... | collective-permute-start | bytes 491528 | tf_op jit(solution)/shard_map/ppermute | solution.py:70
  340.0 11.2 %collective-permute-start.57 = (f32[40,1024]{1,0:T(8,128)}, f32[40,1024]{1,0:T(8,128)}, u32[]{:S(2)}, u32[]{:S(2)}) collective-permute-start(f32[40,1024]{1,0:T(8,128)} %get-tuple-element.217.refs_4_), channel_id=1, source_target_pairs={{0,3},{1,0},{2,1},{3,2},{4,7},{5,4},{6,5},{7,6},{8,11},{9,8},{10,9... | collective-permute-start | bytes 491528 | tf_op jit(solution)/shard_map/ppermute | solution.py:70
  347.1 24.5 %collective-permute-start.48 = (bf16[768,512]{1,0:T(8,128)(2,1)}, bf16[768,512]{1,0:T(8,128)(2,1)}, u32[]{:S(2)}, u32[]{:S(2)}) collective-permute-start(bf16[768,512]{1,0:T(8,128)(2,1)} %get-tuple-element.208), channel_id=1, source_target_pairs={{0,16},{4,20},{8,24},{12,28},{16,0},{20,4},{24,8},{28,12},{32,48},... | collective-permute-start | bytes 2359304 | tf_op jit(solution)/shard_map/ppermute | solution.py:64
  347.9 23.7 %collective-permute-start.49 = (bf16[768,512]{1,0:T(8,128)(2,1)}, bf16[768,512]{1,0:T(8,128)(2,1)}, u32[]{:S(2)}, u32[]{:S(2)}) collective-permute-start(bf16[768,512]{1,0:T(8,128)(2,1)} %get-tuple-element.210), channel_id=1, source_target_pairs={{0,96},{4,100},{8,104},{12,108},{16,112},{20,116},{24,120},{28,124... | collective-permute-start | bytes 2359304 | tf_op jit(solution)/shard_map/ppermute | solution.py:64
  376.3 17.2 %collective-permute-start.58 = (bf16[832,512]{1,0:T(8,128)(2,1)}, bf16[832,512]{1,0:T(8,128)(2,1)S(1)}, u32[]{:S(2)}, u32[]{:S(2)}) collective-permute-start(bf16[832,512]{1,0:T(8,128)(2,1)} %get-tuple-element.222), channel_id=1, source_target_pairs={{0,4},{4,0},{8,12},{12,8},{16,20},{20,16},{24,28},{28,24},{32,36},... | collective-permute-start | bytes 2555912 | tf_op jit(solution)/shard_map/ppermute | solution.py:64
  380.8 33.4 %collective-permute-start.50 = (bf16[768,512]{1,0:T(8,128)(2,1)}, bf16[768,512]{1,0:T(8,128)(2,1)S(1)}, u32[]{:S(2)}, u32[]{:S(2)}) collective-permute-start(bf16[768,512]{1,0:T(8,128)(2,1)} %after.17), channel_id=1, source_target_pairs={{0,64},{4,68},{8,72},{12,76},{16,80},{20,84},{24,88},{28,92},{32,9... | collective-permute-start | bytes 2359304 | tf_op jit(solution)/shard_map/ppermute | solution.py:64
  401.7 19.2 %collective-permute-start.75 = (bf16[128,1024]{1,0:T(8,128)(2,1)S(1)}, bf16[128,1024]{1,0:T(8,128)(2,1)S(1)}, u32[]{:S(2)}, u32[]{:S(2)}) collective-permute-start(bf16[128,1024]{1,0:T(8,128)(2,1)S(1)} %get-tuple-element.267), channel_id=1, source_target_pairs={{0,1},{1,2},{2,3},{3,0},{4,5},{5,6},{6,7},{7,4},{8,9},{9,10},{10,1... | collective-permute-start | bytes 786440 | tf_op jit(solution)/shard_map/ppermute | solution.py:70
  404.8 25.8 %collective-permute-start.77 = (bf16[128,1024]{1,0:T(8,128)(2,1)S(1)}, bf16[128,1024]{1,0:T(8,128)(2,1)S(1)}, u32[]{:S(2)}, u32[]{:S(2)}) collective-permute-start(bf16[128,1024]{1,0:T(8,128)(2,1)S(1)} %get-tuple-element.268), channel_id=1, source_target_pairs={{0,3},{1,0},{2,1},{3,2},{4,7},{5,4},{6,5},{7,6},{8,11},{9,8},{10,9... | collective-permute-start | bytes 786440 | tf_op jit(solution)/shard_map/ppermute | solution.py:70
  421.9 58.2 %collective-permute-start.76 = (bf16[256,1024]{1,0:T(8,128)(2,1)}, bf16[256,1024]{1,0:T(8,128)(2,1)}, u32[]{:S(2)}, u32[]{:S(2)}) collective-permute-start(bf16[256,1024]{1,0:T(8,128)(2,1)} %pad_maximum_fusion.3), channel_id=1, source_target_pairs={{0,1},{1,2},{2,3},{3,0},{4,5},{5,6},{6,7},{7,4},{8,9},{9,10},{10,1... | collective-permute-start | bytes 1572872 | tf_op jit(solution)/shard_map/ppermute | solution.py:70
  425.5 15.4 %collective-permute-start.69 = (bf16[256,512]{1,0:T(8,128)(2,1)}, bf16[256,512]{1,0:T(8,128)(2,1)S(1)}, u32[]{:S(2)}, u32[]{:S(2)}) collective-permute-start(bf16[256,512]{1,0:T(8,128)(2,1)} %get-tuple-element.245), channel_id=1, source_target_pairs={{0,96},{4,100},{8,104},{12,108},{16,112},{20,116},{24,120},{28,124... | collective-permute-start | bytes 786440 | tf_op jit(solution)/shard_map/ppermute | solution.py:64
  429.9 11.6 %collective-permute-start.70 = (bf16[256,512]{1,0:T(8,128)(2,1)}, bf16[256,512]{1,0:T(8,128)(2,1)S(1)}, u32[]{:S(2)}, u32[]{:S(2)}) collective-permute-start(bf16[256,512]{1,0:T(8,128)(2,1)} %get-tuple-element.246), channel_id=1, source_target_pairs={{0,64},{4,68},{8,72},{12,76},{16,80},{20,84},{24,88},{28,92},{32,9... | collective-permute-start | bytes 786440 | tf_op jit(solution)/shard_map/ppermute | solution.py:64
  429.9 15.3 %collective-permute-start.71 = (bf16[256,512]{1,0:T(8,128)(2,1)}, bf16[256,512]{1,0:T(8,128)(2,1)S(1)}, u32[]{:S(2)}, u32[]{:S(2)}) collective-permute-start(bf16[256,512]{1,0:T(8,128)(2,1)} %get-tuple-element.247), channel_id=1, source_target_pairs={{0,32},{4,36},{8,40},{12,44},{16,48},{20,52},{24,56},{28,60},{32,6... | collective-permute-start | bytes 786440 | tf_op jit(solution)/shard_map/ppermute | solution.py:64
  431.5 48.6 %collective-permute-start.78 = (bf16[256,1024]{1,0:T(8,128)(2,1)}, bf16[256,1024]{1,0:T(8,128)(2,1)}, u32[]{:S(2)}, u32[]{:S(2)}) collective-permute-start(bf16[256,1024]{1,0:T(8,128)(2,1)} %pad_maximum_fusion.4), channel_id=1, source_target_pairs={{0,3},{1,0},{2,1},{3,2},{4,7},{5,4},{6,5},{7,6},{8,11},{9,8},{10,9... | collective-permute-start | bytes 1572872 | tf_op jit(solution)/shard_map/ppermute | solution.py:70
  445.2 13.4 %collective-permute-start.74 = (bf16[256,512]{1,0:T(8,128)(2,1)}, bf16[256,512]{1,0:T(8,128)(2,1)S(1)}, u32[]{:S(2)}, u32[]{:S(2)}) collective-permute-start(bf16[256,512]{1,0:T(8,128)(2,1)} %get-tuple-element.251), channel_id=1, source_target_pairs={{0,8},{4,12},{8,16},{12,20},{16,24},{20,28},{24,0},{28,4},{32,40},... | collective-permute-start | bytes 786440 | tf_op jit(solution)/shard_map/ppermute | solution.py:64
  449.4 23.3 %collective-permute-start.79 = (bf16[208,512]{1,0:T(8,128)(2,1)S(1)}, bf16[208,512]{1,0:T(8,128)(2,1)}, u32[]{:S(2)}, u32[]{:S(2)}) collective-permute-start(bf16[208,512]{1,0:T(8,128)(2,1)S(1)} %copy-done.19), channel_id=1, source_target_pairs={{0,24},{4,28},{8,0},{12,4},{16,8},{20,12},{24,16},{28,20},{32,56},... | collective-permute-start | bytes 638984 | tf_op jit(solution)/shard_map/ppermute | solution.py:64
  451.5 21.3 %collective-permute-start.80 = (bf16[208,512]{1,0:T(8,128)(2,1)S(1)}, bf16[208,512]{1,0:T(8,128)(2,1)}, u32[]{:S(2)}, u32[]{:S(2)}) collective-permute-start(bf16[208,512]{1,0:T(8,128)(2,1)S(1)} %copy-done.19), channel_id=1, source_target_pairs={{0,16},{4,20},{8,24},{12,28},{16,0},{20,4},{24,8},{28,12},{32,48},... | collective-permute-start | bytes 638984 | tf_op jit(solution)/shard_map/ppermute | solution.py:64
  458.6 14.1 %collective-permute-start.81 = (bf16[208,512]{1,0:T(8,128)(2,1)S(1)}, bf16[208,512]{1,0:T(8,128)(2,1)}, u32[]{:S(2)}, u32[]{:S(2)}) collective-permute-start(bf16[208,512]{1,0:T(8,128)(2,1)S(1)} %copy-done.19), channel_id=1, source_target_pairs={{0,8},{4,12},{8,16},{12,20},{16,24},{20,28},{24,0},{28,4},{32,40},... | collective-permute-start | bytes 638984 | tf_op jit(solution)/shard_map/ppermute | solution.py:64
  (98 other events, 598.9 us)
Sparse Core Ops, SparseCore 0:
  286.6 52.4 reduce-scatter.1
  355.7 43.6 all-gather.1

commit v3 on v2

--- a/solution.py
+++ b/solution.py
@@ -97,7 +97,7 @@
     behind = (pieces[3][half:].astype(F32) + rest.astype(F32)).astype(BF16)
     ahead = jnp.concatenate([ahead, pieces[1][half:]], axis=0)
     behind = jnp.concatenate([pieces[3][:half], behind], axis=0)
-    return pieces[0], push_tp(ahead, 1), push_tp(behind, -1)
+    return (pieces[0], push_tp(ahead, 1), push_tp(behind, -1)), (first, rest)
 
 
 def ignoring(kernel, first, count):
@@ -126,15 +126,14 @@
 
 
 def attend_kernel(
-    rank, x0, x1, x2, x2_rest, x3, gain, wq, wk, wv, wo, cos, sin, seg_col, seg_row,
+    rank, x0, x1, x2, x3, gain, wq, wk, wv, wo, cos, sin, seg_col, seg_row,
     normed, q_out, k_out, v_out, mixed, lse, br0, br1, br2, br3, vt, bias,
 ):
     me = rank[0]
     lane = lax.broadcasted_iota(jnp.int32, (ROWS, LANES), 1)
     for d, x_ref in enumerate((x0, x1, x2, x3)):
         at = block_at((me + d) % RING)
-        x = jnp.concatenate([x2[...], x2_rest[...]], axis=0) if d == 2 else x_ref[...]
-        x = x.astype(F32)
+        x = x_ref[...].astype(F32)
         inverse = lax.rsqrt(jnp.mean(x * x, axis=-1, keepdims=True) + NORM_EPS)
         low = (x * inverse * gain[...]).astype(BF16)
         normed[at, :] = low
@@ -183,7 +182,7 @@
 def attend(rank, pieces, gain, wq, wk, wv, wo, cos, sin, seg_col, seg_row, *others):
     length = RING * ROWS
     return pl.pallas_call(
-        ignoring(attend_kernel, 15, len(others)),
+        ignoring(attend_kernel, 14, len(others)),
         out_shape=[
             jax.ShapeDtypeStruct((length, WIDTH), BF16),
             jax.ShapeDtypeStruct((length, HEADS * LANES), BF16),
@@ -193,13 +192,13 @@
             jax.ShapeDtypeStruct((8, length), F32),
         ]
         + [jax.ShapeDtypeStruct((ROWS, WIDTH), BF16)] * RING,
-        in_specs=[SCALARS] + [WHOLE] * 14 + [ANYWHERE] * len(others),
+        in_specs=[SCALARS] + [WHOLE] * 13 + [ANYWHERE] * len(others),
         out_specs=[WHOLE] * 10,
         scratch_shapes=[pltpu.VMEM((LANES, length), BF16), pltpu.VMEM((3 * ROWS, ROWS), F32)],
         compiler_params=params(),
         cost_estimate=NO_COST,
         name="attend",
-    )(rank, pieces[0], pieces[1], *pieces[2], pieces[3], gain, wq, wk, wv, wo, cos, sin, seg_col, seg_row, *others)
+    )(rank, *pieces, gain, wq, wk, wv, wo, cos, sin, seg_col, seg_row, *others)
 
 
 def high_low(v):
@@ -207,40 +206,39 @@
     return jnp.concatenate([high, (v - high.astype(F32)).astype(BF16)], axis=1)
 
 
-def high_plus_low(v):
-    return v[:, :ROWS].astype(F32) + v[:, ROWS:].astype(F32)
-
-
-def route_kernel(x, b0, b1, b2, b3, gain, wr, chosen, middle, half_a, half_b, gates_t):
+def route_kernel(x, b0, b1, b2, b3, gain, wr, chosen, table, middle, half_a, half_b, gates_t):
     branch = b0[...].astype(F32) + b1[...].astype(F32) + b2[...].astype(F32) + b3[...].astype(F32)
     mid = x[...].astype(F32) + RES_SCALE * branch
     middle[...] = mid
     inverse = lax.rsqrt(jnp.mean(mid * mid, axis=-1, keepdims=True) + NORM_EPS)
     routed = (mid * inverse * gain[...]).astype(BF16)
-    half_b[...] = routed[:, HALF:]
+    half_b[0:ROWS, :] = routed[:, HALF:]
     logits = jnp.where(chosen[...] > 0.0, dot(routed, wr[...]), NEG_FILL)
     weights = jnp.exp(logits - jnp.max(logits, axis=-1, keepdims=True))
     gates = (weights / jnp.sum(weights, axis=-1, keepdims=True)).T
     gates_t[...] = gates
     half_a[0:ROWS, :] = routed[:, :HALF]
-    half_a[ROWS:, :] = high_low(gates)
-
-
-def route(x, branches, gain, wr, chosen, *others):
-    return pl.pallas_call(
-        ignoring(route_kernel, 8, len(others)),
+    half_a[ROWS : ROWS + EXPERTS, :] = high_low(gates)
+    slots = jnp.concatenate([table[...], jnp.zeros_like(gates)], axis=1).astype(BF16)
+    half_a[ROWS + EXPERTS :, :] = slots
+    half_b[ROWS:, :] = slots
+
+
+def route(x, branches, gain, wr, chosen, table, *others):
+    return pl.pallas_call(
+        ignoring(route_kernel, 9, len(others)),
         out_shape=[
             jax.ShapeDtypeStruct((ROWS, WIDTH), F32),
+            jax.ShapeDtypeStruct((ROWS + 2 * EXPERTS, HALF), BF16),
             jax.ShapeDtypeStruct((ROWS + EXPERTS, HALF), BF16),
-            jax.ShapeDtypeStruct((ROWS, HALF), BF16),
             jax.ShapeDtypeStruct((EXPERTS, ROWS), F32),
         ],
-        in_specs=[WHOLE] * 8 + [ANYWHERE] * len(others),
+        in_specs=[WHOLE] * 9 + [ANYWHERE] * len(others),
         out_specs=[WHOLE] * 4,
         compiler_params=params(),
         cost_estimate=pl.CostEstimate(flops=20_000_000, bytes_accessed=5_000_000, transcendentals=8192),
         name="route",
-    )(x, *branches, gain, wr, chosen, *others)
+    )(x, *branches, gain, wr, chosen, table, *others)
 
 
 PIECE = 8 * CAP
@@ -279,38 +277,27 @@
                 pieces[p][at : at + CAP, :] = filled[(p * 2 + e) * CAP : (p * 2 + e + 1) * CAP, :]
 
 
-def pick_rows(spot, half, blocks, table, picked):
+def pick_rows(spot, half, blocks, first, table, picked):
     for d in range(RING):
-        table[...] = blocks[d][ROWS:, :].astype(F32)
+        table[...] = blocks[d][first : first + EXPERTS, :].astype(F32)
         for p in range(RING):
             for e in range(2):
                 r = line_row(d, p, e)
                 picked[r : r + 1, :] = table[pl.ds(expert_row(spot, half, d, p, e), 1), :]
 
 
-def add_extra(pieces, picked):
-    for p in range(RING):
-        extra = picked[p * 8 : (p + 1) * 8, :]
-        pieces[p][PIECE:, :] = jnp.concatenate([extra, jnp.zeros_like(extra)], axis=0).astype(BF16)
-
-
-def dispatch_cot_kernel(spot, *refs):
-    blocks, pieces, slots, (table, picked) = refs[:8], refs[8:16], refs[16:18], refs[18:]
+def dispatch_kernel(spot, *refs):
+    blocks, pieces, slots, (table, gates, picked) = refs[:8], refs[8:16], refs[16:18], refs[18:]
+    pick_rows(spot, 0, blocks[:4], ROWS, table, gates)
     for half in range(2):
         mine = slice(4 * half, 4 * half + 4)
-        pick_rows(spot, half, blocks[mine], table, picked)
+        pick_rows(spot, half, blocks[mine], ROWS + EXPERTS * (1 - half), table, picked)
         slots[half][...] = picked[:, :ROWS]
         fill_pieces(slots[half], blocks[mine], pieces[mine])
         if half == 0:
-            add_extra(pieces[mine], picked)
-
-
-def dispatch_rows_kernel(spot, slots_a, slots_b, *refs):
-    blocks, pieces, (table, picked) = refs[:8], refs[8:16], refs[16:]
-    fill_pieces(slots_a, blocks[:4], pieces[:4])
-    fill_pieces(slots_b, blocks[4:], pieces[4:])
-    pick_rows(spot, 0, blocks[:4], table, picked)
-    add_extra(pieces[:4], picked)
+            for p in range(RING):
+                at = slice(p * 8, (p + 1) * 8)
+                pieces[p][PIECE:, :] = jnp.concatenate([gates[at, :], picked[at, :]], axis=0).astype(BF16)
 
 
 def combine_kernel(with_extra, slots_a, slots_b, *refs):
@@ -338,49 +325,24 @@
     return jax.ShapeDtypeStruct((rows, HALF), dtype)
 
 
-def payload_kernel(cot, table, half_a, half_b):
-    for half, out in enumerate((half_a, half_b)):
-        out[0:ROWS, :] = cot[:, half * HALF : (half + 1) * HALF]
-        out[ROWS:, :] = table[...]
-
-
-def payload(cot, table, *others):
-    return pl.pallas_call(
-        ignoring(payload_kernel, 2, len(others)),
-        out_shape=[shape_of(ROWS + EXPERTS)] * 2,
-        in_specs=[WHOLE] * 2 + [ANYWHERE] * len(others),
-        out_specs=[WHOLE] * 2,
-        compiler_params=params(),
-        name="payload",
-    )(cot, table, *others)
-
-
-def spread_cot(cot, table, *others):
-    half_a, half_b = payload(cot, table)
-    a1, a3, b1 = push(half_a, -1, 0, 0), push(half_a, -3, 0, 0), push(half_b, 0, -1, 0)
-    later_a, later_b = payload(cot, table, a1, a3, b1, *others)
-    b3, a2, b2 = push(later_b, 0, -3, 0), push(later_a, -2, 0, 0), push(later_b, 0, -2, 0)
-    return [half_a, a1, a2, a3, half_b, b1, b2, b3]
-
-
 def spread_rows(half_a, half_b):
     return [push(half_a, -d, 0, 0) for d in range(RING)] + [push(half_b, 0, -d, 0) for d in range(RING)]
 
 
-def made_pieces(kernel, operands, slot_outputs=0, others=()):
-    count = len(operands)
-    return pl.pallas_call(
-        ignoring(kernel, count, len(others)),
+def dispatch(spot, half_a, half_b):
+    made = pl.pallas_call(
+        dispatch_kernel,
         out_shape=[shape_of(PIECE + EXTRA)] * RING
         + [shape_of(PIECE)] * RING
-        + [jax.ShapeDtypeStruct((EXPERTS, ROWS), F32)] * slot_outputs,
-        in_specs=[SCALARS if v.ndim == 1 else WHOLE for v in operands] + [ANYWHERE] * len(others),
-        out_specs=[WHOLE] * (8 + slot_outputs),
-        scratch_shapes=[TABLE] * 2,
+        + [jax.ShapeDtypeStruct((EXPERTS, ROWS), F32)] * 2,
+        in_specs=[SCALARS] + [WHOLE] * 8,
+        out_specs=[WHOLE] * 10,
+        scratch_shapes=[TABLE] * 3,
         compiler_params=params(),
         cost_estimate=SLOT_COST,
         name="dispatch",
-    )(*operands, *others)
+    )(spot, *spread_rows(half_a, half_b))
+    return exchange(made[:8]), made[8], made[9]
 
 
 def exchange(pieces):
@@ -412,7 +374,7 @@
         in_specs=[WHOLE] * 10 + [ANYWHERE] * len(others),
         out_specs=[WHOLE] * 8,
         compiler_params=params(),
-        cost_estimate=SLOT_COST,
+        cost_estimate=pl.CostEstimate(flops=60_000_000_000, bytes_accessed=0, transcendentals=0),
         name="combine",
     )(slots_a, slots_b, *pieces, *others)
 
@@ -425,17 +387,62 @@
     return got
 
 
+CHIPS = RING * RING
+PAIR = 2 * CAP
+
+
+def chips_matrix(spot, table, step):
+    rows = []
+    for i in range(RING):
+        for e in range(2):
+            expert = (step * RING + i) * 2 + (spot[3] + e) % 2
+            rows.append(slot_matrix(table[pl.ds(expert, 1), :]).astype(BF16))
+    return jnp.concatenate(rows, axis=0)
+
+
+def finish_kernel(spot, table, slots, middle, out, total):
+    step = pl.program_id(0)
+    term = dot_tn(chips_matrix(spot, table, step), slots[...])
+
+    @pl.when(step == 0)
+    def _():
+        total[...] = term
+
+    @pl.when(step > 0)
+    def _():
+        total[...] += term
+
+    @pl.when(step == RING - 1)
+    def _():
+        out[...] = (middle[...] + RES_SCALE * total[...]).astype(BF16)
+
+
+def finish(spot, table, slots, middle):
+    return pl.pallas_call(
+        finish_kernel,
+        grid=(RING,),
+        out_shape=jax.ShapeDtypeStruct((ROWS, WIDTH), BF16),
+        in_specs=[SCALARS, WHOLE, pl.BlockSpec((RING * PAIR, WIDTH), lambda s: (s, 0)), WHOLE],
+        out_specs=pl.BlockSpec((ROWS, WIDTH), lambda s: (0, 0)),
+        scratch_shapes=[pltpu.VMEM((ROWS, WIDTH), F32)],
+        compiler_params=params(),
+        cost_estimate=SLOT_COST,
+        name="finish",
+    )(spot, table, slots, middle)
+
+
+SAME_CORE = [list(range(core, EXPERTS, 2)) for core in range(2)]
+
+
 STEPS = 8
 STEP_ROWS = RING * CAP
 
 
-def expert_kernel(*refs):
-    ra, rb, ca, cb = (refs[4 * i : 4 * i + 4] for i in range(4))
-    weights = refs[16:18]
-    qa, qb, ma, mb = (refs[18 + 4 * i : 22 + 4 * i] for i in range(4))
-    disp_out, dgu_out, inner_out, dex_out = refs[34:38]
-    wgu, wd, rows_in, cot_in, gates_in, slots_in, back_out, moe_out, dgate_out, extra_out = refs[38:48]
-    weight_sem, in_sem, out_sem, extra_sem = refs[48:]
+def expert_kernel(spot, *refs):
+    ra, rb, cot, weights = refs[:4], refs[4:8], refs[8], refs[9:11]
+    qa, qb, moe, (disp_out, dgu_out, inner_out, dex_out) = refs[11:15], refs[15:19], refs[19], refs[20:24]
+    wgu, wd, rows_in, cot_in, gates_in, back_out, moe_out, dgate_out, extra_out = refs[24:33]
+    weight_sem, in_sem, out_sem, extra_sem = refs[33:]
     step = pl.program_id(0)
 
     def loads(e):
@@ -445,29 +452,28 @@
             pltpu.make_async_copy(down, wd.at[e], weight_sem.at[e, 1]),
         ]
 
-    def copies(j, groups, sems, outward):
-        slot, e, dx, made = j % 2, j // 4, j % 4, []
-        for which, (half_a, half_b, buf) in enumerate(groups):
-            ends = [(half_a[dx].at[pl.ds(e * STEP_ROWS, STEP_ROWS)], buf.at[slot, :, pl.ds(0, HALF)])]
-            for dz in range(RING):
-                far = half_b[dz].at[pl.ds((e * 4 + dx) * CAP, CAP)]
-                ends.append((far, buf.at[slot, pl.ds(dz * CAP, CAP), pl.ds(HALF, HALF)]))
-            for n, (far, near) in enumerate(ends):
-                source, target = (near, far) if outward else (far, near)
-                made.append(pltpu.make_async_copy(source, target, sems.at[slot, which * 6 + n]))
-        return made
+    def places(j, half_a, half_b, far, whole, halves):
+        slot, e, dx = j % 2, j // 4, j % 4
+        ends = [(half_a[dx].at[pl.ds(e * STEP_ROWS, STEP_ROWS)], halves.at[slot, :, pl.ds(0, HALF)])]
+        for dz in range(RING):
+            at = pl.ds(dz * CAP, CAP)
+            ends.append((half_b[dz].at[pl.ds((e * 4 + dx) * CAP, CAP)], halves.at[slot, at, pl.ds(HALF, HALF)]))
+            chip = ((spot[1] + dz) % RING) * RING + (spot[2] + dx) % RING
+            if far is cot:
+                ends.append((far.at[chip], whole.at[slot, pl.ds(dz * ROWS, ROWS)]))
+            else:
+                ends.append((far.at[chip, pl.ds(e * CAP, CAP)], whole.at[slot, at]))
+        return ends
 
     def fetches(j):
-        made = copies(j, ((ra, rb, rows_in), (ca, cb, cot_in)), in_sem, False)
-        slot, dx = j % 2, j % 4
-        for which, (far, near) in enumerate(((ra, gates_in), (ca, slots_in))):
-            made.append(
-                pltpu.make_async_copy(far[dx].at[pl.ds(PIECE, EXTRA)], near.at[slot], in_sem.at[slot, which * 6 + 5])
-            )
-        return made
+        slot = j % 2
+        ends = places(j, ra, rb, cot, cot_in, rows_in)
+        ends.append((ra[j % 4].at[pl.ds(PIECE, EXTRA)], gates_in.at[slot]))
+        return [pltpu.make_async_copy(far, near, in_sem.at[slot, n]) for n, (far, near) in enumerate(ends)]
 
     def stores(j):
-        return copies(j, ((qa, qb, back_out), (ma, mb, moe_out)), out_sem, True)
+        ends = places(j, qa, qb, moe, moe_out, back_out)
+        return [pltpu.make_async_copy(near, far, out_sem.at[j % 2, n]) for n, (far, near) in enumerate(ends)]
 
     for j in range(STEPS):
 
@@ -490,10 +496,10 @@
 
     slot = step % 2
     e = step // 4
-    gates = high_plus_low(gates_in[slot])
-    slots = slots_in[slot].astype(F32)
+    extra = gates_in[slot].astype(F32)
+    gates = extra[0:8, :ROWS] + extra[0:8, ROWS:]
     gates = jnp.where(e == 0, gates[0:4, :], gates[4:8, :])
-    slots = jnp.where(e == 0, slots[0:4, :ROWS], slots[4:8, :ROWS])
+    slots = jnp.where(e == 0, extra[8:12, :ROWS], extra[12:16, :ROWS])
     fills = [slot_matrix(slots[dz : dz + 1, :]) for dz in range(RING)]
     gate_slot = jnp.concatenate(
         [jnp.sum(fills[dz] * gates[dz : dz + 1, :], axis=1, keepdims=True) for dz in range(RING)], axis=0
@@ -507,7 +513,10 @@
     inner = (silu * up).astype(BF16)
     inner_out[...] = inner
     made = dot(inner, wd[e]).astype(BF16).astype(F32)
-    dmoe = RES_SCALE * cot_in[slot].astype(F32)
+    dmoe = [
+        dot(fills[dz].astype(BF16), cot_in[slot, dz * ROWS : (dz + 1) * ROWS, :]) for dz in range(RING)
+    ]
+    dmoe = RES_SCALE * jnp.concatenate(dmoe, axis=0)
     dgate_slot = jnp.sum(dmoe * made, axis=1, keepdims=True)
     dgates = [
         jnp.sum(fills[dz] * dgate_slot[dz * CAP : (dz + 1) * CAP, :], axis=0, keepdims=True) for dz in range(RING)
@@ -547,81 +556,113 @@
                     copy.wait()
 
 
-def experts(rows, cots, weights):
+def experts(spot, rows, cots, weights):
     total = STEPS * STEP_ROWS
     wide = pl.BlockSpec((STEP_ROWS, WIDTH), lambda s: (s, 0))
     narrow = pl.BlockSpec((STEP_ROWS, HALF), lambda s: (s, 0))
     buf = pltpu.VMEM((2, STEP_ROWS, WIDTH), BF16)
-    small = pltpu.VMEM((2, EXTRA, HALF), BF16)
     made = pl.pallas_call(
         expert_kernel,
         grid=(STEPS,),
         out_shape=[shape_of(PIECE + EXTRA)] * RING
-        + [shape_of(PIECE)] * 12
+        + [shape_of(PIECE)] * RING
         + [
+            jax.ShapeDtypeStruct((CHIPS, PAIR, WIDTH), BF16),
             jax.ShapeDtypeStruct((total, WIDTH), BF16),
             jax.ShapeDtypeStruct((total, WIDTH), BF16),
             jax.ShapeDtypeStruct((total, HALF), BF16),
             jax.ShapeDtypeStruct((total, WIDTH), BF16),
         ],
-        in_specs=[ANYWHERE] * 18,
-        out_specs=[ANYWHERE] * 16 + [wide, wide, narrow, wide],
+        in_specs=[SCALARS] + [ANYWHERE] * 11,
+        out_specs=[ANYWHERE] * 9 + [wide, wide, narrow, wide],
         scratch_shapes=[
             pltpu.VMEM((2, WIDTH, WIDTH), BF16),
             pltpu.VMEM((2, HALF, WIDTH), BF16),
-            buf, buf, small, small, buf, buf,
+            buf, pltpu.VMEM((2, RING * ROWS, WIDTH), BF16), pltpu.VMEM((2, EXTRA, HALF), BF16), buf, buf,
             pltpu.VMEM((EXPERTS, ROWS), F32),
             pltpu.VMEM((RING, EXTRA, HALF), BF16),
             pltpu.SemaphoreType.DMA((2, 2)),
-            pltpu.SemaphoreType.DMA((2, 12)),
-            pltpu.SemaphoreType.DMA((2, 12)),
+            pltpu.SemaphoreType.DMA((2, 10)),
+            pltpu.SemaphoreType.DMA((2, 10)),
             pltpu.SemaphoreType.DMA((RING,)),
         ],
         compiler_params=params(),
         cost_estimate=pl.CostEstimate(flops=19_000_000_000, bytes_accessed=60_000_000, transcendentals=1_600_000),
         name="experts",
-    )(*rows, *cots, *weights)
-    return made[:8], made[8:16], made[16:]
-
-
-def weight_grads_kernel(which, disp, dgu, inner, dex, out, disp_in, dgu_in, inner_in, dex_in, made, sems, out_sems):
+    )(spot, *rows, cots, *weights)
+    return made[:8], made[8], made[9:]
+
+
+def weight_grads_kernel(which, with_other, *refs):
+    disp, dgu, inner, dex = refs[:4]
+    other, out = refs[4] if with_other else None, refs[4 + with_other]
+    disp_in, dgu_in, inner_in, dex_in, made, other_in, sems, out_sems = refs[5 + with_other :]
     rows = pl.ds(which * 4 * STEP_ROWS, 4 * STEP_ROWS)
-    pairs = ((disp, disp_in), (dgu, dgu_in), (inner, inner_in), (dex, dex_in))
-    fetches = [pltpu.make_async_copy(far.at[rows], near, sems.at[i]) for i, (far, near) in enumerate(pairs)]
+    pairs = [(disp.at[rows], disp_in), (dgu.at[rows], dgu_in), (inner.at[rows], inner_in), (dex.at[rows], dex_in)]
+    if with_other:
+        pairs.append((other, other_in))
+    fetches = [pltpu.make_async_copy(far, near, sems.at[i]) for i, (far, near) in enumerate(pairs)]
     stores = [
         pltpu.make_async_copy(made.at[pl.ds(i * HALF, HALF)], out.at[pl.ds(i * HALF, HALF)], out_sems.at[i])
         for i in range(3)
     ]
     for copy in fetches:
         copy.start()
-    fetches[0].wait()
-    fetches[1].wait()
-    for i in range(2):
-        made[i * HALF : (i + 1) * HALF, :] = dot_tn(disp_in[:, i * HALF : (i + 1) * HALF], dgu_in[...]).astype(BF16)
+    for i, left in enumerate((disp_in, disp_in, inner_in)):
+        if i == 0:
+            fetches[0].wait()
+            fetches[1].wait()
+        if i == 2:
+            fetches[2].wait()
+            fetches[3].wait()
+        if with_other and i == 0:
+            fetches[4].wait()
+        cols = slice(i * HALF, (i + 1) * HALF) if i < 2 else slice(None)
+        grad = dot_tn(left[:, cols], (dgu_in if i < 2 else dex_in)[...])
+        if with_other:
+            grad = grad.astype(BF16).astype(F32) + other_in[i * HALF : (i + 1) * HALF, :].astype(F32)
+        made[i * HALF : (i + 1) * HALF, :] = grad.astype(BF16)
         stores[i].start()
-    fetches[2].wait()
-    fetches[3].wait()
-    made[WIDTH:, :] = dot_tn(inner_in[...], dex_in[...]).astype(BF16)
-    stores[2].start()
     for copy in stores:
         copy.wait()
 
 
-def weight_grads(which, saved):
+def weight_grads(which, saved, *other):
     wide, narrow = pltpu.VMEM((4 * STEP_ROWS, WIDTH), BF16), pltpu.VMEM((4 * STEP_ROWS, HALF), BF16)
-    return pl.pallas_call(
-        lambda *refs: weight_grads_kernel(which, *refs),
+    grads = pltpu.VMEM((WIDTH + HALF, WIDTH), BF16)
+    return pl.pallas_call(
+        lambda *refs: weight_grads_kernel(which, len(other), *refs),
         out_shape=jax.ShapeDtypeStruct((WIDTH + HALF, WIDTH), BF16),
-        in_specs=[ANYWHERE] * 4,
+        in_specs=[ANYWHERE] * (4 + len(other)),
         out_specs=ANYWHERE,
         scratch_shapes=[
-            wide, wide, narrow, wide, pltpu.VMEM((WIDTH + HALF, WIDTH), BF16),
-            pltpu.SemaphoreType.DMA((4,)), pltpu.SemaphoreType.DMA((3,)),
+            wide, wide, narrow, wide, grads, grads, pltpu.SemaphoreType.DMA((5,)), pltpu.SemaphoreType.DMA((3,)),
         ],
         compiler_params=params(),
         cost_estimate=NO_COST,
         name="weight_grads",
-    )(*saved)
+    )(*saved, *other)
+
+
+def cast_grads_kernel(grads, up, down):
+    for i in range(2):
+        up[:, i, :] = grads[0:WIDTH, i * HALF : (i + 1) * HALF].astype(F32)
+    down[...] = grads[WIDTH:, :].astype(F32)
+
+
+def cast_grads(grads):
+    return pl.pallas_call(
+        cast_grads_kernel,
+        out_shape=[
+            jax.ShapeDtypeStruct((WIDTH, 2, HALF), F32),
+            jax.ShapeDtypeStruct((HALF, WIDTH), F32),
+        ],
+        in_specs=[WHOLE],
+        out_specs=[WHOLE] * 2,
+        compiler_params=params(),
+        cost_estimate=NO_COST,
+        name="cast_grads",
+    )(grads)
 
 
 def unroute_kernel(spot, *refs):
@@ -671,7 +712,7 @@
         out_specs=[WHOLE] * 3,
         scratch_shapes=[pltpu.VMEM((EXPERTS, ROWS), F32), pltpu.VMEM((EXPERTS, ROWS), F32)],
         compiler_params=params(),
-        cost_estimate=pl.CostEstimate(flops=100_000_000_000, bytes_accessed=6_000_000, transcendentals=0),
+        cost_estimate=NO_COST,
         name="unroute",
     )(spot, *parts, gates_t, middle, cot, gain, wr_t, *others)
 
@@ -783,7 +824,7 @@
             pltpu.VMEM((length, LANES), F32),
         ],
         compiler_params=params(),
-        cost_estimate=pl.CostEstimate(flops=300_000_000_000, bytes_accessed=14_000_000, transcendentals=4_000_000),
+        cost_estimate=NO_COST,
         name="unattend",
     )(spot, q, k, v, lse, dmixed, normed, gain, wq, wk, wv, cos, sin, seg_col, seg_row)
 
@@ -860,23 +901,21 @@
     )(spot, *refs, *others)
 
 
-def sum_over_ep(spot, normed, dqkv, grad_out, sums, gains, moe_got, beside, finished):
+def sum_over_ep(spot, normed, dqkv, grad_out, sums, gains, dn, finished, output):
     own, other = small_call(
-        pack_kernel, spot, (normed, dqkv, grad_out, *sums), [((PAY, HALF), BF16)] * 2, flops=0, others=moe_got
+        pack_kernel, spot, (normed, dqkv, grad_out, *sums), [((PAY, HALF), BF16)] * 2, flops=0
     )
     got = push(other, 0, 0, 1)
     pieces = small_call(
         reduce_core_kernel, spot, (own, got, *gains), [((QUARTER, HALF), BF16)] * 4, (PAY, HALF)
     )
-    beside[0](pieces[0])
+    dn, halves = scatter_tp(after(dn, pieces[0]))
     pieces = [push(pieces[d], 0, d, 0) for d in range(RING)]
     quarter = [((QUARTER, HALF), BF16)]
-    (line,) = small_call(sum_kernel, spot, pieces, quarter)
-    beside[1](line)
+    (line,) = small_call(sum_kernel, spot, pieces, quarter, others=(*halves, output))
     (line,) = small_call(sum_kernel, spot, [push(line, d, 0, 0) for d in range(RING)], quarter)
-    beside[2](line)
     pieces = [push(line, 0, -d, 0) for d in range(RING)]
-    (half,) = small_call(gather_x_kernel, spot, pieces, [((PAY, HALF), BF16)], others=finished)
+    (half,) = small_call(gather_x_kernel, spot, pieces, [((PAY, HALF), BF16)], others=(*finished, *dn[1:]))
     made = small_call(
         unpack_kernel,
         spot,
@@ -890,7 +929,29 @@
             ((8, WIDTH), F32),
         ],
     )
-    return made
+    return *made, dn
+
+
+def hidden_kernel(a, b, c, hidden, gain, dmiddle, out):
+    dn = a[...].astype(F32) + b[...].astype(F32) + c[...].astype(F32)
+    x = hidden[...].astype(F32)
+    inverse = lax.rsqrt(jnp.mean(x * x, axis=-1, keepdims=True) + NORM_EPS)
+    plain = x * inverse
+    scaled = dn * gain[...]
+    along = jnp.mean(scaled * plain, axis=-1, keepdims=True)
+    out[...] = dmiddle[...] + inverse * (scaled - plain * along)
+
+
+def hidden_grad(dn, hidden, gain, dmiddle):
+    return pl.pallas_call(
+        hidden_kernel,
+        out_shape=jax.ShapeDtypeStruct((ROWS, WIDTH), F32),
+        in_specs=[WHOLE] * 6,
+        out_specs=WHOLE,
+        compiler_params=params(),
+        cost_estimate=NO_COST,
+        name="hidden_grad",
+    )(*dn, hidden, gain, dmiddle)
 
 
 def rope_tables(length):
@@ -911,7 +972,7 @@
     named = expert_ids[:, :, None] == jnp.arange(EXPERTS, dtype=jnp.int32)[None, None, :]
     slot_of = jnp.sum(jnp.where(named, slot_index[:, :, None] + 1, 0), axis=1) - 1
     chosen = (slot_of >= 0).astype(F32)
-    table = jnp.pad(slot_of.T.astype(BF16), ((0, 0), (0, HALF - ROWS)))
+    table = slot_of.T.astype(F32)
 
     gain_one = attn_gain.astype(F32).reshape(1, WIDTH)
     gain_two = ffn_gain.astype(F32).reshape(1, WIDTH)
@@ -919,89 +980,47 @@
     seg_row = segment_ids
     seg_col = segment_ids.reshape(length, 1)
 
-    group = gather_tp(hidden_in)
-    blocks = spread_cot(cotangent, table, group[1], group[3])
-    made = made_pieces(dispatch_cot_kernel, (spot, *blocks), 2, (*group[2], cos, sin, seg_col))
-    slots_a, slots_b = made[8:]
-    cot_pieces = made[:8]
-    cots = exchange_near(cot_pieces)
+    group = [push_tp(hidden_in, -d) for d in range(RING)]
+    cots = lax.all_gather(cotangent, "ep", axis=0, tiled=False, axis_index_groups=SAME_CORE)
     weights = jnp.concatenate([w_gate_up.reshape(WIDTH, 2 * HALF), w_down.reshape(HALF, WIDTH)], axis=0)
-    (weights,) = after((weights,), slots_a)
+    made = attend(spot, group, gain_one, w_query, w_key, w_value, w_output, cos, sin, seg_col, seg_row)
+    normed, q, k, v, mixed, lse = made[:6]
+    branches = [push_tp(made[6 + d], d) for d in range(RING)]
+    (weights,) = after((weights,), lse)
     weights = weights, push(weights, 0, 0, 1)
-
-    made = attend(spot, group, gain_one, w_query, w_key, w_value, w_output, cos, sin, seg_col, seg_row, slots_a)
-    normed, q, k, v, mixed, lse = made[:6]
-    sent = exchange_far(cot_pieces, cots, made[7:10], lse, weights[1])
-    branches = [made[6]] + [push_tp(sent[d], d + 1) for d in range(RING - 1)]
-    middle, half_a, half_b, gates_t = route(
-        hidden_in, branches, gain_two, w_router, chosen, cots[2], cots[6]
-    )
-    blocks = spread_rows(half_a, half_b)
-    rows = exchange(made_pieces(dispatch_rows_kernel, (spot, slots_a, slots_b, *blocks)))
-
-    back, moe_slots, saved = experts(rows, cots, weights)
+    middle, half_a, half_b, gates_t = route(hidden_in, branches, gain_two, w_router, chosen, table, weights[1])
+    rows, slots_a, slots_b = dispatch(spot, half_a, half_b)
+    back, moe_slots, saved = experts(spot, rows, cots, weights)
     got = exchange_near(back)
     (grads_other,) = exchange_far(back, got, (weight_grads(1, saved),))
-    grads_other = push(grads_other, 0, 0, 1)
-    grads_own = weight_grads(0, saved)
-    grads_e = (grads_own.astype(F32) + grads_other.astype(F32)).astype(BF16)
+    grads_e = weight_grads(0, saved, push(grads_other, 0, 0, 1))
     parts = to_owners(combine(slots_a, slots_b, got, True, grads_e))
+    grads_e = lax.psum_scatter(grads_e, "tp", scatter_dimension=0, tiled=True)
 
     dmiddle, dbranch, sums = unroute(
-        spot, parts, gates_t, middle, cotangent, gain_two, w_router.T.astype(F32), grads_e
+        spot, parts, gates_t, middle, cotangent, gain_two, w_router.T.astype(F32)
     )
-    grads_e = lax.psum_scatter(grads_e, "tp", scatter_dimension=0, tiled=True)
     group_grad = gather_tp(dbranch)
     sums = [push_tp(sums, d) for d in range(RING)]
 
-    moe_got = [moe_slots[0], None, None, None, moe_slots[4], None, None, None]
-    one, two, three = after((moe_slots[1], moe_slots[3], moe_slots[5]), dbranch)
-    moe_got[3], moe_got[1], moe_got[7] = push(one, 0, 1, 0), push(two, 0, 3, 0), push(three, 1, 0, 0)
-    one, two = after((moe_slots[7], moe_slots[2]), moe_got[3], moe_got[1], moe_got[7])
-    moe_got[5], moe_got[2] = push(one, 3, 0, 0), push(two, 0, 2, 0)
-    (one,) = after((moe_slots[6],), moe_got[5], moe_got[2])
-    moe_got[6] = push(one, 2, 0, 0)
-
-    (grads_e,) = after((grads_e,), *group_grad[2])
-    grads_e = lax.all_gather(grads_e, "tp", axis=0, tiled=True).astype(F32)
-    grad_up = grads_e[:WIDTH].reshape(1, WIDTH, 2, HALF)
-    grad_down = grads_e[WIDTH:].reshape(1, HALF, WIDTH)
-    dmixed, grad_output = unmix(spot, group_grad, mixed, w_output, moe_got[1], moe_got[3], moe_got[7], *sums[1:])
+    (moe_slots,) = after((moe_slots,), *parts)
+    moe_slots = lax.all_to_all(
+        moe_slots, "ep", split_axis=0, concat_axis=0, tiled=True, axis_index_groups=SAME_CORE
+    )
+
+    dmixed, grad_output = unmix(spot, group_grad, mixed, w_output, *sums[1:])
+    (grads_e,) = after((grads_e,), dmixed)
+    grad_up, grad_down = cast_grads(lax.all_gather(grads_e, "tp", axis=0, tiled=True))
     last = unattend(
         spot, q, k, v, lse, dmixed, normed, gain_one, w_query, w_key, w_value, cos, sin, seg_col, seg_row
     )
     gain = last[1] + push(last[1], 0, 0, 1)
     gains = [push_tp(gain, d) for d in range(RING)]
-    dn, moe_parts = [], []
-
-    def beside_x(piece):
-        dn.extend(scatter_tp(after(last[2:6], piece)))
-
-    def beside_z(line):
-        moe_parts.extend(combine(slots_a, slots_b, after(moe_got, line), False))
-
-    def beside_last(line):
-        moe_parts[:] = to_owners(after(moe_parts, line))
-
-    grad_query, grad_key, grad_value, grad_output, grad_router, grad_gains = sum_over_ep(
-        spot, normed, last[0], grad_output, sums, gains, (moe_got[2], moe_got[5]), (beside_x, beside_z, beside_last),
-        (grad_up, grad_down),
+    output = finish(spot, table, moe_slots.reshape(CHIPS * PAIR, WIDTH), middle)
+    grad_query, grad_key, grad_value, grad_output, grad_router, grad_gains, dn = sum_over_ep(
+        spot, normed, last[0], grad_output, sums, gains, last[2:6], (grad_up, grad_down), output
     )
-    dnormed = dn[0].astype(F32) + dn[1].astype(F32) + dn[2].astype(F32)
-
-    local = hidden_in.astype(F32)
-    inverse = lax.rsqrt(jnp.mean(local * local, axis=-1, keepdims=True) + NORM_EPS)
-    plain = local * inverse
-    scaled = dnormed * gain_one
-    along = jnp.mean(scaled * plain, axis=-1, keepdims=True)
-    grad_hidden = dmiddle + inverse * (scaled - plain * along)
-
-    def four_sum(p):
-        a, b, c, d = (piece.astype(F32) for piece in p)
-        return (a + b) + (c + d)
-
-    moe = jnp.concatenate([four_sum(moe_parts[:4]), four_sum(moe_parts[4:])], axis=1)
-    output = (middle + RES_SCALE * moe).astype(BF16)
+    grad_hidden = hidden_grad(dn, hidden_in, gain_one, dmiddle)
     return (
         output,
         grad_hidden,
@@ -1012,8 +1031,8 @@
         grad_output,
         grad_gains[0],
         grad_router.T,
-        grad_up,
-        grad_down,
+        grad_up.reshape(1, WIDTH, 2, HALF),
+        grad_down.reshape(1, HALF, WIDTH),
     )
 
 

time: 507 us -> 443 us (0.87)
  the two profiles are of different devices: /device:TPU:1 before, /device:TPU:25 now
where the time goes in v3:
time: 443 us; the launch traced here: 435 us
  waiting for transfers between devices  159 us (36%)
  Pallas kernels  150 us (34%)
  starting transfers between devices  74.2 us (17%)
  local copies, waits for them, and re-layouts  26.1 us (6%)
  between operations  14.7 us (3%)
  other arithmetic  10.9 us (2%)
    ppermute x38, waiting for transfers between devices, push(): return lax.ppermute(value, 'ep', pairs)  99.2 us
    ppermute x20, waiting for transfers between devices, push_tp(): lax.ppermute(value, 'tp', [(y, (y + dy) % RING) for y in range(RING)])  59.2 us
    ppermute x38, starting transfers between devices, push(): return lax.ppermute(value, 'ep', pairs)  43.8 us
    pallas_call x1, Pallas kernels, experts(): pl.pallas_call(expert_kernel, grid=(STEPS,), out_shape=[shape_of(PIECE +...  38.7 us
    ppermute x20, starting transfers between devices, push_tp(): lax.ppermute(value, 'tp', [(y, (y + dy) % RING) for y in range(RING)])  23.4 us
    pallas_call x2, Pallas kernels, weight_grads(): pl.pallas_call(lambda *refs: weight_grads_kernel(which, len(other), *refs...  20.6 us
    unnamed x126, local copies, waits for them, and re-layouts  19.1 us
    pallas_call x6, Pallas kernels, small_call(): pl.pallas_call(ignoring(kernel, 1 + len(refs), len(others)), out_shape=[j...  17.4 us
  transfers between devices with their start and end apart: 62, of which 34 were waited for; matrix products, arithmetic and copies ran while one was open for 4% of the time, Pallas kernels for 24%

profile of v3, /device:TPU:25, one launch (start us, length us, event | category | flops | bytes accessed | tf_op | source)
XLA Modules:
  0.0 435.1 jit_solution(1827301597184754489)
XLA Ops:
  9.1 2.0 collective-permute-start.2
  11.1 2.0 fusion.2
  14.9 1.7 copy.46.refs_12_.seg_col
  16.7 2.2 copy.50
  18.9 1.9 pad_maximum_fusion.1
  20.8 2.0 pad_maximum_fusion.refs_0_
  22.8 10.8 %collective-permute-done.refs_2_ = bf16[256,1024]{1,0:T(8,128)(2,1)S(1)} collective-permute-done((bf16[256,1024]{1,0:T(8,128)(2,1)}, bf16[256,1024]{1,0:T(8,128)(2,1)S(1)}, u32[]{:S(2)}, u32[]{:S(2)}) %collective-permute-start) | collective-permute-done | bytes 524320 | tf_op jit(solution)/shard_map/ppermute | solution.py:70
  35.0 17.1 %attend.1 = (bf16[1024,1024]{1,0:T(8,128)(2,1)}, bf16[1024,512]{1,0:T(8,128)(2,1)}, bf16[1024,128]{1,0:T(8,128)(2,1)}, bf16[1024,128]{1,0:T(8,128)(2,1)}, bf16[1...) custom-call(s32[4]{0:T(128)} %pad_add_fusion.refs_0_.spot, ...), custom_call_target="tpu_custom_call" | custom-call | tf_op jit(solution)/shard_map/attend/pallas_call | solution.py:184
  53.7 2.5 collective-permute-start.3
  59.6 18.9 %collective-permute-done.3.refs_2_ = bf16[256,1024]{1,0:T(8,128)(2,1)} collective-permute-done((bf16[256,1024]{1,0:T(8,128)(2,1)}, bf16[256,1024]{1,0:T(8,128)(2,1)}, u32[]{:S(2)}, u32[]{:S(2)}) %collective-permute-start.3) | collective-permute-done | bytes 524320 | tf_op jit(solution)/shard_map/ppermute | solution.py:70
  78.5 4.0 collective-permute-done.5.refs_4_
  84.2 3.6 route.1
  87.8 2.5 collective-permute-start.10
  90.2 3.6 collective-permute-start.7
  96.9 6.0 %collective-permute-done.11.refs_6_ = bf16[288,512]{1,0:T(8,128)(2,1)S(1)} collective-permute-done((bf16[288,512]{1,0:T(8,128)(2,1)}, bf16[288,512]{1,0:T(8,128)(2,1)S(1)}, u32[]{:S(2)}, u32[]{:S(2)}) %collective-permute-start.11) | collective-permute-done | bytes 294944 | tf_op jit(solution)/shard_map/ppermute | solution.py:64
  102.9 5.6 %collective-permute-done.12.refs_7_ = bf16[288,512]{1,0:T(8,128)(2,1)S(1)} collective-permute-done((bf16[288,512]{1,0:T(8,128)(2,1)}, bf16[288,512]{1,0:T(8,128)(2,1)S(1)}, u32[]{:S(2)}, u32[]{:S(2)}) %collective-permute-start.12) | collective-permute-done | bytes 294944 | tf_op jit(solution)/shard_map/ppermute | solution.py:64
  108.5 3.1 collective-permute-done.9.refs_3_
  112.4 6.2 %dispatch.1 = (bf16[784,512]{1,0:T(8,128)(2,1)}, bf16[784,512]{1,0:T(8,128)(2,1)}, bf16[784,512]{1,0:T(8,128)(2,1)}, bf16[784,512]{1,0:T(8,128)(2,1)}, bf16[768,...) custom-call(s32[4]{0:T(128)} %pad_add_fusion.refs_0_.spot, ...), custom_call_target="tpu_custom_call" | custom-call | flops 1000000000 | bytes 5000000 | tf_op jit(solution)/shard_map/dispatch/pallas_call | solution.py:333
  123.1 12.8 %collective-permute-done.16.refs_1_.refs_5_ = bf16[768,512]{1,0:T(8,128)(2,1)S(1)} collective-permute-done((bf16[768,512]{1,0:T(8,128)(2,1)}, bf16[768,512]{1,0:T(8,128)(2,1)S(1)}, u32[]{:S(2)}, u32[]{:S(2)}) %collective-permute-start.16) | collective-permute-done | bytes 786464 | tf_op jit(solution)/shard_map/ppermute | solution.py:64
  137.1 22.7 %collective-permute-done.15.refs_3_ = bf16[784,512]{1,0:T(8,128)(2,1)} collective-permute-done((bf16[784,512]{1,0:T(8,128)(2,1)}, bf16[784,512]{1,0:T(8,128)(2,1)}, u32[]{:S(2)}, u32[]{:S(2)}) %collective-permute-start.15) | collective-permute-done | bytes 802848 | tf_op jit(solution)/shard_map/ppermute | solution.py:64
  160.7 38.7 %experts.1 = (bf16[784,512]{1,0:T(8,128)(2,1)}, bf16[784,512]{1,0:T(8,128)(2,1)}, bf16[784,512]{1,0:T(8,128)(2,1)}, bf16[784,512]{1,0:T(8,128)(2,1)}, bf16[768,5...) custom-call(s32[4]{0:T(128)} %pad_add_fusion.refs_0_.spot, ...), custom_call_target="tpu_custom_call" | custom-call | flops 19000000512 | bytes 60000000 | tf_op jit(solution)/shard_map/experts/pallas_call | solution.py:564
  202.4 9.2 %weight_grads.2.refs_2_ = bf16[1536,1024]{1,0:T(8,128)(2,1)} custom-call(bf16[3072,1024]{1,0:T(8,128)(2,1)} %get-tuple-element.110.refs_0_, bf16[3072,1024]{1,0:T(8,128)(2,1)} %get-tuple-element.111.refs_1_, bf16[3072,512]{1,0:T(8,128)(2,1)} %get-tuple-element.112.refs_2_, bf16[3072,1024]{1,0:T(8,128)(2,1)} %get-tuple-element.113.refs_3_), custom_call_target="tpu_custom_call" | custom-call | tf_op jit(solution)/shard_map/weight_grads/pallas_call | solution.py:633
  211.6 7.5 %collective-permute-done.21.refs_5_.refs_7_ = bf16[768,512]{1,0:T(8,128)(2,1)S(1)} collective-permute-done((bf16[768,512]{1,0:T(8,128)(2,1)}, bf16[768,512]{1,0:T(8,128)(2,1)S(1)}, u32[]{:S(2)}, u32[]{:S(2)}) %collective-permute-start.21) | collective-permute-done | bytes 786464 | tf_op jit(solution)/shard_map/ppermute | solution.py:64
  219.1 2.2 collective-permute-done.22.refs_6_.refs_9_
  223.2 2.3 collective-permute-start.25
  227.0 3.9 collective-permute-done.25.refs_4_
  232.6 11.4 %weight_grads.3.refs_10_ = bf16[1536,1024]{1,0:T(8,128)(2,1)} custom-call(bf16[3072,1024]{1,0:T(8,128)(2,1)} %get-tuple-element.110.refs_0_, bf16[3072,1024]{1,0:T(8,128)(2,1)} %get-tuple-element.111.refs_1_, bf16[3072,512]{1,0:T(8,128)(2,1)} %get-tuple-element.112.refs_2_, bf16[3072,1024]{1,0:T(8,128)(2,1)} %get-tuple-element.113.refs_3_, ...), custom_call_target="tpu_custom_call" | custom-call | tf_op jit(solution)/shard_map/weight_grads/pallas_call | solution.py:633
  244.1 3.5 collective-permute-done.24.refs_8_
  248.7 5.7 %combine.1 = (bf16[272,512]{1,0:T(8,128)(2,1)}, bf16[272,512]{1,0:T(8,128)(2,1)}, bf16[272,512]{1,0:T(8,128)(2,1)}, bf16[272,512]{1,0:T(8,128)(2,1)}, bf16[256,5...) custom-call(f32[32,256]{1,0:T(8,128)} %get-tuple-element.104.refs_0_, ...), custom_call_target="tpu_custom_call" | custom-call | flops 60000002048 | tf_op jit(solution)/shard_map/combine/pallas_call | solution.py:371
  258.1 3.3 collective-permute-done.29.refs_6_
  261.9 2.5 collective-permute-done.30.refs_7_
  264.4 5.5 %collective-permute-done.31.refs_8_ = bf16[256,512]{1,0:T(8,128)(2,1)S(1)} collective-permute-done((bf16[256,512]{1,0:T(8,128)(2,1)}, bf16[256,512]{1,0:T(8,128)(2,1)S(1)}, u32[]{:S(2)}, u32[]{:S(2)}) %collective-permute-start.31) | collective-permute-done | bytes 262176 | tf_op jit(solution)/shard_map/ppermute | solution.py:64
  269.9 1.9 collective-permute-done.28.refs_4_
  272.5 6.9 %all-to-all-start = ((bf16[16,192,1024]{2,1,0:T(8,128)(2,1)}), bf16[16,192,1024]{2,1,0:T(8,128)(2,1)}, u32[]{:S(2)}, u32[]{:S(2)}) async-start(bf16[16,192,1024]{2,1,0:T(8,128)(2,1)} %after.9), calls=%async_computation | async-start | bytes 12582912 | tf_op jit(solution)/shard_map/all_to_all | solution.py:1007
  280.2 5.0 %unroute.1 = (f32[256,1024]{1,0:T(8,128)}, bf16[256,1024]{1,0:T(8,128)(2,1)}, f32[40,1024]{1,0:T(8,128)}) custom-call(s32[4]{0:T(128)} %pad_add_fusion.refs_0_.spot, bf16[272,512]{1,0:T(8,128)(2,1)} %get-tuple-element.121.refs_1_, bf16[272,512]{1,0:T(8,128)(2,1)} %copy-done.5, bf16[272,512]{1,0:T(8,128)(2,1)} %copy-done.6, bf16[272,512]{1,0:T(8,128)(2,1)} %copy-done.7, ...), custom_call_target="tpu_custom_call" | custom-call | tf_op jit(solution)/shard_map/unroute/pallas_call | solution.py:704
  285.2 2.7 collective-permute-start.34
  287.9 11.6 %collective-permute-done.32.refs_2_ = bf16[256,1024]{1,0:T(8,128)(2,1)S(1)} collective-permute-done((bf16[256,1024]{1,0:T(8,128)(2,1)}, bf16[256,1024]{1,0:T(8,128)(2,1)S(1)}, u32[]{:S(2)}, u32[]{:S(2)}) %collective-permute-start.32) | collective-permute-done | bytes 524320 | tf_op jit(solution)/shard_map/ppermute | solution.py:70
  305.7 4.1 collective-permute-done.36.refs_8_.refs_5_
  309.9 1.9 collective-permute-done.37.refs_9_.refs_6_
  313.6 4.3 unmix.1
  317.9 16.1 %unattend.1 = (bf16[1024,512]{1,0:T(8,128)(2,1)}, f32[8,1024]{1,0:T(8,128)}, bf16[256,1024]{1,0:T(8,128)(2,1)}, bf16[256,1024]{1,0:T(8,128)(2,1)}, bf16[256,1024]{1,0:T(8,128)(2,1)}, /*index=5*/bf16[256,1024]{1,0:T(8,128)(2,1)}) custom-call(s32[4]{0:T(128)} %pad_add_fusion.refs_0_.spot, bf16[1024,512]{1,0:T(8,128)(2,1)} %get-tuple-element.130.q_in, ...), custom_call_target="tpu_custom_call" | custom-call | tf_op jit(solution)/shard_map/unattend/pallas_call | solution.py:811
  334.0 4.9 %shard_map.221 = (bf16[832,512]{1,0:T(8,128)(2,1)}, bf16[832,512]{1,0:T(8,128)(2,1)}) custom-call(s32[4]{0:T(128)} %pad_add_fusion.refs_0_.spot, bf16[1024,1024]{1,0:T(8,128)(2,1)} %get-tuple-element.138.normed.refs_1_, bf16[1024,512]{1,0:T(8,128)(2,1)} %get-tuple-element.143.refs_2_, bf16[256,1024]{1,0:T(8,128)(2,1)} %get-tuple-element.144.refs_3_, ...), custom_call_target="tpu_custom_call" | custom-call | bytes 2000000 | tf_op jit(solution)/shard_map/pallas_call | solution.py:893
  339.0 4.1 collective-permute-start.39
  343.2 1.8 collective-permute-done.40
  345.0 2.5 collective-permute-start.41
  349.1 3.7 collective-permute-done.42.refs_5_
  354.9 2.8 shard_map.222
  358.9 2.7 collective-permute-start.44
  362.7 2.4 collective-permute-start.49
  372.6 6.3 %finish.1.refs_7_ = bf16[256,1024]{1,0:T(8,128)(2,1)} custom-call(s32[4]{0:T(128)} %pad_add_fusion.refs_0_.spot, f32[32,256]{1,0:T(8,128)} %convert_bitcast_fusion.1.refs_8_.table, bf16[3072,1024]{1,0:T(8,128)(2,1)} %bitcast.10.slots, f32[256,1024]{1,0:T(8,128)} %get-tuple-element.129.middle.refs_10_), custom_call_target="tpu_custom_call" | custom-call | flops 1000000000 | bytes 5000000 | tf_op jit(solution)/shard_map/finish/pallas_call | solution.py:421
  379.0 2.0 collective-permute-done.49.refs_3_
  382.4 2.0 shard_map.223.refs_1_
  384.4 2.5 collective-permute-start.52
  386.9 2.1 collective-permute-start.53
  389.0 2.6 collective-permute-done.51.refs_2_
  391.6 3.2 collective-permute-done.52.refs_3_
  396.8 2.0 shard_map.224.refs_1_
  398.9 3.6 collective-permute-start.54
  403.0 5.4 %cast_grads.1 = (f32[1024,2,512]{2,1,0:T(2,128)}, f32[512,1024]{1,0:T(8,128)}) custom-call(bf16[1536,1024]{1,0:T(8,128)(2,1)} %all-gather.4.cloned.1.call-done.grads), custom_call_target="tpu_custom_call" | custom-call | tf_op jit(solution)/shard_map/cast_grads/pallas_call | solution.py:654
  408.5 2.9 collective-permute-done.54.refs_2_
  411.4 3.8 collective-permute-done.56.refs_4_
  416.0 2.2 shard_map.225.refs_1_
  419.0 3.4 hidden_grad.1
  423.4 3.3 shard_map.226
  (239 shorter events, 66.6 us)
Async XLA Ops:
  7.2 152.6 %all-gather.6.cloned.1.call-start = ((), (), s32[]{:S(2)}) async-start(), calls=%async_computation.4 | async-start | bytes 8912896 | tf_op jit(solution)/shard_map/all_gather | solution.py:984
  7.9 310.0 %reduce-scatter.2.cloned.1.call-start = ((), (), s32[]{:S(2)}) async-start(), calls=%async_computation.2 | async-start | bytes 3932160 | tf_op jit(solution)/shard_map/reduce_scatter | solution.py:998
  8.0 25.6 %collective-permute-start = (bf16[256,1024]{1,0:T(8,128)(2,1)}, bf16[256,1024]{1,0:T(8,128)(2,1)S(1)}, u32[]{:S(2)}, u32[]{:S(2)}) collective-permute-start(bf16[256,1024]{1,0:T(8,128)(2,1)} %hidden.1), channel_id=1, source_target_pairs={{0,3},{1,0},{2,1},{3,2},{4,7},{5,4},{6,5},{7,6},{8,11},{9,8},{10,9... | collective-permute-start | bytes 1572872 | tf_op jit(solution)/shard_map/ppermute | solution.py:70
  8.5 25.1 %collective-permute-start.1 = (bf16[256,1024]{1,0:T(8,128)(2,1)}, bf16[256,1024]{1,0:T(8,128)(2,1)S(1)}, u32[]{:S(2)}, u32[]{:S(2)}) collective-permute-start(bf16[256,1024]{1,0:T(8,128)(2,1)} %hidden.1), channel_id=1, source_target_pairs={{0,2},{1,3},{2,0},{3,1},{4,6},{5,7},{6,4},{7,5},{8,10},{9,11},{10,... | collective-permute-start | bytes 1572872 | tf_op jit(solution)/shard_map/ppermute | solution.py:70
  9.1 25.1 %collective-permute-start.2 = (bf16[256,1024]{1,0:T(8,128)(2,1)}, bf16[256,1024]{1,0:T(8,128)(2,1)S(1)}, u32[]{:S(2)}, u32[]{:S(2)}) collective-permute-start(bf16[256,1024]{1,0:T(8,128)(2,1)} %hidden.1), channel_id=1, source_target_pairs={{0,1},{1,2},{2,3},{3,0},{4,5},{5,6},{6,7},{7,4},{8,9},{9,10},{10,1... | collective-permute-start | bytes 1572872 | tf_op jit(solution)/shard_map/ppermute | solution.py:70
  52.1 30.4 %collective-permute-start.6 = (bf16[1536,1024]{1,0:T(8,128)(2,1)}, bf16[1536,1024]{1,0:T(8,128)(2,1)S(1)}, u32[]{:S(2)}, u32[]{:S(2)}) collective-permute-start(bf16[1536,1024]{1,0:T(8,128)(2,1)} %after.6.refs_9_), channel_id=1, source_target_pairs={{0,4},{4,0},{8,12},{12,8},{16,20},{20,16},{24,28},{28,24},{32,36},... | collective-permute-start | bytes 9437192 | tf_op jit(solution)/shard_map/ppermute | solution.py:64
  53.7 24.9 %collective-permute-start.3 = (bf16[256,1024]{1,0:T(8,128)(2,1)}, bf16[256,1024]{1,0:T(8,128)(2,1)}, u32[]{:S(2)}, u32[]{:S(2)}) collective-permute-start(bf16[256,1024]{1,0:T(8,128)(2,1)} %get-tuple-element.89), channel_id=1, source_target_pairs={{0,1},{1,2},{2,3},{3,0},{4,5},{5,6},{6,7},{7,4},{8,9},{9,10},{10,1... | collective-permute-start | bytes 1572872 | tf_op jit(solution)/shard_map/ppermute | solution.py:70
  56.2 22.3 %collective-permute-start.4 = (bf16[256,1024]{1,0:T(8,128)(2,1)}, bf16[256,1024]{1,0:T(8,128)(2,1)}, u32[]{:S(2)}, u32[]{:S(2)}) collective-permute-start(bf16[256,1024]{1,0:T(8,128)(2,1)} %get-tuple-element.90), channel_id=1, source_target_pairs={{0,2},{1,3},{2,0},{3,1},{4,6},{5,7},{6,4},{7,5},{8,10},{9,11},{10,... | collective-permute-start | bytes 1572872 | tf_op jit(solution)/shard_map/ppermute | solution.py:70
  56.2 26.3 %collective-permute-start.5 = (bf16[256,1024]{1,0:T(8,128)(2,1)}, bf16[256,1024]{1,0:T(8,128)(2,1)}, u32[]{:S(2)}, u32[]{:S(2)}) collective-permute-start(bf16[256,1024]{1,0:T(8,128)(2,1)} %get-tuple-element.91), channel_id=1, source_target_pairs={{0,3},{1,0},{2,1},{3,2},{4,7},{5,4},{6,5},{7,6},{8,11},{9,8},{10,9... | collective-permute-start | bytes 1572872 | tf_op jit(solution)/shard_map/ppermute | solution.py:70
  87.8 8.3 %collective-permute-start.10 = (bf16[288,512]{1,0:T(8,128)(2,1)}, bf16[288,512]{1,0:T(8,128)(2,1)S(1)}, u32[]{:S(2)}, u32[]{:S(2)}) collective-permute-start(bf16[288,512]{1,0:T(8,128)(2,1)} %get-tuple-element.94.refs_4_), channel_id=1, source_target_pairs={{0,24},{4,28},{8,0},{12,4},{16,8},{20,12},{24,16},{28,20},{32,56},... | collective-permute-start | bytes 884744 | tf_op jit(solution)/shard_map/ppermute | solution.py:64
  90.2 18.3 %collective-permute-start.7 = (bf16[320,512]{1,0:T(8,128)(2,1)}, bf16[320,512]{1,0:T(8,128)(2,1)S(1)}, u32[]{:S(2)}, u32[]{:S(2)}) collective-permute-start(bf16[320,512]{1,0:T(8,128)(2,1)} %get-tuple-element.93.refs_0_), channel_id=1, source_target_pairs={{0,96},{4,100},{8,104},{12,108},{16,112},{20,116},{24,120},{28,124... | collective-permute-start | bytes 983048 | tf_op jit(solution)/shard_map/ppermute | solution.py:64
  93.9 14.6 %collective-permute-start.8 = (bf16[320,512]{1,0:T(8,128)(2,1)}, bf16[320,512]{1,0:T(8,128)(2,1)S(1)}, u32[]{:S(2)}, u32[]{:S(2)}) collective-permute-start(bf16[320,512]{1,0:T(8,128)(2,1)} %get-tuple-element.93.refs_0_), channel_id=1, source_target_pairs={{0,64},{4,68},{8,72},{12,76},{16,80},{20,84},{24,88},{28,92},{32,9... | collective-permute-start | bytes 983048 | tf_op jit(solution)/shard_map/ppermute | solution.py:64
  93.9 17.7 %collective-permute-start.9 = (bf16[320,512]{1,0:T(8,128)(2,1)}, bf16[320,512]{1,0:T(8,128)(2,1)S(1)}, u32[]{:S(2)}, u32[]{:S(2)}) collective-permute-start(bf16[320,512]{1,0:T(8,128)(2,1)} %get-tuple-element.93.refs_0_), channel_id=1, source_target_pairs={{0,32},{4,36},{8,40},{12,44},{16,48},{20,52},{24,56},{28,60},{32,6... | collective-permute-start | bytes 983048 | tf_op jit(solution)/shard_map/ppermute | solution.py:64
  94.6 8.3 %collective-permute-start.11 = (bf16[288,512]{1,0:T(8,128)(2,1)}, bf16[288,512]{1,0:T(8,128)(2,1)S(1)}, u32[]{:S(2)}, u32[]{:S(2)}) collective-permute-start(bf16[288,512]{1,0:T(8,128)(2,1)} %get-tuple-element.94.refs_4_), channel_id=1, source_target_pairs={{0,16},{4,20},{8,24},{12,28},{16,0},{20,4},{24,8},{28,12},{32,48},... | collective-permute-start | bytes 884744 | tf_op jit(solution)/shard_map/ppermute | solution.py:64
  96.1 12.4 %collective-permute-start.12 = (bf16[288,512]{1,0:T(8,128)(2,1)}, bf16[288,512]{1,0:T(8,128)(2,1)S(1)}, u32[]{:S(2)}, u32[]{:S(2)}) collective-permute-start(bf16[288,512]{1,0:T(8,128)(2,1)} %get-tuple-element.94.refs_4_), channel_id=1, source_target_pairs={{0,8},{4,12},{8,16},{12,20},{16,24},{20,28},{24,0},{28,4},{32,40},... | collective-permute-start | bytes 884744 | tf_op jit(solution)/shard_map/ppermute | solution.py:64
  118.5 17.3 %collective-permute-start.16 = (bf16[768,512]{1,0:T(8,128)(2,1)}, bf16[768,512]{1,0:T(8,128)(2,1)S(1)}, u32[]{:S(2)}, u32[]{:S(2)}) collective-permute-start(bf16[768,512]{1,0:T(8,128)(2,1)} %get-tuple-element.100), channel_id=1, source_target_pairs={{0,96},{4,100},{8,104},{12,108},{16,112},{20,116},{24,120},{28,124... | collective-permute-start | bytes 2359304 | tf_op jit(solution)/shard_map/ppermute | solution.py:64
  118.6 17.3 %collective-permute-start.17 = (bf16[768,512]{1,0:T(8,128)(2,1)}, bf16[768,512]{1,0:T(8,128)(2,1)S(1)}, u32[]{:S(2)}, u32[]{:S(2)}) collective-permute-start(bf16[768,512]{1,0:T(8,128)(2,1)} %get-tuple-element.102), channel_id=1, source_target_pairs={{0,32},{4,36},{8,40},{12,44},{16,48},{20,52},{24,56},{28,60},{32,6... | collective-permute-start | bytes 2359304 | tf_op jit(solution)/shard_map/ppermute | solution.py:64
  120.0 17.1 %collective-permute-start.13 = (bf16[784,512]{1,0:T(8,128)(2,1)}, bf16[784,512]{1,0:T(8,128)(2,1)S(1)}, u32[]{:S(2)}, u32[]{:S(2)}) collective-permute-start(bf16[784,512]{1,0:T(8,128)(2,1)} %get-tuple-element.96), channel_id=1, source_target_pairs={{0,24},{4,28},{8,0},{12,4},{16,8},{20,12},{24,16},{28,20},{32,56},... | collective-permute-start | bytes 2408456 | tf_op jit(solution)/shard_map/ppermute | solution.py:64
  121.0 16.1 %collective-permute-start.14 = (bf16[784,512]{1,0:T(8,128)(2,1)}, bf16[784,512]{1,0:T(8,128)(2,1)S(1)}, u32[]{:S(2)}, u32[]{:S(2)}) collective-permute-start(bf16[784,512]{1,0:T(8,128)(2,1)} %get-tuple-element.97), channel_id=1, source_target_pairs={{0,16},{4,20},{8,24},{12,28},{16,0},{20,4},{24,8},{28,12},{32,48},... | collective-permute-start | bytes 2408456 | tf_op jit(solution)/shard_map/ppermute | solution.py:64
  122.3 37.5 %collective-permute-start.15 = (bf16[784,512]{1,0:T(8,128)(2,1)}, bf16[784,512]{1,0:T(8,128)(2,1)}, u32[]{:S(2)}, u32[]{:S(2)}) collective-permute-start(bf16[784,512]{1,0:T(8,128)(2,1)} %get-tuple-element.98), channel_id=1, source_target_pairs={{0,8},{4,12},{8,16},{12,20},{16,24},{20,28},{24,0},{28,4},{32,40},... | collective-permute-start | bytes 2408456 | tf_op jit(solution)/shard_map/ppermute | solution.py:64
  137.1 22.7 %collective-permute-start.18 = (bf16[768,512]{1,0:T(8,128)(2,1)}, bf16[768,512]{1,0:T(8,128)(2,1)S(1)}, u32[]{:S(2)}, u32[]{:S(2)}) collective-permute-start(bf16[768,512]{1,0:T(8,128)(2,1)} %after.7), channel_id=1, source_target_pairs={{0,64},{4,68},{8,72},{12,76},{16,80},{20,84},{24,88},{28,92},{32,9... | collective-permute-start | bytes 2359304 | tf_op jit(solution)/shard_map/ppermute | solution.py:64
  137.1 22.7 %copy-start.48 = (bf16[784,512]{1,0:T(8,128)(2,1)}, bf16[784,512]{1,0:T(8,128)(2,1)S(1)}, u32[]{:S(2)}) copy-start(bf16[784,512]{1,0:T(8,128)(2,1)S(1)} %collective-permute-done.13.refs_1_) | copy-start | bytes 2408452
  137.1 22.7 %copy-start.49 = (bf16[784,512]{1,0:T(8,128)(2,1)}, bf16[784,512]{1,0:T(8,128)(2,1)S(1)}, u32[]{:S(2)}) copy-start(bf16[784,512]{1,0:T(8,128)(2,1)S(1)} %collective-permute-done.14.refs_2_) | copy-start | bytes 2408452
  199.4 22.0 %collective-permute-start.19 = (bf16[784,512]{1,0:T(8,128)(2,1)}, bf16[784,512]{1,0:T(8,128)(2,1)S(1)}, u32[]{:S(2)}, u32[]{:S(2)}) collective-permute-start(bf16[784,512]{1,0:T(8,128)(2,1)} %get-tuple-element.107), channel_id=1, source_target_pairs={{0,24},{4,28},{8,0},{12,4},{16,8},{20,12},{24,16},{28,20},{32,56},... | collective-permute-start | bytes 2408456 | tf_op jit(solution)/shard_map/ppermute | solution.py:64
  199.5 21.9 %collective-permute-start.20 = (bf16[784,512]{1,0:T(8,128)(2,1)}, bf16[784,512]{1,0:T(8,128)(2,1)S(1)}, u32[]{:S(2)}, u32[]{:S(2)}) collective-permute-start(bf16[784,512]{1,0:T(8,128)(2,1)} %get-tuple-element.114), channel_id=1, source_target_pairs={{0,8},{4,12},{8,16},{12,20},{16,24},{20,28},{24,0},{28,4},{32,40},... | collective-permute-start | bytes 2408456 | tf_op jit(solution)/shard_map/ppermute | solution.py:64
  201.0 18.2 %collective-permute-start.21 = (bf16[768,512]{1,0:T(8,128)(2,1)}, bf16[768,512]{1,0:T(8,128)(2,1)S(1)}, u32[]{:S(2)}, u32[]{:S(2)}) collective-permute-start(bf16[768,512]{1,0:T(8,128)(2,1)} %get-tuple-element.115), channel_id=1, source_target_pairs={{0,96},{4,100},{8,104},{12,108},{16,112},{20,116},{24,120},{28,124... | collective-permute-start | bytes 2359304 | tf_op jit(solution)/shard_map/ppermute | solution.py:64
  202.3 19.1 %collective-permute-start.22 = (bf16[768,512]{1,0:T(8,128)(2,1)}, bf16[768,512]{1,0:T(8,128)(2,1)S(1)}, u32[]{:S(2)}, u32[]{:S(2)}) collective-permute-start(bf16[768,512]{1,0:T(8,128)(2,1)} %get-tuple-element.116), channel_id=1, source_target_pairs={{0,32},{4,36},{8,40},{12,44},{16,48},{20,52},{24,56},{28,60},{32,6... | collective-permute-start | bytes 2359304 | tf_op jit(solution)/shard_map/ppermute | solution.py:64
  223.2 7.8 %collective-permute-start.25 = (bf16[1536,1024]{1,0:T(8,128)(2,1)}, bf16[1536,1024]{1,0:T(8,128)(2,1)S(1)}, u32[]{:S(2)}, u32[]{:S(2)}) collective-permute-start(bf16[1536,1024]{1,0:T(8,128)(2,1)} %get-tuple-element.120), channel_id=1, source_target_pairs={{0,4},{4,0},{8,12},{12,8},{16,20},{20,16},{24,28},{28,24},{32,36},... | collective-permute-start | bytes 9437192 | tf_op jit(solution)/shard_map/ppermute | solution.py:64
  225.4 22.1 %collective-permute-start.23 = (bf16[784,512]{1,0:T(8,128)(2,1)}, bf16[784,512]{1,0:T(8,128)(2,1)S(1)}, u32[]{:S(2)}, u32[]{:S(2)}) collective-permute-start(bf16[784,512]{1,0:T(8,128)(2,1)} %get-tuple-element.117), channel_id=1, source_target_pairs={{0,16},{4,20},{8,24},{12,28},{16,0},{20,4},{24,8},{28,12},{32,48},... | collective-permute-start | bytes 2408456 | tf_op jit(solution)/shard_map/ppermute | solution.py:64
  226.8 20.7 %collective-permute-start.24 = (bf16[768,512]{1,0:T(8,128)(2,1)}, bf16[768,512]{1,0:T(8,128)(2,1)S(1)}, u32[]{:S(2)}, u32[]{:S(2)}) collective-permute-start(bf16[768,512]{1,0:T(8,128)(2,1)} %get-tuple-element.119), channel_id=1, source_target_pairs={{0,64},{4,68},{8,72},{12,76},{16,80},{20,84},{24,88},{28,92},{32,9... | collective-permute-start | bytes 2359304 | tf_op jit(solution)/shard_map/ppermute | solution.py:64
  254.4 7.0 %collective-permute-start.29 = (bf16[256,512]{1,0:T(8,128)(2,1)}, bf16[256,512]{1,0:T(8,128)(2,1)S(1)}, u32[]{:S(2)}, u32[]{:S(2)}) collective-permute-start(bf16[256,512]{1,0:T(8,128)(2,1)} %get-tuple-element.126), channel_id=1, source_target_pairs={{0,24},{4,28},{8,0},{12,4},{16,8},{20,12},{24,16},{28,20},{32,56},... | collective-permute-start | bytes 786440 | tf_op jit(solution)/shard_map/ppermute | solution.py:64
  255.4 14.5 %collective-permute-start.26 = (bf16[272,512]{1,0:T(8,128)(2,1)}, bf16[272,512]{1,0:T(8,128)(2,1)S(1)}, u32[]{:S(2)}, u32[]{:S(2)}) collective-permute-start(bf16[272,512]{1,0:T(8,128)(2,1)} %get-tuple-element.122), channel_id=1, source_target_pairs={{0,96},{4,100},{8,104},{12,108},{16,112},{20,116},{24,120},{28,124... | collective-permute-start | bytes 835592 | tf_op jit(solution)/shard_map/ppermute | solution.py:64
  255.5 14.5 %collective-permute-start.27 = (bf16[272,512]{1,0:T(8,128)(2,1)}, bf16[272,512]{1,0:T(8,128)(2,1)S(1)}, u32[]{:S(2)}, u32[]{:S(2)}) collective-permute-start(bf16[272,512]{1,0:T(8,128)(2,1)} %get-tuple-element.123), channel_id=1, source_target_pairs={{0,64},{4,68},{8,72},{12,76},{16,80},{20,84},{24,88},{28,92},{32,9... | collective-permute-start | bytes 835592 | tf_op jit(solution)/shard_map/ppermute | solution.py:64
  256.2 15.7 %collective-permute-start.28 = (bf16[272,512]{1,0:T(8,128)(2,1)}, bf16[272,512]{1,0:T(8,128)(2,1)S(1)}, u32[]{:S(2)}, u32[]{:S(2)}) collective-permute-start(bf16[272,512]{1,0:T(8,128)(2,1)} %get-tuple-element.124), channel_id=1, source_target_pairs={{0,32},{4,36},{8,40},{12,44},{16,48},{20,52},{24,56},{28,60},{32,6... | collective-permute-start | bytes 835592 | tf_op jit(solution)/shard_map/ppermute | solution.py:64
  256.9 7.6 %collective-permute-start.30 = (bf16[256,512]{1,0:T(8,128)(2,1)}, bf16[256,512]{1,0:T(8,128)(2,1)S(1)}, u32[]{:S(2)}, u32[]{:S(2)}) collective-permute-start(bf16[256,512]{1,0:T(8,128)(2,1)} %get-tuple-element.127), channel_id=1, source_target_pairs={{0,16},{4,20},{8,24},{12,28},{16,0},{20,4},{24,8},{28,12},{32,48},... | collective-permute-start | bytes 786440 | tf_op jit(solution)/shard_map/ppermute | solution.py:64
  261.4 8.5 %collective-permute-start.31 = (bf16[256,512]{1,0:T(8,128)(2,1)}, bf16[256,512]{1,0:T(8,128)(2,1)S(1)}, u32[]{:S(2)}, u32[]{:S(2)}) collective-permute-start(bf16[256,512]{1,0:T(8,128)(2,1)} %get-tuple-element.128), channel_id=1, source_target_pairs={{0,8},{4,12},{8,16},{12,20},{16,24},{20,28},{24,0},{28,4},{32,40},... | collective-permute-start | bytes 786440 | tf_op jit(solution)/shard_map/ppermute | solution.py:64
  272.5 100.1 %all-to-all-start = ((bf16[16,192,1024]{2,1,0:T(8,128)(2,1)}), bf16[16,192,1024]{2,1,0:T(8,128)(2,1)}, u32[]{:S(2)}, u32[]{:S(2)}) async-start(bf16[16,192,1024]{2,1,0:T(8,128)(2,1)} %after.9), calls=%async_computation | async-start | bytes 12582912 | tf_op jit(solution)/shard_map/all_to_all | solution.py:1007
  279.5 123.6 %all-gather.4.cloned.1.call-start = ((), (), s32[]{:S(2)}) async-start(), calls=%async_computation.3 | async-start | bytes 3932160 | tf_op jit(solution)/shard_map/all_gather | solution.py:1013
  285.2 14.3 %collective-permute-start.32 = (bf16[256,1024]{1,0:T(8,128)(2,1)}, bf16[256,1024]{1,0:T(8,128)(2,1)S(1)}, u32[]{:S(2)}, u32[]{:S(2)}) collective-permute-start(bf16[256,1024]{1,0:T(8,128)(2,1)} %get-tuple-element.134.refs_1_), channel_id=1, source_target_pairs={{0,3},{1,0},{2,1},{3,2},{4,7},{5,4},{6,5},{7,6},{8,11},{9,8},{10,9... | collective-permute-start | bytes 1572872 | tf_op jit(solution)/shard_map/ppermute | solution.py:70
  285.2 16.1 %collective-permute-start.34 = (bf16[256,1024]{1,0:T(8,128)(2,1)}, bf16[256,1024]{1,0:T(8,128)(2,1)S(1)}, u32[]{:S(2)}, u32[]{:S(2)}) collective-permute-start(bf16[256,1024]{1,0:T(8,128)(2,1)} %get-tuple-element.134.refs_1_), channel_id=1, source_target_pairs={{0,1},{1,2},{2,3},{3,0},{4,5},{5,6},{6,7},{7,4},{8,9},{9,10},{10,1... | collective-permute-start | bytes 1572872 | tf_op jit(solution)/shard_map/ppermute | solution.py:70
  299.5 13.3 %collective-permute-start.33 = (bf16[128,1024]{1,0:T(8,128)(2,1)S(1)}, bf16[128,1024]{1,0:T(8,128)(2,1)S(1)}, u32[]{:S(2)}, u32[]{:S(2)}) collective-permute-start(bf16[128,1024]{1,0:T(8,128)(2,1)S(1)} %slice.40), channel_id=1, source_target_pairs={{0,3},{1,0},{2,1},{3,2},{4,7},{5,4},{6,5},{7,6},{8,11},{9,8},{10,9... | collective-permute-start | bytes 786440 | tf_op jit(solution)/shard_map/ppermute | solution.py:70
  301.3 11.5 %collective-permute-start.35 = (bf16[128,1024]{1,0:T(8,128)(2,1)S(1)}, bf16[128,1024]{1,0:T(8,128)(2,1)S(1)}, u32[]{:S(2)}, u32[]{:S(2)}) collective-permute-start(bf16[128,1024]{1,0:T(8,128)(2,1)S(1)} %slice.41), channel_id=1, source_target_pairs={{0,1},{1,2},{2,3},{3,0},{4,5},{5,6},{6,7},{7,4},{8,9},{9,10},{10,1... | collective-permute-start | bytes 786440 | tf_op jit(solution)/shard_map/ppermute | solution.py:70
  302.4 7.5 %collective-permute-start.36 = (f32[40,1024]{1,0:T(8,128)}, f32[40,1024]{1,0:T(8,128)S(1)}, u32[]{:S(2)}, u32[]{:S(2)}) collective-permute-start(f32[40,1024]{1,0:T(8,128)} %get-tuple-element.136.refs_4_), channel_id=1, source_target_pairs={{0,1},{1,2},{2,3},{3,0},{4,5},{5,6},{6,7},{7,4},{8,9},{9,10},{10,1... | collective-permute-start | bytes 491528 | tf_op jit(solution)/shard_map/ppermute | solution.py:70
  303.8 7.9 %collective-permute-start.37 = (f32[40,1024]{1,0:T(8,128)}, f32[40,1024]{1,0:T(8,128)S(1)}, u32[]{:S(2)}, u32[]{:S(2)}) collective-permute-start(f32[40,1024]{1,0:T(8,128)} %get-tuple-element.136.refs_4_), channel_id=1, source_target_pairs={{0,2},{1,3},{2,0},{3,1},{4,6},{5,7},{6,4},{7,5},{8,10},{9,11},{10,... | collective-permute-start | bytes 491528 | tf_op jit(solution)/shard_map/ppermute | solution.py:70
  304.8 8.0 %collective-permute-start.38 = (f32[40,1024]{1,0:T(8,128)}, f32[40,1024]{1,0:T(8,128)S(1)}, u32[]{:S(2)}, u32[]{:S(2)}) collective-permute-start(f32[40,1024]{1,0:T(8,128)} %get-tuple-element.136.refs_4_), channel_id=1, source_target_pairs={{0,3},{1,0},{2,1},{3,2},{4,7},{5,4},{6,5},{7,6},{8,11},{9,8},{10,9... | collective-permute-start | bytes 491528 | tf_op jit(solution)/shard_map/ppermute | solution.py:70
  339.0 15.0 %collective-permute-start.39 = (bf16[832,512]{1,0:T(8,128)(2,1)}, bf16[832,512]{1,0:T(8,128)(2,1)S(1)}, u32[]{:S(2)}, u32[]{:S(2)}) collective-permute-start(bf16[832,512]{1,0:T(8,128)(2,1)} %get-tuple-element.146), channel_id=1, source_target_pairs={{0,4},{4,0},{8,12},{12,8},{16,20},{20,16},{24,28},{28,24},{32,36},... | collective-permute-start | bytes 2555912 | tf_op jit(solution)/shard_map/ppermute | solution.py:64
  343.1 1.9 collective-permute-start.40
  345.0 4.1 collective-permute-start.41
  347.6 5.3 %collective-permute-start.42 = (f32[8,1024]{1,0:T(8,128)S(1)}, f32[8,1024]{1,0:T(8,128)S(1)}, u32[]{:S(2)}, u32[]{:S(2)}) collective-permute-start(f32[8,1024]{1,0:T(8,128)S(1)} %add.34.refs_3_), channel_id=1, source_target_pairs={{0,2},{1,3},{2,0},{3,1},{4,6},{5,7},{6,4},{7,5},{8,10},{9,11},{10,... | collective-permute-start | bytes 98312 | tf_op jit(solution)/shard_map/ppermute | solution.py:70
  348.4 5.6 %collective-permute-start.43 = (f32[8,1024]{1,0:T(8,128)S(1)}, f32[8,1024]{1,0:T(8,128)S(1)}, u32[]{:S(2)}, u32[]{:S(2)}) collective-permute-start(f32[8,1024]{1,0:T(8,128)S(1)} %add.34.refs_3_), channel_id=1, source_target_pairs={{0,3},{1,0},{2,1},{3,2},{4,7},{5,4},{6,5},{7,6},{8,11},{9,8},{10,9... | collective-permute-start | bytes 98312 | tf_op jit(solution)/shard_map/ppermute | solution.py:70
  358.9 9.4 %collective-permute-start.46 = (bf16[128,1024]{1,0:T(8,128)(2,1)S(1)}, bf16[128,1024]{1,0:T(8,128)(2,1)S(1)}, u32[]{:S(2)}, u32[]{:S(2)}) collective-permute-start(bf16[128,1024]{1,0:T(8,128)(2,1)S(1)} %get-tuple-element.165), channel_id=1, source_target_pairs={{0,3},{1,0},{2,1},{3,2},{4,7},{5,4},{6,5},{7,6},{8,11},{9,8},{10,9... | collective-permute-start | bytes 786440 | tf_op jit(solution)/shard_map/ppermute | solution.py:70
  358.9 11.6 %collective-permute-start.44 = (bf16[128,1024]{1,0:T(8,128)(2,1)S(1)}, bf16[128,1024]{1,0:T(8,128)(2,1)S(1)}, u32[]{:S(2)}, u32[]{:S(2)}) collective-permute-start(bf16[128,1024]{1,0:T(8,128)(2,1)S(1)} %get-tuple-element.166), channel_id=1, source_target_pairs={{0,1},{1,2},{2,3},{3,0},{4,5},{5,6},{6,7},{7,4},{8,9},{9,10},{10,1... | collective-permute-start | bytes 786440 | tf_op jit(solution)/shard_map/ppermute | solution.py:70
  361.6 17.3 %collective-permute-start.48 = (bf16[208,512]{1,0:T(8,128)(2,1)}, bf16[208,512]{1,0:T(8,128)(2,1)S(1)}, u32[]{:S(2)}, u32[]{:S(2)}) collective-permute-start(bf16[208,512]{1,0:T(8,128)(2,1)} %get-tuple-element.154), channel_id=1, source_target_pairs={{0,8},{4,12},{8,16},{12,20},{16,24},{20,28},{24,0},{28,4},{32,40},... | collective-permute-start | bytes 638984 | tf_op jit(solution)/shard_map/ppermute | solution.py:64
  362.7 18.2 %collective-permute-start.49 = (bf16[208,512]{1,0:T(8,128)(2,1)}, bf16[208,512]{1,0:T(8,128)(2,1)S(1)}, u32[]{:S(2)}, u32[]{:S(2)}) collective-permute-start(bf16[208,512]{1,0:T(8,128)(2,1)} %get-tuple-element.155), channel_id=1, source_target_pairs={{0,16},{4,20},{8,24},{12,28},{16,0},{20,4},{24,8},{28,12},{32,48},... | collective-permute-start | bytes 638984 | tf_op jit(solution)/shard_map/ppermute | solution.py:64
  365.1 15.9 %collective-permute-start.50 = (bf16[208,512]{1,0:T(8,128)(2,1)S(1)}, bf16[208,512]{1,0:T(8,128)(2,1)S(1)}, u32[]{:S(2)}, u32[]{:S(2)}) collective-permute-start(bf16[208,512]{1,0:T(8,128)(2,1)S(1)} %copy-done.61), channel_id=1, source_target_pairs={{0,24},{4,28},{8,0},{12,4},{16,8},{20,12},{24,16},{28,20},{32,56},... | collective-permute-start | bytes 638984 | tf_op jit(solution)/shard_map/ppermute | solution.py:64
  369.5 39.0 %collective-permute-start.47 = (bf16[256,1024]{1,0:T(8,128)(2,1)S(1)}, bf16[256,1024]{1,0:T(8,128)(2,1)S(1)}, u32[]{:S(2)}, u32[]{:S(2)}) collective-permute-start(bf16[256,1024]{1,0:T(8,128)(2,1)S(1)} %pad_maximum_fusion.4), channel_id=1, source_target_pairs={{0,3},{1,0},{2,1},{3,2},{4,7},{5,4},{6,5},{7,6},{8,11},{9,8},{10,9... | collective-permute-start | bytes 1572872 | tf_op jit(solution)/shard_map/ppermute | solution.py:70
  370.7 37.8 %collective-permute-start.45 = (bf16[256,1024]{1,0:T(8,128)(2,1)S(1)}, bf16[256,1024]{1,0:T(8,128)(2,1)S(1)}, u32[]{:S(2)}, u32[]{:S(2)}) collective-permute-start(bf16[256,1024]{1,0:T(8,128)(2,1)S(1)} %pad_maximum_fusion.3), channel_id=1, source_target_pairs={{0,1},{1,2},{2,3},{3,0},{4,5},{5,6},{6,7},{7,4},{8,9},{9,10},{10,1... | collective-permute-start | bytes 1572872 | tf_op jit(solution)/shard_map/ppermute | solution.py:70
  384.4 7.2 %collective-permute-start.51 = (bf16[208,512]{1,0:T(8,128)(2,1)}, bf16[208,512]{1,0:T(8,128)(2,1)S(1)}, u32[]{:S(2)}, u32[]{:S(2)}) collective-permute-start(bf16[208,512]{1,0:T(8,128)(2,1)} %shard_map.223.refs_1_), channel_id=1, source_target_pairs={{0,32},{4,36},{8,40},{12,44},{16,48},{20,52},{24,56},{28,60},{32,6... | collective-permute-start | bytes 638984 | tf_op jit(solution)/shard_map/ppermute | solution.py:64
  384.4 10.3 %collective-permute-start.52 = (bf16[208,512]{1,0:T(8,128)(2,1)}, bf16[208,512]{1,0:T(8,128)(2,1)S(1)}, u32[]{:S(2)}, u32[]{:S(2)}) collective-permute-start(bf16[208,512]{1,0:T(8,128)(2,1)} %shard_map.223.refs_1_), channel_id=1, source_target_pairs={{0,64},{4,68},{8,72},{12,76},{16,80},{20,84},{24,88},{28,92},{32,9... | collective-permute-start | bytes 638984 | tf_op jit(solution)/shard_map/ppermute | solution.py:64
  386.9 9.2 %collective-permute-start.53 = (bf16[208,512]{1,0:T(8,128)(2,1)}, bf16[208,512]{1,0:T(8,128)(2,1)S(1)}, u32[]{:S(2)}, u32[]{:S(2)}) collective-permute-start(bf16[208,512]{1,0:T(8,128)(2,1)} %shard_map.223.refs_1_), channel_id=1, source_target_pairs={{0,96},{4,100},{8,104},{12,108},{16,112},{20,116},{24,120},{28,124... | collective-permute-start | bytes 638984 | tf_op jit(solution)/shard_map/ppermute | solution.py:64
  398.9 12.6 %collective-permute-start.54 = (bf16[208,512]{1,0:T(8,128)(2,1)}, bf16[208,512]{1,0:T(8,128)(2,1)S(1)}, u32[]{:S(2)}, u32[]{:S(2)}) collective-permute-start(bf16[208,512]{1,0:T(8,128)(2,1)} %shard_map.224.refs_1_), channel_id=1, source_target_pairs={{0,24},{4,28},{8,0},{12,4},{16,8},{20,12},{24,16},{28,20},{32,56},... | collective-permute-start | bytes 638984 | tf_op jit(solution)/shard_map/ppermute | solution.py:64
  402.5 9.0 %collective-permute-start.55 = (bf16[208,512]{1,0:T(8,128)(2,1)}, bf16[208,512]{1,0:T(8,128)(2,1)S(1)}, u32[]{:S(2)}, u32[]{:S(2)}) collective-permute-start(bf16[208,512]{1,0:T(8,128)(2,1)} %shard_map.224.refs_1_), channel_id=1, source_target_pairs={{0,16},{4,20},{8,24},{12,28},{16,0},{20,4},{24,8},{28,12},{32,48},... | collective-permute-start | bytes 638984 | tf_op jit(solution)/shard_map/ppermute | solution.py:64
  402.5 12.8 %collective-permute-start.56 = (bf16[208,512]{1,0:T(8,128)(2,1)}, bf16[208,512]{1,0:T(8,128)(2,1)S(1)}, u32[]{:S(2)}, u32[]{:S(2)}) collective-permute-start(bf16[208,512]{1,0:T(8,128)(2,1)} %shard_map.224.refs_1_), channel_id=1, source_target_pairs={{0,8},{4,12},{8,16},{12,20},{16,24},{20,28},{24,0},{28,4},{32,40},... | collective-permute-start | bytes 638984 | tf_op jit(solution)/shard_map/ppermute | solution.py:64
  418.2 4.3 collective-permute-start.57
  (60 other events, 226.6 us)
Sparse Core Ops, SparseCore 0:
  10.2 72.9 all-gather.5
  244.2 36.4 reduce-scatter.1
  318.0 45.4 all-gather.3

commit v4 on v3

--- a/solution.py
+++ b/solution.py
@@ -90,14 +90,26 @@
     return rows, after_me, across, before_me
 
 
-def scatter_tp(pieces):
-    half = pieces[2].shape[0] // 2
-    first, rest = push_tp(pieces[2][:half], 1), push_tp(pieces[2][half:], -1)
-    ahead = (pieces[1][:half].astype(F32) + first.astype(F32)).astype(BF16)
-    behind = (pieces[3][half:].astype(F32) + rest.astype(F32)).astype(BF16)
-    ahead = jnp.concatenate([ahead, pieces[1][half:]], axis=0)
-    behind = jnp.concatenate([pieces[3][:half], behind], axis=0)
-    return (pieces[0], push_tp(ahead, 1), push_tp(behind, -1)), (first, rest)
+def add_halves_kernel(one, three, first, rest, ahead, behind):
+    half = first.shape[0]
+    ahead[0:half, :] = (one[0:half, :].astype(F32) + first[...].astype(F32)).astype(BF16)
+    ahead[half:, :] = one[half:, :]
+    behind[0:half, :] = three[0:half, :]
+    behind[half:, :] = (three[half:, :].astype(F32) + rest[...].astype(F32)).astype(BF16)
+
+
+def scatter_tp(own, one, two, two_rest, three):
+    first, rest = push_tp(two, 1), push_tp(two_rest, -1)
+    ahead, behind = pl.pallas_call(
+        add_halves_kernel,
+        out_shape=[jax.ShapeDtypeStruct(one.shape, BF16)] * 2,
+        in_specs=[WHOLE] * 4,
+        out_specs=[WHOLE] * 2,
+        compiler_params=params(),
+        cost_estimate=NO_COST,
+        name="add_halves",
+    )(one, three, first, rest)
+    return (own, push_tp(ahead, 1), push_tp(behind, -1)), (first, rest)
 
 
 def ignoring(kernel, first, count):
@@ -241,7 +253,7 @@
     )(x, *branches, gain, wr, chosen, table, *others)
 
 
-PIECE = 8 * CAP
+PIECE = RING * CAP
 EXTRA = 16
 
 
@@ -273,8 +285,7 @@
         filled = dot(line_matrix(slots, d), rows[d][0:ROWS, :]).astype(BF16)
         for p in range(RING):
             for e in range(2):
-                at = (e * 4 + d) * CAP
-                pieces[p][at : at + CAP, :] = filled[(p * 2 + e) * CAP : (p * 2 + e + 1) * CAP, :]
+                pieces[e * 4 + p][d * CAP : (d + 1) * CAP, :] = filled[(p * 2 + e) * CAP : (p * 2 + e + 1) * CAP, :]
 
 
 def pick_rows(spot, half, blocks, first, table, picked):
@@ -287,32 +298,33 @@
 
 
 def dispatch_kernel(spot, *refs):
-    blocks, pieces, slots, (table, gates, picked) = refs[:8], refs[8:16], refs[16:18], refs[18:]
+    blocks, pieces, slots, (table, gates, picked) = refs[:8], (refs[8:16], refs[16:24]), refs[24:26], refs[26:]
     pick_rows(spot, 0, blocks[:4], ROWS, table, gates)
     for half in range(2):
-        mine = slice(4 * half, 4 * half + 4)
-        pick_rows(spot, half, blocks[mine], ROWS + EXPERTS * (1 - half), table, picked)
+        mine = blocks[4 * half : 4 * half + 4]
+        pick_rows(spot, half, mine, ROWS + EXPERTS * (1 - half), table, picked)
         slots[half][...] = picked[:, :ROWS]
-        fill_pieces(slots[half], blocks[mine], pieces[mine])
+        fill_pieces(slots[half], mine, pieces[half])
         if half == 0:
             for p in range(RING):
-                at = slice(p * 8, (p + 1) * 8)
-                pieces[p][PIECE:, :] = jnp.concatenate([gates[at, :], picked[at, :]], axis=0).astype(BF16)
-
-
-def combine_kernel(with_extra, slots_a, slots_b, *refs):
+                for e in range(2):
+                    at = slice(p * 8 + e * 4, p * 8 + e * 4 + 4)
+                    extra = jnp.concatenate([gates[at, :], picked[at, :], jnp.zeros((8, HALF), F32)], axis=0)
+                    pieces[0][e * 4 + p][PIECE:, :] = extra.astype(BF16)
+
+
+def combine_kernel(slots_a, slots_b, *refs):
     everyone = range(RING)
     for half, slots in enumerate((slots_a, slots_b)):
-        pieces, rows = refs[4 * half : 4 * half + 4], refs[8 + 4 * half : 12 + 4 * half]
+        pieces, rows = refs[8 * half : 8 * half + 8], refs[16 + 4 * half : 20 + 4 * half]
         for d in everyone:
-            filled = jnp.concatenate(
-                [pieces[p][(e * 4 + d) * CAP : (e * 4 + d + 1) * CAP, :] for p in everyone for e in range(2)], axis=0
-            )
+            filled = [pieces[e * 4 + p][d * CAP : (d + 1) * CAP, :] for p in everyone for e in range(2)]
+            filled = jnp.concatenate(filled, axis=0)
             rows[d][0:ROWS, :] = dot_tn(line_matrix(slots, d), filled).astype(BF16)
-        if half == 0 and with_extra:
-            tables = [pieces[p][PIECE:, :].astype(F32) for p in everyone]
+        if half == 0:
+            tables = [pieces[i][PIECE:, :].astype(F32) for i in range(8)]
             for d in everyone:
-                picked = [tables[p][e * 4 + d : e * 4 + d + 1, :] for p in everyone for e in range(2)]
+                picked = [tables[e * 4 + p][d : d + 1, :] for p in everyone for e in range(2)]
                 extra = jnp.concatenate(picked + [jnp.zeros((8, HALF), F32)], axis=0)
                 rows[d][ROWS:, :] = extra.astype(BF16)
 
@@ -332,46 +344,43 @@
 def dispatch(spot, half_a, half_b):
     made = pl.pallas_call(
         dispatch_kernel,
-        out_shape=[shape_of(PIECE + EXTRA)] * RING
-        + [shape_of(PIECE)] * RING
+        out_shape=[shape_of(PIECE + EXTRA)] * 8
+        + [shape_of(PIECE)] * 8
         + [jax.ShapeDtypeStruct((EXPERTS, ROWS), F32)] * 2,
         in_specs=[SCALARS] + [WHOLE] * 8,
-        out_specs=[WHOLE] * 10,
+        out_specs=[WHOLE] * 18,
         scratch_shapes=[TABLE] * 3,
         compiler_params=params(),
         cost_estimate=SLOT_COST,
         name="dispatch",
     )(spot, *spread_rows(half_a, half_b))
-    return exchange(made[:8]), made[8], made[9]
-
-
-def exchange(pieces):
-    got = exchange_near(pieces)
-    got[2] = push(pieces[2], 0, 2, 0)
-    (last,) = after((pieces[6],), got[5], got[7])
-    got[6] = push(last, 2, 0, 0)
-    return got
-
-
-def exchange_near(pieces):
-    got = [pieces[0], None, None, None, pieces[4], None, None, None]
-    got[3], got[1] = push(pieces[1], 0, 1, 0), push(pieces[3], 0, 3, 0)
-    got[7], got[5] = push(pieces[5], 1, 0, 0), push(pieces[7], 3, 0, 0)
-    return got
-
-
-def exchange_far(pieces, got, with_them, *others):
-    held = after((pieces[2], pieces[6], *with_them), got[1], got[3], got[5], got[7], *others)
-    got[2], got[6] = push(held[0], 0, 2, 0), push(held[1], 2, 0, 0)
-    return held[2:]
-
-
-def combine(slots_a, slots_b, pieces, with_extra, *others):
-    rows_a = shape_of(ROWS + EXTRA) if with_extra else shape_of(ROWS)
-    return pl.pallas_call(
-        ignoring(lambda *refs: combine_kernel(with_extra, *refs), 10, len(others)),
-        out_shape=[rows_a] * RING + [shape_of(ROWS)] * RING,
-        in_specs=[WHOLE] * 10 + [ANYWHERE] * len(others),
+    return (made[:8], made[8:16]), made[16], made[17]
+
+
+class Pieces:
+    def __init__(self, half_a, half_b):
+        self.made = list(half_a), list(half_b)
+        self.got = [half_a[0], None, None, None], [half_b[0], None, None, None]
+
+    def send(self, half, p, held=None):
+        piece = self.made[half][p] if held is None else held
+        self.got[half][-p % RING] = push(piece, 0, p, 0) if half == 0 else push(piece, p, 0, 0)
+        return self.got[half][-p % RING]
+
+    def send_near(self, held=(None,) * 4):
+        places = (0, 1), (0, 3), (1, 1), (1, 3)
+        return [self.send(half, p, piece) for (half, p), piece in zip(places, held)]
+
+    def near(self):
+        return self.made[0][1], self.made[0][3], self.made[1][1], self.made[1][3]
+
+
+def combine(slots_a, slots_b, first, second, *others):
+    pieces = [*first.got[0], *second.got[0], *first.got[1], *second.got[1]]
+    return pl.pallas_call(
+        ignoring(combine_kernel, 18, len(others)),
+        out_shape=[shape_of(ROWS + EXTRA)] * RING + [shape_of(ROWS)] * RING,
+        in_specs=[WHOLE] * 18 + [ANYWHERE] * len(others),
         out_specs=[WHOLE] * 8,
         compiler_params=params(),
         cost_estimate=pl.CostEstimate(flops=60_000_000_000, bytes_accessed=0, transcendentals=0),
@@ -434,85 +443,81 @@
 SAME_CORE = [list(range(core, EXPERTS, 2)) for core in range(2)]
 
 
-STEPS = 8
+STEPS = RING
 STEP_ROWS = RING * CAP
 
 
-def expert_kernel(spot, *refs):
-    ra, rb, cot, weights = refs[:4], refs[4:8], refs[8], refs[9:11]
-    qa, qb, moe, (disp_out, dgu_out, inner_out, dex_out) = refs[11:15], refs[15:19], refs[19], refs[20:24]
-    wgu, wd, rows_in, cot_in, gates_in, back_out, moe_out, dgate_out, extra_out = refs[24:33]
-    weight_sem, in_sem, out_sem, extra_sem = refs[33:]
+def expert_kernel(e, spot, *refs):
+    ra, rb, cot, weights = refs[:4], refs[4:8], refs[8], refs[9]
+    refs = refs[10 + e :]
+    qa, qb, moe, (disp_out, dgu_out, inner_out, dex_out) = refs[:4], refs[4:8], refs[8], refs[9:13]
+    wgu, wd, rows_in, cot_in, extra_in, back_out, moe_out, extra_out, weight_sem, in_sem, out_sem = refs[13:]
     step = pl.program_id(0)
-
-    def loads(e):
-        up, down = weights[e].at[pl.ds(0, WIDTH)], weights[e].at[pl.ds(WIDTH, HALF)]
-        return [
-            pltpu.make_async_copy(up, wgu.at[e], weight_sem.at[e, 0]),
-            pltpu.make_async_copy(down, wd.at[e], weight_sem.at[e, 1]),
+    loads = [
+        pltpu.make_async_copy(weights.at[pl.ds(0, WIDTH)], wgu, weight_sem.at[0]),
+        pltpu.make_async_copy(weights.at[pl.ds(WIDTH, HALF)], wd, weight_sem.at[1]),
+    ]
+
+    def places(dx, half_a, half_b, halves, extra):
+        slot = dx % 2
+        ends = [
+            (half_a[dx].at[pl.ds(0, PIECE)], halves.at[slot, :, pl.ds(0, HALF)]),
+            (half_a[dx].at[pl.ds(PIECE, EXTRA)], extra.at[slot]),
         ]
-
-    def places(j, half_a, half_b, far, whole, halves):
-        slot, e, dx = j % 2, j // 4, j % 4
-        ends = [(half_a[dx].at[pl.ds(e * STEP_ROWS, STEP_ROWS)], halves.at[slot, :, pl.ds(0, HALF)])]
         for dz in range(RING):
-            at = pl.ds(dz * CAP, CAP)
-            ends.append((half_b[dz].at[pl.ds((e * 4 + dx) * CAP, CAP)], halves.at[slot, at, pl.ds(HALF, HALF)]))
-            chip = ((spot[1] + dz) % RING) * RING + (spot[2] + dx) % RING
-            if far is cot:
-                ends.append((far.at[chip], whole.at[slot, pl.ds(dz * ROWS, ROWS)]))
-            else:
-                ends.append((far.at[chip, pl.ds(e * CAP, CAP)], whole.at[slot, at]))
+            ends.append((half_b[dz].at[pl.ds(dx * CAP, CAP)], halves.at[slot, pl.ds(dz * CAP, CAP), pl.ds(HALF, HALF)]))
         return ends
 
-    def fetches(j):
-        slot = j % 2
-        ends = places(j, ra, rb, cot, cot_in, rows_in)
-        ends.append((ra[j % 4].at[pl.ds(PIECE, EXTRA)], gates_in.at[slot]))
-        return [pltpu.make_async_copy(far, near, in_sem.at[slot, n]) for n, (far, near) in enumerate(ends)]
-
-    def stores(j):
-        ends = places(j, qa, qb, moe, moe_out, back_out)
-        return [pltpu.make_async_copy(near, far, out_sem.at[j % 2, n]) for n, (far, near) in enumerate(ends)]
+    def chip(dz, dx):
+        return ((spot[1] + dz) % RING) * RING + (spot[2] + dx) % RING
+
+    def fetches(dx):
+        ends = places(dx, ra, rb, rows_in, extra_in)
+        for dz in range(RING):
+            ends.append((cot.at[chip(dz, dx)], cot_in.at[dx % 2, pl.ds(dz * ROWS, ROWS)]))
+        return [pltpu.make_async_copy(far, near, in_sem.at[dx % 2, n]) for n, (far, near) in enumerate(ends)]
+
+    def stores(dx):
+        ends = places(dx, qa, qb, back_out, extra_out)
+        for dz in range(RING):
+            ends.append((moe.at[chip(dz, dx), pl.ds(e * CAP, CAP)], moe_out.at[dx % 2, pl.ds(dz * CAP, CAP)]))
+        return [pltpu.make_async_copy(near, far, out_sem.at[dx % 2, n]) for n, (far, near) in enumerate(ends)]
 
     for j in range(STEPS):
 
         @pl.when(step == j)
         def _():
             if j == 0:
-                for copy in fetches(0) + loads(0) + loads(1):
+                for copy in fetches(0) + loads:
                     copy.start()
             if j + 1 < STEPS:
                 for copy in fetches(j + 1):
                     copy.start()
             for copy in fetches(j):
                 copy.wait()
-            if j % 4 == 0:
-                for copy in loads(j // 4):
+            if j == 0:
+                for copy in loads:
                     copy.wait()
             if j >= 2:
                 for copy in stores(j - 2):
                     copy.wait()
 
     slot = step % 2
-    e = step // 4
-    extra = gates_in[slot].astype(F32)
-    gates = extra[0:8, :ROWS] + extra[0:8, ROWS:]
-    gates = jnp.where(e == 0, gates[0:4, :], gates[4:8, :])
-    slots = jnp.where(e == 0, extra[8:12, :ROWS], extra[12:16, :ROWS])
-    fills = [slot_matrix(slots[dz : dz + 1, :]) for dz in range(RING)]
+    extra = extra_in[slot].astype(F32)
+    gates = extra[0:4, :ROWS] + extra[0:4, ROWS:]
+    fills = [slot_matrix(extra[4 + dz : 5 + dz, :ROWS]) for dz in range(RING)]
     gate_slot = jnp.concatenate(
         [jnp.sum(fills[dz] * gates[dz : dz + 1, :], axis=1, keepdims=True) for dz in range(RING)], axis=0
     )
     rows = rows_in[slot]
     disp_out[...] = rows
-    gate_up = dot(rows, wgu[e])
+    gate_up = dot(rows, wgu[...])
     gate, up = gate_up[:, :HALF], gate_up[:, HALF:]
     sigmoid = jax.nn.sigmoid(gate)
     silu = gate * sigmoid
     inner = (silu * up).astype(BF16)
     inner_out[...] = inner
-    made = dot(inner, wd[e]).astype(BF16).astype(F32)
+    made = dot(inner, wd[...]).astype(BF16).astype(F32)
     dmoe = [
         dot(fills[dz].astype(BF16), cot_in[slot, dz * ROWS : (dz + 1) * ROWS, :]) for dz in range(RING)
     ]
@@ -521,18 +526,16 @@
     dgates = [
         jnp.sum(fills[dz] * dgate_slot[dz * CAP : (dz + 1) * CAP, :], axis=0, keepdims=True) for dz in range(RING)
     ]
-    at_row = pl.multiple_of((step % 4) * 8, 8)
-    dgates = jnp.concatenate(dgates + dgates, axis=0)
-    first = lax.broadcasted_iota(jnp.int32, (8, ROWS), 0) < 4
-    dgate_out[pl.ds(at_row, 8), :] = jnp.where(first == (e == 0), dgates, dgate_out[pl.ds(at_row, 8), :])
+    dgates = jnp.concatenate(dgates + [jnp.zeros((EXTRA - RING, ROWS), F32)], axis=0)
+    extra_out[slot] = high_low(dgates)
     moe_out[slot] = (gate_slot * made).astype(BF16)
     dex = (gate_slot * dmoe).astype(BF16)
     dex_out[...] = dex
-    dinner = dot_nt(dex, wd[e])
+    dinner = dot_nt(dex, wd[...])
     dgate = dinner * up * sigmoid * (1.0 + gate * (1.0 - sigmoid))
     dgu = jnp.concatenate([dgate.astype(BF16), (dinner * silu).astype(BF16)], axis=1)
     dgu_out[...] = dgu
-    back_out[slot] = dot_nt(dgu, wgu[e]).astype(BF16)
+    back_out[slot] = dot_nt(dgu, wgu[...]).astype(BF16)
 
     for j in range(STEPS):
 
@@ -541,28 +544,17 @@
             for copy in stores(j):
                 copy.start()
             if j == STEPS - 1:
-                last = []
-                for dx in range(RING):
-                    extra = high_low(dgate_out[dx * 8 : (dx + 1) * 8, :]).astype(F32)
-                    extra_out[dx] = jnp.concatenate([extra, jnp.zeros_like(extra)], axis=0).astype(BF16)
-                    last.append(
-                        pltpu.make_async_copy(
-                            extra_out.at[dx], qa[dx].at[pl.ds(PIECE, EXTRA)], extra_sem.at[dx]
-                        )
-                    )
-                for copy in last:
-                    copy.start()
-                for copy in stores(j - 1) + stores(j) + last:
+                for copy in stores(j - 1) + stores(j):
                     copy.wait()
 
 
-def experts(spot, rows, cots, weights):
+def expert(spot, e, pieces, cots, weights, *moe):
     total = STEPS * STEP_ROWS
     wide = pl.BlockSpec((STEP_ROWS, WIDTH), lambda s: (s, 0))
     narrow = pl.BlockSpec((STEP_ROWS, HALF), lambda s: (s, 0))
-    buf = pltpu.VMEM((2, STEP_ROWS, WIDTH), BF16)
+    buf, small = pltpu.VMEM((2, STEP_ROWS, WIDTH), BF16), pltpu.VMEM((2, EXTRA, HALF), BF16)
     made = pl.pallas_call(
-        expert_kernel,
+        lambda *refs: expert_kernel(e, *refs),
         grid=(STEPS,),
         out_shape=[shape_of(PIECE + EXTRA)] * RING
         + [shape_of(PIECE)] * RING
@@ -573,32 +565,29 @@
             jax.ShapeDtypeStruct((total, HALF), BF16),
             jax.ShapeDtypeStruct((total, WIDTH), BF16),
         ],
-        in_specs=[SCALARS] + [ANYWHERE] * 11,
+        in_specs=[SCALARS] + [ANYWHERE] * (10 + e),
         out_specs=[ANYWHERE] * 9 + [wide, wide, narrow, wide],
         scratch_shapes=[
-            pltpu.VMEM((2, WIDTH, WIDTH), BF16),
-            pltpu.VMEM((2, HALF, WIDTH), BF16),
-            buf, pltpu.VMEM((2, RING * ROWS, WIDTH), BF16), pltpu.VMEM((2, EXTRA, HALF), BF16), buf, buf,
-            pltpu.VMEM((EXPERTS, ROWS), F32),
-            pltpu.VMEM((RING, EXTRA, HALF), BF16),
-            pltpu.SemaphoreType.DMA((2, 2)),
+            pltpu.VMEM((WIDTH, WIDTH), BF16),
+            pltpu.VMEM((HALF, WIDTH), BF16),
+            buf, pltpu.VMEM((2, RING * ROWS, WIDTH), BF16), small, buf, buf, small,
+            pltpu.SemaphoreType.DMA((2,)),
             pltpu.SemaphoreType.DMA((2, 10)),
             pltpu.SemaphoreType.DMA((2, 10)),
-            pltpu.SemaphoreType.DMA((RING,)),
         ],
-        compiler_params=params(),
-        cost_estimate=pl.CostEstimate(flops=19_000_000_000, bytes_accessed=60_000_000, transcendentals=1_600_000),
-        name="experts",
-    )(spot, *rows, cots, *weights)
-    return made[:8], made[8], made[9:]
-
-
-def weight_grads_kernel(which, with_other, *refs):
+        input_output_aliases={11: 8} if e else {},
+        compiler_params=params(),
+        cost_estimate=NO_COST,
+        name="expert",
+    )(spot, *pieces.got[0], *pieces.got[1], cots, weights, *moe)
+    return Pieces(made[:4], made[4:8]), made[8], made[9:]
+
+
+def weight_grads_kernel(with_other, *refs):
     disp, dgu, inner, dex = refs[:4]
     other, out = refs[4] if with_other else None, refs[4 + with_other]
     disp_in, dgu_in, inner_in, dex_in, made, other_in, sems, out_sems = refs[5 + with_other :]
-    rows = pl.ds(which * 4 * STEP_ROWS, 4 * STEP_ROWS)
-    pairs = [(disp.at[rows], disp_in), (dgu.at[rows], dgu_in), (inner.at[rows], inner_in), (dex.at[rows], dex_in)]
+    pairs = [(disp, disp_in), (dgu, dgu_in), (inner, inner_in), (dex, dex_in)]
     if with_other:
         pairs.append((other, other_in))
     fetches = [pltpu.make_async_copy(far, near, sems.at[i]) for i, (far, near) in enumerate(pairs)]
@@ -627,11 +616,11 @@
         copy.wait()
 
 
-def weight_grads(which, saved, *other):
+def weight_grads(saved, *other):
     wide, narrow = pltpu.VMEM((4 * STEP_ROWS, WIDTH), BF16), pltpu.VMEM((4 * STEP_ROWS, HALF), BF16)
     grads = pltpu.VMEM((WIDTH + HALF, WIDTH), BF16)
     return pl.pallas_call(
-        lambda *refs: weight_grads_kernel(which, len(other), *refs),
+        lambda *refs: weight_grads_kernel(len(other), *refs),
         out_shape=jax.ShapeDtypeStruct((WIDTH + HALF, WIDTH), BF16),
         in_specs=[ANYWHERE] * (4 + len(other)),
         out_specs=ANYWHERE,
@@ -650,19 +639,19 @@
     down[...] = grads[WIDTH:, :].astype(F32)
 
 
-def cast_grads(grads):
-    return pl.pallas_call(
-        cast_grads_kernel,
+def cast_grads(grads, *others):
+    return pl.pallas_call(
+        ignoring(cast_grads_kernel, 1, len(others)),
         out_shape=[
             jax.ShapeDtypeStruct((WIDTH, 2, HALF), F32),
             jax.ShapeDtypeStruct((HALF, WIDTH), F32),
         ],
-        in_specs=[WHOLE],
+        in_specs=[WHOLE] + [ANYWHERE] * len(others),
         out_specs=[WHOLE] * 2,
         compiler_params=params(),
         cost_estimate=NO_COST,
         name="cast_grads",
-    )(grads)
+    )(grads, *others)
 
 
 def unroute_kernel(spot, *refs):
@@ -755,7 +744,7 @@
 
 def unattend_kernel(
     spot, q_in, k_in, v_in, lse, dmixed, normed, gain, wq, wk, wv, cos, sin, seg_col, seg_row,
-    dqkv, dgain, dn0, dn1, dn2, dn3, kt, bias, dk, dv,
+    dqkv, dgain, dn0, dn1, dn2, dn2_rest, dn3, kt, bias, dk, dv,
 ):
     me = spot[0]
     lane = lax.broadcasted_iota(jnp.int32, (ROWS, LANES), 1)
@@ -797,11 +786,16 @@
         gain_sum = term if b == 0 else gain_sum + term
         dn = dn.astype(BF16)
         relative = (b - me + RING) % RING
-        for d, ref in enumerate((dn0, dn1, dn2, dn3)):
+        for d, ref in ((0, dn0), (1, dn1), (3, dn3)):
 
             @pl.when(relative == d)
             def _():
                 ref[...] = dn
+
+        @pl.when(relative == 2)
+        def _():
+            dn2[...] = dn[: ROWS // 2, :]
+            dn2_rest[...] = dn[ROWS // 2 :, :]
 
     dgain[...] = jnp.broadcast_to(gain_sum / gain[...], (8, WIDTH))
 
@@ -814,9 +808,9 @@
             jax.ShapeDtypeStruct((length, HALF), BF16),
             jax.ShapeDtypeStruct((8, WIDTH), F32),
         ]
-        + [jax.ShapeDtypeStruct((ROWS, WIDTH), BF16)] * RING,
+        + [jax.ShapeDtypeStruct((rows, WIDTH), BF16) for rows in (ROWS, ROWS, ROWS // 2, ROWS // 2, ROWS)],
         in_specs=[SCALARS] + [WHOLE] * 14,
-        out_specs=[WHOLE] * 6,
+        out_specs=[WHOLE] * 7,
         scratch_shapes=[
             pltpu.VMEM((LANES, length), BF16),
             pltpu.VMEM((3 * ROWS, ROWS), F32),
@@ -862,9 +856,9 @@
 def reduce_core_kernel(spot, own, got, g0, g1, g2, g3, p0, p1, p2, p3, total):
     total[...] = add_all((own, got))
     gain = (g0[...] + g1[...]) + (g2[...] + g3[...])
-    mine = jnp.where(spot[3] == 0, gain[0:1, :HALF], gain[0:1, HALF:])
     row = lax.broadcasted_iota(jnp.int32, (32, HALF), 0)
-    total[GAINS:, :] = jnp.where(row == 1, mine, total[GAINS:, :].astype(F32)).astype(BF16)
+    tail = jnp.where(row == 1, gain[0:1, :HALF], total[GAINS:, :].astype(F32))
+    total[GAINS:, :] = jnp.where(row == 2, gain[0:1, HALF:], tail).astype(BF16)
     for d, piece in enumerate((p0, p1, p2, p3)):
         piece[...] = total[quarter_rows((spot[2] + d) % RING), :]
 
@@ -886,7 +880,10 @@
         value[at, :] = half[0:HALF, 3 * LANES :].astype(F32)
         grad_out[:, at] = half[HALF:768, :].astype(F32)
         router[:, at] = half[768:GAINS, :].astype(F32)
-        gains[:, at] = half[GAINS:, :].astype(F32)[0:8, :]
+        gains[0:1, at] = half[GAINS:, :].astype(F32)[0:1, :]
+    both = own[GAINS:, :].astype(F32)[0:8, :] + got[GAINS:, :].astype(F32)[0:8, :]
+    gains[1:2, :HALF] = both[1:2, :]
+    gains[1:2, HALF:] = both[2:3, :]
 
 
 def small_call(kernel, spot, refs, shapes, scratch=None, flops=1_000_000, others=()):
@@ -901,7 +898,7 @@
     )(spot, *refs, *others)
 
 
-def sum_over_ep(spot, normed, dqkv, grad_out, sums, gains, dn, finished, output):
+def sum_over_ep(spot, normed, dqkv, grad_out, sums, gains, dn, output, moe_slots):
     own, other = small_call(
         pack_kernel, spot, (normed, dqkv, grad_out, *sums), [((PAY, HALF), BF16)] * 2, flops=0
     )
@@ -909,13 +906,13 @@
     pieces = small_call(
         reduce_core_kernel, spot, (own, got, *gains), [((QUARTER, HALF), BF16)] * 4, (PAY, HALF)
     )
-    dn, halves = scatter_tp(after(dn, pieces[0]))
+    dn, halves = scatter_tp(*after(dn, pieces[0]))
     pieces = [push(pieces[d], 0, d, 0) for d in range(RING)]
     quarter = [((QUARTER, HALF), BF16)]
-    (line,) = small_call(sum_kernel, spot, pieces, quarter, others=(*halves, output))
-    (line,) = small_call(sum_kernel, spot, [push(line, d, 0, 0) for d in range(RING)], quarter)
+    (line,) = small_call(sum_kernel, spot, pieces, quarter, others=(*halves, moe_slots))
+    (line,) = small_call(sum_kernel, spot, [push(line, d, 0, 0) for d in range(RING)], quarter, others=(output,))
     pieces = [push(line, 0, -d, 0) for d in range(RING)]
-    (half,) = small_call(gather_x_kernel, spot, pieces, [((PAY, HALF), BF16)], others=(*finished, *dn[1:]))
+    (half,) = small_call(gather_x_kernel, spot, pieces, [((PAY, HALF), BF16)], others=dn[1:])
     made = small_call(
         unpack_kernel,
         spot,
@@ -989,13 +986,29 @@
     (weights,) = after((weights,), lse)
     weights = weights, push(weights, 0, 0, 1)
     middle, half_a, half_b, gates_t = route(hidden_in, branches, gain_two, w_router, chosen, table, weights[1])
-    rows, slots_a, slots_b = dispatch(spot, half_a, half_b)
-    back, moe_slots, saved = experts(spot, rows, cots, weights)
-    got = exchange_near(back)
-    (grads_other,) = exchange_far(back, got, (weight_grads(1, saved),))
-    grads_e = weight_grads(0, saved, push(grads_other, 0, 0, 1))
-    parts = to_owners(combine(slots_a, slots_b, got, True, grads_e))
-    grads_e = lax.psum_scatter(grads_e, "tp", scatter_dimension=0, tiled=True)
+    (pieces_a, pieces_b), slots_a, slots_b = dispatch(spot, half_a, half_b)
+    first, second = Pieces(pieces_a[:4], pieces_b[:4]), Pieces(pieces_a[4:], pieces_b[4:])
+    near = first.send_near()
+    far = [first.send(0, 2)]
+    held = after((pieces_b[2], pieces_b[6]), near[2], near[3])
+    far += [first.send(1, 2, held[0]), second.send(1, 2, held[1])]
+    held = after(second.near()[:2], *near)
+    second.send(0, 1, held[0]), second.send(0, 3, held[1])
+    held = after((*second.near()[2:], pieces_a[6]), *near, *far)
+    second.send(1, 1, held[0]), second.send(1, 3, held[1]), second.send(0, 2, held[2])
+
+    back_first, moe_slots, saved = expert(spot, 0, first, cots, weights[0])
+    near = back_first.send_near()
+    near.append(back_first.send(0, 2))
+    back_second, moe_slots, saved_other = expert(spot, 1, second, cots, weights[1], moe_slots)
+    held = after((back_first.made[1][2], *back_second.near()), *near)
+    back_first.send(1, 2, held[0])
+    near = back_second.send_near(held[1:])
+    held = after((back_second.made[0][2], back_second.made[1][2], weight_grads(saved_other)), *near)
+    back_second.send(0, 2, held[0])
+    back_second.send(1, 2, held[1])
+    grads_e = weight_grads(saved, push(held[2], 0, 0, 1))
+    parts = to_owners(combine(slots_a, slots_b, back_first, back_second))
 
     dmiddle, dbranch, sums = unroute(
         spot, parts, gates_t, middle, cotangent, gain_two, w_router.T.astype(F32)
@@ -1003,24 +1016,24 @@
     group_grad = gather_tp(dbranch)
     sums = [push_tp(sums, d) for d in range(RING)]
 
-    (moe_slots,) = after((moe_slots,), *parts)
+    (moe_slots,) = after((moe_slots,), *parts, grads_e)
     moe_slots = lax.all_to_all(
         moe_slots, "ep", split_axis=0, concat_axis=0, tiled=True, axis_index_groups=SAME_CORE
     )
 
-    dmixed, grad_output = unmix(spot, group_grad, mixed, w_output, *sums[1:])
-    (grads_e,) = after((grads_e,), dmixed)
-    grad_up, grad_down = cast_grads(lax.all_gather(grads_e, "tp", axis=0, tiled=True))
+    (summed_e,) = after((grads_e,), *group_grad[2])
+    summed = lax.psum(summed_e, "tp")
+    dmixed, grad_output = unmix(spot, group_grad, mixed, w_output, *sums[1:], summed_e)
     last = unattend(
         spot, q, k, v, lse, dmixed, normed, gain_one, w_query, w_key, w_value, cos, sin, seg_col, seg_row
     )
-    gain = last[1] + push(last[1], 0, 0, 1)
-    gains = [push_tp(gain, d) for d in range(RING)]
+    gains = [push_tp(last[1], d) for d in range(RING)]
     output = finish(spot, table, moe_slots.reshape(CHIPS * PAIR, WIDTH), middle)
     grad_query, grad_key, grad_value, grad_output, grad_router, grad_gains, dn = sum_over_ep(
-        spot, normed, last[0], grad_output, sums, gains, last[2:6], (grad_up, grad_down), output
+        spot, normed, last[0], grad_output, sums, gains, last[2:], output, moe_slots
     )
     grad_hidden = hidden_grad(dn, hidden_in, gain_one, dmiddle)
+    grad_up, grad_down = cast_grads(summed, grad_query)
     return (
         output,
         grad_hidden,

time: 443 us -> 442 us (level)
  the two profiles are of different devices: /device:TPU:25 before, /device:TPU:1 now
where the time goes in v4:
time: 442 us; the launch traced here: 434 us
  Pallas kernels  157 us (36%)
  starting transfers between devices  119 us (27%)
  waiting for transfers between devices  106 us (24%)
  local copies, waits for them, and re-layouts  26.5 us (6%)
  between operations  15.2 us (3%)
  other arithmetic  9.65 us (2%)
    ppermute x49, starting transfers between devices, push(): return lax.ppermute(value, 'ep', pairs)  85.2 us
    ppermute x20, waiting for transfers between devices, push_tp(): lax.ppermute(value, 'tp', [(y, (y + dy) % RING) for y in range(RING)])  59.8 us
    ppermute x49, waiting for transfers between devices, push(): return lax.ppermute(value, 'ep', pairs)  45.1 us
    pallas_call x2, Pallas kernels, expert(): pl.pallas_call(lambda *refs: expert_kernel(e, *refs), grid=(STEPS,), out_...  44.1 us
    ppermute x20, starting transfers between devices, push_tp(): lax.ppermute(value, 'tp', [(y, (y + dy) % RING) for y in range(RING)])  27.3 us
    unnamed x148, local copies, waits for them, and re-layouts  22.5 us
    pallas_call x2, Pallas kernels, weight_grads(): pl.pallas_call(lambda *refs: weight_grads_kernel(len(other), *refs), out_...  20.7 us
    pallas_call x6, Pallas kernels, small_call(): pl.pallas_call(ignoring(kernel, 1 + len(refs), len(others)), out_shape=[j...  17.1 us
  transfers between devices with their start and end apart: 72, of which 25 were waited for; matrix products, arithmetic and copies ran while one was open for 4% of the time, Pallas kernels for 35%

profile of v4, /device:TPU:1, one launch (start us, length us, event | category | flops | bytes accessed | tf_op | source)
XLA Modules:
  0.0 433.8 jit_solution(10379540621459655182)
XLA Ops:
  7.9 3.6 collective-permute-start
  12.6 2.0 fusion.2
  18.2 2.2 copy.63
  20.4 1.9 pad_maximum_fusion.1
  22.3 2.0 pad_maximum_fusion.refs_0_
  24.3 9.3 %collective-permute-done.refs_2_ = bf16[256,1024]{1,0:T(8,128)(2,1)S(1)} collective-permute-done((bf16[256,1024]{1,0:T(8,128)(2,1)}, bf16[256,1024]{1,0:T(8,128)(2,1)S(1)}, u32[]{:S(2)}, u32[]{:S(2)}) %collective-permute-start) | collective-permute-done | bytes 524320 | tf_op jit(solution)/shard_map/ppermute | solution.py:70
  33.6 4.8 %collective-permute-done.2.refs_4_ = bf16[256,1024]{1,0:T(8,128)(2,1)S(1)} collective-permute-done((bf16[256,1024]{1,0:T(8,128)(2,1)}, bf16[256,1024]{1,0:T(8,128)(2,1)S(1)}, u32[]{:S(2)}, u32[]{:S(2)}) %collective-permute-start.2) | collective-permute-done | bytes 524320 | tf_op jit(solution)/shard_map/ppermute | solution.py:70
  39.1 17.0 %attend.1 = (bf16[1024,1024]{1,0:T(8,128)(2,1)}, bf16[1024,512]{1,0:T(8,128)(2,1)}, bf16[1024,128]{1,0:T(8,128)(2,1)}, bf16[1024,128]{1,0:T(8,128)(2,1)}, bf16[1...) custom-call(s32[4]{0:T(128)} %pad_add_fusion.refs_0_.spot, ...), custom_call_target="tpu_custom_call" | custom-call | tf_op jit(solution)/shard_map/attend/pallas_call | solution.py:196
  62.4 20.2 %collective-permute-done.3.refs_2_ = bf16[256,1024]{1,0:T(8,128)(2,1)} collective-permute-done((bf16[256,1024]{1,0:T(8,128)(2,1)}, bf16[256,1024]{1,0:T(8,128)(2,1)}, u32[]{:S(2)}, u32[]{:S(2)}) %collective-permute-start.3) | collective-permute-done | bytes 524320 | tf_op jit(solution)/shard_map/ppermute | solution.py:70
  84.7 3.6 route.1
  88.2 2.7 collective-permute-start.10
  91.0 3.5 collective-permute-start.7
  96.9 5.9 %collective-permute-done.11.refs_6_ = bf16[288,512]{1,0:T(8,128)(2,1)S(1)} collective-permute-done((bf16[288,512]{1,0:T(8,128)(2,1)}, bf16[288,512]{1,0:T(8,128)(2,1)S(1)}, u32[]{:S(2)}, u32[]{:S(2)}) %collective-permute-start.11) | collective-permute-done | bytes 294944 | tf_op jit(solution)/shard_map/ppermute | solution.py:64
  102.8 6.2 %collective-permute-done.12.refs_7_ = bf16[288,512]{1,0:T(8,128)(2,1)S(1)} collective-permute-done((bf16[288,512]{1,0:T(8,128)(2,1)}, bf16[288,512]{1,0:T(8,128)(2,1)S(1)}, u32[]{:S(2)}, u32[]{:S(2)}) %collective-permute-start.12) | collective-permute-done | bytes 294944 | tf_op jit(solution)/shard_map/ppermute | solution.py:64
  109.0 3.2 collective-permute-done.9.refs_3_
  113.0 6.2 %dispatch.1 = (bf16[400,512]{1,0:T(8,128)(2,1)}, bf16[400,512]{1,0:T(8,128)(2,1)}, bf16[400,512]{1,0:T(8,128)(2,1)}, bf16[400,512]{1,0:T(8,128)(2,1)}, bf16[400,...) custom-call(s32[4]{0:T(128)} %pad_add_fusion.refs_0_.spot, ...), custom_call_target="tpu_custom_call" | custom-call | flops 1000000000 | bytes 5000000 | tf_op jit(solution)/shard_map/dispatch/pallas_call | solution.py:345
  119.2 2.7 collective-permute-start.16
  122.1 2.7 collective-permute-start.14
  124.7 3.9 collective-permute-done.15.refs_4_.refs_2_.refs_5_.refs_8_
  129.5 3.0 collective-permute-start.20
  138.3 8.4 %collective-permute-done.20.refs_9_.refs_7_ = bf16[384,512]{1,0:T(8,128)(2,1)S(1)} collective-permute-done((bf16[384,512]{1,0:T(8,128)(2,1)}, bf16[384,512]{1,0:T(8,128)(2,1)S(1)}, u32[]{:S(2)}, u32[]{:S(2)}) %collective-permute-start.20) | collective-permute-done | bytes 393248 | tf_op jit(solution)/shard_map/ppermute | solution.py:64
  147.5 2.9 collective-permute-start.21
  151.8 22.0 %expert.2 = (bf16[400,512]{1,0:T(8,128)(2,1)}, bf16[400,512]{1,0:T(8,128)(2,1)}, bf16[400,512]{1,0:T(8,128)(2,1)}, bf16[400,512]{1,0:T(8,128)(2,1)}, bf16[384,51...) custom-call(s32[4]{0:T(128)} %pad_add_fusion.refs_0_.spot, ...), custom_call_target="tpu_custom_call" | custom-call | tf_op jit(solution)/shard_map/expert/pallas_call | solution.py:556
  177.6 2.0 collective-permute-start.29
  179.6 22.1 %expert.3 = (bf16[400,512]{1,0:T(8,128)(2,1)}, bf16[400,512]{1,0:T(8,128)(2,1)}, bf16[400,512]{1,0:T(8,128)(2,1)}, bf16[400,512]{1,0:T(8,128)(2,1)}, bf16[384,51...) custom-call(s32[4]{0:T(128)} %pad_add_fusion.refs_0_.spot, ...), custom_call_target="tpu_custom_call", output_to_operand_aliasing={{8}: (11, {})} | custom-call | tf_op jit(solution)/shard_map/expert/pallas_call | solution.py:556
  203.3 2.8 collective-permute-start.30
  206.1 2.7 collective-permute-start.33
  208.7 9.2 %weight_grads.2.refs_2_ = bf16[1536,1024]{1,0:T(8,128)(2,1)} custom-call(bf16[1536,1024]{1,0:T(8,128)(2,1)} %get-tuple-element.174.refs_0_, bf16[1536,1024]{1,0:T(8,128)(2,1)} %get-tuple-element.175.refs_1_, bf16[1536,512]{1,0:T(8,128)(2,1)} %get-tuple-element.176.refs_2_, bf16[1536,1024]{1,0:T(8,128)(2,1)} %get-tuple-element.177.refs_3_), custom_call_target="tpu_custom_call" | custom-call | tf_op jit(solution)/shard_map/weight_grads/pallas_call | solution.py:622
  219.2 2.6 collective-permute-start.34
  221.8 3.0 collective-permute-start.36
  224.7 12.6 %collective-permute-start.43 = (bf16[1536,1024]{1,0:T(8,128)(2,1)}, bf16[1536,1024]{1,0:T(8,128)(2,1)S(1)}, u32[]{:S(2)}, u32[]{:S(2)}) collective-permute-start(bf16[1536,1024]{1,0:T(8,128)(2,1)} %get-tuple-element.198), channel_id=1, source_target_pairs={{0,4},{4,0},{8,12},{12,8},{16,20},{20,16},{24,28},{28,24},{32,36},... | collective-permute-start | bytes 9437192 | tf_op jit(solution)/shard_map/ppermute | solution.py:64
  238.3 5.8 %combine.1 = (bf16[272,512]{1,0:T(8,128)(2,1)}, bf16[272,512]{1,0:T(8,128)(2,1)}, bf16[272,512]{1,0:T(8,128)(2,1)}, bf16[272,512]{1,0:T(8,128)(2,1)}, bf16[256,5...) custom-call(f32[32,256]{1,0:T(8,128)} %get-tuple-element.157.refs_0_, ...), custom_call_target="tpu_custom_call" | custom-call | flops 60000002048 | tf_op jit(solution)/shard_map/combine/pallas_call | solution.py:380
  244.2 3.3 collective-permute-start.37
  252.2 11.5 %weight_grads.3.refs_9_.refs_0_ = bf16[1536,1024]{1,0:T(8,128)(2,1)} custom-call(bf16[1536,1024]{1,0:T(8,128)(2,1)} %get-tuple-element.194.refs_0_, bf16[1536,1024]{1,0:T(8,128)(2,1)} %get-tuple-element.195.refs_1_, bf16[1536,512]{1,0:T(8,128)(2,1)} %get-tuple-element.196.refs_2_, bf16[1536,1024]{1,0:T(8,128)(2,1)} %get-tuple-element.197.refs_3_, ...), custom_call_target="tpu_custom_call" | custom-call | tf_op jit(solution)/shard_map/weight_grads/pallas_call | solution.py:622
  264.8 6.6 %all-to-all-start = ((bf16[16,192,1024]{2,1,0:T(8,128)(2,1)}), bf16[16,192,1024]{2,1,0:T(8,128)(2,1)}, u32[]{:S(2)}, u32[]{:S(2)}) async-start(bf16[16,192,1024]{2,1,0:T(8,128)(2,1)} %after.15), calls=%async_computation | async-start | bytes 12582912 | tf_op jit(solution)/shard_map/all_to_all | solution.py:1020
  272.0 5.0 %unroute.1 = (f32[256,1024]{1,0:T(8,128)}, bf16[256,1024]{1,0:T(8,128)(2,1)}, f32[40,1024]{1,0:T(8,128)}) custom-call(s32[4]{0:T(128)} %pad_add_fusion.refs_0_.spot, bf16[272,512]{1,0:T(8,128)(2,1)} %get-tuple-element.186.refs_1_, bf16[272,512]{1,0:T(8,128)(2,1)} %copy-done.13, bf16[272,512]{1,0:T(8,128)(2,1)} %copy-done.14, bf16[272,512]{1,0:T(8,128)(2,1)} %copy-done.15, ...), custom_call_target="tpu_custom_call" | custom-call | tf_op jit(solution)/shard_map/unroute/pallas_call | solution.py:693
  278.0 4.2 collective-permute-start.46
  282.2 7.1 %collective-permute-done.44.refs_2_ = bf16[256,1024]{1,0:T(8,128)(2,1)S(1)} collective-permute-done((bf16[256,1024]{1,0:T(8,128)(2,1)}, bf16[256,1024]{1,0:T(8,128)(2,1)S(1)}, u32[]{:S(2)}, u32[]{:S(2)}) %collective-permute-start.44) | collective-permute-done | bytes 524320 | tf_op jit(solution)/shard_map/ppermute | solution.py:70
  295.6 3.3 collective-permute-done.47.refs_2_.refs_4_
  299.5 4.6 %collective-permute-done.48.refs_8_.refs_5_ = f32[40,1024]{1,0:T(8,128)S(1)} collective-permute-done((f32[40,1024]{1,0:T(8,128)}, f32[40,1024]{1,0:T(8,128)S(1)}, u32[]{:S(2)}, u32[]{:S(2)}) %collective-permute-start.48) | collective-permute-done | bytes 163872 | tf_op jit(solution)/shard_map/ppermute | solution.py:70
  304.9 4.2 unmix.1
  309.9 15.8 %unattend.1 = (bf16[1024,512]{1,0:T(8,128)(2,1)}, f32[8,1024]{1,0:T(8,128)}, bf16[256,1024]{1,0:T(8,128)(2,1)}, bf16[256,1024]{1,0:T(8,128)(2,1)}, bf16[128,1024...) custom-call(s32[4]{0:T(128)} %pad_add_fusion.refs_0_.spot, ...), custom_call_target="tpu_custom_call" | custom-call | tf_op jit(solution)/shard_map/unattend/pallas_call | solution.py:805
  325.7 4.7 %shard_map.221 = (bf16[832,512]{1,0:T(8,128)(2,1)}, bf16[832,512]{1,0:T(8,128)(2,1)}) custom-call(s32[4]{0:T(128)} %pad_add_fusion.refs_0_.spot, bf16[1024,1024]{1,0:T(8,128)(2,1)} %get-tuple-element.208.normed.refs_1_, bf16[1024,512]{1,0:T(8,128)(2,1)} %get-tuple-element.214.refs_2_, bf16[256,1024]{1,0:T(8,128)(2,1)} %get-tuple-element.215.refs_3_, ...), custom_call_target="tpu_custom_call" | custom-call | bytes 2000000 | tf_op jit(solution)/shard_map/pallas_call | solution.py:890
  330.4 13.2 %collective-permute-start.51 = (bf16[832,512]{1,0:T(8,128)(2,1)}, bf16[832,512]{1,0:T(8,128)(2,1)S(1)}, u32[]{:S(2)}, u32[]{:S(2)}) collective-permute-start(bf16[832,512]{1,0:T(8,128)(2,1)} %get-tuple-element.217), channel_id=1, source_target_pairs={{0,4},{4,0},{8,12},{12,8},{16,20},{20,16},{24,28},{28,24},{32,36},... | collective-permute-start | bytes 2555912 | tf_op jit(solution)/shard_map/ppermute | solution.py:64
  344.2 2.6 collective-permute-start.53
  347.5 1.8 collective-permute-done.52.refs_4_
  349.2 1.7 collective-permute-done.53.refs_5_
  351.9 2.8 shard_map.222
  355.6 1.8 collective-permute-start.56
  358.8 2.4 collective-permute-start.60
  362.3 5.9 %collective-permute-done.55.first.refs_5_ = bf16[128,1024]{1,0:T(8,128)(2,1)S(1)} collective-permute-done((bf16[128,1024]{1,0:T(8,128)(2,1)}, bf16[128,1024]{1,0:T(8,128)(2,1)S(1)}, u32[]{:S(2)}, u32[]{:S(2)}) %collective-permute-start.55) | collective-permute-done | bytes 262176 | tf_op jit(solution)/shard_map/ppermute | solution.py:70
  369.1 2.4 add_halves.1
  371.5 2.7 collective-permute-start.58
  375.0 2.1 shard_map.223.refs_1_
  378.3 2.6 collective-permute-start.63
  382.0 6.4 %finish.1.refs_5_ = bf16[256,1024]{1,0:T(8,128)(2,1)} custom-call(s32[4]{0:T(128)} %pad_add_fusion.refs_0_.spot, f32[32,256]{1,0:T(8,128)} %convert_bitcast_fusion.1.refs_8_.table, bf16[3072,1024]{1,0:T(8,128)(2,1)} %bitcast.10.slots, f32[256,1024]{1,0:T(8,128)} %get-tuple-element.199.middle.refs_10_), custom_call_target="tpu_custom_call" | custom-call | flops 1000000000 | bytes 5000000 | tf_op jit(solution)/shard_map/finish/pallas_call | solution.py:430
  390.7 2.0 shard_map.224.refs_1_
  392.8 2.4 collective-permute-start.65
  396.4 4.6 %collective-permute-done.65.refs_2_ = bf16[208,512]{1,0:T(8,128)(2,1)S(1)} collective-permute-done((bf16[208,512]{1,0:T(8,128)(2,1)}, bf16[208,512]{1,0:T(8,128)(2,1)S(1)}, u32[]{:S(2)}, u32[]{:S(2)}) %collective-permute-start.65) | collective-permute-done | bytes 213024 | tf_op jit(solution)/shard_map/ppermute | solution.py:64
  401.7 5.8 %collective-permute-done.67.refs_4_ = bf16[208,512]{1,0:T(8,128)(2,1)S(1)} collective-permute-done((bf16[208,512]{1,0:T(8,128)(2,1)}, bf16[208,512]{1,0:T(8,128)(2,1)S(1)}, u32[]{:S(2)}, u32[]{:S(2)}) %collective-permute-start.67) | collective-permute-done | bytes 213024 | tf_op jit(solution)/shard_map/ppermute | solution.py:64
  408.2 2.2 shard_map.225.refs_1_
  412.1 3.4 hidden_grad.1
  416.4 3.3 shard_map.226
  421.1 5.4 %cast_grads.1 = (f32[1024,2,512]{2,1,0:T(2,128)}, f32[512,1024]{1,0:T(8,128)}) custom-call(bf16[1536,1024]{1,0:T(8,128)(2,1)} %all-reduce.2.cloned.1.call-done.refs_0_, f32[1024,256]{1,0:T(8,128)} %get-tuple-element.117.refs_1_), custom_call_target="tpu_custom_call" | custom-call | tf_op jit(solution)/shard_map/cast_grads/pallas_call | solution.py:643
  (277 shorter events, 68.6 us)
Async XLA Ops:
  7.2 144.6 %all-gather.3.cloned.1.call-start = ((), (), s32[]{:S(2)}) async-start(), calls=%async_computation.2 | async-start | bytes 8912896 | tf_op jit(solution)/shard_map/all_gather | solution.py:981
  7.9 25.6 %collective-permute-start = (bf16[256,1024]{1,0:T(8,128)(2,1)}, bf16[256,1024]{1,0:T(8,128)(2,1)S(1)}, u32[]{:S(2)}, u32[]{:S(2)}) collective-permute-start(bf16[256,1024]{1,0:T(8,128)(2,1)} %hidden.1), channel_id=1, source_target_pairs={{0,3},{1,0},{2,1},{3,2},{4,7},{5,4},{6,5},{7,6},{8,11},{9,8},{10,9... | collective-permute-start | bytes 1572872 | tf_op jit(solution)/shard_map/ppermute | solution.py:70
  11.5 22.0 %collective-permute-start.1 = (bf16[256,1024]{1,0:T(8,128)(2,1)}, bf16[256,1024]{1,0:T(8,128)(2,1)S(1)}, u32[]{:S(2)}, u32[]{:S(2)}) collective-permute-start(bf16[256,1024]{1,0:T(8,128)(2,1)} %hidden.1), channel_id=1, source_target_pairs={{0,2},{1,3},{2,0},{3,1},{4,6},{5,7},{6,4},{7,5},{8,10},{9,11},{10,... | collective-permute-start | bytes 1572872 | tf_op jit(solution)/shard_map/ppermute | solution.py:70
  11.9 26.4 %collective-permute-start.2 = (bf16[256,1024]{1,0:T(8,128)(2,1)}, bf16[256,1024]{1,0:T(8,128)(2,1)S(1)}, u32[]{:S(2)}, u32[]{:S(2)}) collective-permute-start(bf16[256,1024]{1,0:T(8,128)(2,1)} %hidden.1), channel_id=1, source_target_pairs={{0,1},{1,2},{2,3},{3,0},{4,5},{5,6},{6,7},{7,4},{8,9},{9,10},{10,1... | collective-permute-start | bytes 1572872 | tf_op jit(solution)/shard_map/ppermute | solution.py:70
  56.2 26.7 %collective-permute-start.6 = (bf16[1536,1024]{1,0:T(8,128)(2,1)}, bf16[1536,1024]{1,0:T(8,128)(2,1)S(1)}, u32[]{:S(2)}, u32[]{:S(2)}) collective-permute-start(bf16[1536,1024]{1,0:T(8,128)(2,1)} %after.9.refs_10_), channel_id=1, source_target_pairs={{0,4},{4,0},{8,12},{12,8},{16,20},{20,16},{24,28},{28,24},{32,36},... | collective-permute-start | bytes 9437192 | tf_op jit(solution)/shard_map/ppermute | solution.py:64
  56.9 25.7 %collective-permute-start.3 = (bf16[256,1024]{1,0:T(8,128)(2,1)}, bf16[256,1024]{1,0:T(8,128)(2,1)}, u32[]{:S(2)}, u32[]{:S(2)}) collective-permute-start(bf16[256,1024]{1,0:T(8,128)(2,1)} %get-tuple-element.126), channel_id=1, source_target_pairs={{0,1},{1,2},{2,3},{3,0},{4,5},{5,6},{6,7},{7,4},{8,9},{9,10},{10,1... | collective-permute-start | bytes 1572872 | tf_op jit(solution)/shard_map/ppermute | solution.py:70
  56.9 25.7 %collective-permute-start.4 = (bf16[256,1024]{1,0:T(8,128)(2,1)}, bf16[256,1024]{1,0:T(8,128)(2,1)}, u32[]{:S(2)}, u32[]{:S(2)}) collective-permute-start(bf16[256,1024]{1,0:T(8,128)(2,1)} %get-tuple-element.127), channel_id=1, source_target_pairs={{0,2},{1,3},{2,0},{3,1},{4,6},{5,7},{6,4},{7,5},{8,10},{9,11},{10,... | collective-permute-start | bytes 1572872 | tf_op jit(solution)/shard_map/ppermute | solution.py:70
  58.3 24.6 %collective-permute-start.5 = (bf16[256,1024]{1,0:T(8,128)(2,1)}, bf16[256,1024]{1,0:T(8,128)(2,1)}, u32[]{:S(2)}, u32[]{:S(2)}) collective-permute-start(bf16[256,1024]{1,0:T(8,128)(2,1)} %get-tuple-element.128), channel_id=1, source_target_pairs={{0,3},{1,0},{2,1},{3,2},{4,7},{5,4},{6,5},{7,6},{8,11},{9,8},{10,9... | collective-permute-start | bytes 1572872 | tf_op jit(solution)/shard_map/ppermute | solution.py:70
  88.2 7.8 %collective-permute-start.10 = (bf16[288,512]{1,0:T(8,128)(2,1)}, bf16[288,512]{1,0:T(8,128)(2,1)S(1)}, u32[]{:S(2)}, u32[]{:S(2)}) collective-permute-start(bf16[288,512]{1,0:T(8,128)(2,1)} %get-tuple-element.131.refs_4_), channel_id=1, source_target_pairs={{0,24},{4,28},{8,0},{12,4},{16,8},{20,12},{24,16},{28,20},{32,56},... | collective-permute-start | bytes 884744 | tf_op jit(solution)/shard_map/ppermute | solution.py:64
  91.0 18.0 %collective-permute-start.7 = (bf16[320,512]{1,0:T(8,128)(2,1)}, bf16[320,512]{1,0:T(8,128)(2,1)S(1)}, u32[]{:S(2)}, u32[]{:S(2)}) collective-permute-start(bf16[320,512]{1,0:T(8,128)(2,1)} %get-tuple-element.130.refs_0_), channel_id=1, source_target_pairs={{0,96},{4,100},{8,104},{12,108},{16,112},{20,116},{24,120},{28,124... | collective-permute-start | bytes 983048 | tf_op jit(solution)/shard_map/ppermute | solution.py:64
  94.5 14.5 %collective-permute-start.8 = (bf16[320,512]{1,0:T(8,128)(2,1)}, bf16[320,512]{1,0:T(8,128)(2,1)S(1)}, u32[]{:S(2)}, u32[]{:S(2)}) collective-permute-start(bf16[320,512]{1,0:T(8,128)(2,1)} %get-tuple-element.130.refs_0_), channel_id=1, source_target_pairs={{0,64},{4,68},{8,72},{12,76},{16,80},{20,84},{24,88},{28,92},{32,9... | collective-permute-start | bytes 983048 | tf_op jit(solution)/shard_map/ppermute | solution.py:64
  94.5 17.7 %collective-permute-start.9 = (bf16[320,512]{1,0:T(8,128)(2,1)}, bf16[320,512]{1,0:T(8,128)(2,1)S(1)}, u32[]{:S(2)}, u32[]{:S(2)}) collective-permute-start(bf16[320,512]{1,0:T(8,128)(2,1)} %get-tuple-element.130.refs_0_), channel_id=1, source_target_pairs={{0,32},{4,36},{8,40},{12,44},{16,48},{20,52},{24,56},{28,60},{32,6... | collective-permute-start | bytes 983048 | tf_op jit(solution)/shard_map/ppermute | solution.py:64
  96.1 12.9 %collective-permute-start.12 = (bf16[288,512]{1,0:T(8,128)(2,1)}, bf16[288,512]{1,0:T(8,128)(2,1)S(1)}, u32[]{:S(2)}, u32[]{:S(2)}) collective-permute-start(bf16[288,512]{1,0:T(8,128)(2,1)} %get-tuple-element.131.refs_4_), channel_id=1, source_target_pairs={{0,8},{4,12},{8,16},{12,20},{16,24},{20,28},{24,0},{28,4},{32,40},... | collective-permute-start | bytes 884744 | tf_op jit(solution)/shard_map/ppermute | solution.py:64
  119.1 9.5 %collective-permute-start.15 = (bf16[384,512]{1,0:T(8,128)(2,1)}, bf16[384,512]{1,0:T(8,128)(2,1)S(1)}, u32[]{:S(2)}, u32[]{:S(2)}) collective-permute-start(bf16[384,512]{1,0:T(8,128)(2,1)} %get-tuple-element.137), channel_id=1, source_target_pairs={{0,32},{4,36},{8,40},{12,44},{16,48},{20,52},{24,56},{28,60},{32,6... | collective-permute-start | bytes 1179656 | tf_op jit(solution)/shard_map/ppermute | solution.py:64
  119.2 9.4 %collective-permute-start.16 = (bf16[384,512]{1,0:T(8,128)(2,1)}, bf16[384,512]{1,0:T(8,128)(2,1)S(1)}, u32[]{:S(2)}, u32[]{:S(2)}) collective-permute-start(bf16[384,512]{1,0:T(8,128)(2,1)} %get-tuple-element.138), channel_id=1, source_target_pairs={{0,96},{4,100},{8,104},{12,108},{16,112},{20,116},{24,120},{28,124... | collective-permute-start | bytes 1179656 | tf_op jit(solution)/shard_map/ppermute | solution.py:64
  121.9 11.8 %collective-permute-start.13 = (bf16[400,512]{1,0:T(8,128)(2,1)}, bf16[400,512]{1,0:T(8,128)(2,1)S(1)}, u32[]{:S(2)}, u32[]{:S(2)}) collective-permute-start(bf16[400,512]{1,0:T(8,128)(2,1)} %get-tuple-element.135), channel_id=1, source_target_pairs={{0,8},{4,12},{8,16},{12,20},{16,24},{20,28},{24,0},{28,4},{32,40},... | collective-permute-start | bytes 1228808 | tf_op jit(solution)/shard_map/ppermute | solution.py:64
  122.1 11.6 %collective-permute-start.14 = (bf16[400,512]{1,0:T(8,128)(2,1)}, bf16[400,512]{1,0:T(8,128)(2,1)S(1)}, u32[]{:S(2)}, u32[]{:S(2)}) collective-permute-start(bf16[400,512]{1,0:T(8,128)(2,1)} %get-tuple-element.136), channel_id=1, source_target_pairs={{0,24},{4,28},{8,0},{12,4},{16,8},{20,12},{24,16},{28,20},{32,56},... | collective-permute-start | bytes 1228808 | tf_op jit(solution)/shard_map/ppermute | solution.py:64
  124.7 12.8 %collective-permute-start.18 = (bf16[400,512]{1,0:T(8,128)(2,1)}, bf16[400,512]{1,0:T(8,128)(2,1)S(1)}, u32[]{:S(2)}, u32[]{:S(2)}) collective-permute-start(bf16[400,512]{1,0:T(8,128)(2,1)} %get-tuple-element.143), channel_id=1, source_target_pairs={{0,16},{4,20},{8,24},{12,28},{16,0},{20,4},{24,8},{28,12},{32,48},... | collective-permute-start | bytes 1228808 | tf_op jit(solution)/shard_map/ppermute | solution.py:64
  129.5 8.8 %collective-permute-start.19 = (bf16[384,512]{1,0:T(8,128)(2,1)}, bf16[384,512]{1,0:T(8,128)(2,1)S(1)}, u32[]{:S(2)}, u32[]{:S(2)}) collective-permute-start(bf16[384,512]{1,0:T(8,128)(2,1)} %get-tuple-element.146), channel_id=1, source_target_pairs={{0,64},{4,68},{8,72},{12,76},{16,80},{20,84},{24,88},{28,92},{32,9... | collective-permute-start | bytes 1179656 | tf_op jit(solution)/shard_map/ppermute | solution.py:64
  129.5 17.2 %collective-permute-start.20 = (bf16[384,512]{1,0:T(8,128)(2,1)}, bf16[384,512]{1,0:T(8,128)(2,1)S(1)}, u32[]{:S(2)}, u32[]{:S(2)}) collective-permute-start(bf16[384,512]{1,0:T(8,128)(2,1)} %get-tuple-element.147), channel_id=1, source_target_pairs={{0,64},{4,68},{8,72},{12,76},{16,80},{20,84},{24,88},{28,92},{32,9... | collective-permute-start | bytes 1179656 | tf_op jit(solution)/shard_map/ppermute | solution.py:64
  134.5 39.3 %collective-permute-start.17 = (bf16[400,512]{1,0:T(8,128)(2,1)}, bf16[400,512]{1,0:T(8,128)(2,1)S(1)}, u32[]{:S(2)}, u32[]{:S(2)}) collective-permute-start(bf16[400,512]{1,0:T(8,128)(2,1)} %get-tuple-element.139), channel_id=1, source_target_pairs={{0,24},{4,28},{8,0},{12,4},{16,8},{20,12},{24,16},{28,20},{32,56},... | collective-permute-start | bytes 1228808 | tf_op jit(solution)/shard_map/ppermute | solution.py:64
  135.9 38.7 %collective-permute-start.22 = (bf16[400,512]{1,0:T(8,128)(2,1)}, bf16[400,512]{1,0:T(8,128)(2,1)S(1)}, u32[]{:S(2)}, u32[]{:S(2)}) collective-permute-start(bf16[400,512]{1,0:T(8,128)(2,1)} %get-tuple-element.149), channel_id=1, source_target_pairs={{0,8},{4,12},{8,16},{12,20},{16,24},{20,28},{24,0},{28,4},{32,40},... | collective-permute-start | bytes 1228808 | tf_op jit(solution)/shard_map/ppermute | solution.py:64
  147.5 30.2 %collective-permute-start.21 = (bf16[400,512]{1,0:T(8,128)(2,1)}, bf16[400,512]{1,0:T(8,128)(2,1)S(1)}, u32[]{:S(2)}, u32[]{:S(2)}) collective-permute-start(bf16[400,512]{1,0:T(8,128)(2,1)} %get-tuple-element.148), channel_id=1, source_target_pairs={{0,16},{4,20},{8,24},{12,28},{16,0},{20,4},{24,8},{28,12},{32,48},... | collective-permute-start | bytes 1228808 | tf_op jit(solution)/shard_map/ppermute | solution.py:64
  150.3 24.2 %collective-permute-start.23 = (bf16[384,512]{1,0:T(8,128)(2,1)}, bf16[384,512]{1,0:T(8,128)(2,1)S(1)}, u32[]{:S(2)}, u32[]{:S(2)}) collective-permute-start(bf16[384,512]{1,0:T(8,128)(2,1)} %get-tuple-element.151), channel_id=1, source_target_pairs={{0,96},{4,100},{8,104},{12,108},{16,112},{20,116},{24,120},{28,124... | collective-permute-start | bytes 1179656 | tf_op jit(solution)/shard_map/ppermute | solution.py:64
  150.3 25.9 %collective-permute-start.24 = (bf16[384,512]{1,0:T(8,128)(2,1)}, bf16[384,512]{1,0:T(8,128)(2,1)S(1)}, u32[]{:S(2)}, u32[]{:S(2)}) collective-permute-start(bf16[384,512]{1,0:T(8,128)(2,1)} %get-tuple-element.152), channel_id=1, source_target_pairs={{0,32},{4,36},{8,40},{12,44},{16,48},{20,52},{24,56},{28,60},{32,6... | collective-permute-start | bytes 1179656 | tf_op jit(solution)/shard_map/ppermute | solution.py:64
  173.9 27.9 %collective-permute-start.25 = (bf16[400,512]{1,0:T(8,128)(2,1)}, bf16[400,512]{1,0:T(8,128)(2,1)S(1)}, u32[]{:S(2)}, u32[]{:S(2)}) collective-permute-start(bf16[400,512]{1,0:T(8,128)(2,1)} %get-tuple-element.160), channel_id=1, source_target_pairs={{0,24},{4,28},{8,0},{12,4},{16,8},{20,12},{24,16},{28,20},{32,56},... | collective-permute-start | bytes 1228808 | tf_op jit(solution)/shard_map/ppermute | solution.py:64
  174.5 27.3 %collective-permute-start.26 = (bf16[400,512]{1,0:T(8,128)(2,1)}, bf16[400,512]{1,0:T(8,128)(2,1)S(1)}, u32[]{:S(2)}, u32[]{:S(2)}) collective-permute-start(bf16[400,512]{1,0:T(8,128)(2,1)} %get-tuple-element.161), channel_id=1, source_target_pairs={{0,16},{4,20},{8,24},{12,28},{16,0},{20,4},{24,8},{28,12},{32,48},... | collective-permute-start | bytes 1228808 | tf_op jit(solution)/shard_map/ppermute | solution.py:64
  175.4 26.4 %collective-permute-start.27 = (bf16[400,512]{1,0:T(8,128)(2,1)}, bf16[400,512]{1,0:T(8,128)(2,1)S(1)}, u32[]{:S(2)}, u32[]{:S(2)}) collective-permute-start(bf16[400,512]{1,0:T(8,128)(2,1)} %get-tuple-element.162), channel_id=1, source_target_pairs={{0,8},{4,12},{8,16},{12,20},{16,24},{20,28},{24,0},{28,4},{32,40},... | collective-permute-start | bytes 1228808 | tf_op jit(solution)/shard_map/ppermute | solution.py:64
  176.9 24.8 %collective-permute-start.28 = (bf16[384,512]{1,0:T(8,128)(2,1)}, bf16[384,512]{1,0:T(8,128)(2,1)S(1)}, u32[]{:S(2)}, u32[]{:S(2)}) collective-permute-start(bf16[384,512]{1,0:T(8,128)(2,1)} %get-tuple-element.169), channel_id=1, source_target_pairs={{0,32},{4,36},{8,40},{12,44},{16,48},{20,52},{24,56},{28,60},{32,6... | collective-permute-start | bytes 1179656 | tf_op jit(solution)/shard_map/ppermute | solution.py:64
  177.6 24.1 %collective-permute-start.29 = (bf16[384,512]{1,0:T(8,128)(2,1)}, bf16[384,512]{1,0:T(8,128)(2,1)S(1)}, u32[]{:S(2)}, u32[]{:S(2)}) collective-permute-start(bf16[384,512]{1,0:T(8,128)(2,1)} %get-tuple-element.170), channel_id=1, source_target_pairs={{0,96},{4,100},{8,104},{12,108},{16,112},{20,116},{24,120},{28,124... | collective-permute-start | bytes 1179656 | tf_op jit(solution)/shard_map/ppermute | solution.py:64
  203.3 14.7 %collective-permute-start.30 = (bf16[400,512]{1,0:T(8,128)(2,1)}, bf16[400,512]{1,0:T(8,128)(2,1)S(1)}, u32[]{:S(2)}, u32[]{:S(2)}) collective-permute-start(bf16[400,512]{1,0:T(8,128)(2,1)} %get-tuple-element.171), channel_id=1, source_target_pairs={{0,24},{4,28},{8,0},{12,4},{16,8},{20,12},{24,16},{28,20},{32,56},... | collective-permute-start | bytes 1228808 | tf_op jit(solution)/shard_map/ppermute | solution.py:64
  206.1 12.0 %collective-permute-start.31 = (bf16[400,512]{1,0:T(8,128)(2,1)}, bf16[400,512]{1,0:T(8,128)(2,1)S(1)}, u32[]{:S(2)}, u32[]{:S(2)}) collective-permute-start(bf16[400,512]{1,0:T(8,128)(2,1)} %get-tuple-element.178), channel_id=1, source_target_pairs={{0,8},{4,12},{8,16},{12,20},{16,24},{20,28},{24,0},{28,4},{32,40},... | collective-permute-start | bytes 1228808 | tf_op jit(solution)/shard_map/ppermute | solution.py:64
  206.1 11.9 %collective-permute-start.32 = (bf16[384,512]{1,0:T(8,128)(2,1)}, bf16[384,512]{1,0:T(8,128)(2,1)S(1)}, u32[]{:S(2)}, u32[]{:S(2)}) collective-permute-start(bf16[384,512]{1,0:T(8,128)(2,1)} %get-tuple-element.179), channel_id=1, source_target_pairs={{0,32},{4,36},{8,40},{12,44},{16,48},{20,52},{24,56},{28,60},{32,6... | collective-permute-start | bytes 1179656 | tf_op jit(solution)/shard_map/ppermute | solution.py:64
  206.1 11.9 %collective-permute-start.33 = (bf16[384,512]{1,0:T(8,128)(2,1)}, bf16[384,512]{1,0:T(8,128)(2,1)S(1)}, u32[]{:S(2)}, u32[]{:S(2)}) collective-permute-start(bf16[384,512]{1,0:T(8,128)(2,1)} %get-tuple-element.180), channel_id=1, source_target_pairs={{0,96},{4,100},{8,104},{12,108},{16,112},{20,116},{24,120},{28,124... | collective-permute-start | bytes 1179656 | tf_op jit(solution)/shard_map/ppermute | solution.py:64
  219.2 18.2 %collective-permute-start.34 = (bf16[400,512]{1,0:T(8,128)(2,1)}, bf16[400,512]{1,0:T(8,128)(2,1)S(1)}, u32[]{:S(2)}, u32[]{:S(2)}) collective-permute-start(bf16[400,512]{1,0:T(8,128)(2,1)} %get-tuple-element.181), channel_id=1, source_target_pairs={{0,16},{4,20},{8,24},{12,28},{16,0},{20,4},{24,8},{28,12},{32,48},... | collective-permute-start | bytes 1228808 | tf_op jit(solution)/shard_map/ppermute | solution.py:64
  221.8 15.6 %collective-permute-start.35 = (bf16[384,512]{1,0:T(8,128)(2,1)S(1)}, bf16[384,512]{1,0:T(8,128)(2,1)S(1)}, u32[]{:S(2)}, u32[]{:S(2)}) collective-permute-start(bf16[384,512]{1,0:T(8,128)(2,1)S(1)} %copy-done.42), channel_id=1, source_target_pairs={{0,64},{4,68},{8,72},{12,76},{16,80},{20,84},{24,88},{28,92},{32,9... | collective-permute-start | bytes 1179656 | tf_op jit(solution)/shard_map/ppermute | solution.py:64
  221.8 15.6 %collective-permute-start.36 = (bf16[384,512]{1,0:T(8,128)(2,1)}, bf16[384,512]{1,0:T(8,128)(2,1)S(1)}, u32[]{:S(2)}, u32[]{:S(2)}) collective-permute-start(bf16[384,512]{1,0:T(8,128)(2,1)} %get-tuple-element.185), channel_id=1, source_target_pairs={{0,64},{4,68},{8,72},{12,76},{16,80},{20,84},{24,88},{28,92},{32,9... | collective-permute-start | bytes 1179656 | tf_op jit(solution)/shard_map/ppermute | solution.py:64
  224.7 25.8 %collective-permute-start.43 = (bf16[1536,1024]{1,0:T(8,128)(2,1)}, bf16[1536,1024]{1,0:T(8,128)(2,1)S(1)}, u32[]{:S(2)}, u32[]{:S(2)}) collective-permute-start(bf16[1536,1024]{1,0:T(8,128)(2,1)} %get-tuple-element.198), channel_id=1, source_target_pairs={{0,4},{4,0},{8,12},{12,8},{16,20},{20,16},{24,28},{28,24},{32,36},... | collective-permute-start | bytes 9437192 | tf_op jit(solution)/shard_map/ppermute | solution.py:64
  244.2 19.6 %collective-permute-start.37 = (bf16[272,512]{1,0:T(8,128)(2,1)}, bf16[272,512]{1,0:T(8,128)(2,1)S(1)}, u32[]{:S(2)}, u32[]{:S(2)}) collective-permute-start(bf16[272,512]{1,0:T(8,128)(2,1)} %get-tuple-element.187), channel_id=1, source_target_pairs={{0,96},{4,100},{8,104},{12,108},{16,112},{20,116},{24,120},{28,124... | collective-permute-start | bytes 835592 | tf_op jit(solution)/shard_map/ppermute | solution.py:64
  247.5 16.2 %collective-permute-start.38 = (bf16[272,512]{1,0:T(8,128)(2,1)}, bf16[272,512]{1,0:T(8,128)(2,1)S(1)}, u32[]{:S(2)}, u32[]{:S(2)}) collective-permute-start(bf16[272,512]{1,0:T(8,128)(2,1)} %get-tuple-element.188), channel_id=1, source_target_pairs={{0,64},{4,68},{8,72},{12,76},{16,80},{20,84},{24,88},{28,92},{32,9... | collective-permute-start | bytes 835592 | tf_op jit(solution)/shard_map/ppermute | solution.py:64
  247.5 16.3 %collective-permute-start.39 = (bf16[272,512]{1,0:T(8,128)(2,1)}, bf16[272,512]{1,0:T(8,128)(2,1)S(1)}, u32[]{:S(2)}, u32[]{:S(2)}) collective-permute-start(bf16[272,512]{1,0:T(8,128)(2,1)} %get-tuple-element.189), channel_id=1, source_target_pairs={{0,32},{4,36},{8,40},{12,44},{16,48},{20,52},{24,56},{28,60},{32,6... | collective-permute-start | bytes 835592 | tf_op jit(solution)/shard_map/ppermute | solution.py:64
  249.6 14.1 %collective-permute-start.41 = (bf16[256,512]{1,0:T(8,128)(2,1)}, bf16[256,512]{1,0:T(8,128)(2,1)S(1)}, u32[]{:S(2)}, u32[]{:S(2)}) collective-permute-start(bf16[256,512]{1,0:T(8,128)(2,1)} %get-tuple-element.192), channel_id=1, source_target_pairs={{0,16},{4,20},{8,24},{12,28},{16,0},{20,4},{24,8},{28,12},{32,48},... | collective-permute-start | bytes 786440 | tf_op jit(solution)/shard_map/ppermute | solution.py:64
  250.5 13.2 %collective-permute-start.42 = (bf16[256,512]{1,0:T(8,128)(2,1)}, bf16[256,512]{1,0:T(8,128)(2,1)S(1)}, u32[]{:S(2)}, u32[]{:S(2)}) collective-permute-start(bf16[256,512]{1,0:T(8,128)(2,1)} %get-tuple-element.193), channel_id=1, source_target_pairs={{0,8},{4,12},{8,16},{12,20},{16,24},{20,28},{24,0},{28,4},{32,40},... | collective-permute-start | bytes 786440 | tf_op jit(solution)/shard_map/ppermute | solution.py:64
  264.8 109.4 %all-to-all-start = ((bf16[16,192,1024]{2,1,0:T(8,128)(2,1)}), bf16[16,192,1024]{2,1,0:T(8,128)(2,1)}, u32[]{:S(2)}, u32[]{:S(2)}) async-start(bf16[16,192,1024]{2,1,0:T(8,128)(2,1)} %after.15), calls=%async_computation | async-start | bytes 12582912 | tf_op jit(solution)/shard_map/all_to_all | solution.py:1020
  277.0 12.3 %collective-permute-start.44 = (bf16[256,1024]{1,0:T(8,128)(2,1)}, bf16[256,1024]{1,0:T(8,128)(2,1)S(1)}, u32[]{:S(2)}, u32[]{:S(2)}) collective-permute-start(bf16[256,1024]{1,0:T(8,128)(2,1)} %get-tuple-element.204.refs_1_), channel_id=1, source_target_pairs={{0,3},{1,0},{2,1},{3,2},{4,7},{5,4},{6,5},{7,6},{8,11},{9,8},{10,9... | collective-permute-start | bytes 1572872 | tf_op jit(solution)/shard_map/ppermute | solution.py:70
  278.0 11.4 %collective-permute-start.46 = (bf16[256,1024]{1,0:T(8,128)(2,1)}, bf16[256,1024]{1,0:T(8,128)(2,1)S(1)}, u32[]{:S(2)}, u32[]{:S(2)}) collective-permute-start(bf16[256,1024]{1,0:T(8,128)(2,1)} %get-tuple-element.204.refs_1_), channel_id=1, source_target_pairs={{0,1},{1,2},{2,3},{3,0},{4,5},{5,6},{6,7},{7,4},{8,9},{9,10},{10,1... | collective-permute-start | bytes 1572872 | tf_op jit(solution)/shard_map/ppermute | solution.py:70
  289.5 9.4 %collective-permute-start.47 = (bf16[128,1024]{1,0:T(8,128)(2,1)S(1)}, bf16[128,1024]{1,0:T(8,128)(2,1)S(1)}, u32[]{:S(2)}, u32[]{:S(2)}) collective-permute-start(bf16[128,1024]{1,0:T(8,128)(2,1)S(1)} %slice.17), channel_id=1, source_target_pairs={{0,1},{1,2},{2,3},{3,0},{4,5},{5,6},{6,7},{7,4},{8,9},{9,10},{10,1... | collective-permute-start | bytes 786440 | tf_op jit(solution)/shard_map/ppermute | solution.py:70
  291.0 13.1 %collective-permute-start.48 = (f32[40,1024]{1,0:T(8,128)}, f32[40,1024]{1,0:T(8,128)S(1)}, u32[]{:S(2)}, u32[]{:S(2)}) collective-permute-start(f32[40,1024]{1,0:T(8,128)} %get-tuple-element.206.refs_4_), channel_id=1, source_target_pairs={{0,1},{1,2},{2,3},{3,0},{4,5},{5,6},{6,7},{7,4},{8,9},{9,10},{10,1... | collective-permute-start | bytes 491528 | tf_op jit(solution)/shard_map/ppermute | solution.py:70
  292.3 11.8 %collective-permute-start.49 = (f32[40,1024]{1,0:T(8,128)}, f32[40,1024]{1,0:T(8,128)S(1)}, u32[]{:S(2)}, u32[]{:S(2)}) collective-permute-start(f32[40,1024]{1,0:T(8,128)} %get-tuple-element.206.refs_4_), channel_id=1, source_target_pairs={{0,2},{1,3},{2,0},{3,1},{4,6},{5,7},{6,4},{7,5},{8,10},{9,11},{10,... | collective-permute-start | bytes 491528 | tf_op jit(solution)/shard_map/ppermute | solution.py:70
  293.4 10.7 %collective-permute-start.50 = (f32[40,1024]{1,0:T(8,128)}, f32[40,1024]{1,0:T(8,128)S(1)}, u32[]{:S(2)}, u32[]{:S(2)}) collective-permute-start(f32[40,1024]{1,0:T(8,128)} %get-tuple-element.206.refs_4_), channel_id=1, source_target_pairs={{0,3},{1,0},{2,1},{3,2},{4,7},{5,4},{6,5},{7,6},{8,11},{9,8},{10,9... | collective-permute-start | bytes 491528 | tf_op jit(solution)/shard_map/ppermute | solution.py:70
  309.1 112.0 %all-reduce.2.cloned.1.call-start = ((), (), s32[]{:S(2)}) async-start(), calls=%async_computation.1 | async-start | bytes 6291456 | tf_op jit(solution)/shard_map/psum | solution.py:1025
  330.4 20.7 %collective-permute-start.51 = (bf16[832,512]{1,0:T(8,128)(2,1)}, bf16[832,512]{1,0:T(8,128)(2,1)S(1)}, u32[]{:S(2)}, u32[]{:S(2)}) collective-permute-start(bf16[832,512]{1,0:T(8,128)(2,1)} %get-tuple-element.217), channel_id=1, source_target_pairs={{0,4},{4,0},{8,12},{12,8},{16,20},{20,16},{24,28},{28,24},{32,36},... | collective-permute-start | bytes 2555912 | tf_op jit(solution)/shard_map/ppermute | solution.py:64
  354.7 13.5 %collective-permute-start.55 = (bf16[128,1024]{1,0:T(8,128)(2,1)}, bf16[128,1024]{1,0:T(8,128)(2,1)S(1)}, u32[]{:S(2)}, u32[]{:S(2)}) collective-permute-start(bf16[128,1024]{1,0:T(8,128)(2,1)} %get-tuple-element.223), channel_id=1, source_target_pairs={{0,1},{1,2},{2,3},{3,0},{4,5},{5,6},{6,7},{7,4},{8,9},{9,10},{10,1... | collective-permute-start | bytes 786440 | tf_op jit(solution)/shard_map/ppermute | solution.py:70
  355.6 12.7 %collective-permute-start.56 = (bf16[128,1024]{1,0:T(8,128)(2,1)}, bf16[128,1024]{1,0:T(8,128)(2,1)S(1)}, u32[]{:S(2)}, u32[]{:S(2)}) collective-permute-start(bf16[128,1024]{1,0:T(8,128)(2,1)} %get-tuple-element.224), channel_id=1, source_target_pairs={{0,3},{1,0},{2,1},{3,2},{4,7},{5,4},{6,5},{7,6},{8,11},{9,8},{10,9... | collective-permute-start | bytes 786440 | tf_op jit(solution)/shard_map/ppermute | solution.py:70
  357.4 16.7 %collective-permute-start.59 = (bf16[208,512]{1,0:T(8,128)(2,1)}, bf16[208,512]{1,0:T(8,128)(2,1)S(1)}, u32[]{:S(2)}, u32[]{:S(2)}) collective-permute-start(bf16[208,512]{1,0:T(8,128)(2,1)} %get-tuple-element.228), channel_id=1, source_target_pairs={{0,8},{4,12},{8,16},{12,20},{16,24},{20,28},{24,0},{28,4},{32,40},... | collective-permute-start | bytes 638984 | tf_op jit(solution)/shard_map/ppermute | solution.py:64
  358.8 15.4 %collective-permute-start.60 = (bf16[208,512]{1,0:T(8,128)(2,1)}, bf16[208,512]{1,0:T(8,128)(2,1)S(1)}, u32[]{:S(2)}, u32[]{:S(2)}) collective-permute-start(bf16[208,512]{1,0:T(8,128)(2,1)} %get-tuple-element.229), channel_id=1, source_target_pairs={{0,16},{4,20},{8,24},{12,28},{16,0},{20,4},{24,8},{28,12},{32,48},... | collective-permute-start | bytes 638984 | tf_op jit(solution)/shard_map/ppermute | solution.py:64
  361.1 13.0 %collective-permute-start.61 = (bf16[208,512]{1,0:T(8,128)(2,1)}, bf16[208,512]{1,0:T(8,128)(2,1)S(1)}, u32[]{:S(2)}, u32[]{:S(2)}) collective-permute-start(bf16[208,512]{1,0:T(8,128)(2,1)} %get-tuple-element.230), channel_id=1, source_target_pairs={{0,24},{4,28},{8,0},{12,4},{16,8},{20,12},{24,16},{28,20},{32,56},... | collective-permute-start | bytes 638984 | tf_op jit(solution)/shard_map/ppermute | solution.py:64
  371.5 24.9 %collective-permute-start.57 = (bf16[256,1024]{1,0:T(8,128)(2,1)}, bf16[256,1024]{1,0:T(8,128)(2,1)S(1)}, u32[]{:S(2)}, u32[]{:S(2)}) collective-permute-start(bf16[256,1024]{1,0:T(8,128)(2,1)} %get-tuple-element.225), channel_id=1, source_target_pairs={{0,1},{1,2},{2,3},{3,0},{4,5},{5,6},{6,7},{7,4},{8,9},{9,10},{10,1... | collective-permute-start | bytes 1572872 | tf_op jit(solution)/shard_map/ppermute | solution.py:70
  371.5 24.9 %collective-permute-start.58 = (bf16[256,1024]{1,0:T(8,128)(2,1)}, bf16[256,1024]{1,0:T(8,128)(2,1)S(1)}, u32[]{:S(2)}, u32[]{:S(2)}) collective-permute-start(bf16[256,1024]{1,0:T(8,128)(2,1)} %get-tuple-element.226), channel_id=1, source_target_pairs={{0,3},{1,0},{2,1},{3,2},{4,7},{5,4},{6,5},{7,6},{8,11},{9,8},{10,9... | collective-permute-start | bytes 1572872 | tf_op jit(solution)/shard_map/ppermute | solution.py:70
  377.0 11.3 %collective-permute-start.62 = (bf16[208,512]{1,0:T(8,128)(2,1)}, bf16[208,512]{1,0:T(8,128)(2,1)S(1)}, u32[]{:S(2)}, u32[]{:S(2)}) collective-permute-start(bf16[208,512]{1,0:T(8,128)(2,1)} %shard_map.223.refs_1_), channel_id=1, source_target_pairs={{0,32},{4,36},{8,40},{12,44},{16,48},{20,52},{24,56},{28,60},{32,6... | collective-permute-start | bytes 638984 | tf_op jit(solution)/shard_map/ppermute | solution.py:64
  378.3 11.1 %collective-permute-start.63 = (bf16[208,512]{1,0:T(8,128)(2,1)}, bf16[208,512]{1,0:T(8,128)(2,1)S(1)}, u32[]{:S(2)}, u32[]{:S(2)}) collective-permute-start(bf16[208,512]{1,0:T(8,128)(2,1)} %shard_map.223.refs_1_), channel_id=1, source_target_pairs={{0,64},{4,68},{8,72},{12,76},{16,80},{20,84},{24,88},{28,92},{32,9... | collective-permute-start | bytes 638984 | tf_op jit(solution)/shard_map/ppermute | solution.py:64
  380.9 8.5 %collective-permute-start.64 = (bf16[208,512]{1,0:T(8,128)(2,1)}, bf16[208,512]{1,0:T(8,128)(2,1)S(1)}, u32[]{:S(2)}, u32[]{:S(2)}) collective-permute-start(bf16[208,512]{1,0:T(8,128)(2,1)} %shard_map.223.refs_1_), channel_id=1, source_target_pairs={{0,96},{4,100},{8,104},{12,108},{16,112},{20,116},{24,120},{28,124... | collective-permute-start | bytes 638984 | tf_op jit(solution)/shard_map/ppermute | solution.py:64
  392.8 8.1 %collective-permute-start.65 = (bf16[208,512]{1,0:T(8,128)(2,1)}, bf16[208,512]{1,0:T(8,128)(2,1)S(1)}, u32[]{:S(2)}, u32[]{:S(2)}) collective-permute-start(bf16[208,512]{1,0:T(8,128)(2,1)} %shard_map.224.refs_1_), channel_id=1, source_target_pairs={{0,24},{4,28},{8,0},{12,4},{16,8},{20,12},{24,16},{28,20},{32,56},... | collective-permute-start | bytes 638984 | tf_op jit(solution)/shard_map/ppermute | solution.py:64
  395.8 11.7 %collective-permute-start.67 = (bf16[208,512]{1,0:T(8,128)(2,1)}, bf16[208,512]{1,0:T(8,128)(2,1)S(1)}, u32[]{:S(2)}, u32[]{:S(2)}) collective-permute-start(bf16[208,512]{1,0:T(8,128)(2,1)} %shard_map.224.refs_1_), channel_id=1, source_target_pairs={{0,8},{4,12},{8,16},{12,20},{16,24},{20,28},{24,0},{28,4},{32,40},... | collective-permute-start | bytes 638984 | tf_op jit(solution)/shard_map/ppermute | solution.py:64
  (81 other events, 274.0 us)
Sparse Core Ops, SparseCore 0:
  10.2 74.0 all-gather.2
  312.3 100.0 all-reduce.1
